TPU v7x, 32 devices: a whole 2x2x4 slice. The times are simulated.
32 devices in a mesh: dp: 2 (over x), expert: 16 (over z, y, core).
Axes of the slice: x: 2, y: 2, z: 4, core: 2. Of those that a mesh axis runs over, the one named last changes fastest.
Arguments:
- tokens: bfloat16 [4096, 1024], P(('dp', 'expert')), may hold values from -6 to 6
- d_output: bfloat16 [4096, 1024], P(('dp', 'expert')), may hold values from -6 to 6
- combine: float32 [4096, 8], P(('dp', 'expert')), may hold values from 0.05 to 1
- routes: int32 [4096, 8], P(('dp', 'expert')), may hold values from 0 to 15, all different within a row; in each aligned block of 128 rows (0 to 127, 128 to 255, ...) at most 72 rows name the same one
- gate_weight: bfloat16 [16, 1024, 384], P('expert', 'dp'), may hold values from -0.1875 to 0.1875
- up_weight: bfloat16 [16, 1024, 384], P('expert', 'dp'), may hold values from -0.1875 to 0.1875
- down_weight: bfloat16 [16, 384, 1024], P('expert', None, 'dp'), may hold values from -0.3125 to 0.3125
Outputs:
- d_tokens: bfloat16 [4096, 1024], P(('dp', 'expert'))
- d_gate_weight: float32 [16, 1024, 384], P('expert', 'dp')
- d_up_weight: float32 [16, 1024, 384], P('expert', 'dp')
- d_down_weight: float32 [16, 384, 1024], P('expert', None, 'dp')
Inputs may be any that keep to these rules, and one draw needn't show every extreme that they name: `routes`: among the 128 tokens of one device, each expert id is named by at most 72 rows; some expert is named by exactly 72 rows on some device. The ids of one token differ.
All inputs are finite; a program needn't handle non-finite values.
Results may differ from a plain program's by a relative error of at most 0.015.
Values may be sent and summed in bfloat16 or wider, within the bound.
No kernel may reach another device: no remote copies, remote signals or barrier semaphores. Data moves between devices by JAX's collectives and lax.ppermute only.
A program may use at most 64 MiB of HBM per device.

v0:
```python
import jax
import jax.numpy as jnp
from jax import lax
from jax.sharding import PartitionSpec as P


def route_slots(routes, experts):
    matches = (routes[:, :, None] == jnp.arange(experts, dtype=jnp.int32)[None, None, :]).astype(
        jnp.int32
    )
    per_token = jnp.sum(matches, axis=1)
    earlier = jnp.cumsum(per_token, axis=0) - per_token
    return jnp.sum(matches * earlier[:, None, :], axis=2)


def row_work(row_inputs, row_grads, gate_up, down_matrix):
    hidden_units = down_matrix.shape[0]
    preact = jnp.dot(row_inputs, gate_up, preferred_element_type=jnp.float32)
    gate_pre = preact[:, :hidden_units]
    up_pre = preact[:, hidden_units:]
    gate_sigmoid = jax.nn.sigmoid(gate_pre)
    hidden = (gate_pre * gate_sigmoid * up_pre).astype(jnp.bfloat16)
    d_hidden = jnp.dot(row_grads, down_matrix.T, preferred_element_type=jnp.float32)
    d_gate_pre = d_hidden * up_pre * gate_sigmoid * (1.0 + gate_pre * (1.0 - gate_sigmoid))
    d_up_pre = d_hidden * gate_pre * gate_sigmoid
    d_preact = jnp.concatenate([d_gate_pre, d_up_pre], axis=1).astype(jnp.bfloat16)
    d_rows = jnp.dot(d_preact, gate_up.T, preferred_element_type=jnp.float32).astype(jnp.bfloat16)
    return (d_rows, hidden, d_preact)


def body(tokens, d_output, combine, routes, gate_weight, up_weight, down_weight):
    experts = lax.axis_size("expert")
    tok_count = tokens.shape[0]
    model_width = tokens.shape[1]
    top_count = routes.shape[1]
    capacity = max(2, (9 * tok_count * top_count + 8 * experts - 1) // (8 * experts))
    slot_count = experts * capacity
    slot_index = route_slots(routes, experts)
    position = (routes * capacity + slot_index).reshape(-1)
    spread_inputs = jnp.repeat(tokens, top_count, axis=0)
    scaled = (
        (combine[:, :, None] * d_output[:, None, :].astype(jnp.float32))
        .astype(jnp.bfloat16)
        .reshape(-1, model_width)
    )
    send_inputs = (
        jnp.zeros((slot_count, model_width), jnp.bfloat16)
        .at[position]
        .set(spread_inputs)
        .reshape(experts, capacity, model_width)
    )
    send_grads = (
        jnp.zeros((slot_count, model_width), jnp.bfloat16)
        .at[position]
        .set(scaled)
        .reshape(experts, capacity, model_width)
    )
    whole_gate, whole_up, whole_down = (
        lax.all_gather(gate_weight, "dp", axis=1, tiled=True),
        lax.all_gather(up_weight, "dp", axis=1, tiled=True),
        lax.all_gather(down_weight, "dp", axis=2, tiled=True),
    )
    gate_up = jnp.concatenate([whole_gate[0], whole_up[0]], axis=1)
    down_matrix = whole_down[0]
    hidden_units = down_matrix.shape[0]
    recv_inputs, recv_grads = (
        lax.all_to_all(send_inputs, "expert", split_axis=0, concat_axis=0, tiled=True),
        lax.all_to_all(send_grads, "expert", split_axis=0, concat_axis=0, tiled=True),
    )
    flat_inputs = recv_inputs.reshape(-1, model_width)
    flat_grads = recv_grads.reshape(-1, model_width)
    d_rows, hidden, d_preact = row_work(flat_inputs, flat_grads, gate_up, down_matrix)
    returned = lax.all_to_all(
        d_rows.reshape(experts, capacity, model_width),
        "expert",
        split_axis=0,
        concat_axis=0,
        tiled=True,
    )
    route_rows = returned.reshape(-1, model_width)[position].reshape(
        tok_count, top_count, model_width
    )
    d_tokens = jnp.sum(route_rows.astype(jnp.float32), axis=1).astype(jnp.bfloat16)
    gate_up_grad = jnp.dot(flat_inputs.T, d_preact, preferred_element_type=jnp.float32)
    down_grad = jnp.dot(flat_grads.T, hidden, preferred_element_type=jnp.float32)
    stacked = jnp.concatenate([gate_up_grad, down_grad], axis=1)
    summed = lax.psum_scatter(
        stacked.astype(jnp.bfloat16), "dp", scatter_dimension=0, tiled=True
    ).astype(jnp.float32)
    d_gate_weight = summed[:, :hidden_units][None]
    d_up_weight = summed[:, hidden_units : 2 * hidden_units][None]
    d_down_weight = summed[:, 2 * hidden_units :].T[None]
    return (d_tokens, d_gate_weight, d_up_weight, d_down_weight)


def solution(mesh):
    placed = (
        P(("dp", "expert"), None),
        P(("dp", "expert"), None),
        P(("dp", "expert"), None),
        P(("dp", "expert"), None),
        P("expert", "dp", None),
        P("expert", "dp", None),
        P("expert", None, "dp"),
    )
    return jax.shard_map(
        body,
        mesh=mesh,
        in_specs=placed,
        out_specs=(
            P(("dp", "expert"), None),
            P("expert", "dp", None),
            P("expert", "dp", None),
            P("expert", None, "dp"),
        ),
        check_vma=False,
    )
```

profile of v0, /device:TPU:15, one launch (start us, length us, event | category | flops | bytes accessed | tf_op | source)
XLA Modules:
  0.0 230.8 jit_solution(1077959032336873731)
XLA Ops:
  7.2 0.7 convert_reduce_fusion
  7.9 0.1 copy.19
  8.0 0.2 reduce_window_sum.11
  8.3 0.7 select_reduce_fusion
  9.0 0.7 multiply_add_fusion
  9.7 0.1 copy.22
  9.9 7.0 %scatter_custom_fusion.1 = bf16[1152,1024]{1,0:T(8,128)(2,1)} fusion(s32[1024]{0:T(1024)S(1)} %bitcast.44, bf16[]{:T(256)} %constant.5.clone.1, bf16[128,1024]{1,0:T(8,128)(2,1)S(1)} %copy-done), kind=kCustom, calls=%fused_computation.9 | custom fusion | bytes 2621442 | tf_op jit(solution)/shard_map/scatter | solution.py:49
  16.9 6.7 %all-to-all-start.1 = ((bf16[16,72,1024]{2,1,0:T(8,128)(2,1)}), bf16[16,72,1024]{2,1,0:T(8,128)(2,1)S(1)}, u32[]{:S(2)}, u32[]{:S(2)}) async-start(bf16[16,72,1024]{2,1,0:T(8,128)(2,1)} %bitcast.6), calls=%async_computation.1 | async-start | bytes 4718592 | tf_op jit(solution)/shard_map/all_to_all | solution.py:67
  23.6 0.1 copy.23
  23.8 7.4 %scatter_custom_fusion = bf16[1152,1024]{1,0:T(8,128)(2,1)} fusion(s32[1024]{0:T(1024)S(1)} %bitcast.45, f32[128,1024]{1,0:T(8,128)S(1)} %convert_element_type.25, f32[1024]{0:T(1024)S(1)} %mul.60, bf16[]{:T(256)} %constant.5.clone.1), kind=kCustom, calls=%fused_computation.7 | custom fusion | flops 2097152 | bytes 2887682 | tf_op jit(solution)/shard_map/scatter | solution.py:55
  31.2 45.4 %all-to-all-done.1 = bf16[16,72,1024]{2,1,0:T(8,128)(2,1)S(1)} async-done(((bf16[16,72,1024]{2,1,0:T(8,128)(2,1)}), bf16[16,72,1024]{2,1,0:T(8,128)(2,1)S(1)}, u32[]{:S(2)}, u32[]{:S(2)}) %all-to-all-start.1) | async-done | bytes 2359328 | tf_op jit(solution)/shard_map/all_to_all | solution.py:67
  76.6 4.9 %all-to-all-start = ((bf16[16,72,1024]{2,1,0:T(8,128)(2,1)}), bf16[16,72,1024]{2,1,0:T(8,128)(2,1)}, u32[]{:S(2)}, u32[]{:S(2)}) async-start(bf16[16,72,1024]{2,1,0:T(8,128)(2,1)} %bitcast.2), calls=%async_computation | async-start | bytes 4718592 | tf_op jit(solution)/shard_map/all_to_all | solution.py:68
  81.6 11.5 %all_gather.10 = bf16[1,1024,384]{2,1,0:T(8,128)(2,1)S(1)} all-gather(bf16[1,512,384]{2,1,0:T(8,128)(2,1)} %param.11), channel_id=1, replica_groups=mesh['dp'=2,'expert'=16] {'dp'}, dimensions={1}, use_global_device_ids=true | all-gather | bytes 1179648 | tf_op jit(solution)/shard_map/all_gather | solution.py:59
  93.0 10.5 %all_gather.11 = bf16[1,1024,384]{2,1,0:T(8,128)(2,1)S(1)} all-gather(bf16[1,512,384]{2,1,0:T(8,128)(2,1)} %param.12), channel_id=1, replica_groups=mesh['dp'=2,'expert'=16] {'dp'}, dimensions={1}, use_global_device_ids=true | all-gather | bytes 1179648 | tf_op jit(solution)/shard_map/all_gather | solution.py:60
  103.5 9.7 %all_gather.9 = bf16[1,384,1024]{2,1,0:T(8,128)(2,1)} all-gather(bf16[1,384,512]{2,1,0:T(8,128)(2,1)S(1)} %copy-done.4), channel_id=1, replica_groups=mesh['dp'=2,'expert'=16] {'dp'}, dimensions={2}, use_global_device_ids=true | all-gather | bytes 1179648 | tf_op jit(solution)/shard_map/all_gather | solution.py:61
  113.2 4.0 %fusion.10 = f32[1152,768]{0,1:T(8,128)} fusion(bf16[1152,1024]{1,0:T(8,128)(2,1)S(1)} %bitcast.37, bf16[1024,384]{1,0:T(8,128)(2,1)S(1)} %bitcast.42, bf16[1024,384]{1,0:T(8,128)(2,1)S(1)} %bitcast.40), kind=kOutput, calls=%fused_computation.24 | convolution fusion | flops 1815085056 | bytes 7471104 | tf_op jit(solution)/shard_map/dot_general | solution.py:18
  117.2 17.5 %all-to-all-done = bf16[16,72,1024]{2,1,0:T(8,128)(2,1)} async-done(((bf16[16,72,1024]{2,1,0:T(8,128)(2,1)}), bf16[16,72,1024]{2,1,0:T(8,128)(2,1)}, u32[]{:S(2)}, u32[]{:S(2)}) %all-to-all-start) | async-done | bytes 2359328 | tf_op jit(solution)/shard_map/all_to_all | solution.py:68
  134.7 4.1 %convolution_convert_fusion.2 = bf16[1024,384]{0,1:T(8,128)(2,1)S(1)} fusion(bf16[1152,1024]{1,0:T(8,128)(2,1)} %bitcast.3, f32[1152,768]{0,1:T(8,128)} %fusion.10), kind=kOutput, calls=%fused_computation.20 | convolution fusion | flops 909017088 | bytes 6684672 | tf_op jit(solution)/shard_map/dot_general | solution.py:85
  138.8 3.3 %multiply_convert_fusion.2 = (bf16[1152,384]{0,1:T(8,128)(2,1)S(1)}, bf16[1152,384]{0,1:T(8,128)(2,1)S(1)}) fusion(f32[1152,768]{0,1:T(8,128)S(1)} %copy-done.7, bf16[1152,1024]{1,0:T(8,128)(2,1)} %bitcast.3, bf16[1,384,1024]{2,1,0:T(8,128)(2,1)S(1)} %copy-done.3), kind=kOutput, calls=%fused_computation.16 | convolution fusion | flops 911720448 | bytes 8454144 | tf_op jit(solution)/shard_map/dot_general | solution.py:23
  142.1 2.2 convolution_convert_fusion.1
  144.3 1.6 pad_maximum_fusion
  146.0 1.1 copy-done.2
  147.1 0.3 copy-done.9
  147.3 4.6 %convolution_convert_fusion = bf16[1152,1024]{1,0:T(8,128)(2,1)} fusion(bf16[1152,384]{0,1:T(8,128)(2,1)} %copy-done.10, bf16[1152,384]{0,1:T(8,128)(2,1)S(1)} %copy-done.9, bf16[1024,384]{1,0:T(8,128)(2,1)S(1)} %bitcast.43, bf16[1024,384]{1,0:T(8,128)(2,1)S(1)} %bitcast.41), kind=kOutput, calls=%fused_computation.5 | convolution fusion | flops 1819803648 | bytes 5701632 | tf_op jit(solution)/shard_map/dot_general | solution.py:27
  152.0 4.9 %all-to-all-start.2 = ((bf16[16,72,1024]{2,1,0:T(8,128)(2,1)}), bf16[16,72,1024]{2,1,0:T(8,128)(2,1)S(1)}, u32[]{:S(2)}, u32[]{:S(2)}) async-start(bf16[16,72,1024]{2,1,0:T(8,128)(2,1)} %bitcast.39), calls=%async_computation.2 | async-start | bytes 4718592 | tf_op jit(solution)/shard_map/all_to_all | solution.py:73
  156.9 53.0 %all-to-all-done.2 = bf16[16,72,1024]{2,1,0:T(8,128)(2,1)S(1)} async-done(((bf16[16,72,1024]{2,1,0:T(8,128)(2,1)}), bf16[16,72,1024]{2,1,0:T(8,128)(2,1)S(1)}, u32[]{:S(2)}, u32[]{:S(2)}) %all-to-all-start.2) | async-done | bytes 2359328 | tf_op jit(solution)/shard_map/all_to_all | solution.py:73
  209.9 5.3 %gather_fusion = bf16[1024,1024]{1,0:T(8,128)(2,1)} fusion(bf16[1152,1024]{1,0:T(8,128)(2,1)S(1)} %bitcast.36, s32[1024]{0:T(1024)S(1)} %broadcast_clamp_fusion), kind=kCustom, calls=%fused_computation | custom fusion | bytes 4198400 | tf_op jit(solution)/shard_map/gather | solution.py:80
  215.3 3.7 %bitcast_reduce_fusion = bf16[128,1024]{1,0:T(8,128)(2,1)} fusion(bf16[1024,1024]{1,0:T(8,128)(2,1)} %gather_fusion), kind=kLoop, calls=%fused_computation.8 | loop fusion | flops 917504 | bytes 2359296 | tf_op jit(solution)/shard_map/reduce_sum | solution.py:83
  219.0 1.6 convert_element_type.29
  220.6 1.1 slice_bitcast_fusion
  221.7 1.1 copy.24
  222.8 1.1 copy.25
  (30 shorter events, 0.4 us)
Async XLA Ops:
  7.2 2.7 %copy-start = (bf16[128,1024]{1,0:T(8,128)(2,1)S(1)}, bf16[128,1024]{1,0:T(8,128)(2,1)}, u32[]{:S(2)}) copy-start(bf16[128,1024]{1,0:T(8,128)(2,1)} %param.7) | copy-start | bytes 786436
  16.9 6.7 %copy-start.5 = (bf16[128,1024]{1,0:T(8,128)(2,1)S(1)}, bf16[128,1024]{1,0:T(8,128)(2,1)}, u32[]{:S(2)}) copy-start(bf16[128,1024]{1,0:T(8,128)(2,1)} %param.8) | copy-start | bytes 786436
  16.9 6.7 %copy-start.6 = (f32[128,8]{0,1:T(8,128)S(1)}, f32[128,8]{0,1:T(8,128)}, u32[]{:S(2)}) copy-start(f32[128,8]{0,1:T(8,128)} %param.9) | copy-start | bytes 12292
  16.9 59.7 %all-to-all-start.1 = ((bf16[16,72,1024]{2,1,0:T(8,128)(2,1)}), bf16[16,72,1024]{2,1,0:T(8,128)(2,1)S(1)}, u32[]{:S(2)}, u32[]{:S(2)}) async-start(bf16[16,72,1024]{2,1,0:T(8,128)(2,1)} %bitcast.6), calls=%async_computation.1 | async-start | bytes 4718592 | tf_op jit(solution)/shard_map/all_to_all | solution.py:67
  76.6 58.1 %all-to-all-start = ((bf16[16,72,1024]{2,1,0:T(8,128)(2,1)}), bf16[16,72,1024]{2,1,0:T(8,128)(2,1)}, u32[]{:S(2)}, u32[]{:S(2)}) async-start(bf16[16,72,1024]{2,1,0:T(8,128)(2,1)} %bitcast.2), calls=%async_computation | async-start | bytes 4718592 | tf_op jit(solution)/shard_map/all_to_all | solution.py:68
  81.5 137.5 %reduce-scatter.2.cloned.1.call-start = ((), (), s32[]{:S(2)}) async-start(), calls=%async_computation.4 | async-start | bytes 3538944 | tf_op jit(solution)/shard_map/reduce_scatter | solution.py:87
  81.6 22.0 %copy-start.4 = (bf16[1,384,512]{2,1,0:T(8,128)(2,1)S(1)}, bf16[1,384,512]{2,1,0:T(8,128)(2,1)}, u32[]{:S(2)}) copy-start(bf16[1,384,512]{2,1,0:T(8,128)(2,1)} %param.13) | copy-start | bytes 1179652
  103.5 9.7 %copy-start.1 = (bf16[1,1024,384]{2,1,0:T(8,128)(2,1)}, bf16[1,1024,384]{2,1,0:T(8,128)(2,1)S(1)}, u32[]{:S(2)}) copy-start(bf16[1,1024,384]{2,1,0:T(8,128)(2,1)S(1)} %all_gather.11) | copy-start | bytes 2359300
  134.7 4.1 %copy-start.3 = (bf16[1,384,1024]{2,1,0:T(8,128)(2,1)S(1)}, bf16[1,384,1024]{2,1,0:T(8,128)(2,1)}, u32[]{:S(2)}) copy-start(bf16[1,384,1024]{2,1,0:T(8,128)(2,1)} %all_gather.9) | copy-start | bytes 2359300
  134.7 4.1 %copy-start.7 = (f32[1152,768]{0,1:T(8,128)S(1)}, f32[1152,768]{0,1:T(8,128)}, u32[]{:S(2)}) copy-start(f32[1152,768]{0,1:T(8,128)} %fusion.10) | copy-start | bytes 10616836
  142.1 2.2 copy-start.8
  142.1 2.2 copy-start.10
  145.9 1.1 copy-start.2
  145.9 1.4 copy-start.9
  152.0 57.9 %all-to-all-start.2 = ((bf16[16,72,1024]{2,1,0:T(8,128)(2,1)}), bf16[16,72,1024]{2,1,0:T(8,128)(2,1)S(1)}, u32[]{:S(2)}, u32[]{:S(2)}) async-start(bf16[16,72,1024]{2,1,0:T(8,128)(2,1)} %bitcast.39), calls=%async_computation.2 | async-start | bytes 4718592 | tf_op jit(solution)/shard_map/all_to_all | solution.py:73
Sparse Core Ops, SparseCore 0:
  146.1 33.2 reduce-scatter.1
where the time goes:
time: 231 us
  waiting for transfers between devices  116 us (50%)
  blocking collectives  31.6 us (14%)
  matrix products  18.2 us (8%)
  local copies, waits for them, and re-layouts  17.7 us (8%)
  other arithmetic  16.7 us (7%)
  starting transfers between devices  16.5 us (7%)
  between operations  14.2 us (6%)
    all_to_all x1, waiting for transfers between devices, body(): lax.all_to_all(d_rows.reshape(experts, capacity, model_width), 'expert',...  53 us
    all_to_all x1, waiting for transfers between devices, body(): lax.all_to_all(send_inputs, 'expert', split_axis=0, concat_axis=0, tiled=...  45.4 us
    all_to_all x1, waiting for transfers between devices, body(): lax.all_to_all(send_grads, 'expert', split_axis=0, concat_axis=0, tiled=T...  17.5 us
    all_gather x1, blocking collectives, body(): lax.all_gather(gate_weight, 'dp', axis=1, tiled=True)  11.5 us
    all_gather x1, blocking collectives, body(): lax.all_gather(up_weight, 'dp', axis=1, tiled=True)  10.5 us
    all_gather x1, blocking collectives, body(): lax.all_gather(down_weight, 'dp', axis=2, tiled=True)  9.66 us
    scatter x1, other arithmetic, body(): send_grads = jnp.zeros((slot_count, model_width), jnp.bfloat16).at[positi...  7.37 us
    scatter x1, local copies, waits for them, and re-layouts, body(): send_inputs = jnp.zeros((slot_count, model_width), jnp.bfloat16).at[posit...  6.97 us
  transfers between devices with their start and end apart: 4, of which 3 were waited for; matrix products, arithmetic and copies ran while one was open for 11% of the time, Pallas kernels for 0%

commit v1 on v0

--- a/solution.py
+++ b/solution.py
@@ -1,9 +1,342 @@
+import functools
+
 import jax
 import jax.numpy as jnp
 from jax import lax
+from jax.experimental import pallas as pl
+from jax.experimental.pallas import tpu as pltpu
 from jax.sharding import PartitionSpec as P
 
-
+F32 = jnp.float32
+BF16 = jnp.bfloat16
+LANES = 128
+VMEM_BYTES = 56 * 1024 * 1024
+
+
+def vmem():
+    return pl.BlockSpec(memory_space=pltpu.VMEM)
+
+
+def smem():
+    return pl.BlockSpec(memory_space=pltpu.SMEM)
+
+
+def hbm():
+    return pl.BlockSpec(memory_space=pl.ANY)
+
+
+def params():
+    return pltpu.CompilerParams(vmem_limit_bytes=VMEM_BYTES)
+
+
+def pack_kernel(experts, tokens, d_output, combine, routes, out):
+    rows, width = tokens.shape
+    out[:, :width] = tokens[...]
+    out[:, width : 2 * width] = d_output[...]
+    lane = lax.broadcasted_iota(jnp.int32, (rows, LANES), 1)
+    expert = lax.rem(lane, experts)
+    dense = jnp.zeros((rows, LANES), F32)
+    for k in range(routes.shape[1]):
+        dense = dense + jnp.where(expert == routes[:, k : k + 1], combine[:, k : k + 1], 0.0)
+    high = dense.astype(BF16).astype(F32)
+    rest = dense - high
+    middle = rest.astype(BF16).astype(F32)
+    low = rest - middle
+    parts = jnp.where(
+        lane < experts,
+        high,
+        jnp.where(lane < 2 * experts, middle, jnp.where(lane < 3 * experts, low, 0.0)),
+    )
+    out[:, 2 * width :] = parts.astype(BF16)
+
+
+def pack(experts, tokens, d_output, combine, routes):
+    rows, width = tokens.shape
+    return pl.pallas_call(
+        functools.partial(pack_kernel, experts),
+        out_shape=jax.ShapeDtypeStruct((rows, 2 * width + LANES), BF16),
+        in_specs=[vmem()] * 4,
+        out_specs=vmem(),
+        compiler_params=params(),
+    )(tokens, d_output, combine, routes)
+
+
+def dot(a, b, dims):
+    return lax.dot_general(a, b, (dims, ((), ())), preferred_element_type=F32)
+
+
+def row_math(experts, expert, blocks, gate_up, down):
+    width, hidden_units = gate_up.shape[0], down.shape[0]
+    tok = jnp.concatenate([b[:, :width] for b in blocks], axis=0)
+    grad = jnp.concatenate([b[:, width : 2 * width] for b in blocks], axis=0)
+    parts = jnp.concatenate([b[:, 2 * width :] for b in blocks], axis=0).astype(F32)
+    lane = lax.broadcasted_iota(jnp.int32, parts.shape, 1)
+    mine = (lax.rem(lane, experts) == expert) & (lane < 3 * experts)
+    weight = jnp.sum(jnp.where(mine, parts, 0.0), axis=1, keepdims=True)
+    scaled = (weight * grad.astype(F32)).astype(BF16)
+    preact = dot(tok, gate_up[...], ((1,), (0,)))
+    gate_pre = preact[:, :hidden_units]
+    up_pre = preact[:, hidden_units:]
+    sig = jax.nn.sigmoid(gate_pre)
+    silu = gate_pre * sig
+    hidden = (silu * up_pre).astype(BF16)
+    d_hidden = dot(scaled, down[...], ((1,), (1,)))
+    d_gate = (d_hidden * up_pre * sig * (1.0 + gate_pre * (1.0 - sig))).astype(BF16)
+    d_up = (d_hidden * silu).astype(BF16)
+    d_preact = jnp.concatenate([d_gate, d_up], axis=1)
+    d_rows = dot(d_preact, gate_up[...], ((1,), (1,))).astype(BF16)
+    return tok, scaled, hidden, d_preact, d_rows
+
+
+def rows_kernel(experts, count, first, last, *refs):
+    refs = list(refs)
+    scal = refs.pop(0)
+    blocks = [refs.pop(0) for _ in range(count)]
+    if first:
+        halves = [refs.pop(0) for _ in range(6)]
+    else:
+        gate_up, down = refs.pop(0), refs.pop(0)
+        if not last:
+            sum_gu_in, sum_d_in = refs.pop(0), refs.pop(0)
+    own_rows, pair_rows = refs.pop(0), refs.pop(0)
+    if last:
+        sv_dpre, sv_scaled, sv_hidden = refs.pop(0), refs.pop(0), refs.pop(0)
+    else:
+        sum_gu, sum_d = refs.pop(0), refs.pop(0)
+        if first:
+            gate_up, down = refs.pop(0), refs.pop(0)
+        sv_tok, sv_scaled, sv_hidden, sv_dpre = (refs.pop(0) for _ in range(4))
+        if first:
+            sems = refs.pop(0)
+    part, expert = scal[0], scal[1]
+    if first:
+        size, hidden_units = halves[0].shape[0], halves[0].shape[1]
+        copies = []
+        for i in range(2):
+            at = pl.multiple_of((part if i == 0 else 1 - part) * size, size)
+            gate, up, dn = halves[3 * i : 3 * i + 3]
+            copies += [
+                pltpu.make_async_copy(gate, gate_up.at[pl.ds(at, size), pl.ds(0, hidden_units)], sems.at[3 * i]),
+                pltpu.make_async_copy(up, gate_up.at[pl.ds(at, size), pl.ds(hidden_units, hidden_units)], sems.at[3 * i + 1]),
+                pltpu.make_async_copy(dn, down.at[:, pl.ds(at, size)], sems.at[3 * i + 2]),
+            ]
+        for c in copies:
+            c.start()
+        for c in copies:
+            c.wait()
+    rows = blocks[0].shape[0]
+    half = count // 2
+    for i in range(0, count, 2):
+        tok, scaled, hidden, d_preact, d_rows = row_math(experts, expert, blocks[i : i + 2], gate_up, down)
+        span = pl.ds(i * rows, 2 * rows)
+        if not last:
+            sv_tok[span, :] = tok
+        sv_scaled[span, :] = scaled
+        sv_hidden[span, :] = hidden
+        sv_dpre[span, :] = d_preact
+        for j in (i, i + 1):
+            piece = d_rows[(j - i) * rows : (j - i + 1) * rows]
+            if j < half:
+                own_rows[pl.ds(j * rows, rows), :] = piece
+            else:
+                pair_rows[pl.ds((j - half) * rows, rows), :] = piece
+    if last:
+        return
+    width = sum_gu.shape[0]
+    step = 256
+    for at in range(0, width, step):
+        new = dot(sv_tok[:, at : at + step], sv_dpre[...], ((0,), (0,)))
+        if not first:
+            new = new + sum_gu_in[at : at + step, :]
+        sum_gu[at : at + step, :] = new
+    for at in range(0, width, step):
+        new = dot(sv_hidden[...], sv_scaled[:, at : at + step], ((0,), (0,)))
+        if not first:
+            new = new + sum_d_in[:, at : at + step]
+        sum_d[:, at : at + step] = new
+
+
+def rows_call(experts, scal, blocks, weights, sums, width, hidden_units):
+    first = len(weights) == 6
+    last = not first and sums is None
+    count = len(blocks)
+    rows = blocks[0].shape[0]
+    total = count * rows
+    sds = jax.ShapeDtypeStruct
+    out = [sds((total // 2, width), BF16)] * 2
+    scratch = []
+    if last:
+        out += [sds((total, 2 * hidden_units), BF16), sds((total, width), BF16), sds((total, hidden_units), BF16)]
+    else:
+        out += [sds((width, 2 * hidden_units), F32), sds((hidden_units, width), F32)]
+        if first:
+            out += [sds((width, 2 * hidden_units), BF16), sds((hidden_units, width), BF16)]
+        scratch += [
+            pltpu.VMEM((total, width), BF16),
+            pltpu.VMEM((total, width), BF16),
+            pltpu.VMEM((total, hidden_units), BF16),
+            pltpu.VMEM((total, 2 * hidden_units), BF16),
+        ]
+        if first:
+            scratch += [pltpu.SemaphoreType.DMA((6,))]
+    operands = [scal] + list(blocks) + list(weights)
+    specs = [smem()] + [vmem()] * count + [hbm() if first else vmem()] * len(weights)
+    if sums is not None:
+        operands += list(sums)
+        specs += [vmem()] * 2
+    macs = total * width * hidden_units * (4 if last else 8)
+    return pl.pallas_call(
+        functools.partial(rows_kernel, experts, count, first, last),
+        out_shape=out,
+        in_specs=specs,
+        out_specs=[vmem()] * len(out),
+        scratch_shapes=scratch,
+        cost_estimate=pl.CostEstimate(flops=2 * macs, bytes_accessed=12 * 1024 * 1024, transcendentals=total * hidden_units),
+        compiler_params=params(),
+    )(*operands)
+
+
+def half_kernel(count, scal, *refs):
+    blocks = refs[:count]
+    dpre, scaled, hidden, sum_gu, sum_d, out_gu, out_d = refs[count:]
+    tok = jnp.concatenate([b[...] for b in blocks], axis=0)
+    out_gu[...] = (sum_gu[...] + dot(tok, dpre[...], ((0,), (0,)))).astype(BF16)
+    out_d[...] = (sum_d[...] + dot(hidden[...], scaled[...], ((0,), (0,)))).astype(BF16)
+
+
+def half_call(which, blocks, dpre, scaled, hidden, sum_gu, sum_d):
+    width = sum_gu.shape[0]
+    size = width // 2
+    hidden_units = hidden.shape[1]
+    count = len(blocks)
+    rows = blocks[0].shape[0]
+    whole = lambda a: pl.BlockSpec(a.shape, lambda i, s: (0, 0))
+    side = lambda r: pl.BlockSpec((r, size), lambda i, s: (0, s[0]))
+    return pl.pallas_call(
+        functools.partial(half_kernel, count),
+        out_shape=[
+            jax.ShapeDtypeStruct((size, 2 * hidden_units), BF16),
+            jax.ShapeDtypeStruct((hidden_units, size), BF16),
+        ],
+        grid_spec=pltpu.PrefetchScalarGridSpec(
+            num_scalar_prefetch=1,
+            grid=(1,),
+            in_specs=[side(rows)] * count
+            + [whole(dpre), side(scaled.shape[0]), whole(hidden)]
+            + [pl.BlockSpec((size, 2 * hidden_units), lambda i, s: (s[0], 0)), side(hidden_units)],
+            out_specs=[
+                pl.BlockSpec((size, 2 * hidden_units), lambda i, s: (0, 0)),
+                pl.BlockSpec((hidden_units, size), lambda i, s: (0, 0)),
+            ],
+        ),
+        cost_estimate=pl.CostEstimate(flops=2 * 256 * size * 1152, bytes_accessed=5 * 1024 * 1024, transcendentals=0),
+        compiler_params=params(),
+    )(which, *blocks, dpre, scaled, hidden, sum_gu, sum_d)
+
+
+Z, Y, CORES = 4, 2, 2
+
+
+def pairs_of(move):
+    out = []
+    for z in range(Z):
+        for y in range(Y):
+            for c in range(CORES):
+                to = move(z, y, c)
+                if to is not None:
+                    out.append(((z * Y + y) * CORES + c, (to[0] * Y + to[1]) * CORES + to[2]))
+    return out
+
+
+def along_z(table):
+    return pairs_of(lambda z, y, c: (table[z], y, c) if z in table else None)
+
+
+SWAP_CORE = pairs_of(lambda z, y, c: (z, y, 1 - c))
+SWAP_Y = pairs_of(lambda z, y, c: (z, 1 - y, c))
+OUTER = along_z({0: 1, 1: 0, 2: 3, 3: 2})
+INNER = along_z({1: 2, 2: 1})
+OUTWARD = along_z({1: 0, 2: 3})
+SKIP_TO_INNER = along_z({0: 2, 3: 1})
+SKIP_TO_OUTER = along_z({1: 3, 2: 0})
+ENDS = along_z({0: 3, 3: 0})
+
+
+def dense_body(tokens, d_output, combine, routes, gate_weight, up_weight, down_weight):
+    experts = lax.axis_size("expert")
+    width = tokens.shape[1]
+    rows = tokens.shape[0]
+    hidden_units = gate_weight.shape[2]
+    part = lax.axis_index("dp")
+    expert = lax.axis_index("expert")
+    z = expert // (Y * CORES)
+    inner = (z == 1) | (z == 2)
+    scal = jnp.stack([part, expert]).astype(jnp.int32)
+
+    move = lambda a, pairs: lax.ppermute(a, "expert", pairs)
+    across = lambda a: lax.ppermute(a, "dp", [(0, 1), (1, 0)])
+
+    gate, up, down = gate_weight[0], up_weight[0], down_weight[0]
+    own = pack(experts, tokens, d_output, combine, routes)
+    gate2, up2, down2 = across(gate), across(up), across(down)
+
+    b1 = move(own, OUTER)
+    f1 = move(own, INNER)
+    y0 = move(own, SWAP_Y)
+    c0 = move(own, SWAP_CORE)
+    f2 = move(b1, INNER)
+    g1 = move(f1, OUTWARD)
+    y1 = move(b1, SWAP_Y)
+    c1 = move(b1, SWAP_CORE)
+    cy0 = move(y0, SWAP_CORE)
+    b2 = jnp.where(inner, f1, g1)
+    y2 = move(b2, SWAP_Y)
+    c2 = move(b2, SWAP_CORE)
+    cy1 = move(y1, SWAP_CORE)
+    g2 = move(f2, OUTWARD)
+    b3 = jnp.where(inner, f2, g2)
+    y3 = move(b3, SWAP_Y)
+    c3 = move(b3, SWAP_CORE)
+    cy2 = move(y2, SWAP_CORE)
+    cy3 = move(y3, SWAP_CORE)
+
+    call = lambda blocks, weights, sums: rows_call(experts, scal, blocks, weights, sums, width, hidden_units)
+    own_a, pair_a, sum_gu, sum_d, gate_up, down_whole = call(
+        [own, b1, y0, c0, c1, cy0], [gate, up, down, gate2, up2, down2], None
+    )
+    back_a = move(pair_a, SWAP_CORE)
+    own_b, pair_b, sum_gu, sum_d = call(
+        [b2, b3, y1, y2, c2, c3, cy1, cy2], [gate_up, down_whole], [sum_gu, sum_d]
+    )
+    back_b = move(pair_b, SWAP_CORE)
+    own_c, pair_c, dpre, scaled, hidden = call([y3, cy3], [gate_up, down_whole], None)
+    back_c = move(pair_c, SWAP_CORE)
+
+    last = [y3, cy3]
+    send_gu, send_d = half_call((1 - part)[None].astype(jnp.int32), last, dpre, scaled, hidden, sum_gu, sum_d)
+    got_gu, got_d = across(send_gu), across(send_d)
+    keep_gu, keep_d = half_call(part[None].astype(jnp.int32), last, dpre, scaled, hidden, sum_gu, sum_d)
+
+    add = lambda *terms: sum(t.astype(F32) for t in terms).astype(BF16)
+    ry0 = move(add(own_a[2 * rows :], back_a[2 * rows :]), SWAP_Y)
+    ry12 = move(add(own_b[2 * rows :], back_b[2 * rows :]), SWAP_Y)
+    ry3 = move(add(own_c, back_c), SWAP_Y)
+    s0 = add(own_a[:rows], back_a[:rows], ry0)
+    s1 = add(own_a[rows : 2 * rows], back_a[rows : 2 * rows], ry12[:rows])
+    s2 = add(own_b[:rows], back_b[:rows], ry12[rows:])
+    s3 = add(own_b[rows : 2 * rows], back_b[rows : 2 * rows], ry3)
+    d_tokens = add(
+        s0,
+        move(s1, OUTER),
+        move(s2, INNER),
+        move(s2, SKIP_TO_INNER),
+        move(s3, SKIP_TO_OUTER),
+        move(s3, ENDS),
+    )
+    d_gate = (keep_gu[:, :hidden_units].astype(F32) + got_gu[:, :hidden_units].astype(F32))[None]
+    d_up = (keep_gu[:, hidden_units:].astype(F32) + got_gu[:, hidden_units:].astype(F32))[None]
+    d_down = (keep_d.astype(F32) + got_d.astype(F32))[None]
+    return (d_tokens, d_gate, d_up, d_down)
 def route_slots(routes, experts):
     matches = (routes[:, :, None] == jnp.arange(experts, dtype=jnp.int32)[None, None, :]).astype(
         jnp.int32
@@ -28,7 +361,7 @@
     return (d_rows, hidden, d_preact)
 
 
-def body(tokens, d_output, combine, routes, gate_weight, up_weight, down_weight):
+def routed_body(tokens, d_output, combine, routes, gate_weight, up_weight, down_weight):
     experts = lax.axis_size("expert")
     tok_count = tokens.shape[0]
     model_width = tokens.shape[1]
@@ -103,8 +436,9 @@
         P("expert", "dp", None),
         P("expert", None, "dp"),
     )
+    dense = mesh.shape["expert"] == Z * Y * CORES and mesh.shape["dp"] == 2
     return jax.shard_map(
-        body,
+        dense_body if dense else routed_body,
         mesh=mesh,
         in_specs=placed,
         out_specs=(

time: 231 us -> 174 us (0.75)
  the two profiles are of different devices: /device:TPU:15 before, /device:TPU:0 now
where the time goes in v1:
time: 174 us; the launch traced here: 172 us
  waiting for transfers between devices  81.7 us (47%)
  Pallas kernels  38.9 us (22%)
  starting transfers between devices  37.1 us (21%)
  other arithmetic  7.15 us (4%)
  local copies, waits for them, and re-layouts  6.06 us (3%)
    ppermute x28, waiting for transfers between devices, dense_body(): move = lambda a, pairs: lax.ppermute(a, 'expert', pairs)  59.6 us
    ppermute x28, starting transfers between devices, dense_body(): move = lambda a, pairs: lax.ppermute(a, 'expert', pairs)  31.5 us
    pallas_call x3, Pallas kernels, rows_call(): pl.pallas_call(functools.partial(rows_kernel, experts, count, first, last...  29.5 us
    ppermute x5, waiting for transfers between devices, dense_body(): across = lambda a: lax.ppermute(a, 'dp', [(0, 1), (1, 0)])  22.1 us
    pallas_call x2, Pallas kernels, half_call(): pl.pallas_call(functools.partial(half_kernel, count), out_shape=[jax.Shap...  7.06 us
    unnamed x46, local copies, waits for them, and re-layouts  6.06 us
    ppermute x5, starting transfers between devices, dense_body(): across = lambda a: lax.ppermute(a, 'dp', [(0, 1), (1, 0)])  5.54 us
    convert_element_type x4, other arithmetic, dense_body(): add = lambda *terms: sum((t.astype(F32) for t in terms)).astype(BF16)  3.98 us
  transfers between devices with their start and end apart: 33, of which 10 were waited for; matrix products, arithmetic and copies ran while one was open for 3% of the time, Pallas kernels for 21%

profile of v1, /device:TPU:0, one launch (start us, length us, event | category | flops | bytes accessed | tf_op | source)
XLA Modules:
  0.0 171.9 jit_solution(525092218299534898)
XLA Ops:
  0.6 1.4 copy.11.combine
  2.0 1.4 copy.12.routes
  3.5 2.3 %shard_map.102.refs_1_ = bf16[128,2176]{1,0:T(8,128)(2,1)} custom-call(bf16[128,1024]{1,0:T(8,128)(2,1)} %tokens.1, bf16[128,1024]{1,0:T(8,128)(2,1)} %d_output.1, f32[128,8]{1,0:T(8,128)} %copy.11.combine, s32[128,8]{1,0:T(8,128)} %copy.12.routes), custom_call_target="tpu_custom_call" | custom-call | tf_op jit(solution)/shard_map/pallas_call | solution.py:55
  6.6 5.9 %collective-permute-start = (bf16[128,2176]{1,0:T(8,128)(2,1)}, bf16[128,2176]{1,0:T(8,128)(2,1)S(1)}, u32[]{:S(2)}, u32[]{:S(2)}) collective-permute-start(bf16[128,2176]{1,0:T(8,128)(2,1)} %shard_map.102.refs_1_), channel_id=1, source_target_pairs={{0,4},{1,5},{2,6},{3,7},{4,0},{5,1},{6,2},{7,3},{8,12},{9,13},{10,... | collective-permute-start | bytes 1671176 | tf_op jit(solution)/shard_map/ppermute | solution.py:276
  12.5 1.3 collective-permute-start.11
  13.7 11.3 %collective-permute-done.refs_2_ = bf16[128,2176]{1,0:T(8,128)(2,1)S(1)} collective-permute-done((bf16[128,2176]{1,0:T(8,128)(2,1)}, bf16[128,2176]{1,0:T(8,128)(2,1)S(1)}, u32[]{:S(2)}, u32[]{:S(2)}) %collective-permute-start) | collective-permute-done | bytes 557088 | tf_op jit(solution)/shard_map/ppermute | solution.py:276
  25.7 1.6 collective-permute-start.1
  27.3 1.5 collective-permute-start.5
  29.3 9.1 %collective-permute-done.11 = bf16[128,2176]{1,0:T(8,128)(2,1)S(1)} collective-permute-done((bf16[128,2176]{1,0:T(8,128)(2,1)S(1)}, bf16[128,2176]{1,0:T(8,128)(2,1)S(1)}, u32[]{:S(2)}, u32[]{:S(2)}) %collective-permute-start.11) | collective-permute-done | bytes 557088 | tf_op jit(solution)/shard_map/ppermute | solution.py:276
  38.4 1.5 collective-permute-start.7
  41.3 6.7 %collective-permute-done.6.refs_11_ = bf16[512,384]{1,0:T(8,128)(2,1)} collective-permute-done((bf16[512,384]{1,0:T(8,128)(2,1)}, bf16[512,384]{1,0:T(8,128)(2,1)}, u32[]{:S(2)}, u32[]{:S(2)}) %collective-permute-start.6) | collective-permute-done | bytes 393248 | tf_op jit(solution)/shard_map/ppermute | solution.py:277
  48.1 6.0 %collective-permute-done.7.refs_12_ = bf16[384,512]{1,0:T(8,128)(2,1)S(1)} collective-permute-done((bf16[384,512]{1,0:T(8,128)(2,1)}, bf16[384,512]{1,0:T(8,128)(2,1)S(1)}, u32[]{:S(2)}, u32[]{:S(2)}) %collective-permute-start.7) | collective-permute-done | bytes 393248 | tf_op jit(solution)/shard_map/ppermute | solution.py:277
  54.8 1.4 collective-permute-start.15
  56.5 13.1 %collective-permute-done.14.refs_3_ = bf16[128,2176]{1,0:T(8,128)(2,1)S(1)} collective-permute-done((bf16[128,2176]{1,0:T(8,128)(2,1)S(1)}, bf16[128,2176]{1,0:T(8,128)(2,1)S(1)}, u32[]{:S(2)}, u32[]{:S(2)}) %collective-permute-start.14) | collective-permute-done | bytes 557088 | tf_op jit(solution)/shard_map/ppermute | solution.py:276
  70.1 8.1 %collective-permute-done.15.refs_4_ = bf16[128,2176]{1,0:T(8,128)(2,1)S(1)} collective-permute-done((bf16[128,2176]{1,0:T(8,128)(2,1)S(1)}, bf16[128,2176]{1,0:T(8,128)(2,1)S(1)}, u32[]{:S(2)}, u32[]{:S(2)}) %collective-permute-start.15) | collective-permute-done | bytes 557088 | tf_op jit(solution)/shard_map/ppermute | solution.py:276
  79.9 11.5 %shard_map.103 = (bf16[384,1024]{1,0:T(8,128)(2,1)}, bf16[384,1024]{1,0:T(8,128)(2,1)}, f32[1024,768]{1,0:T(8,128)}, f32[384,1024]{1,0:T(8,128)}, bf16[1024,768]{1,0:T(8,128)(2,1)}, /*index=5*/bf16[384,1024]{1,0:T(8,128)(2,1)}) custom-call(s32[2]{0:T(128)} %pad_add_fusion.refs_0_, bf16[128,2176]{1,0:T(8,128)(2,1)} %shard_map.102.refs_1_, ...), custom_call_target="tpu_custom_call" | custom-call | flops 4831838208 | bytes 12582912 | tf_op jit(solution)/shard_map/pallas_call | solution.py:188
  93.3 13.6 %shard_map.104 = (bf16[512,1024]{1,0:T(8,128)(2,1)}, bf16[512,1024]{1,0:T(8,128)(2,1)}, f32[1024,768]{1,0:T(8,128)}, f32[384,1024]{1,0:T(8,128)}) custom-call(s32[2]{0:T(128)} %pad_add_fusion.refs_0_, bf16[128,2176]{1,0:T(8,128)(2,1)} %copy-done.5, bf16[128,2176]{1,0:T(8,128)(2,1)} %copy-done.6, bf16[128,2176]{1,0:T(8,128)(2,1)} %copy-done.12, ...), custom_call_target="tpu_custom_call" | custom-call | flops 6442450944 | bytes 12582912 | tf_op jit(solution)/shard_map/pallas_call | solution.py:188
  107.6 3.6 %collective-permute-done.26.refs_2_.refs_1_ = bf16[128,2176]{1,0:T(8,128)(2,1)S(1)} collective-permute-done((bf16[128,2176]{1,0:T(8,128)(2,1)S(1)}, bf16[128,2176]{1,0:T(8,128)(2,1)S(1)}, u32[]{:S(2)}, u32[]{:S(2)}) %collective-permute-start.26) | collective-permute-done | bytes 557088 | tf_op jit(solution)/shard_map/ppermute | solution.py:276
  112.0 4.5 %shard_map.105 = (bf16[128,1024]{1,0:T(8,128)(2,1)}, bf16[128,1024]{1,0:T(8,128)(2,1)}, bf16[256,768]{1,0:T(8,128)(2,1)}, bf16[256,1024]{1,0:T(8,128)(2,1)}, bf16[256,384]{1,0:T(8,128)(2,1)}) custom-call(s32[2]{0:T(128)} %pad_add_fusion.refs_0_, bf16[128,2176]{1,0:T(8,128)(2,1)} %copy-done, bf16[128,2176]{1,0:T(8,128)(2,1)} %copy-done.1, ...), custom_call_target="tpu_custom_call" | custom-call | flops 805306368 | bytes 12582912 | tf_op jit(solution)/shard_map/pallas_call | solution.py:188
  116.9 1.6 collective-permute-start.21
  118.5 1.4 collective-permute-start.28
  119.9 3.5 %shard_map.107 = (bf16[512,768]{1,0:T(8,128)(2,1)}, bf16[384,512]{1,0:T(8,128)(2,1)}) custom-call(s32[1]{0:T(128)} %bitcast.5.scal, bf16[128,2176]{1,0:T(8,128)(2,1)} %copy-done, bf16[128,2176]{1,0:T(8,128)(2,1)} %copy-done.1, bf16[256,768]{1,0:T(8,128)(2,1)} %get-tuple-element.33.refs_2_, bf16[256,1024]{1,0:T(8,128)(2,1)} %get-tuple-element.34.refs_3_, ...), custom_call_target="tpu_custom_call" | custom-call | flops 301989888 | bytes 5242880 | tf_op jit(solution)/shard_map/pallas_call | solution.py:215
  123.4 1.5 collective-permute-start.31
  125.5 3.5 %shard_map.106 = (bf16[512,768]{1,0:T(8,128)(2,1)}, bf16[384,512]{1,0:T(8,128)(2,1)}) custom-call(s32[1]{0:T(128)} %bitcast.scal, bf16[128,2176]{1,0:T(8,128)(2,1)} %copy-done, bf16[128,2176]{1,0:T(8,128)(2,1)} %copy-done.1, bf16[256,768]{1,0:T(8,128)(2,1)} %get-tuple-element.33.refs_2_, bf16[256,1024]{1,0:T(8,128)(2,1)} %get-tuple-element.34.refs_3_, ...), custom_call_target="tpu_custom_call" | custom-call | flops 301989888 | bytes 5242880 | tf_op jit(solution)/shard_map/pallas_call | solution.py:215
  129.0 7.8 %collective-permute-done.28 = bf16[128,1024]{1,0:T(8,128)(2,1)} collective-permute-done((bf16[128,1024]{1,0:T(8,128)(2,1)S(1)}, bf16[128,1024]{1,0:T(8,128)(2,1)}, u32[]{:S(2)}, u32[]{:S(2)}) %collective-permute-start.28) | collective-permute-done | bytes 262176 | tf_op jit(solution)/shard_map/ppermute | solution.py:276
  136.8 1.7 %add_convert_fusion.7 = (bf16[128,1024]{1,0:T(8,128)(2,1)S(1)}, bf16[128,1024]{1,0:T(8,128)(2,1)S(1)}, bf16[128,1024]{1,0:T(8,128)(2,1)S(1)}, bf16[128,1024]{1,0:T(8,128)(2,1)S(1)}) fusion(bf16[384,1024]{1,0:T(8,128)(2,1)} %collective-permute-done.8, bf16[384,1024]{1,0:T(8,128)(2,1)S(1)} %copy-done.3, bf16[256,1024]{1,0:T(8,128)(2,1)S(1)} %collective-permute-done.21, ...), kind=kLoop, calls=%fused_computation.12 | loop fusion | flops 2883584 | bytes 3932160 | tf_op jit(solution)/shard_map/convert_element_type | solution.py:320
  138.6 3.4 %collective-permute-start.30 = (bf16[128,1024]{1,0:T(8,128)(2,1)S(1)}, bf16[128,1024]{1,0:T(8,128)(2,1)S(1)}, u32[]{:S(2)}, u32[]{:S(2)}) collective-permute-start(bf16[128,1024]{1,0:T(8,128)(2,1)S(1)} %get-tuple-element.48), channel_id=1, source_target_pairs={{0,12},{1,13},{2,14},{3,15},{12,0},{13,1},{14,2},{15,3},{16,28},{1... | collective-permute-start | bytes 786440 | tf_op jit(solution)/shard_map/ppermute | solution.py:276
  142.0 9.4 %collective-permute-done.32 = bf16[384,512]{1,0:T(8,128)(2,1)S(1)} collective-permute-done((bf16[384,512]{1,0:T(8,128)(2,1)}, bf16[384,512]{1,0:T(8,128)(2,1)S(1)}, u32[]{:S(2)}, u32[]{:S(2)}) %collective-permute-start.32) | collective-permute-done | bytes 393248 | tf_op jit(solution)/shard_map/ppermute | solution.py:277
  153.7 5.7 %collective-permute-start.24 = (bf16[128,1024]{1,0:T(8,128)(2,1)S(1)}, bf16[128,1024]{1,0:T(8,128)(2,1)S(1)}, u32[]{:S(2)}, u32[]{:S(2)}) collective-permute-start(bf16[128,1024]{1,0:T(8,128)(2,1)S(1)} %get-tuple-element.49), channel_id=1, source_target_pairs={{0,8},{1,9},{2,10},{3,11},{12,4},{13,5},{14,6},{15,7},{16,24},{17,... | collective-permute-start | bytes 786440 | tf_op jit(solution)/shard_map/ppermute | solution.py:276
  162.0 1.3 add_bitcast_fusion.1
  163.3 6.6 %collective-permute-done.29 = bf16[128,1024]{1,0:T(8,128)(2,1)S(1)} collective-permute-done((bf16[128,1024]{1,0:T(8,128)(2,1)S(1)}, bf16[128,1024]{1,0:T(8,128)(2,1)S(1)}, u32[]{:S(2)}, u32[]{:S(2)}) %collective-permute-start.29) | collective-permute-done | bytes 262176 | tf_op jit(solution)/shard_map/ppermute | solution.py:276
  169.9 2.0 %add_convert_fusion.1 = bf16[128,1024]{1,0:T(8,128)(2,1)} fusion(bf16[128,1024]{1,0:T(8,128)(2,1)S(1)} %collective-permute-done.30, bf16[128,1024]{1,0:T(8,128)(2,1)S(1)} %collective-permute-done.29, bf16[128,1024]{1,0:T(8,128)(2,1)S(1)} %collective-permute-done.24, bf16[128,1024]{1,0:T(8,128)(2,1)S(1)} %collective-permute-done.23, ...), kind=kLoop, calls=%fused_computation.6 | loop fusion | flops 2359296 | bytes 2359296 | tf_op jit(solution)/shard_map/convert_element_type | solution.py:320
  (95 shorter events, 15.8 us)
Async XLA Ops:
  5.7 6.7 %collective-permute-start.10 = (bf16[128,2176]{1,0:T(8,128)(2,1)}, bf16[128,2176]{1,0:T(8,128)(2,1)S(1)}, u32[]{:S(2)}, u32[]{:S(2)}) collective-permute-start(bf16[128,2176]{1,0:T(8,128)(2,1)} %shard_map.102.refs_1_), channel_id=1, source_target_pairs={{4,8},{5,9},{6,10},{7,11},{8,4},{9,5},{10,6},{11,7},{20,24},{21,25... | collective-permute-start | bytes 1671176 | tf_op jit(solution)/shard_map/ppermute | solution.py:276
  6.6 18.4 %collective-permute-start = (bf16[128,2176]{1,0:T(8,128)(2,1)}, bf16[128,2176]{1,0:T(8,128)(2,1)S(1)}, u32[]{:S(2)}, u32[]{:S(2)}) collective-permute-start(bf16[128,2176]{1,0:T(8,128)(2,1)} %shard_map.102.refs_1_), channel_id=1, source_target_pairs={{0,4},{1,5},{2,6},{3,7},{4,0},{5,1},{6,2},{7,3},{8,12},{9,13},{10,... | collective-permute-start | bytes 1671176 | tf_op jit(solution)/shard_map/ppermute | solution.py:276
  12.5 25.9 %collective-permute-start.11 = (bf16[128,2176]{1,0:T(8,128)(2,1)S(1)}, bf16[128,2176]{1,0:T(8,128)(2,1)S(1)}, u32[]{:S(2)}, u32[]{:S(2)}) collective-permute-start(bf16[128,2176]{1,0:T(8,128)(2,1)S(1)} %collective-permute-done.10), channel_id=1, source_target_pairs={{4,0},{5,1},{6,2},{7,3},{8,12},{9,13},{10,14},{11,15},{20,16},{21,... | collective-permute-start | bytes 1671176 | tf_op jit(solution)/shard_map/ppermute | solution.py:276
  25.0 14.9 %collective-permute-start.12 = (bf16[128,2176]{1,0:T(8,128)(2,1)S(1)}, bf16[128,2176]{1,0:T(8,128)(2,1)S(1)}, u32[]{:S(2)}, u32[]{:S(2)}) collective-permute-start(bf16[128,2176]{1,0:T(8,128)(2,1)S(1)} %collective-permute-done.refs_2_), channel_id=1, source_target_pairs={{4,8},{5,9},{6,10},{7,11},{8,4},{9,5},{10,6},{11,7},{20,24},{21,25... | collective-permute-start | bytes 1671176 | tf_op jit(solution)/shard_map/ppermute | solution.py:276
  25.7 28.9 %collective-permute-start.1 = (bf16[128,2176]{1,0:T(8,128)(2,1)}, bf16[128,2176]{1,0:T(8,128)(2,1)S(1)}, u32[]{:S(2)}, u32[]{:S(2)}) collective-permute-start(bf16[128,2176]{1,0:T(8,128)(2,1)} %shard_map.102.refs_1_), channel_id=1, source_target_pairs={{0,2},{1,3},{2,0},{3,1},{4,6},{5,7},{6,4},{7,5},{8,10},{9,11},{10,... | collective-permute-start | bytes 1671176 | tf_op jit(solution)/shard_map/ppermute | solution.py:276
  27.3 14.0 %collective-permute-start.5 = (bf16[512,384]{1,0:T(8,128)(2,1)}, bf16[512,384]{1,0:T(8,128)(2,1)}, u32[]{:S(2)}, u32[]{:S(2)}) collective-permute-start(bf16[512,384]{1,0:T(8,128)(2,1)} %bitcast.12), channel_id=1, source_target_pairs={{0,16},{16,0},{1,17},{17,1},{2,18},{18,2},{3,19},{19,3},{4,20},{20... | collective-permute-start | bytes 1179656 | tf_op jit(solution)/shard_map/ppermute | solution.py:277
  28.8 19.3 %collective-permute-start.6 = (bf16[512,384]{1,0:T(8,128)(2,1)}, bf16[512,384]{1,0:T(8,128)(2,1)}, u32[]{:S(2)}, u32[]{:S(2)}) collective-permute-start(bf16[512,384]{1,0:T(8,128)(2,1)} %bitcast.14), channel_id=1, source_target_pairs={{0,16},{16,0},{1,17},{17,1},{2,18},{18,2},{3,19},{19,3},{4,20},{20... | collective-permute-start | bytes 1179656 | tf_op jit(solution)/shard_map/ppermute | solution.py:277
  38.4 15.7 %collective-permute-start.7 = (bf16[384,512]{1,0:T(8,128)(2,1)}, bf16[384,512]{1,0:T(8,128)(2,1)S(1)}, u32[]{:S(2)}, u32[]{:S(2)}) collective-permute-start(bf16[384,512]{1,0:T(8,128)(2,1)} %bitcast.16), channel_id=1, source_target_pairs={{0,16},{16,0},{1,17},{17,1},{2,18},{18,2},{3,19},{19,3},{4,20},{20... | collective-permute-start | bytes 1179656 | tf_op jit(solution)/shard_map/ppermute | solution.py:277
  39.9 14.7 %collective-permute-start.13 = (bf16[128,2176]{1,0:T(8,128)(2,1)S(1)}, bf16[128,2176]{1,0:T(8,128)(2,1)S(1)}, u32[]{:S(2)}, u32[]{:S(2)}) collective-permute-start(bf16[128,2176]{1,0:T(8,128)(2,1)S(1)} %collective-permute-done.12), channel_id=1, source_target_pairs={{4,0},{5,1},{6,2},{7,3},{8,12},{9,13},{10,14},{11,15},{20,16},{21,... | collective-permute-start | bytes 1671176 | tf_op jit(solution)/shard_map/ppermute | solution.py:276
  41.3 15.0 %collective-permute-start.2 = (bf16[128,2176]{1,0:T(8,128)(2,1)S(1)}, bf16[128,2176]{1,0:T(8,128)(2,1)S(1)}, u32[]{:S(2)}, u32[]{:S(2)}) collective-permute-start(bf16[128,2176]{1,0:T(8,128)(2,1)S(1)} %copy-done.7), channel_id=1, source_target_pairs={{0,1},{1,0},{2,3},{3,2},{4,5},{5,4},{6,7},{7,6},{8,9},{9,8},{10,11... | collective-permute-start | bytes 1671176 | tf_op jit(solution)/shard_map/ppermute | solution.py:276
  48.1 21.5 %collective-permute-start.3 = (bf16[128,2176]{1,0:T(8,128)(2,1)S(1)}, bf16[128,2176]{1,0:T(8,128)(2,1)S(1)}, u32[]{:S(2)}, u32[]{:S(2)}) collective-permute-start(bf16[128,2176]{1,0:T(8,128)(2,1)S(1)} %collective-permute-done.refs_2_), channel_id=1, source_target_pairs={{0,1},{1,0},{2,3},{3,2},{4,5},{5,4},{6,7},{7,6},{8,9},{9,8},{10,11... | collective-permute-start | bytes 1671176 | tf_op jit(solution)/shard_map/ppermute | solution.py:276
  54.1 15.6 %collective-permute-start.14 = (bf16[128,2176]{1,0:T(8,128)(2,1)S(1)}, bf16[128,2176]{1,0:T(8,128)(2,1)S(1)}, u32[]{:S(2)}, u32[]{:S(2)}) collective-permute-start(bf16[128,2176]{1,0:T(8,128)(2,1)S(1)} %collective-permute-done.refs_2_), channel_id=1, source_target_pairs={{0,2},{1,3},{2,0},{3,1},{4,6},{5,7},{6,4},{7,5},{8,10},{9,11},{10,... | collective-permute-start | bytes 1671176 | tf_op jit(solution)/shard_map/ppermute | solution.py:276
  54.6 24.5 %collective-permute-start.4 = (bf16[128,2176]{1,0:T(8,128)(2,1)S(1)}, bf16[128,2176]{1,0:T(8,128)(2,1)S(1)}, u32[]{:S(2)}, u32[]{:S(2)}) collective-permute-start(bf16[128,2176]{1,0:T(8,128)(2,1)S(1)} %collective-permute-done.1.refs_3_), channel_id=1, source_target_pairs={{0,1},{1,0},{2,3},{3,2},{4,5},{5,4},{6,7},{7,6},{8,9},{9,8},{10,11... | collective-permute-start | bytes 1671176 | tf_op jit(solution)/shard_map/ppermute | solution.py:276
  54.8 23.5 %collective-permute-start.15 = (bf16[128,2176]{1,0:T(8,128)(2,1)S(1)}, bf16[128,2176]{1,0:T(8,128)(2,1)S(1)}, u32[]{:S(2)}, u32[]{:S(2)}) collective-permute-start(bf16[128,2176]{1,0:T(8,128)(2,1)S(1)} %broadcast_select_fusion.1.refs_1_), channel_id=1, source_target_pairs={{0,2},{1,3},{2,0},{3,1},{4,6},{5,7},{6,4},{7,5},{8,10},{9,11},{10,... | collective-permute-start | bytes 1671176 | tf_op jit(solution)/shard_map/ppermute | solution.py:276
  56.3 35.7 %collective-permute-start.16 = (bf16[128,2176]{1,0:T(8,128)(2,1)S(1)}, bf16[128,2176]{1,0:T(8,128)(2,1)S(1)}, u32[]{:S(2)}, u32[]{:S(2)}) collective-permute-start(bf16[128,2176]{1,0:T(8,128)(2,1)S(1)} %broadcast_select_fusion.1.refs_1_), channel_id=1, source_target_pairs={{0,1},{1,0},{2,3},{3,2},{4,5},{5,4},{6,7},{7,6},{8,9},{9,8},{10,11... | collective-permute-start | bytes 1671176 | tf_op jit(solution)/shard_map/ppermute | solution.py:276
  69.6 22.3 %collective-permute-start.18 = (bf16[128,2176]{1,0:T(8,128)(2,1)S(1)}, bf16[128,2176]{1,0:T(8,128)(2,1)S(1)}, u32[]{:S(2)}, u32[]{:S(2)}) collective-permute-start(bf16[128,2176]{1,0:T(8,128)(2,1)S(1)} %collective-permute-done.14.refs_3_), channel_id=1, source_target_pairs={{0,1},{1,0},{2,3},{3,2},{4,5},{5,4},{6,7},{7,6},{8,9},{9,8},{10,11... | collective-permute-start | bytes 1671176 | tf_op jit(solution)/shard_map/ppermute | solution.py:276
  69.6 22.3 %collective-permute-start.17 = (bf16[128,2176]{1,0:T(8,128)(2,1)S(1)}, bf16[128,2176]{1,0:T(8,128)(2,1)S(1)}, u32[]{:S(2)}, u32[]{:S(2)}) collective-permute-start(bf16[128,2176]{1,0:T(8,128)(2,1)S(1)} %broadcast_select_fusion.refs_2_), channel_id=1, source_target_pairs={{0,1},{1,0},{2,3},{3,2},{4,5},{5,4},{6,7},{7,6},{8,9},{9,8},{10,11... | collective-permute-start | bytes 1671176 | tf_op jit(solution)/shard_map/ppermute | solution.py:276
  78.3 13.7 %collective-permute-start.19 = (bf16[128,2176]{1,0:T(8,128)(2,1)S(1)}, bf16[128,2176]{1,0:T(8,128)(2,1)S(1)}, u32[]{:S(2)}, u32[]{:S(2)}) collective-permute-start(bf16[128,2176]{1,0:T(8,128)(2,1)S(1)} %collective-permute-done.15.refs_4_), channel_id=1, source_target_pairs={{0,1},{1,0},{2,3},{3,2},{4,5},{5,4},{6,7},{7,6},{8,9},{9,8},{10,11... | collective-permute-start | bytes 1671176 | tf_op jit(solution)/shard_map/ppermute | solution.py:276
  91.4 15.7 %collective-permute-start.25 = (bf16[128,2176]{1,0:T(8,128)(2,1)S(1)}, bf16[128,2176]{1,0:T(8,128)(2,1)S(1)}, u32[]{:S(2)}, u32[]{:S(2)}) collective-permute-start(bf16[128,2176]{1,0:T(8,128)(2,1)S(1)} %broadcast_select_fusion.refs_2_), channel_id=1, source_target_pairs={{0,2},{1,3},{2,0},{3,1},{4,6},{5,7},{6,4},{7,5},{8,10},{9,11},{10,... | collective-permute-start | bytes 1671176 | tf_op jit(solution)/shard_map/ppermute | solution.py:276
  106.9 9.8 %collective-permute-start.20 = (bf16[512,1024]{1,0:T(8,128)(2,1)}, bf16[512,1024]{1,0:T(8,128)(2,1)S(1)}, u32[]{:S(2)}, u32[]{:S(2)}) collective-permute-start(bf16[512,1024]{1,0:T(8,128)(2,1)} %get-tuple-element.30), channel_id=1, source_target_pairs={{0,1},{1,0},{2,3},{3,2},{4,5},{5,4},{6,7},{7,6},{8,9},{9,8},{10,11... | collective-permute-start | bytes 3145736 | tf_op jit(solution)/shard_map/ppermute | solution.py:276
  107.1 4.1 %collective-permute-start.26 = (bf16[128,2176]{1,0:T(8,128)(2,1)S(1)}, bf16[128,2176]{1,0:T(8,128)(2,1)S(1)}, u32[]{:S(2)}, u32[]{:S(2)}) collective-permute-start(bf16[128,2176]{1,0:T(8,128)(2,1)S(1)} %collective-permute-done.25.refs_1_.refs_0_), channel_id=1, source_target_pairs={{0,1},{1,0},{2,3},{3,2},{4,5},{5,4},{6,7},{7,6},{8,9},{9,8},{10,11... | collective-permute-start | bytes 1671176 | tf_op jit(solution)/shard_map/ppermute | solution.py:276
  107.4 21.6 %collective-permute-start.8 = (bf16[384,1024]{1,0:T(8,128)(2,1)}, bf16[384,1024]{1,0:T(8,128)(2,1)}, u32[]{:S(2)}, u32[]{:S(2)}) collective-permute-start(bf16[384,1024]{1,0:T(8,128)(2,1)} %get-tuple-element.24), channel_id=1, source_target_pairs={{0,1},{1,0},{2,3},{3,2},{4,5},{5,4},{6,7},{7,6},{8,9},{9,8},{10,11... | collective-permute-start | bytes 2359304 | tf_op jit(solution)/shard_map/ppermute | solution.py:276
  116.9 20.0 %collective-permute-start.21 = (bf16[256,1024]{1,0:T(8,128)(2,1)S(1)}, bf16[256,1024]{1,0:T(8,128)(2,1)S(1)}, u32[]{:S(2)}, u32[]{:S(2)}) collective-permute-start(bf16[256,1024]{1,0:T(8,128)(2,1)S(1)} %add_convert_fusion), channel_id=1, source_target_pairs={{0,2},{1,3},{2,0},{3,1},{4,6},{5,7},{6,4},{7,5},{8,10},{9,11},{10,... | collective-permute-start | bytes 1572872 | tf_op jit(solution)/shard_map/ppermute | solution.py:276
  118.5 18.3 %collective-permute-start.28 = (bf16[128,1024]{1,0:T(8,128)(2,1)S(1)}, bf16[128,1024]{1,0:T(8,128)(2,1)}, u32[]{:S(2)}, u32[]{:S(2)}) collective-permute-start(bf16[128,1024]{1,0:T(8,128)(2,1)S(1)} %add_convert_fusion.3), channel_id=1, source_target_pairs={{0,2},{1,3},{2,0},{3,1},{4,6},{5,7},{6,4},{7,5},{8,10},{9,11},{10,... | collective-permute-start | bytes 786440 | tf_op jit(solution)/shard_map/ppermute | solution.py:276
  123.4 36.7 %collective-permute-start.31 = (bf16[512,768]{1,0:T(8,128)(2,1)}, bf16[512,768]{1,0:T(8,128)(2,1)S(1)}, u32[]{:S(2)}, u32[]{:S(2)}) collective-permute-start(bf16[512,768]{1,0:T(8,128)(2,1)} %get-tuple-element.39), channel_id=1, source_target_pairs={{0,16},{16,0},{1,17},{17,1},{2,18},{18,2},{3,19},{19,3},{4,20},{20... | collective-permute-start | bytes 2359304 | tf_op jit(solution)/shard_map/ppermute | solution.py:277
  124.9 26.5 %collective-permute-start.32 = (bf16[384,512]{1,0:T(8,128)(2,1)}, bf16[384,512]{1,0:T(8,128)(2,1)S(1)}, u32[]{:S(2)}, u32[]{:S(2)}) collective-permute-start(bf16[384,512]{1,0:T(8,128)(2,1)} %get-tuple-element.41), channel_id=1, source_target_pairs={{0,16},{16,0},{1,17},{17,1},{2,18},{18,2},{3,19},{19,3},{4,20},{20... | collective-permute-start | bytes 1179656 | tf_op jit(solution)/shard_map/ppermute | solution.py:277
  138.6 22.8 %collective-permute-start.30 = (bf16[128,1024]{1,0:T(8,128)(2,1)S(1)}, bf16[128,1024]{1,0:T(8,128)(2,1)S(1)}, u32[]{:S(2)}, u32[]{:S(2)}) collective-permute-start(bf16[128,1024]{1,0:T(8,128)(2,1)S(1)} %get-tuple-element.48), channel_id=1, source_target_pairs={{0,12},{1,13},{2,14},{3,15},{12,0},{13,1},{14,2},{15,3},{16,28},{1... | collective-permute-start | bytes 786440 | tf_op jit(solution)/shard_map/ppermute | solution.py:276
  152.4 17.4 %collective-permute-start.29 = (bf16[128,1024]{1,0:T(8,128)(2,1)S(1)}, bf16[128,1024]{1,0:T(8,128)(2,1)S(1)}, u32[]{:S(2)}, u32[]{:S(2)}) collective-permute-start(bf16[128,1024]{1,0:T(8,128)(2,1)S(1)} %get-tuple-element.48), channel_id=1, source_target_pairs={{4,12},{5,13},{6,14},{7,15},{8,0},{9,1},{10,2},{11,3},{20,28},{21,... | collective-permute-start | bytes 786440 | tf_op jit(solution)/shard_map/ppermute | solution.py:276
  153.7 16.2 %collective-permute-start.24 = (bf16[128,1024]{1,0:T(8,128)(2,1)S(1)}, bf16[128,1024]{1,0:T(8,128)(2,1)S(1)}, u32[]{:S(2)}, u32[]{:S(2)}) collective-permute-start(bf16[128,1024]{1,0:T(8,128)(2,1)S(1)} %get-tuple-element.49), channel_id=1, source_target_pairs={{0,8},{1,9},{2,10},{3,11},{12,4},{13,5},{14,6},{15,7},{16,24},{17,... | collective-permute-start | bytes 786440 | tf_op jit(solution)/shard_map/ppermute | solution.py:276
  159.4 10.4 %collective-permute-start.23 = (bf16[128,1024]{1,0:T(8,128)(2,1)S(1)}, bf16[128,1024]{1,0:T(8,128)(2,1)S(1)}, u32[]{:S(2)}, u32[]{:S(2)}) collective-permute-start(bf16[128,1024]{1,0:T(8,128)(2,1)S(1)} %get-tuple-element.49), channel_id=1, source_target_pairs={{4,8},{5,9},{6,10},{7,11},{8,4},{9,5},{10,6},{11,7},{20,24},{21,25... | collective-permute-start | bytes 786440 | tf_op jit(solution)/shard_map/ppermute | solution.py:276
  160.1 9.7 %collective-permute-start.22 = (bf16[128,1024]{1,0:T(8,128)(2,1)S(1)}, bf16[128,1024]{1,0:T(8,128)(2,1)S(1)}, u32[]{:S(2)}, u32[]{:S(2)}) collective-permute-start(bf16[128,1024]{1,0:T(8,128)(2,1)S(1)} %get-tuple-element.47), channel_id=1, source_target_pairs={{0,4},{1,5},{2,6},{3,7},{4,0},{5,1},{6,2},{7,3},{8,12},{9,13},{10,... | collective-permute-start | bytes 786440 | tf_op jit(solution)/shard_map/ppermute | solution.py:276
  161.3 8.5 %collective-permute-start.9 = (bf16[128,1024]{1,0:T(8,128)(2,1)S(1)}, bf16[128,1024]{1,0:T(8,128)(2,1)S(1)}, u32[]{:S(2)}, u32[]{:S(2)}) collective-permute-start(bf16[128,1024]{1,0:T(8,128)(2,1)S(1)} %get-tuple-element.46), channel_id=1, source_target_pairs={{0,2},{1,3},{2,0},{3,1},{4,6},{5,7},{6,4},{7,5},{8,10},{9,11},{10,... | collective-permute-start | bytes 786440 | tf_op jit(solution)/shard_map/ppermute | solution.py:276
  (23 other events, 317.3 us)

commit v2 on v0

--- a/solution.py
+++ b/solution.py
@@ -1,7 +1,327 @@
+import functools
+
 import jax
 import jax.numpy as jnp
 from jax import lax
+from jax.experimental import pallas as pl
+from jax.experimental.pallas import tpu as pltpu
 from jax.sharding import PartitionSpec as P
+
+F32 = jnp.float32
+BF16 = jnp.bfloat16
+LANES = 128
+VMEM_BYTES = 56 * 1024 * 1024
+
+
+def vmem():
+    return pl.BlockSpec(memory_space=pltpu.VMEM)
+
+
+def smem():
+    return pl.BlockSpec(memory_space=pltpu.SMEM)
+
+
+def hbm():
+    return pl.BlockSpec(memory_space=pl.ANY)
+
+
+def params():
+    return pltpu.CompilerParams(vmem_limit_bytes=VMEM_BYTES)
+
+
+def cost():
+    return pl.CostEstimate(flops=1024, bytes_accessed=1024, transcendentals=0)
+
+
+def dot(a, b, dims):
+    return lax.dot_general(a, b, (dims, ((), ())), preferred_element_type=F32)
+
+
+def pack_kernel(experts, tokens, d_output, combine, routes, out):
+    rows, width = tokens.shape
+    out[:, :width] = tokens[...]
+    out[:, width : 2 * width] = d_output[...]
+    line = lax.broadcasted_iota(jnp.int32, (LANES, rows), 0)
+    expert = lax.rem(line, experts)
+    dense = jnp.zeros((LANES, rows), F32)
+    for k in range(routes.shape[0]):
+        dense = dense + jnp.where(expert == routes[k : k + 1, :], combine[k : k + 1, :], 0.0)
+    high = dense.astype(BF16).astype(F32)
+    rest = dense - high
+    middle = rest.astype(BF16).astype(F32)
+    low = rest - middle
+    parts = jnp.where(
+        line < experts,
+        high,
+        jnp.where(line < 2 * experts, middle, jnp.where(line < 3 * experts, low, 0.0)),
+    )
+    out[:, 2 * width :] = parts.T.astype(BF16)
+
+
+def pack(experts, tokens, d_output, combine, routes):
+    rows, width = tokens.shape
+    return pl.pallas_call(
+        functools.partial(pack_kernel, experts),
+        out_shape=jax.ShapeDtypeStruct((rows, 2 * width + LANES), BF16),
+        in_specs=[vmem()] * 4,
+        out_specs=vmem(),
+        cost_estimate=cost(),
+        compiler_params=params(),
+    )(tokens, d_output, combine.T, routes.T)
+
+
+def pack_weights_kernel(gate, up, down, out):
+    hidden_units = gate.shape[1]
+    out[:, :hidden_units] = gate[...]
+    out[:, hidden_units : 2 * hidden_units] = up[...]
+    out[:, 2 * hidden_units :] = down[...].T
+
+
+def pack_weights(gate, up, down):
+    size, hidden_units = gate.shape
+    return pl.pallas_call(
+        pack_weights_kernel,
+        out_shape=jax.ShapeDtypeStruct((size, 3 * hidden_units), BF16),
+        in_specs=[vmem()] * 3,
+        out_specs=vmem(),
+        cost_estimate=cost(),
+        compiler_params=params(),
+    )(gate, up, down)
+
+
+def rows_kernel(experts, count, scal, *refs):
+    refs = list(refs)
+    blocks = [refs.pop(0) for _ in range(count)]
+    weights = [refs.pop(0) for _ in range(4)]
+    out_rows = [refs.pop(0) for _ in range(count)]
+    kept = [refs.pop(0) for _ in range(4)]
+    held, total, sems = refs
+    part, expert = scal[0], scal[1]
+    size = weights[0].shape[0]
+    hidden_units = weights[0].shape[1] // 3
+    width = 2 * size
+    rows = blocks[0].shape[0]
+    copies = [pltpu.make_async_copy(weights[i], held.at[i], sems.at[i]) for i in range(4)]
+    for c in copies:
+        c.start()
+    sides = [pl.multiple_of(part * size, size), pl.multiple_of((1 - part) * size, size)]
+    both = 2 * hidden_units
+    for which in range(2):
+        scaled_out, grads_out = kept[2 * which], kept[2 * which + 1]
+        copies[2 * which].wait()
+        copies[2 * which + 1].wait()
+        for i in range(0, count, 2):
+            group = blocks[i : i + 2]
+            span = slice(i * rows, (i + len(group)) * rows)
+            parts = jnp.concatenate([b[:, 2 * width :] for b in group], axis=0).astype(F32)
+            lane = lax.broadcasted_iota(jnp.int32, parts.shape, 1)
+            wanted = expert if which == 0 else expert + 1 - 2 * lax.rem(expert, 2)
+            mine = (lax.rem(lane, experts) == wanted) & (lane < 3 * experts)
+            weight = jnp.sum(jnp.where(mine, parts, 0.0), axis=1, keepdims=True)
+            preact = None
+            d_hidden = None
+            for side in range(2):
+                at = sides[side]
+                tok = jnp.concatenate([b[:, pl.ds(at, size)] for b in group], axis=0)
+                grad = jnp.concatenate([b[:, pl.ds(pl.multiple_of(width + at, size), size)] for b in group], axis=0)
+                scaled = (weight * grad.astype(F32)).astype(BF16)
+                scaled_out[span, pl.ds(at, size)] = scaled
+                half = held.at[2 * which + side]
+                p = dot(tok, half[:, :both], ((1,), (0,)))
+                h = dot(scaled, half[:, both:], ((1,), (0,)))
+                preact = p if side == 0 else preact + p
+                d_hidden = h if side == 0 else d_hidden + h
+            gate_pre = preact[:, :hidden_units]
+            up_pre = preact[:, hidden_units:]
+            sig = jax.nn.sigmoid(gate_pre)
+            silu = gate_pre * sig
+            d_gate = (d_hidden * up_pre * sig * (1.0 + gate_pre * (1.0 - sig))).astype(BF16)
+            d_up = (d_hidden * silu).astype(BF16)
+            grads_out[span, :hidden_units] = d_gate
+            grads_out[span, hidden_units:both] = d_up
+            grads_out[span, both:] = (silu * up_pre).astype(BF16)
+            d_preact = jnp.concatenate([d_gate, d_up], axis=1)
+            for side in range(2):
+                at = sides[side]
+                d_rows = dot(d_preact, held[2 * which + side, :, :both], ((1,), (1,)))
+                if which == 0:
+                    total[span, pl.ds(at, size)] = d_rows
+                else:
+                    d_rows = (d_rows + total[span, pl.ds(at, size)]).astype(BF16)
+                    for j in range(len(group)):
+                        out_rows[i + j][:, pl.ds(at, size)] = d_rows[j * rows : (j + 1) * rows]
+
+
+def rows_call(experts, scal, blocks, weights):
+    count = len(blocks)
+    rows = blocks[0].shape[0]
+    size, stacked = weights[0].shape
+    total = count * rows
+    sds = jax.ShapeDtypeStruct
+    out = [sds((rows, 2 * size), BF16)] * count + [sds((total, 2 * size), BF16), sds((total, stacked), BF16)] * 2
+    return pl.pallas_call(
+        functools.partial(rows_kernel, experts, count),
+        out_shape=out,
+        in_specs=[smem()] + [vmem()] * count + [hbm()] * 4,
+        out_specs=[vmem()] * len(out),
+        scratch_shapes=[
+            pltpu.VMEM((4, size, stacked), BF16),
+            pltpu.VMEM((total, 2 * size), F32),
+            pltpu.SemaphoreType.DMA((4,)),
+        ],
+        cost_estimate=cost(),
+        compiler_params=params(),
+    )(scal, *blocks, *weights)
+
+
+def half_kernel(count, groups, side, *refs):
+    blocks = refs[:count]
+    scaled = refs[count : count + groups]
+    grads = refs[count + groups : count + 2 * groups]
+    out = refs[-1]
+    both = 2 * (out.shape[1] // 3)
+    tok = jnp.concatenate([b[...] for b in blocks], axis=0)
+    grad = jnp.concatenate([s[...] for s in scaled], axis=0)
+    made = jnp.concatenate([g[...] for g in grads], axis=0)
+    out[:, :both] = dot(tok, made[:, :both], ((0,), (0,))).astype(BF16)
+    out[:, both:] = dot(grad, made[:, both:], ((0,), (0,))).astype(BF16)
+
+
+def half_call(side, blocks, scaled, grads):
+    size = scaled[0].shape[1] // 2
+    stacked = grads[0].shape[1]
+    half = lambda a: pl.BlockSpec((a.shape[0], size), lambda i, s: (0, s[0]))
+    whole = lambda a: pl.BlockSpec(a.shape, lambda i, s: (0, 0))
+    return pl.pallas_call(
+        functools.partial(half_kernel, len(blocks), len(scaled)),
+        out_shape=jax.ShapeDtypeStruct((size, stacked), BF16),
+        grid_spec=pltpu.PrefetchScalarGridSpec(
+            num_scalar_prefetch=1,
+            grid=(1,),
+            in_specs=[half(b) for b in blocks] + [half(s) for s in scaled] + [whole(g) for g in grads],
+            out_specs=pl.BlockSpec((size, stacked), lambda i, s: (0, 0)),
+        ),
+        cost_estimate=cost(),
+        compiler_params=params(),
+    )(side, *blocks, *scaled, *grads)
+
+
+def finish_kernel(keep, from_core, from_part, d_gate, d_up, d_down):
+    hidden_units = d_gate.shape[1]
+    group = (keep[...].astype(F32) + from_core[...].astype(F32)).astype(BF16).astype(F32)
+    whole = group + from_part[...].astype(F32)
+    d_gate[...] = whole[:, :hidden_units]
+    d_up[...] = whole[:, hidden_units : 2 * hidden_units]
+    d_down[...] = whole[:, 2 * hidden_units :].T
+
+
+def finish(keep, from_core, from_part):
+    size, stacked = keep.shape
+    hidden_units = stacked // 3
+    sds = jax.ShapeDtypeStruct
+    return pl.pallas_call(
+        finish_kernel,
+        out_shape=[sds((size, hidden_units), F32), sds((size, hidden_units), F32), sds((hidden_units, size), F32)],
+        in_specs=[vmem()] * 3,
+        out_specs=[vmem()] * 3,
+        cost_estimate=cost(),
+        compiler_params=params(),
+    )(keep, from_core, from_part)
+
+
+Z, Y, CORES = 4, 2, 2
+
+
+def pairs_of(move):
+    out = []
+    for z in range(Z):
+        for y in range(Y):
+            for c in range(CORES):
+                to = move(z, y, c)
+                if to is not None:
+                    out.append(((z * Y + y) * CORES + c, (to[0] * Y + to[1]) * CORES + to[2]))
+    return out
+
+
+def along_z(table):
+    return pairs_of(lambda z, y, c: (table[z], y, c) if z in table else None)
+
+
+SWAP_CORE = pairs_of(lambda z, y, c: (z, y, 1 - c))
+SWAP_Y = pairs_of(lambda z, y, c: (z, 1 - y, c))
+OUTER = along_z({0: 1, 1: 0, 2: 3, 3: 2})
+INNER = along_z({1: 2, 2: 1})
+OUTWARD = along_z({1: 0, 2: 3})
+SKIP_TO_INNER = along_z({0: 2, 3: 1})
+SKIP_TO_OUTER = along_z({1: 3, 2: 0})
+ENDS = along_z({0: 3, 3: 0})
+
+
+def after(value, *others):
+    return lax.optimization_barrier((value,) + others)[0]
+
+
+def dense_body(tokens, d_output, combine, routes, gate_weight, up_weight, down_weight):
+    experts = lax.axis_size("expert")
+    part = lax.axis_index("dp")
+    expert = lax.axis_index("expert")
+    z = expert // (Y * CORES)
+    inner = (z == 1) | (z == 2)
+    scal = jnp.stack([part, expert]).astype(jnp.int32)
+    mine = part[None].astype(jnp.int32)
+    other = (1 - part)[None].astype(jnp.int32)
+
+    move = lambda a, pairs: lax.ppermute(a, "expert", pairs)
+    across = lambda a: lax.ppermute(a, "dp", [(0, 1), (1, 0)])
+
+    own = pack(experts, tokens, d_output, combine, routes)
+    w_own = pack_weights(gate_weight[0], up_weight[0], down_weight[0])
+    w_part = across(w_own)
+    w_core = move(w_own, SWAP_CORE)
+    w_both = move(w_part, SWAP_CORE)
+    weights = [w_own, w_part, w_core, w_both]
+
+    b1 = move(own, OUTER)
+    f1 = move(own, INNER)
+    y0 = move(own, SWAP_Y)
+    f2 = move(b1, INNER)
+    y1 = move(b1, SWAP_Y)
+    g1 = move(f1, OUTWARD)
+    b2 = jnp.where(inner, f1, g1)
+    y2 = move(b2, SWAP_Y)
+    g2 = move(f2, OUTWARD)
+    b3 = jnp.where(inner, f2, g2)
+    y3 = move(b3, SWAP_Y)
+
+    p0, p1, q0, *kept_a = rows_call(experts, scal, [own, b1, y0], weights)
+    p2, q1, p3, q2, *kept_b = rows_call(experts, scal, [b2, y1, b3, y2], weights)
+    q3, *kept_c = rows_call(experts, scal, [y3], weights)
+    r0, r1, r2, r3 = (move(q, SWAP_Y) for q in (q0, q1, q2, q3))
+
+    blocks = [own, b1, y0, b2, y1, b3, y2, y3]
+    kept = [kept_a, kept_b, kept_c]
+    half = lambda side, which: half_call(side, blocks, [k[2 * which] for k in kept], [k[2 * which + 1] for k in kept])
+    got = move(half(other, 1), SWAP_CORE)
+    send = (half(other, 0).astype(F32) + got.astype(F32)).astype(BF16)
+    from_part = across(send)
+    from_core = move(half(mine, 1), SWAP_CORE)
+    keep = half(mine, 0)
+
+    add = lambda *terms: sum(t.astype(F32) for t in terms).astype(BF16)
+    s1 = add(p1, r1)
+    s2 = add(p2, r2)
+    s3 = add(p3, r3)
+    d_tokens = add(
+        p0,
+        r0,
+        move(s1, OUTER),
+        move(s2, INNER),
+        move(s2, SKIP_TO_INNER),
+        move(s3, SKIP_TO_OUTER),
+        move(s3, ENDS),
+    )
+    d_gate, d_up, d_down = finish(keep, from_core, from_part)
+    return (d_tokens, d_gate[None], d_up[None], d_down[None])
 
 
 def route_slots(routes, experts):
@@ -28,7 +348,7 @@
     return (d_rows, hidden, d_preact)
 
 
-def body(tokens, d_output, combine, routes, gate_weight, up_weight, down_weight):
+def routed_body(tokens, d_output, combine, routes, gate_weight, up_weight, down_weight):
     experts = lax.axis_size("expert")
     tok_count = tokens.shape[0]
     model_width = tokens.shape[1]
@@ -103,8 +423,9 @@
         P("expert", "dp", None),
         P("expert", None, "dp"),
     )
+    dense = mesh.shape["expert"] == Z * Y * CORES and mesh.shape["dp"] == 2
     return jax.shard_map(
-        body,
+        dense_body if dense else routed_body,
         mesh=mesh,
         in_specs=placed,
         out_specs=(

time: 231 us -> 170 us (0.74)
  the two profiles are of different devices: /device:TPU:15 before, /device:TPU:0 now
where the time goes in v2:
time: 170 us; the launch traced here: 169 us
  waiting for transfers between devices  75.1 us (44%)
  Pallas kernels  53.1 us (31%)
  starting transfers between devices  31.9 us (19%)
  other arithmetic  4.53 us (3%)
  local copies, waits for them, and re-layouts  3.72 us (2%)
    ppermute x22, waiting for transfers between devices, dense_body(): move = lambda a, pairs: lax.ppermute(a, 'expert', pairs)  62.6 us
    ppermute x22, starting transfers between devices, dense_body(): move = lambda a, pairs: lax.ppermute(a, 'expert', pairs)  28.8 us
    pallas_call x3, Pallas kernels, rows_call(): pl.pallas_call(functools.partial(rows_kernel, experts, count), out_shape=...  24.8 us
    pallas_call x4, Pallas kernels, half_call(): pl.pallas_call(functools.partial(half_kernel, len(blocks), len(scaled)),...  19.9 us
    ppermute x2, waiting for transfers between devices, dense_body(): across = lambda a: lax.ppermute(a, 'dp', [(0, 1), (1, 0)])  12.5 us
    pallas_call x1, Pallas kernels, finish(): pl.pallas_call(finish_kernel, out_shape=[sds((size, hidden_units), F32),...  3.86 us
    unnamed x36, local copies, waits for them, and re-layouts  3.72 us
  transfers between devices with their start and end apart: 24, of which 9 were waited for; matrix products, arithmetic and copies ran while one was open for 3% of the time, Pallas kernels for 19%

profile of v2, /device:TPU:0, one launch (start us, length us, event | category | flops | bytes accessed | tf_op | source)
XLA Modules:
  0.0 169.3 jit_solution(17311226899076903379)
XLA Ops:
  0.6 2.0 %shard_map.102.refs_0_ = bf16[128,2176]{1,0:T(8,128)(2,1)} custom-call(bf16[128,1024]{1,0:T(8,128)(2,1)} %tokens.1, bf16[128,1024]{1,0:T(8,128)(2,1)} %d_output.1, f32[8,128]{1,0:T(8,128)} %bitcast.14, s32[8,128]{1,0:T(8,128)} %bitcast.15), custom_call_target="tpu_custom_call" | custom-call | flops 1024 | bytes 1024 | tf_op jit(solution)/shard_map/pallas_call | solution.py:63
  2.6 3.0 %collective-permute-start = (bf16[128,2176]{1,0:T(8,128)(2,1)}, bf16[128,2176]{1,0:T(8,128)(2,1)S(1)}, u32[]{:S(2)}, u32[]{:S(2)}) collective-permute-start(bf16[128,2176]{1,0:T(8,128)(2,1)} %shard_map.102.refs_0_), channel_id=1, source_target_pairs={{0,4},{1,5},{2,6},{3,7},{4,0},{5,1},{6,2},{7,3},{8,12},{9,13},{10,... | collective-permute-start | bytes 1671176 | tf_op jit(solution)/shard_map/ppermute | solution.py:274
  5.6 2.5 %shard_map.103.refs_3_.refs_4_.refs_1_ = bf16[512,1152]{1,0:T(8,128)(2,1)} custom-call(bf16[512,384]{1,0:T(8,128)(2,1)} %bitcast.11, bf16[512,384]{1,0:T(8,128)(2,1)} %bitcast.12, bf16[384,512]{1,0:T(8,128)(2,1)} %bitcast.13), custom_call_target="tpu_custom_call" | custom-call | flops 1024 | bytes 1024 | tf_op jit(solution)/shard_map/pallas_call | solution.py:82
  8.1 1.5 collective-permute-start.2
  9.6 8.8 %collective-permute-done.refs_1_ = bf16[128,2176]{1,0:T(8,128)(2,1)S(1)} collective-permute-done((bf16[128,2176]{1,0:T(8,128)(2,1)}, bf16[128,2176]{1,0:T(8,128)(2,1)S(1)}, u32[]{:S(2)}, u32[]{:S(2)}) %collective-permute-start) | collective-permute-done | bytes 557088 | tf_op jit(solution)/shard_map/ppermute | solution.py:274
  19.9 1.3 collective-permute-start.10
  21.3 1.8 %collective-permute-start.1 = (bf16[128,2176]{1,0:T(8,128)(2,1)S(1)}, bf16[128,2176]{1,0:T(8,128)(2,1)S(1)}, u32[]{:S(2)}, u32[]{:S(2)}) collective-permute-start(bf16[128,2176]{1,0:T(8,128)(2,1)S(1)} %copy-done), channel_id=1, source_target_pairs={{0,2},{1,3},{2,0},{3,1},{4,6},{5,7},{6,4},{7,5},{8,10},{9,11},{10,... | collective-permute-start | bytes 1671176 | tf_op jit(solution)/shard_map/ppermute | solution.py:274
  23.4 12.5 %collective-permute-done.2.refs_4_.refs_5_.refs_2_ = bf16[512,1152]{1,0:T(8,128)(2,1)} collective-permute-done((bf16[512,1152]{1,0:T(8,128)(2,1)}, bf16[512,1152]{1,0:T(8,128)(2,1)}, u32[]{:S(2)}, u32[]{:S(2)}) %collective-permute-start.2) | collective-permute-done | bytes 1179680 | tf_op jit(solution)/shard_map/ppermute | solution.py:275
  37.2 10.9 %collective-permute-done.10 = bf16[128,2176]{1,0:T(8,128)(2,1)} collective-permute-done((bf16[128,2176]{1,0:T(8,128)(2,1)S(1)}, bf16[128,2176]{1,0:T(8,128)(2,1)}, u32[]{:S(2)}, u32[]{:S(2)}) %collective-permute-start.10) | collective-permute-done | bytes 557088 | tf_op jit(solution)/shard_map/ppermute | solution.py:274
  49.2 11.8 %collective-permute-done.7 = bf16[128,2176]{1,0:T(8,128)(2,1)S(1)} collective-permute-done((bf16[128,2176]{1,0:T(8,128)(2,1)S(1)}, bf16[128,2176]{1,0:T(8,128)(2,1)S(1)}, u32[]{:S(2)}, u32[]{:S(2)}) %collective-permute-start.7) | collective-permute-done | bytes 557088 | tf_op jit(solution)/shard_map/ppermute | solution.py:274
  61.7 1.6 collective-permute-start.11
  63.8 12.9 %collective-permute-done.17.refs_0_.refs_7_ = bf16[128,2176]{1,0:T(8,128)(2,1)} collective-permute-done((bf16[128,2176]{1,0:T(8,128)(2,1)S(1)}, bf16[128,2176]{1,0:T(8,128)(2,1)}, u32[]{:S(2)}, u32[]{:S(2)}) %collective-permute-start.17) | collective-permute-done | bytes 557088 | tf_op jit(solution)/shard_map/ppermute | solution.py:274
  76.7 5.6 %shard_map.106 = (bf16[128,1024]{1,0:T(8,128)(2,1)}, bf16[128,1024]{1,0:T(8,128)(2,1)}, bf16[128,1152]{1,0:T(8,128)(2,1)}, bf16[128,1024]{1,0:T(8,128)(2,1)}, bf16[128,1152]{1,0:T(8,128)(2,1)}) custom-call(s32[2]{0:T(128)} %pad_add_fusion.scal, bf16[128,2176]{1,0:T(8,128)(2,1)} %collective-permute-done.17.refs_0_.refs_7_, ...), custom_call_target="tpu_custom_call" | custom-call | flops 1024 | bytes 1024 | tf_op jit(solution)/shard_map/pallas_call | solution.py:162
  83.2 8.7 %shard_map.104 = (bf16[128,1024]{1,0:T(8,128)(2,1)}, bf16[128,1024]{1,0:T(8,128)(2,1)}, bf16[128,1024]{1,0:T(8,128)(2,1)}, bf16[384,1024]{1,0:T(8,128)(2,1)}, bf...) custom-call(s32[2]{0:T(128)} %pad_add_fusion.scal, ...), custom_call_target="tpu_custom_call" | custom-call | flops 1024 | bytes 1024 | tf_op jit(solution)/shard_map/pallas_call | solution.py:162
  92.8 10.5 %shard_map.105 = (bf16[128,1024]{1,0:T(8,128)(2,1)}, bf16[128,1024]{1,0:T(8,128)(2,1)}, bf16[128,1024]{1,0:T(8,128)(2,1)}, bf16[128,1024]{1,0:T(8,128)(2,1)}, bf...) custom-call(s32[2]{0:T(128)} %pad_add_fusion.scal, ...), custom_call_target="tpu_custom_call" | custom-call | flops 1024 | bytes 1024 | tf_op jit(solution)/shard_map/pallas_call | solution.py:162
  103.2 4.9 %shard_map.110 = bf16[512,1152]{1,0:T(8,128)(2,1)} custom-call(s32[1]{0:T(128)} %bitcast.7.side, bf16[128,2176]{1,0:T(8,128)(2,1)} %shard_map.102.refs_0_, bf16[128,2176]{1,0:T(8,128)(2,1)} %copy-done.3, bf16[128,2176]{1,0:T(8,128)(2,1)} %copy-done.4, bf16[128,2176]{1,0:T(8,128)(2,1)} %copy-done.2, bf16[128,2176]{1,0:T(8,128)(2,1)} %copy-done.5, ...), custom_call_target="tpu_custom_call" | custom-call | flops 1024 | bytes 1024 | tf_op jit(solution)/shard_map/pallas_call | solution.py:195
  108.3 5.2 %shard_map.108 = bf16[512,1152]{1,0:T(8,128)(2,1)} custom-call(s32[1]{0:T(128)} %bitcast.side, bf16[128,2176]{1,0:T(8,128)(2,1)} %shard_map.102.refs_0_, bf16[128,2176]{1,0:T(8,128)(2,1)} %copy-done.3, bf16[128,2176]{1,0:T(8,128)(2,1)} %copy-done.4, bf16[128,2176]{1,0:T(8,128)(2,1)} %copy-done.2, bf16[128,2176]{1,0:T(8,128)(2,1)} %copy-done.5, ...), custom_call_target="tpu_custom_call" | custom-call | flops 1024 | bytes 1024 | tf_op jit(solution)/shard_map/pallas_call | solution.py:195
  114.4 1.5 collective-permute-start.14
  116.4 4.9 %shard_map.109 = bf16[512,1152]{1,0:T(8,128)(2,1)} custom-call(s32[1]{0:T(128)} %bitcast.7.side, bf16[128,2176]{1,0:T(8,128)(2,1)} %shard_map.102.refs_0_, bf16[128,2176]{1,0:T(8,128)(2,1)} %copy-done.3, bf16[128,2176]{1,0:T(8,128)(2,1)} %copy-done.4, bf16[128,2176]{1,0:T(8,128)(2,1)} %copy-done.2, bf16[128,2176]{1,0:T(8,128)(2,1)} %copy-done.5, ...), custom_call_target="tpu_custom_call" | custom-call | flops 1024 | bytes 1024 | tf_op jit(solution)/shard_map/pallas_call | solution.py:195
  121.4 1.6 collective-permute-start.5
  123.0 1.5 add_convert_fusion
  124.5 1.6 collective-permute-start.23
  126.2 2.5 %collective-permute-done.14 = bf16[128,1024]{1,0:T(8,128)(2,1)S(1)} collective-permute-done((bf16[128,1024]{1,0:T(8,128)(2,1)S(1)}, bf16[128,1024]{1,0:T(8,128)(2,1)S(1)}, u32[]{:S(2)}, u32[]{:S(2)}) %collective-permute-start.14) | collective-permute-done | bytes 262176 | tf_op jit(solution)/shard_map/ppermute | solution.py:274
  128.7 2.4 %collective-permute-start.13 = (bf16[128,1024]{1,0:T(8,128)(2,1)S(1)}, bf16[128,1024]{1,0:T(8,128)(2,1)S(1)}, u32[]{:S(2)}, u32[]{:S(2)}) collective-permute-start(bf16[128,1024]{1,0:T(8,128)(2,1)S(1)} %add_convert_fusion.4), channel_id=1, source_target_pairs={{0,4},{1,5},{2,6},{3,7},{4,0},{5,1},{6,2},{7,3},{8,12},{9,13},{10,... | collective-permute-start | bytes 786440 | tf_op jit(solution)/shard_map/ppermute | solution.py:274
  131.2 3.1 %collective-permute-done.18 = bf16[128,1024]{1,0:T(8,128)(2,1)S(1)} collective-permute-done((bf16[128,1024]{1,0:T(8,128)(2,1)S(1)}, bf16[128,1024]{1,0:T(8,128)(2,1)S(1)}, u32[]{:S(2)}, u32[]{:S(2)}) %collective-permute-start.18) | collective-permute-done | bytes 262176 | tf_op jit(solution)/shard_map/ppermute | solution.py:274
  135.0 4.0 %collective-permute-done.5 = bf16[128,1024]{1,0:T(8,128)(2,1)S(1)} collective-permute-done((bf16[128,1024]{1,0:T(8,128)(2,1)S(1)}, bf16[128,1024]{1,0:T(8,128)(2,1)S(1)}, u32[]{:S(2)}, u32[]{:S(2)}) %collective-permute-start.5) | collective-permute-done | bytes 262176 | tf_op jit(solution)/shard_map/ppermute | solution.py:274
  139.0 5.3 %collective-permute-start.16 = (bf16[128,1024]{1,0:T(8,128)(2,1)S(1)}, bf16[128,1024]{1,0:T(8,128)(2,1)S(1)}, u32[]{:S(2)}, u32[]{:S(2)}) collective-permute-start(bf16[128,1024]{1,0:T(8,128)(2,1)S(1)} %add_convert_fusion.3), channel_id=1, source_target_pairs={{0,8},{1,9},{2,10},{3,11},{12,4},{13,5},{14,6},{15,7},{16,24},{17,... | collective-permute-start | bytes 786440 | tf_op jit(solution)/shard_map/ppermute | solution.py:274
  144.4 1.3 collective-permute-start.19
  145.7 3.2 %collective-permute-start.20 = (bf16[128,1024]{1,0:T(8,128)(2,1)S(1)}, bf16[128,1024]{1,0:T(8,128)(2,1)S(1)}, u32[]{:S(2)}, u32[]{:S(2)}) collective-permute-start(bf16[128,1024]{1,0:T(8,128)(2,1)S(1)} %add_convert_fusion.2), channel_id=1, source_target_pairs={{0,12},{1,13},{2,14},{3,15},{12,0},{13,1},{14,2},{15,3},{16,28},{1... | collective-permute-start | bytes 786440 | tf_op jit(solution)/shard_map/ppermute | solution.py:274
  148.9 4.9 %shard_map.107.keep = bf16[512,1152]{1,0:T(8,128)(2,1)} custom-call(s32[1]{0:T(128)} %bitcast.side, bf16[128,2176]{1,0:T(8,128)(2,1)} %shard_map.102.refs_0_, bf16[128,2176]{1,0:T(8,128)(2,1)} %copy-done.3, bf16[128,2176]{1,0:T(8,128)(2,1)} %copy-done.4, bf16[128,2176]{1,0:T(8,128)(2,1)} %copy-done.2, bf16[128,2176]{1,0:T(8,128)(2,1)} %copy-done.5, ...), custom_call_target="tpu_custom_call" | custom-call | flops 1024 | bytes 1024 | tf_op jit(solution)/shard_map/pallas_call | solution.py:195
  153.9 8.5 %collective-permute-done.19 = bf16[128,1024]{1,0:T(8,128)(2,1)S(1)} collective-permute-done((bf16[128,1024]{1,0:T(8,128)(2,1)S(1)}, bf16[128,1024]{1,0:T(8,128)(2,1)S(1)}, u32[]{:S(2)}, u32[]{:S(2)}) %collective-permute-start.19) | collective-permute-done | bytes 262176 | tf_op jit(solution)/shard_map/ppermute | solution.py:274
  165.4 3.9 %shard_map.111 = (f32[512,384]{1,0:T(8,128)}, f32[512,384]{1,0:T(8,128)}, f32[384,512]{1,0:T(8,128)}) custom-call(bf16[512,1152]{1,0:T(8,128)(2,1)} %shard_map.107.keep, bf16[512,1152]{1,0:T(8,128)(2,1)} %copy-done.6, bf16[512,1152]{1,0:T(8,128)(2,1)} %copy-done.7), custom_call_target="tpu_custom_call" | custom-call | flops 1024 | bytes 1024 | tf_op jit(solution)/shard_map/pallas_call | solution.py:222
  (70 shorter events, 12.5 us)
Async XLA Ops:
  2.6 15.9 %collective-permute-start = (bf16[128,2176]{1,0:T(8,128)(2,1)}, bf16[128,2176]{1,0:T(8,128)(2,1)S(1)}, u32[]{:S(2)}, u32[]{:S(2)}) collective-permute-start(bf16[128,2176]{1,0:T(8,128)(2,1)} %shard_map.102.refs_0_), channel_id=1, source_target_pairs={{0,4},{1,5},{2,6},{3,7},{4,0},{5,1},{6,2},{7,3},{8,12},{9,13},{10,... | collective-permute-start | bytes 1671176 | tf_op jit(solution)/shard_map/ppermute | solution.py:274
  5.6 13.5 %copy-start = (bf16[128,2176]{1,0:T(8,128)(2,1)S(1)}, bf16[128,2176]{1,0:T(8,128)(2,1)}, u32[]{:S(2)}) copy-start(bf16[128,2176]{1,0:T(8,128)(2,1)} %shard_map.102.refs_0_) | copy-start | bytes 1671172
  8.1 27.7 %collective-permute-start.2 = (bf16[512,1152]{1,0:T(8,128)(2,1)}, bf16[512,1152]{1,0:T(8,128)(2,1)}, u32[]{:S(2)}, u32[]{:S(2)}) collective-permute-start(bf16[512,1152]{1,0:T(8,128)(2,1)} %shard_map.103.refs_3_.refs_4_.refs_1_), channel_id=1, source_target_pairs={{0,16},{16,0},{1,17},{17,1},{2,18},{18,2},{3,19},{19,3},{4,20},{20... | collective-permute-start | bytes 3538952 | tf_op jit(solution)/shard_map/ppermute | solution.py:275
  18.5 43.2 %copy-start.3 = (bf16[128,2176]{1,0:T(8,128)(2,1)}, bf16[128,2176]{1,0:T(8,128)(2,1)S(1)}, u32[]{:S(2)}) copy-start(bf16[128,2176]{1,0:T(8,128)(2,1)S(1)} %collective-permute-done.refs_1_) | copy-start | bytes 1671172
  18.5 1.4 collective-permute-start.9
  19.2 3.9 %collective-permute-start.6 = (bf16[128,2176]{1,0:T(8,128)(2,1)S(1)}, bf16[128,2176]{1,0:T(8,128)(2,1)S(1)}, u32[]{:S(2)}, u32[]{:S(2)}) collective-permute-start(bf16[128,2176]{1,0:T(8,128)(2,1)S(1)} %copy-done), channel_id=1, source_target_pairs={{4,8},{5,9},{6,10},{7,11},{8,4},{9,5},{10,6},{11,7},{20,24},{21,25... | collective-permute-start | bytes 1671176 | tf_op jit(solution)/shard_map/ppermute | solution.py:274
  19.9 28.2 %copy-start.9 = (bf16[128,2176]{1,0:T(8,128)(2,1)}, bf16[128,2176]{1,0:T(8,128)(2,1)S(1)}, u32[]{:S(2)}) copy-start(bf16[128,2176]{1,0:T(8,128)(2,1)S(1)} %collective-permute-done.9) | copy-start | bytes 1671172
  19.9 28.2 %collective-permute-start.10 = (bf16[128,2176]{1,0:T(8,128)(2,1)S(1)}, bf16[128,2176]{1,0:T(8,128)(2,1)}, u32[]{:S(2)}, u32[]{:S(2)}) collective-permute-start(bf16[128,2176]{1,0:T(8,128)(2,1)S(1)} %collective-permute-done.9), channel_id=1, source_target_pairs={{4,0},{5,1},{6,2},{7,3},{8,12},{9,13},{10,14},{11,15},{20,16},{21,... | collective-permute-start | bytes 1671176 | tf_op jit(solution)/shard_map/ppermute | solution.py:274
  21.2 40.5 %collective-permute-start.3 = (bf16[512,1152]{1,0:T(8,128)(2,1)}, bf16[512,1152]{1,0:T(8,128)(2,1)}, u32[]{:S(2)}, u32[]{:S(2)}) collective-permute-start(bf16[512,1152]{1,0:T(8,128)(2,1)} %shard_map.103.refs_3_.refs_4_.refs_1_), channel_id=1, source_target_pairs={{0,1},{1,0},{2,3},{3,2},{4,5},{5,4},{6,7},{7,6},{8,9},{9,8},{10,11... | collective-permute-start | bytes 3538952 | tf_op jit(solution)/shard_map/ppermute | solution.py:274
  21.3 61.1 %collective-permute-start.1 = (bf16[128,2176]{1,0:T(8,128)(2,1)S(1)}, bf16[128,2176]{1,0:T(8,128)(2,1)S(1)}, u32[]{:S(2)}, u32[]{:S(2)}) collective-permute-start(bf16[128,2176]{1,0:T(8,128)(2,1)S(1)} %copy-done), channel_id=1, source_target_pairs={{0,2},{1,3},{2,0},{3,1},{4,6},{5,7},{6,4},{7,5},{8,10},{9,11},{10,... | collective-permute-start | bytes 1671176 | tf_op jit(solution)/shard_map/ppermute | solution.py:274
  23.0 38.0 %copy-start.8 = (bf16[128,2176]{1,0:T(8,128)(2,1)}, bf16[128,2176]{1,0:T(8,128)(2,1)S(1)}, u32[]{:S(2)}) copy-start(bf16[128,2176]{1,0:T(8,128)(2,1)S(1)} %collective-permute-done.6) | copy-start | bytes 1671172
  23.0 68.9 %collective-permute-start.8 = (bf16[128,2176]{1,0:T(8,128)(2,1)S(1)}, bf16[128,2176]{1,0:T(8,128)(2,1)S(1)}, u32[]{:S(2)}, u32[]{:S(2)}) collective-permute-start(bf16[128,2176]{1,0:T(8,128)(2,1)S(1)} %collective-permute-done.refs_1_), channel_id=1, source_target_pairs={{0,2},{1,3},{2,0},{3,1},{4,6},{5,7},{6,4},{7,5},{8,10},{9,11},{10,... | collective-permute-start | bytes 1671176 | tf_op jit(solution)/shard_map/ppermute | solution.py:274
  35.9 25.2 %collective-permute-start.7 = (bf16[128,2176]{1,0:T(8,128)(2,1)S(1)}, bf16[128,2176]{1,0:T(8,128)(2,1)S(1)}, u32[]{:S(2)}, u32[]{:S(2)}) collective-permute-start(bf16[128,2176]{1,0:T(8,128)(2,1)S(1)} %collective-permute-done.6), channel_id=1, source_target_pairs={{4,0},{5,1},{6,2},{7,3},{8,12},{9,13},{10,14},{11,15},{20,16},{21,... | collective-permute-start | bytes 1671176 | tf_op jit(solution)/shard_map/ppermute | solution.py:274
  48.1 28.6 %collective-permute-start.4 = (bf16[512,1152]{1,0:T(8,128)(2,1)}, bf16[512,1152]{1,0:T(8,128)(2,1)}, u32[]{:S(2)}, u32[]{:S(2)}) collective-permute-start(bf16[512,1152]{1,0:T(8,128)(2,1)} %collective-permute-done.2.refs_4_.refs_5_.refs_2_), channel_id=1, source_target_pairs={{0,1},{1,0},{2,3},{3,2},{4,5},{5,4},{6,7},{7,6},{8,9},{9,8},{10,11... | collective-permute-start | bytes 3538952 | tf_op jit(solution)/shard_map/ppermute | solution.py:274
  49.2 33.1 %copy-start.1 = (bf16[128,2176]{1,0:T(8,128)(2,1)}, bf16[128,2176]{1,0:T(8,128)(2,1)S(1)}, u32[]{:S(2)}) copy-start(bf16[128,2176]{1,0:T(8,128)(2,1)S(1)} %broadcast_select_fusion.refs_2_.refs_5_) | copy-start | bytes 1671172
  61.1 15.7 %collective-permute-start.17 = (bf16[128,2176]{1,0:T(8,128)(2,1)S(1)}, bf16[128,2176]{1,0:T(8,128)(2,1)}, u32[]{:S(2)}, u32[]{:S(2)}) collective-permute-start(bf16[128,2176]{1,0:T(8,128)(2,1)S(1)} %broadcast_select_fusion.refs_2_.refs_5_), channel_id=1, source_target_pairs={{0,2},{1,3},{2,0},{3,1},{4,6},{5,7},{6,4},{7,5},{8,10},{9,11},{10,... | collective-permute-start | bytes 1671176 | tf_op jit(solution)/shard_map/ppermute | solution.py:274
  61.7 20.7 %copy-start.2 = (bf16[128,2176]{1,0:T(8,128)(2,1)}, bf16[128,2176]{1,0:T(8,128)(2,1)S(1)}, u32[]{:S(2)}) copy-start(bf16[128,2176]{1,0:T(8,128)(2,1)S(1)} %broadcast_select_fusion.1.refs_0_.refs_3_) | copy-start | bytes 1671172
  61.7 30.3 %collective-permute-start.11 = (bf16[128,2176]{1,0:T(8,128)(2,1)S(1)}, bf16[128,2176]{1,0:T(8,128)(2,1)}, u32[]{:S(2)}, u32[]{:S(2)}) collective-permute-start(bf16[128,2176]{1,0:T(8,128)(2,1)S(1)} %broadcast_select_fusion.1.refs_0_.refs_3_), channel_id=1, source_target_pairs={{0,2},{1,3},{2,0},{3,1},{4,6},{5,7},{6,4},{7,5},{8,10},{9,11},{10,... | collective-permute-start | bytes 1671176 | tf_op jit(solution)/shard_map/ppermute | solution.py:274
  108.2 13.2 %collective-permute-start.22 = (bf16[512,1152]{1,0:T(8,128)(2,1)}, bf16[512,1152]{1,0:T(8,128)(2,1)S(1)}, u32[]{:S(2)}, u32[]{:S(2)}) collective-permute-start(bf16[512,1152]{1,0:T(8,128)(2,1)} %shard_map.110), channel_id=1, source_target_pairs={{0,1},{1,0},{2,3},{3,2},{4,5},{5,4},{6,7},{7,6},{8,9},{9,8},{10,11... | collective-permute-start | bytes 3538952 | tf_op jit(solution)/shard_map/ppermute | solution.py:274
  113.4 49.9 %collective-permute-start.21 = (bf16[512,1152]{1,0:T(8,128)(2,1)}, bf16[512,1152]{1,0:T(8,128)(2,1)S(1)}, u32[]{:S(2)}, u32[]{:S(2)}) collective-permute-start(bf16[512,1152]{1,0:T(8,128)(2,1)} %shard_map.108), channel_id=1, source_target_pairs={{0,1},{1,0},{2,3},{3,2},{4,5},{5,4},{6,7},{7,6},{8,9},{9,8},{10,11... | collective-permute-start | bytes 3538952 | tf_op jit(solution)/shard_map/ppermute | solution.py:274
  113.9 10.6 %collective-permute-start.12 = (bf16[128,1024]{1,0:T(8,128)(2,1)S(1)}, bf16[128,1024]{1,0:T(8,128)(2,1)S(1)}, u32[]{:S(2)}, u32[]{:S(2)}) collective-permute-start(bf16[128,1024]{1,0:T(8,128)(2,1)S(1)} %copy-done.17), channel_id=1, source_target_pairs={{0,2},{1,3},{2,0},{3,1},{4,6},{5,7},{6,4},{7,5},{8,10},{9,11},{10,... | collective-permute-start | bytes 786440 | tf_op jit(solution)/shard_map/ppermute | solution.py:274
  114.4 14.3 %collective-permute-start.14 = (bf16[128,1024]{1,0:T(8,128)(2,1)S(1)}, bf16[128,1024]{1,0:T(8,128)(2,1)S(1)}, u32[]{:S(2)}, u32[]{:S(2)}) collective-permute-start(bf16[128,1024]{1,0:T(8,128)(2,1)S(1)} %copy-done.16), channel_id=1, source_target_pairs={{0,2},{1,3},{2,0},{3,1},{4,6},{5,7},{6,4},{7,5},{8,10},{9,11},{10,... | collective-permute-start | bytes 786440 | tf_op jit(solution)/shard_map/ppermute | solution.py:274
  115.9 18.4 %collective-permute-start.18 = (bf16[128,1024]{1,0:T(8,128)(2,1)S(1)}, bf16[128,1024]{1,0:T(8,128)(2,1)S(1)}, u32[]{:S(2)}, u32[]{:S(2)}) collective-permute-start(bf16[128,1024]{1,0:T(8,128)(2,1)S(1)} %copy-done.15), channel_id=1, source_target_pairs={{0,2},{1,3},{2,0},{3,1},{4,6},{5,7},{6,4},{7,5},{8,10},{9,11},{10,... | collective-permute-start | bytes 786440 | tf_op jit(solution)/shard_map/ppermute | solution.py:274
  121.4 17.6 %collective-permute-start.5 = (bf16[128,1024]{1,0:T(8,128)(2,1)S(1)}, bf16[128,1024]{1,0:T(8,128)(2,1)S(1)}, u32[]{:S(2)}, u32[]{:S(2)}) collective-permute-start(bf16[128,1024]{1,0:T(8,128)(2,1)S(1)} %copy-done.14), channel_id=1, source_target_pairs={{0,2},{1,3},{2,0},{3,1},{4,6},{5,7},{6,4},{7,5},{8,10},{9,11},{10,... | collective-permute-start | bytes 786440 | tf_op jit(solution)/shard_map/ppermute | solution.py:274
  124.5 10.4 %copy-start.10 = (bf16[128,1024]{1,0:T(8,128)(2,1)S(1)}, bf16[128,1024]{1,0:T(8,128)(2,1)}, u32[]{:S(2)}) copy-start(bf16[128,1024]{1,0:T(8,128)(2,1)} %get-tuple-element.33) | copy-start | bytes 786436
  124.5 38.8 %collective-permute-start.23 = (bf16[512,1152]{1,0:T(8,128)(2,1)S(1)}, bf16[512,1152]{1,0:T(8,128)(2,1)S(1)}, u32[]{:S(2)}, u32[]{:S(2)}) collective-permute-start(bf16[512,1152]{1,0:T(8,128)(2,1)S(1)} %add_convert_fusion), channel_id=1, source_target_pairs={{0,16},{16,0},{1,17},{17,1},{2,18},{18,2},{3,19},{19,3},{4,20},{20... | collective-permute-start | bytes 3538952 | tf_op jit(solution)/shard_map/ppermute | solution.py:275
  128.7 15.7 %collective-permute-start.13 = (bf16[128,1024]{1,0:T(8,128)(2,1)S(1)}, bf16[128,1024]{1,0:T(8,128)(2,1)S(1)}, u32[]{:S(2)}, u32[]{:S(2)}) collective-permute-start(bf16[128,1024]{1,0:T(8,128)(2,1)S(1)} %add_convert_fusion.4), channel_id=1, source_target_pairs={{0,4},{1,5},{2,6},{3,7},{4,0},{5,1},{6,2},{7,3},{8,12},{9,13},{10,... | collective-permute-start | bytes 786440 | tf_op jit(solution)/shard_map/ppermute | solution.py:274
  134.3 11.4 %collective-permute-start.15 = (bf16[128,1024]{1,0:T(8,128)(2,1)S(1)}, bf16[128,1024]{1,0:T(8,128)(2,1)S(1)}, u32[]{:S(2)}, u32[]{:S(2)}) collective-permute-start(bf16[128,1024]{1,0:T(8,128)(2,1)S(1)} %add_convert_fusion.3), channel_id=1, source_target_pairs={{4,8},{5,9},{6,10},{7,11},{8,4},{9,5},{10,6},{11,7},{20,24},{21,25... | collective-permute-start | bytes 786440 | tf_op jit(solution)/shard_map/ppermute | solution.py:274
  135.0 27.3 %copy-start.13 = (bf16[128,1024]{1,0:T(8,128)(2,1)S(1)}, bf16[128,1024]{1,0:T(8,128)(2,1)}, u32[]{:S(2)}) copy-start(bf16[128,1024]{1,0:T(8,128)(2,1)} %get-tuple-element.27) | copy-start | bytes 786436
  139.0 14.8 %collective-permute-start.16 = (bf16[128,1024]{1,0:T(8,128)(2,1)S(1)}, bf16[128,1024]{1,0:T(8,128)(2,1)S(1)}, u32[]{:S(2)}, u32[]{:S(2)}) collective-permute-start(bf16[128,1024]{1,0:T(8,128)(2,1)S(1)} %add_convert_fusion.3), channel_id=1, source_target_pairs={{0,8},{1,9},{2,10},{3,11},{12,4},{13,5},{14,6},{15,7},{16,24},{17,... | collective-permute-start | bytes 786440 | tf_op jit(solution)/shard_map/ppermute | solution.py:274
  144.4 17.9 %collective-permute-start.19 = (bf16[128,1024]{1,0:T(8,128)(2,1)S(1)}, bf16[128,1024]{1,0:T(8,128)(2,1)S(1)}, u32[]{:S(2)}, u32[]{:S(2)}) collective-permute-start(bf16[128,1024]{1,0:T(8,128)(2,1)S(1)} %add_convert_fusion.2), channel_id=1, source_target_pairs={{4,12},{5,13},{6,14},{7,15},{8,0},{9,1},{10,2},{11,3},{20,28},{21,... | collective-permute-start | bytes 786440 | tf_op jit(solution)/shard_map/ppermute | solution.py:274
  145.7 16.6 %collective-permute-start.20 = (bf16[128,1024]{1,0:T(8,128)(2,1)S(1)}, bf16[128,1024]{1,0:T(8,128)(2,1)S(1)}, u32[]{:S(2)}, u32[]{:S(2)}) collective-permute-start(bf16[128,1024]{1,0:T(8,128)(2,1)S(1)} %add_convert_fusion.2), channel_id=1, source_target_pairs={{0,12},{1,13},{2,14},{3,15},{12,0},{13,1},{14,2},{15,3},{16,28},{1... | collective-permute-start | bytes 786440 | tf_op jit(solution)/shard_map/ppermute | solution.py:274
  (10 other events, 42.7 us)

commit v3 on v2

--- a/solution.py
+++ b/solution.py
@@ -89,92 +89,96 @@
     )(gate, up, down)
 
 
-def rows_kernel(experts, count, scal, *refs):
+def rows_kernel(experts, count, merged, scal, *refs):
     refs = list(refs)
     blocks = [refs.pop(0) for _ in range(count)]
-    weights = [refs.pop(0) for _ in range(4)]
-    out_rows = [refs.pop(0) for _ in range(count)]
-    kept = [refs.pop(0) for _ in range(4)]
+    sets = (len(refs) - 3 - merged) // 2
+    raw = [refs.pop(0) for _ in range(sets)]
+    out_rows = [refs.pop(0) for _ in range(merged)]
+    kept = [refs.pop(0) for _ in range(sets)]
     held, total, sems = refs
     part, expert = scal[0], scal[1]
-    size = weights[0].shape[0]
-    hidden_units = weights[0].shape[1] // 3
+    size = raw[0].shape[0]
+    hidden_units = raw[0].shape[1] // 3
+    both = 2 * hidden_units
     width = 2 * size
     rows = blocks[0].shape[0]
-    copies = [pltpu.make_async_copy(weights[i], held.at[i], sems.at[i]) for i in range(4)]
+    copies = [pltpu.make_async_copy(raw[i], held.at[i], sems.at[i]) for i in range(sets)]
     for c in copies:
         c.start()
     sides = [pl.multiple_of(part * size, size), pl.multiple_of((1 - part) * size, size)]
-    both = 2 * hidden_units
-    for which in range(2):
+    parts = jnp.concatenate([b[:, 2 * width :] for b in blocks], axis=0).astype(F32)
+    lane = lax.broadcasted_iota(jnp.int32, parts.shape, 1)
+    toks = [jnp.concatenate([b[:, pl.ds(at, size)] for b in blocks], axis=0) for at in sides]
+    for which in range(sets // 2):
         scaled_out, grads_out = kept[2 * which], kept[2 * which + 1]
-        copies[2 * which].wait()
-        copies[2 * which + 1].wait()
-        for i in range(0, count, 2):
-            group = blocks[i : i + 2]
-            span = slice(i * rows, (i + len(group)) * rows)
-            parts = jnp.concatenate([b[:, 2 * width :] for b in group], axis=0).astype(F32)
-            lane = lax.broadcasted_iota(jnp.int32, parts.shape, 1)
-            wanted = expert if which == 0 else expert + 1 - 2 * lax.rem(expert, 2)
-            mine = (lax.rem(lane, experts) == wanted) & (lane < 3 * experts)
-            weight = jnp.sum(jnp.where(mine, parts, 0.0), axis=1, keepdims=True)
-            preact = None
-            d_hidden = None
-            for side in range(2):
-                at = sides[side]
-                tok = jnp.concatenate([b[:, pl.ds(at, size)] for b in group], axis=0)
-                grad = jnp.concatenate([b[:, pl.ds(pl.multiple_of(width + at, size), size)] for b in group], axis=0)
-                scaled = (weight * grad.astype(F32)).astype(BF16)
-                scaled_out[span, pl.ds(at, size)] = scaled
-                half = held.at[2 * which + side]
-                p = dot(tok, half[:, :both], ((1,), (0,)))
-                h = dot(scaled, half[:, both:], ((1,), (0,)))
-                preact = p if side == 0 else preact + p
-                d_hidden = h if side == 0 else d_hidden + h
-            gate_pre = preact[:, :hidden_units]
-            up_pre = preact[:, hidden_units:]
-            sig = jax.nn.sigmoid(gate_pre)
-            silu = gate_pre * sig
-            d_gate = (d_hidden * up_pre * sig * (1.0 + gate_pre * (1.0 - sig))).astype(BF16)
-            d_up = (d_hidden * silu).astype(BF16)
-            grads_out[span, :hidden_units] = d_gate
-            grads_out[span, hidden_units:both] = d_up
-            grads_out[span, both:] = (silu * up_pre).astype(BF16)
-            d_preact = jnp.concatenate([d_gate, d_up], axis=1)
-            for side in range(2):
-                at = sides[side]
-                d_rows = dot(d_preact, held[2 * which + side, :, :both], ((1,), (1,)))
-                if which == 0:
-                    total[span, pl.ds(at, size)] = d_rows
-                else:
-                    d_rows = (d_rows + total[span, pl.ds(at, size)]).astype(BF16)
-                    for j in range(len(group)):
-                        out_rows[i + j][:, pl.ds(at, size)] = d_rows[j * rows : (j + 1) * rows]
-
-
-def rows_call(experts, scal, blocks, weights):
-    count = len(blocks)
+        for c in copies[2 * which : 2 * which + 2]:
+            c.wait()
+        wanted = expert if which == 0 else expert + 1 - 2 * lax.rem(expert, 2)
+        mine = (lax.rem(lane, experts) == wanted) & (lane < 3 * experts)
+        weight = jnp.sum(jnp.where(mine, parts, 0.0), axis=1, keepdims=True)
+        preact = None
+        d_hidden = None
+        for side in range(2):
+            at = sides[side]
+            grad_at = pl.multiple_of(width + at, size)
+            grad = jnp.concatenate([b[:, pl.ds(grad_at, size)] for b in blocks], axis=0)
+            scaled = (weight * grad.astype(F32)).astype(BF16)
+            scaled_out[:, pl.ds(at, size)] = scaled
+            p = dot(toks[side], held[2 * which + side, :, :both], ((1,), (0,)))
+            h = dot(scaled, held[2 * which + side, :, both:], ((1,), (0,)))
+            preact = p if side == 0 else preact + p
+            d_hidden = h if side == 0 else d_hidden + h
+        gate_pre = preact[:, :hidden_units]
+        up_pre = preact[:, hidden_units:]
+        sig = jax.nn.sigmoid(gate_pre)
+        silu = gate_pre * sig
+        d_gate = (d_hidden * up_pre * sig * (1.0 + gate_pre * (1.0 - sig))).astype(BF16)
+        d_up = (d_hidden * silu).astype(BF16)
+        grads_out[:, :hidden_units] = d_gate
+        grads_out[:, hidden_units:both] = d_up
+        grads_out[:, both:] = (silu * up_pre).astype(BF16)
+        d_preact = jnp.concatenate([d_gate, d_up], axis=1)
+        for side in range(2):
+            at = sides[side]
+            d_rows = dot(d_preact, held[2 * which + side, :, :both], ((1,), (1,)))
+            if which > 0:
+                d_rows = d_rows + total[:, pl.ds(at, size)]
+            if which + 1 < sets // 2:
+                total[:, pl.ds(at, size)] = d_rows
+            else:
+                d_rows = d_rows.astype(BF16)
+                row = 0
+                for out in out_rows:
+                    out[:, pl.ds(at, size)] = d_rows[row : row + out.shape[0]]
+                    row += out.shape[0]
+
+
+def rows_call(experts, scal, groups, weights):
+    blocks = [b for group in groups for b in group]
+    count, sets = len(blocks), len(weights)
     rows = blocks[0].shape[0]
     size, stacked = weights[0].shape
     total = count * rows
     sds = jax.ShapeDtypeStruct
-    out = [sds((rows, 2 * size), BF16)] * count + [sds((total, 2 * size), BF16), sds((total, stacked), BF16)] * 2
+    out = [sds((len(group) * rows, 2 * size), BF16) for group in groups]
+    out += [sds((total, 2 * size), BF16), sds((total, stacked), BF16)] * (sets // 2)
     return pl.pallas_call(
-        functools.partial(rows_kernel, experts, count),
+        functools.partial(rows_kernel, experts, count, len(groups)),
         out_shape=out,
-        in_specs=[smem()] + [vmem()] * count + [hbm()] * 4,
+        in_specs=[smem()] + [vmem()] * count + [hbm()] * sets,
         out_specs=[vmem()] * len(out),
         scratch_shapes=[
-            pltpu.VMEM((4, size, stacked), BF16),
+            pltpu.VMEM((sets, size, stacked), BF16),
             pltpu.VMEM((total, 2 * size), F32),
-            pltpu.SemaphoreType.DMA((4,)),
+            pltpu.SemaphoreType.DMA((sets,)),
         ],
         cost_estimate=cost(),
         compiler_params=params(),
     )(scal, *blocks, *weights)
 
 
-def half_kernel(count, groups, side, *refs):
+def half_kernel(count, groups, adds, side, *refs):
     blocks = refs[:count]
     scaled = refs[count : count + groups]
     grads = refs[count + groups : count + 2 * groups]
@@ -183,50 +187,59 @@
     tok = jnp.concatenate([b[...] for b in blocks], axis=0)
     grad = jnp.concatenate([s[...] for s in scaled], axis=0)
     made = jnp.concatenate([g[...] for g in grads], axis=0)
-    out[:, :both] = dot(tok, made[:, :both], ((0,), (0,))).astype(BF16)
-    out[:, both:] = dot(grad, made[:, both:], ((0,), (0,))).astype(BF16)
-
-
-def half_call(side, blocks, scaled, grads):
+    gate_up = dot(tok, made[:, :both], ((0,), (0,)))
+    down = dot(grad, made[:, both:], ((0,), (0,)))
+    if adds:
+        more = refs[count + 2 * groups]
+        gate_up = gate_up + more[:, :both].astype(F32)
+        down = down + more[:, both:].astype(F32)
+    out[:, :both] = gate_up.astype(BF16)
+    out[:, both:] = down.astype(BF16)
+
+
+def half_call(side, blocks, scaled, grads, more=None):
     size = scaled[0].shape[1] // 2
     stacked = grads[0].shape[1]
     half = lambda a: pl.BlockSpec((a.shape[0], size), lambda i, s: (0, s[0]))
     whole = lambda a: pl.BlockSpec(a.shape, lambda i, s: (0, 0))
+    extra = [] if more is None else [more]
     return pl.pallas_call(
-        functools.partial(half_kernel, len(blocks), len(scaled)),
+        functools.partial(half_kernel, len(blocks), len(scaled), len(extra)),
         out_shape=jax.ShapeDtypeStruct((size, stacked), BF16),
         grid_spec=pltpu.PrefetchScalarGridSpec(
             num_scalar_prefetch=1,
             grid=(1,),
-            in_specs=[half(b) for b in blocks] + [half(s) for s in scaled] + [whole(g) for g in grads],
+            in_specs=[half(b) for b in blocks] + [half(s) for s in scaled] + [whole(g) for g in [*grads, *extra]],
             out_specs=pl.BlockSpec((size, stacked), lambda i, s: (0, 0)),
         ),
         cost_estimate=cost(),
         compiler_params=params(),
-    )(side, *blocks, *scaled, *grads)
-
-
-def finish_kernel(keep, from_core, from_part, d_gate, d_up, d_down):
+    )(side, *blocks, *scaled, *grads, *extra)
+
+
+def finish_kernel(keep, from_part, d_gate, d_up, d_down):
     hidden_units = d_gate.shape[1]
-    group = (keep[...].astype(F32) + from_core[...].astype(F32)).astype(BF16).astype(F32)
-    whole = group + from_part[...].astype(F32)
+    whole = keep[...].astype(F32) + from_part[...].astype(F32)
     d_gate[...] = whole[:, :hidden_units]
     d_up[...] = whole[:, hidden_units : 2 * hidden_units]
     d_down[...] = whole[:, 2 * hidden_units :].T
 
 
-def finish(keep, from_core, from_part):
+def finish(keep, from_part):
     size, stacked = keep.shape
     hidden_units = stacked // 3
     sds = jax.ShapeDtypeStruct
+    step = size // 4
+    piece = lambda n: pl.BlockSpec((step, n), lambda i: (i, 0))
     return pl.pallas_call(
         finish_kernel,
         out_shape=[sds((size, hidden_units), F32), sds((size, hidden_units), F32), sds((hidden_units, size), F32)],
-        in_specs=[vmem()] * 3,
-        out_specs=[vmem()] * 3,
+        grid=(size // step,),
+        in_specs=[piece(stacked)] * 2,
+        out_specs=[piece(hidden_units), piece(hidden_units), pl.BlockSpec((hidden_units, step), lambda i: (0, i))],
         cost_estimate=cost(),
         compiler_params=params(),
-    )(keep, from_core, from_part)
+    )(keep, from_part)
 
 
 Z, Y, CORES = 4, 2, 2
@@ -274,43 +287,55 @@
     move = lambda a, pairs: lax.ppermute(a, "expert", pairs)
     across = lambda a: lax.ppermute(a, "dp", [(0, 1), (1, 0)])
 
-    own = pack(experts, tokens, d_output, combine, routes)
+    swap = lambda a: move(a, SWAP_CORE)
     w_own = pack_weights(gate_weight[0], up_weight[0], down_weight[0])
     w_part = across(w_own)
-    w_core = move(w_own, SWAP_CORE)
-    w_both = move(w_part, SWAP_CORE)
-    weights = [w_own, w_part, w_core, w_both]
+    own = pack(experts, tokens, d_output, combine, routes)
 
     b1 = move(own, OUTER)
     f1 = move(own, INNER)
     y0 = move(own, SWAP_Y)
+    w_core = swap(w_own)
     f2 = move(b1, INNER)
-    y1 = move(b1, SWAP_Y)
+    y1 = move(after(b1, y0), SWAP_Y)
     g1 = move(f1, OUTWARD)
     b2 = jnp.where(inner, f1, g1)
-    y2 = move(b2, SWAP_Y)
+    y2 = move(after(b2, y1, w_part), SWAP_Y)
+    w_both = swap(w_part)
+    weights = [w_own, w_part, w_core, w_both]
     g2 = move(f2, OUTWARD)
     b3 = jnp.where(inner, f2, g2)
-    y3 = move(b3, SWAP_Y)
-
-    p0, p1, q0, *kept_a = rows_call(experts, scal, [own, b1, y0], weights)
-    p2, q1, p3, q2, *kept_b = rows_call(experts, scal, [b2, y1, b3, y2], weights)
-    q3, *kept_c = rows_call(experts, scal, [y3], weights)
-    r0, r1, r2, r3 = (move(q, SWAP_Y) for q in (q0, q1, q2, q3))
-
-    blocks = [own, b1, y0, b2, y1, b3, y2, y3]
-    kept = [kept_a, kept_b, kept_c]
-    half = lambda side, which: half_call(side, blocks, [k[2 * which] for k in kept], [k[2 * which + 1] for k in kept])
-    got = move(half(other, 1), SWAP_CORE)
-    send = (half(other, 0).astype(F32) + got.astype(F32)).astype(BF16)
+
+    p0, p1, q0, *kept_a = rows_call(experts, scal, [[own], [b1], [y0]], weights)
+    y3 = move(after(b3, y2, p0), SWAP_Y)
+    p2, p3, q12, *kept_b = rows_call(experts, scal, [[b2], [b3], [y1, y2]], weights)
+
+    blocks = [own, b1, y0, b2, b3, y1, y2]
+    kept = [kept_a, kept_b]
+    others = lambda side, first: half_call(side, [first] + blocks[1:], [k[2] for k in kept], [k[3] for k in kept])
+    to_core = others(other, own)
+    y3 = after(y3, p2, to_core)
+    r12 = move(after(q12, y3), SWAP_Y)
+    r0 = move(after(q0, y3), SWAP_Y)
+
+    cy3 = swap(y3)
+    last, pair, scaled_c, grads_c = rows_call(experts, scal, [[y3], [cy3]], weights[:2])
+    q3 = last.astype(F32) + swap(pair).astype(F32)
+    all_blocks = blocks + [y3, cy3]
+    mine_of = lambda side, more: half_call(
+        side, all_blocks, [k[0] for k in kept] + [scaled_c], [k[1] for k in kept] + [grads_c], more
+    )
+    send = mine_of(other, swap(to_core))
     from_part = across(send)
-    from_core = move(half(mine, 1), SWAP_CORE)
-    keep = half(mine, 0)
-
+    keep = mine_of(mine, swap(others(mine, after(own, send))))
+
+    rows = own.shape[0]
+    r1, r2 = r12[:rows], r12[rows:]
+    r3 = move(after(q3.astype(BF16), r0, r12), SWAP_Y)
     add = lambda *terms: sum(t.astype(F32) for t in terms).astype(BF16)
     s1 = add(p1, r1)
     s2 = add(p2, r2)
-    s3 = add(p3, r3)
+    s3 = after(add(p3, r3), keep)
     d_tokens = add(
         p0,
         r0,
@@ -320,7 +345,7 @@
         move(s3, SKIP_TO_OUTER),
         move(s3, ENDS),
     )
-    d_gate, d_up, d_down = finish(keep, from_core, from_part)
+    d_gate, d_up, d_down = finish(keep, from_part)
     return (d_tokens, d_gate[None], d_up[None], d_down[None])
 
 

time: 170 us -> 168 us (0.988)
  waiting for transfers between devices: 75.1 us -> 68.2 us
  Pallas kernels: 53.1 us -> 55.3 us
  local copies, waits for them, and re-layouts: 3.72 us -> 5.79 us
    ppermute x2, waiting for transfers between devices: 12.5 us -> 3.66 us  [dense_body(): across = lambda a: lax.ppermute(a, 'dp', [(0, 1), (1, 0)])]
    pallas_call x7, Pallas kernels: 44.8 us -> 46.8 us  [the longest x3 25.2 us: rows_call(): pl.pallas_call(functools.partial(rows_kernel, experts, count, len(groups)...]
    unnamed x36 -> x46, local copies, waits for them, and re-layouts: 3.72 us -> 5.79 us
    ppermute x22 -> x23, waiting for transfers between devices: 62.6 us -> 64.6 us  [dense_body(): move = lambda a, pairs: lax.ppermute(a, 'expert', pairs)]
    ppermute x22 -> x23, starting transfers between devices: 28.8 us -> 29.4 us  [dense_body(): move = lambda a, pairs: lax.ppermute(a, 'expert', pairs)]
  transfers between devices with their start and end apart: 24 -> 25, of which waited for: 9 -> 9; matrix products, arithmetic and copies ran while one was open for 3% -> 2% of each run, Pallas kernels for 19% -> 16%
where the time goes in v3:
time: 168 us; the launch traced here: 167 us
  waiting for transfers between devices  68.2 us (41%)
  Pallas kernels  55.3 us (33%)
  starting transfers between devices  32.8 us (20%)
  local copies, waits for them, and re-layouts  5.79 us (3%)
  other arithmetic  3.91 us (2%)
    ppermute x23, waiting for transfers between devices, dense_body(): move = lambda a, pairs: lax.ppermute(a, 'expert', pairs)  64.6 us
    ppermute x23, starting transfers between devices, dense_body(): move = lambda a, pairs: lax.ppermute(a, 'expert', pairs)  29.4 us
    pallas_call x3, Pallas kernels, rows_call(): pl.pallas_call(functools.partial(rows_kernel, experts, count, len(groups)...  25.2 us
    pallas_call x4, Pallas kernels, half_call(): pl.pallas_call(functools.partial(half_kernel, len(blocks), len(scaled), l...  21.7 us
    unnamed x46, local copies, waits for them, and re-layouts  5.79 us
    pallas_call x1, Pallas kernels, finish(): pl.pallas_call(finish_kernel, out_shape=[sds((size, hidden_units), F32),...  3.96 us
    ppermute x2, waiting for transfers between devices, dense_body(): across = lambda a: lax.ppermute(a, 'dp', [(0, 1), (1, 0)])  3.66 us
    ppermute x2, starting transfers between devices, dense_body(): across = lambda a: lax.ppermute(a, 'dp', [(0, 1), (1, 0)])  3.44 us
  transfers between devices with their start and end apart: 25, of which 9 were waited for; matrix products, arithmetic and copies ran while one was open for 2% of the time, Pallas kernels for 16%

profile of v3, /device:TPU:0, one launch (start us, length us, event | category | flops | bytes accessed | tf_op | source)
XLA Modules:
  0.0 167.0 jit_solution(5526586573026195845)
XLA Ops:
  0.6 2.5 %shard_map.103.refs_3_.refs_4_.refs_2_ = bf16[512,1152]{1,0:T(8,128)(2,1)} custom-call(bf16[512,384]{1,0:T(8,128)(2,1)} %bitcast.11, bf16[512,384]{1,0:T(8,128)(2,1)} %bitcast.12, bf16[384,512]{1,0:T(8,128)(2,1)} %bitcast.13), custom_call_target="tpu_custom_call" | custom-call | flops 1024 | bytes 1024 | tf_op jit(solution)/shard_map/pallas_call | solution.py:82
  3.1 2.9 %collective-permute-start.2 = (bf16[512,1152]{1,0:T(8,128)(2,1)}, bf16[512,1152]{1,0:T(8,128)(2,1)S(1)}, u32[]{:S(2)}, u32[]{:S(2)}) collective-permute-start(bf16[512,1152]{1,0:T(8,128)(2,1)} %shard_map.103.refs_3_.refs_4_.refs_2_), channel_id=1, source_target_pairs={{0,16},{16,0},{1,17},{17,1},{2,18},{18,2},{3,19},{19,3},{4,20},{20... | collective-permute-start | bytes 3538952 | tf_op jit(solution)/shard_map/ppermute | solution.py:288
  6.1 2.0 %shard_map.102.refs_0_ = bf16[128,2176]{1,0:T(8,128)(2,1)} custom-call(bf16[128,1024]{1,0:T(8,128)(2,1)} %tokens.1, bf16[128,1024]{1,0:T(8,128)(2,1)} %d_output.1, f32[8,128]{1,0:T(8,128)} %bitcast.14, s32[8,128]{1,0:T(8,128)} %bitcast.15), custom_call_target="tpu_custom_call" | custom-call | flops 1024 | bytes 1024 | tf_op jit(solution)/shard_map/pallas_call | solution.py:63
  8.0 1.6 collective-permute-start
  9.6 1.5 collective-permute-start.7
  11.1 1.5 collective-permute-start.1
  12.6 9.7 %collective-permute-done.refs_1_ = bf16[128,2176]{1,0:T(8,128)(2,1)S(1)} collective-permute-done((bf16[128,2176]{1,0:T(8,128)(2,1)}, bf16[128,2176]{1,0:T(8,128)(2,1)S(1)}, u32[]{:S(2)}, u32[]{:S(2)}) %collective-permute-start) | collective-permute-done | bytes 557088 | tf_op jit(solution)/shard_map/ppermute | solution.py:287
  22.3 1.5 collective-permute-start.5
  23.8 1.3 collective-permute-start.8
  25.8 1.5 collective-permute-start.9
  28.6 3.7 %collective-permute-done.2.refs_4_.refs_5_.refs_3_ = bf16[512,1152]{1,0:T(8,128)(2,1)S(1)} collective-permute-done((bf16[512,1152]{1,0:T(8,128)(2,1)}, bf16[512,1152]{1,0:T(8,128)(2,1)S(1)}, u32[]{:S(2)}, u32[]{:S(2)}) %collective-permute-start.2) | collective-permute-done | bytes 1179680 | tf_op jit(solution)/shard_map/ppermute | solution.py:288
  32.2 8.7 %collective-permute-done.8 = bf16[128,2176]{1,0:T(8,128)(2,1)} collective-permute-done((bf16[128,2176]{1,0:T(8,128)(2,1)}, bf16[128,2176]{1,0:T(8,128)(2,1)}, u32[]{:S(2)}, u32[]{:S(2)}) %collective-permute-start.8) | collective-permute-done | bytes 557088 | tf_op jit(solution)/shard_map/ppermute | solution.py:287
  42.2 1.6 collective-permute-start.10
  43.7 8.3 %collective-permute-done.6 = bf16[128,2176]{1,0:T(8,128)(2,1)S(1)} collective-permute-done((bf16[128,2176]{1,0:T(8,128)(2,1)}, bf16[128,2176]{1,0:T(8,128)(2,1)S(1)}, u32[]{:S(2)}, u32[]{:S(2)}) %collective-permute-start.6) | collective-permute-done | bytes 557088 | tf_op jit(solution)/shard_map/ppermute | solution.py:287
  55.0 9.0 %shard_map.104 = (bf16[128,1024]{1,0:T(8,128)(2,1)}, bf16[128,1024]{1,0:T(8,128)(2,1)}, bf16[128,1024]{1,0:T(8,128)(2,1)}, bf16[384,1024]{1,0:T(8,128)(2,1)}, bf...) custom-call(s32[2]{0:T(128)} %pad_add_fusion.scal, ...), custom_call_target="tpu_custom_call" | custom-call | flops 1024 | bytes 1024 | tf_op jit(solution)/shard_map/pallas_call | solution.py:166
  64.9 11.0 %shard_map.105 = (bf16[128,1024]{1,0:T(8,128)(2,1)}, bf16[128,1024]{1,0:T(8,128)(2,1)}, bf16[256,1024]{1,0:T(8,128)(2,1)}, bf16[512,1024]{1,0:T(8,128)(2,1)}, bf...) custom-call(s32[2]{0:T(128)} %pad_add_fusion.scal, bf16[128,2176]{1,0:T(8,128)(2,1)} %copy-done, ...), custom_call_target="tpu_custom_call" | custom-call | flops 1024 | bytes 1024 | tf_op jit(solution)/shard_map/pallas_call | solution.py:166
  75.9 4.8 %shard_map.106 = bf16[512,1152]{1,0:T(8,128)(2,1)} custom-call(s32[1]{0:T(128)} %bitcast.7.side, bf16[128,2176]{1,0:T(8,128)(2,1)} %shard_map.102.refs_0_, bf16[128,2176]{1,0:T(8,128)(2,1)} %copy-done.2, bf16[128,2176]{1,0:T(8,128)(2,1)} %copy-done.3, bf16[128,2176]{1,0:T(8,128)(2,1)} %copy-done, bf16[128,2176]{1,0:T(8,128)(2,1)} %broadcast_select_fusion.1.refs_1_.refs_4_, ...), custom_call_target="tpu_custom_call" | custom-call | flops 1024 | bytes 1024 | tf_op jit(solution)/shard_map/pallas_call | solution.py:206
  80.7 1.6 collective-permute-start.11
  82.3 13.5 %collective-permute-done.11.refs_0_.refs_7_ = bf16[128,2176]{1,0:T(8,128)(2,1)S(1)} collective-permute-done((bf16[128,2176]{1,0:T(8,128)(2,1)S(1)}, bf16[128,2176]{1,0:T(8,128)(2,1)S(1)}, u32[]{:S(2)}, u32[]{:S(2)}) %collective-permute-start.11) | collective-permute-done | bytes 557088 | tf_op jit(solution)/shard_map/ppermute | solution.py:287
  95.8 2.0 %collective-permute-done.17.refs_1_.refs_8_ = bf16[128,2176]{1,0:T(8,128)(2,1)S(1)} collective-permute-done((bf16[128,2176]{1,0:T(8,128)(2,1)S(1)}, bf16[128,2176]{1,0:T(8,128)(2,1)S(1)}, u32[]{:S(2)}, u32[]{:S(2)}) %collective-permute-start.17) | collective-permute-done | bytes 557088 | tf_op jit(solution)/shard_map/ppermute | solution.py:287
  98.5 5.2 %shard_map.107 = (bf16[128,1024]{1,0:T(8,128)(2,1)}, bf16[128,1024]{1,0:T(8,128)(2,1)}, bf16[256,1024]{1,0:T(8,128)(2,1)}, bf16[256,1152]{1,0:T(8,128)(2,1)}) custom-call(s32[2]{0:T(128)} %pad_add_fusion.scal, bf16[128,2176]{1,0:T(8,128)(2,1)} %copy-done.7, bf16[128,2176]{1,0:T(8,128)(2,1)} %copy-done.8, ...), custom_call_target="tpu_custom_call" | custom-call | flops 1024 | bytes 1024 | tf_op jit(solution)/shard_map/pallas_call | solution.py:166
  104.8 6.0 %shard_map.108 = bf16[512,1152]{1,0:T(8,128)(2,1)} custom-call(s32[1]{0:T(128)} %bitcast.7.side, bf16[128,2176]{1,0:T(8,128)(2,1)} %shard_map.102.refs_0_, bf16[128,2176]{1,0:T(8,128)(2,1)} %copy-done.2, bf16[128,2176]{1,0:T(8,128)(2,1)} %copy-done.3, bf16[128,2176]{1,0:T(8,128)(2,1)} %copy-done, bf16[128,2176]{1,0:T(8,128)(2,1)} %broadcast_select_fusion.1.refs_1_.refs_4_, ...), custom_call_target="tpu_custom_call" | custom-call | flops 1024 | bytes 1024 | tf_op jit(solution)/shard_map/pallas_call | solution.py:206
  110.9 5.0 %shard_map.109 = bf16[512,1152]{1,0:T(8,128)(2,1)} custom-call(s32[1]{0:T(128)} %bitcast.side, bf16[128,2176]{1,0:T(8,128)(2,1)} %shard_map.102.refs_0_, bf16[128,2176]{1,0:T(8,128)(2,1)} %copy-done.2, bf16[128,2176]{1,0:T(8,128)(2,1)} %copy-done.3, bf16[128,2176]{1,0:T(8,128)(2,1)} %copy-done, bf16[128,2176]{1,0:T(8,128)(2,1)} %broadcast_select_fusion.1.refs_1_.refs_4_, ...), custom_call_target="tpu_custom_call" | custom-call | flops 1024 | bytes 1024 | tf_op jit(solution)/shard_map/pallas_call | solution.py:206
  116.5 1.5 collective-permute-start.13
  119.7 16.4 %collective-permute-done.12 = bf16[128,1024]{1,0:T(8,128)(2,1)S(1)} collective-permute-done((bf16[128,1024]{1,0:T(8,128)(2,1)S(1)}, bf16[128,1024]{1,0:T(8,128)(2,1)S(1)}, u32[]{:S(2)}, u32[]{:S(2)}) %collective-permute-start.12) | collective-permute-done | bytes 262176 | tf_op jit(solution)/shard_map/ppermute | solution.py:287
  136.0 1.5 collective-permute-start.19
  138.4 5.3 %collective-permute-start.16 = (bf16[128,1024]{1,0:T(8,128)(2,1)S(1)}, bf16[128,1024]{1,0:T(8,128)(2,1)S(1)}, u32[]{:S(2)}, u32[]{:S(2)}) collective-permute-start(bf16[128,1024]{1,0:T(8,128)(2,1)S(1)} %get-tuple-element.65), channel_id=1, source_target_pairs={{0,8},{1,9},{2,10},{3,11},{12,4},{13,5},{14,6},{15,7},{16,24},{17,... | collective-permute-start | bytes 786440 | tf_op jit(solution)/shard_map/ppermute | solution.py:287
  145.3 5.9 %shard_map.110.keep = bf16[512,1152]{1,0:T(8,128)(2,1)} custom-call(s32[1]{0:T(128)} %bitcast.side, bf16[128,2176]{1,0:T(8,128)(2,1)} %shard_map.102.refs_0_, bf16[128,2176]{1,0:T(8,128)(2,1)} %copy-done.2, bf16[128,2176]{1,0:T(8,128)(2,1)} %copy-done.3, bf16[128,2176]{1,0:T(8,128)(2,1)} %copy-done, ...), custom_call_target="tpu_custom_call" | custom-call | flops 1024 | bytes 1024 | tf_op jit(solution)/shard_map/pallas_call | solution.py:206
  151.2 1.4 collective-permute-start.22
  152.6 4.4 %collective-permute-start.23 = (bf16[128,1024]{1,0:T(8,128)(2,1)S(1)}, bf16[128,1024]{1,0:T(8,128)(2,1)S(1)}, u32[]{:S(2)}, u32[]{:S(2)}) collective-permute-start(bf16[128,1024]{1,0:T(8,128)(2,1)S(1)} %add_convert_fusion.1), channel_id=1, source_target_pairs={{0,12},{1,13},{2,14},{3,15},{12,0},{13,1},{14,2},{15,3},{16,28},{1... | collective-permute-start | bytes 786440 | tf_op jit(solution)/shard_map/ppermute | solution.py:287
  157.1 4.0 %shard_map.111 = (f32[512,384]{1,0:T(8,128)}, f32[512,384]{1,0:T(8,128)}, f32[384,512]{1,0:T(8,128)}) custom-call(bf16[512,1152]{1,0:T(8,128)(2,1)} %shard_map.110.keep, bf16[512,1152]{1,0:T(8,128)(2,1)} %copy-done.14), custom_call_target="tpu_custom_call" | custom-call | flops 1024 | bytes 1024 | tf_op jit(solution)/shard_map/pallas_call | solution.py:234
  161.0 5.0 %collective-permute-done.22 = bf16[128,1024]{1,0:T(8,128)(2,1)S(1)} collective-permute-done((bf16[128,1024]{1,0:T(8,128)(2,1)S(1)}, bf16[128,1024]{1,0:T(8,128)(2,1)S(1)}, u32[]{:S(2)}, u32[]{:S(2)}) %collective-permute-start.22) | collective-permute-done | bytes 262176 | tf_op jit(solution)/shard_map/ppermute | solution.py:287
  (81 shorter events, 14.4 us)
Async XLA Ops:
  3.1 29.1 %collective-permute-start.2 = (bf16[512,1152]{1,0:T(8,128)(2,1)}, bf16[512,1152]{1,0:T(8,128)(2,1)S(1)}, u32[]{:S(2)}, u32[]{:S(2)}) collective-permute-start(bf16[512,1152]{1,0:T(8,128)(2,1)} %shard_map.103.refs_3_.refs_4_.refs_2_), channel_id=1, source_target_pairs={{0,16},{16,0},{1,17},{17,1},{2,18},{18,2},{3,19},{19,3},{4,20},{20... | collective-permute-start | bytes 3538952 | tf_op jit(solution)/shard_map/ppermute | solution.py:288
  8.0 14.3 %collective-permute-start = (bf16[128,2176]{1,0:T(8,128)(2,1)}, bf16[128,2176]{1,0:T(8,128)(2,1)S(1)}, u32[]{:S(2)}, u32[]{:S(2)}) collective-permute-start(bf16[128,2176]{1,0:T(8,128)(2,1)} %shard_map.102.refs_0_), channel_id=1, source_target_pairs={{0,4},{1,5},{2,6},{3,7},{4,0},{5,1},{6,2},{7,3},{8,12},{9,13},{10,... | collective-permute-start | bytes 1671176 | tf_op jit(solution)/shard_map/ppermute | solution.py:287
  9.6 14.2 %collective-permute-start.7 = (bf16[128,2176]{1,0:T(8,128)(2,1)}, bf16[128,2176]{1,0:T(8,128)(2,1)}, u32[]{:S(2)}, u32[]{:S(2)}) collective-permute-start(bf16[128,2176]{1,0:T(8,128)(2,1)} %shard_map.102.refs_0_), channel_id=1, source_target_pairs={{4,8},{5,9},{6,10},{7,11},{8,4},{9,5},{10,6},{11,7},{20,24},{21,25... | collective-permute-start | bytes 1671176 | tf_op jit(solution)/shard_map/ppermute | solution.py:287
  11.1 14.7 %collective-permute-start.1 = (bf16[128,2176]{1,0:T(8,128)(2,1)}, bf16[128,2176]{1,0:T(8,128)(2,1)S(1)}, u32[]{:S(2)}, u32[]{:S(2)}) collective-permute-start(bf16[128,2176]{1,0:T(8,128)(2,1)} %shard_map.102.refs_0_), channel_id=1, source_target_pairs={{0,2},{1,3},{2,0},{3,1},{4,6},{5,7},{6,4},{7,5},{8,10},{9,11},{10,... | collective-permute-start | bytes 1671176 | tf_op jit(solution)/shard_map/ppermute | solution.py:287
  22.3 30.6 %copy-start.2 = (bf16[128,2176]{1,0:T(8,128)(2,1)}, bf16[128,2176]{1,0:T(8,128)(2,1)S(1)}, u32[]{:S(2)}) copy-start(bf16[128,2176]{1,0:T(8,128)(2,1)S(1)} %collective-permute-done.refs_1_) | copy-start | bytes 1671172
  22.3 5.0 %collective-permute-start.5 = (bf16[128,2176]{1,0:T(8,128)(2,1)S(1)}, bf16[128,2176]{1,0:T(8,128)(2,1)}, u32[]{:S(2)}, u32[]{:S(2)}) collective-permute-start(bf16[128,2176]{1,0:T(8,128)(2,1)S(1)} %collective-permute-done.refs_1_), channel_id=1, source_target_pairs={{4,8},{5,9},{6,10},{7,11},{8,4},{9,5},{10,6},{11,7},{20,24},{21,25... | collective-permute-start | bytes 1671176 | tf_op jit(solution)/shard_map/ppermute | solution.py:287
  23.8 17.2 %collective-permute-start.8 = (bf16[128,2176]{1,0:T(8,128)(2,1)}, bf16[128,2176]{1,0:T(8,128)(2,1)}, u32[]{:S(2)}, u32[]{:S(2)}) collective-permute-start(bf16[128,2176]{1,0:T(8,128)(2,1)} %collective-permute-done.7), channel_id=1, source_target_pairs={{4,0},{5,1},{6,2},{7,3},{8,12},{9,13},{10,14},{11,15},{20,16},{21,... | collective-permute-start | bytes 1671176 | tf_op jit(solution)/shard_map/ppermute | solution.py:287
  25.1 27.9 %collective-permute-start.3 = (bf16[512,1152]{1,0:T(8,128)(2,1)}, bf16[512,1152]{1,0:T(8,128)(2,1)S(1)}, u32[]{:S(2)}, u32[]{:S(2)}) collective-permute-start(bf16[512,1152]{1,0:T(8,128)(2,1)} %shard_map.103.refs_3_.refs_4_.refs_2_), channel_id=1, source_target_pairs={{0,1},{1,0},{2,3},{3,2},{4,5},{5,4},{6,7},{7,6},{8,9},{9,8},{10,11... | collective-permute-start | bytes 3538952 | tf_op jit(solution)/shard_map/ppermute | solution.py:287
  25.8 27.2 %copy-start.3 = (bf16[128,2176]{1,0:T(8,128)(2,1)}, bf16[128,2176]{1,0:T(8,128)(2,1)S(1)}, u32[]{:S(2)}) copy-start(bf16[128,2176]{1,0:T(8,128)(2,1)S(1)} %collective-permute-done.1.refs_2_) | copy-start | bytes 1671172
  25.8 16.4 %collective-permute-start.9 = (bf16[128,2176]{1,0:T(8,128)(2,1)S(1)}, bf16[128,2176]{1,0:T(8,128)(2,1)S(1)}, u32[]{:S(2)}, u32[]{:S(2)}) collective-permute-start(bf16[128,2176]{1,0:T(8,128)(2,1)S(1)} %collective-permute-done.refs_1_), channel_id=1, source_target_pairs={{0,2},{1,3},{2,0},{3,1},{4,6},{5,7},{6,4},{7,5},{8,10},{9,11},{10,... | collective-permute-start | bytes 1671176 | tf_op jit(solution)/shard_map/ppermute | solution.py:287
  27.3 24.8 %collective-permute-start.6 = (bf16[128,2176]{1,0:T(8,128)(2,1)}, bf16[128,2176]{1,0:T(8,128)(2,1)S(1)}, u32[]{:S(2)}, u32[]{:S(2)}) collective-permute-start(bf16[128,2176]{1,0:T(8,128)(2,1)} %collective-permute-done.5), channel_id=1, source_target_pairs={{4,0},{5,1},{6,2},{7,3},{8,12},{9,13},{10,14},{11,15},{20,16},{21,... | collective-permute-start | bytes 1671176 | tf_op jit(solution)/shard_map/ppermute | solution.py:287
  32.2 20.8 %collective-permute-start.4 = (bf16[512,1152]{1,0:T(8,128)(2,1)S(1)}, bf16[512,1152]{1,0:T(8,128)(2,1)S(1)}, u32[]{:S(2)}, u32[]{:S(2)}) collective-permute-start(bf16[512,1152]{1,0:T(8,128)(2,1)S(1)} %collective-permute-done.2.refs_4_.refs_5_.refs_3_), channel_id=1, source_target_pairs={{0,1},{1,0},{2,3},{3,2},{4,5},{5,4},{6,7},{7,6},{8,9},{9,8},{10,11... | collective-permute-start | bytes 3538952 | tf_op jit(solution)/shard_map/ppermute | solution.py:287
  42.1 21.9 %copy-start = (bf16[128,2176]{1,0:T(8,128)(2,1)}, bf16[128,2176]{1,0:T(8,128)(2,1)S(1)}, u32[]{:S(2)}) copy-start(bf16[128,2176]{1,0:T(8,128)(2,1)S(1)} %broadcast_select_fusion.refs_0_.refs_3_) | copy-start | bytes 1671172
  42.1 21.9 %copy-start.4 = (bf16[128,2176]{1,0:T(8,128)(2,1)}, bf16[128,2176]{1,0:T(8,128)(2,1)S(1)}, u32[]{:S(2)}) copy-start(bf16[128,2176]{1,0:T(8,128)(2,1)S(1)} %collective-permute-done.9.refs_2_.refs_5_) | copy-start | bytes 1671172
  42.2 21.9 %collective-permute-start.10 = (bf16[128,2176]{1,0:T(8,128)(2,1)S(1)}, bf16[128,2176]{1,0:T(8,128)(2,1)S(1)}, u32[]{:S(2)}, u32[]{:S(2)}) collective-permute-start(bf16[128,2176]{1,0:T(8,128)(2,1)S(1)} %broadcast_select_fusion.refs_0_.refs_3_), channel_id=1, source_target_pairs={{0,2},{1,3},{2,0},{3,1},{4,6},{5,7},{6,4},{7,5},{8,10},{9,11},{10,... | collective-permute-start | bytes 1671176 | tf_op jit(solution)/shard_map/ppermute | solution.py:287
  80.7 23.0 %collective-permute-start.20 = (bf16[512,1152]{1,0:T(8,128)(2,1)}, bf16[512,1152]{1,0:T(8,128)(2,1)S(1)}, u32[]{:S(2)}, u32[]{:S(2)}) collective-permute-start(bf16[512,1152]{1,0:T(8,128)(2,1)} %shard_map.106), channel_id=1, source_target_pairs={{0,1},{1,0},{2,3},{3,2},{4,5},{5,4},{6,7},{7,6},{8,9},{9,8},{10,11... | collective-permute-start | bytes 3538952 | tf_op jit(solution)/shard_map/ppermute | solution.py:287
  80.7 15.0 %collective-permute-start.11 = (bf16[128,2176]{1,0:T(8,128)(2,1)S(1)}, bf16[128,2176]{1,0:T(8,128)(2,1)S(1)}, u32[]{:S(2)}, u32[]{:S(2)}) collective-permute-start(bf16[128,2176]{1,0:T(8,128)(2,1)S(1)} %copy-done.1), channel_id=1, source_target_pairs={{0,2},{1,3},{2,0},{3,1},{4,6},{5,7},{6,4},{7,5},{8,10},{9,11},{10,... | collective-permute-start | bytes 1671176 | tf_op jit(solution)/shard_map/ppermute | solution.py:287
  95.8 2.0 %collective-permute-start.17 = (bf16[128,2176]{1,0:T(8,128)(2,1)S(1)}, bf16[128,2176]{1,0:T(8,128)(2,1)S(1)}, u32[]{:S(2)}, u32[]{:S(2)}) collective-permute-start(bf16[128,2176]{1,0:T(8,128)(2,1)S(1)} %collective-permute-done.11.refs_0_.refs_7_), channel_id=1, source_target_pairs={{0,1},{1,0},{2,3},{3,2},{4,5},{5,4},{6,7},{7,6},{8,9},{9,8},{10,11... | collective-permute-start | bytes 1671176 | tf_op jit(solution)/shard_map/ppermute | solution.py:287
  110.9 26.7 %copy-start.17 = (bf16[128,1024]{1,0:T(8,128)(2,1)S(1)}, bf16[128,1024]{1,0:T(8,128)(2,1)}, u32[]{:S(2)}) copy-start(bf16[128,1024]{1,0:T(8,128)(2,1)} %get-tuple-element.46) | copy-start | bytes 786436
  110.9 26.7 %copy-start.18 = (bf16[128,1024]{1,0:T(8,128)(2,1)S(1)}, bf16[128,1024]{1,0:T(8,128)(2,1)}, u32[]{:S(2)}) copy-start(bf16[128,1024]{1,0:T(8,128)(2,1)} %get-tuple-element.39) | copy-start | bytes 786436
  115.9 28.4 %collective-permute-start.21 = (bf16[512,1152]{1,0:T(8,128)(2,1)}, bf16[512,1152]{1,0:T(8,128)(2,1)S(1)}, u32[]{:S(2)}, u32[]{:S(2)}) collective-permute-start(bf16[512,1152]{1,0:T(8,128)(2,1)} %shard_map.109), channel_id=1, source_target_pairs={{0,1},{1,0},{2,3},{3,2},{4,5},{5,4},{6,7},{7,6},{8,9},{9,8},{10,11... | collective-permute-start | bytes 3538952 | tf_op jit(solution)/shard_map/ppermute | solution.py:287
  116.0 36.6 %collective-permute-start.24 = (bf16[512,1152]{1,0:T(8,128)(2,1)S(1)}, bf16[512,1152]{1,0:T(8,128)(2,1)S(1)}, u32[]{:S(2)}, u32[]{:S(2)}) collective-permute-start(bf16[512,1152]{1,0:T(8,128)(2,1)S(1)} %copy-done.11), channel_id=1, source_target_pairs={{0,16},{16,0},{1,17},{17,1},{2,18},{18,2},{3,19},{19,3},{4,20},{20... | collective-permute-start | bytes 3538952 | tf_op jit(solution)/shard_map/ppermute | solution.py:288
  116.5 19.5 %collective-permute-start.13 = (bf16[256,1024]{1,0:T(8,128)(2,1)S(1)}, bf16[256,1024]{1,0:T(8,128)(2,1)S(1)}, u32[]{:S(2)}, u32[]{:S(2)}) collective-permute-start(bf16[256,1024]{1,0:T(8,128)(2,1)S(1)} %copy-done.20), channel_id=1, source_target_pairs={{0,2},{1,3},{2,0},{3,1},{4,6},{5,7},{6,4},{7,5},{8,10},{9,11},{10,... | collective-permute-start | bytes 1572872 | tf_op jit(solution)/shard_map/ppermute | solution.py:287
  118.0 1.5 collective-permute-start.18
  118.0 18.0 %collective-permute-start.12 = (bf16[128,1024]{1,0:T(8,128)(2,1)S(1)}, bf16[128,1024]{1,0:T(8,128)(2,1)S(1)}, u32[]{:S(2)}, u32[]{:S(2)}) collective-permute-start(bf16[128,1024]{1,0:T(8,128)(2,1)S(1)} %copy-done.21), channel_id=1, source_target_pairs={{0,2},{1,3},{2,0},{3,1},{4,6},{5,7},{6,4},{7,5},{8,10},{9,11},{10,... | collective-permute-start | bytes 786440 | tf_op jit(solution)/shard_map/ppermute | solution.py:287
  119.6 24.6 %copy-start.15 = (bf16[128,1024]{1,0:T(8,128)(2,1)S(1)}, bf16[128,1024]{1,0:T(8,128)(2,1)}, u32[]{:S(2)}) copy-start(bf16[128,1024]{1,0:T(8,128)(2,1)} %get-tuple-element.49) | copy-start | bytes 786436
  136.0 7.7 %collective-permute-start.19 = (bf16[128,1024]{1,0:T(8,128)(2,1)S(1)}, bf16[128,1024]{1,0:T(8,128)(2,1)S(1)}, u32[]{:S(2)}, u32[]{:S(2)}) collective-permute-start(bf16[128,1024]{1,0:T(8,128)(2,1)S(1)} %add_convert_fusion.2), channel_id=1, source_target_pairs={{0,2},{1,3},{2,0},{3,1},{4,6},{5,7},{6,4},{7,5},{8,10},{9,11},{10,... | collective-permute-start | bytes 786440 | tf_op jit(solution)/shard_map/ppermute | solution.py:287
  137.8 23.3 %collective-permute-start.15 = (bf16[128,1024]{1,0:T(8,128)(2,1)S(1)}, bf16[128,1024]{1,0:T(8,128)(2,1)S(1)}, u32[]{:S(2)}, u32[]{:S(2)}) collective-permute-start(bf16[128,1024]{1,0:T(8,128)(2,1)S(1)} %get-tuple-element.65), channel_id=1, source_target_pairs={{4,8},{5,9},{6,10},{7,11},{8,4},{9,5},{10,6},{11,7},{20,24},{21,25... | collective-permute-start | bytes 786440 | tf_op jit(solution)/shard_map/ppermute | solution.py:287
  138.4 22.6 %collective-permute-start.16 = (bf16[128,1024]{1,0:T(8,128)(2,1)S(1)}, bf16[128,1024]{1,0:T(8,128)(2,1)S(1)}, u32[]{:S(2)}, u32[]{:S(2)}) collective-permute-start(bf16[128,1024]{1,0:T(8,128)(2,1)S(1)} %get-tuple-element.65), channel_id=1, source_target_pairs={{0,8},{1,9},{2,10},{3,11},{12,4},{13,5},{14,6},{15,7},{16,24},{17,... | collective-permute-start | bytes 786440 | tf_op jit(solution)/shard_map/ppermute | solution.py:287
  143.8 17.2 %collective-permute-start.14 = (bf16[128,1024]{1,0:T(8,128)(2,1)S(1)}, bf16[128,1024]{1,0:T(8,128)(2,1)S(1)}, u32[]{:S(2)}, u32[]{:S(2)}) collective-permute-start(bf16[128,1024]{1,0:T(8,128)(2,1)S(1)} %get-tuple-element.64), channel_id=1, source_target_pairs={{0,4},{1,5},{2,6},{3,7},{4,0},{5,1},{6,2},{7,3},{8,12},{9,13},{10,... | collective-permute-start | bytes 786440 | tf_op jit(solution)/shard_map/ppermute | solution.py:287
  151.2 14.8 %collective-permute-start.22 = (bf16[128,1024]{1,0:T(8,128)(2,1)S(1)}, bf16[128,1024]{1,0:T(8,128)(2,1)S(1)}, u32[]{:S(2)}, u32[]{:S(2)}) collective-permute-start(bf16[128,1024]{1,0:T(8,128)(2,1)S(1)} %add_convert_fusion.1), channel_id=1, source_target_pairs={{4,12},{5,13},{6,14},{7,15},{8,0},{9,1},{10,2},{11,3},{20,28},{21,... | collective-permute-start | bytes 786440 | tf_op jit(solution)/shard_map/ppermute | solution.py:287
  152.6 13.4 %collective-permute-start.23 = (bf16[128,1024]{1,0:T(8,128)(2,1)S(1)}, bf16[128,1024]{1,0:T(8,128)(2,1)S(1)}, u32[]{:S(2)}, u32[]{:S(2)}) collective-permute-start(bf16[128,1024]{1,0:T(8,128)(2,1)S(1)} %add_convert_fusion.1), channel_id=1, source_target_pairs={{0,12},{1,13},{2,14},{3,15},{12,0},{13,1},{14,2},{15,3},{16,28},{1... | collective-permute-start | bytes 786440 | tf_op jit(solution)/shard_map/ppermute | solution.py:287
  (16 other events, 86.6 us)

commit v4 on v3

--- a/solution.py
+++ b/solution.py
@@ -29,8 +29,8 @@
     return pltpu.CompilerParams(vmem_limit_bytes=VMEM_BYTES)
 
 
-def cost():
-    return pl.CostEstimate(flops=1024, bytes_accessed=1024, transcendentals=0)
+def cost(flops, moved):
+    return pl.CostEstimate(flops=int(flops), bytes_accessed=int(moved), transcendentals=0)
 
 
 def dot(a, b, dims):
@@ -65,7 +65,7 @@
         out_shape=jax.ShapeDtypeStruct((rows, 2 * width + LANES), BF16),
         in_specs=[vmem()] * 4,
         out_specs=vmem(),
-        cost_estimate=cost(),
+        cost_estimate=cost(0, 3 * rows * width * 2 * 2),
         compiler_params=params(),
     )(tokens, d_output, combine.T, routes.T)
 
@@ -84,7 +84,7 @@
         out_shape=jax.ShapeDtypeStruct((size, 3 * hidden_units), BF16),
         in_specs=[vmem()] * 3,
         out_specs=vmem(),
-        cost_estimate=cost(),
+        cost_estimate=cost(0, 6 * size * hidden_units * 4),
         compiler_params=params(),
     )(gate, up, down)
 
@@ -173,7 +173,7 @@
             pltpu.VMEM((total, 2 * size), F32),
             pltpu.SemaphoreType.DMA((sets,)),
         ],
-        cost_estimate=cost(),
+        cost_estimate=cost(24 * total * size * stacked * sets // 2, 1 << 20),
         compiler_params=params(),
     )(scal, *blocks, *weights)
 
@@ -212,7 +212,7 @@
             in_specs=[half(b) for b in blocks] + [half(s) for s in scaled] + [whole(g) for g in [*grads, *extra]],
             out_specs=pl.BlockSpec((size, stacked), lambda i, s: (0, 0)),
         ),
-        cost_estimate=cost(),
+        cost_estimate=cost(1024, 1024),
         compiler_params=params(),
     )(side, *blocks, *scaled, *grads, *extra)
 
@@ -237,7 +237,7 @@
         grid=(size // step,),
         in_specs=[piece(stacked)] * 2,
         out_specs=[piece(hidden_units), piece(hidden_units), pl.BlockSpec((hidden_units, step), lambda i: (0, i))],
-        cost_estimate=cost(),
+        cost_estimate=cost(1024, 1024),
         compiler_params=params(),
     )(keep, from_part)
 
@@ -304,10 +304,9 @@
     w_both = swap(w_part)
     weights = [w_own, w_part, w_core, w_both]
     g2 = move(f2, OUTWARD)
-    b3 = jnp.where(inner, f2, g2)
-
     p0, p1, q0, *kept_a = rows_call(experts, scal, [[own], [b1], [y0]], weights)
-    y3 = move(after(b3, y2, p0), SWAP_Y)
+    b3 = jnp.where(inner, f2, after(g2, p0))
+    y3 = move(after(b3, y2), SWAP_Y)
     p2, p3, q12, *kept_b = rows_call(experts, scal, [[b2], [b3], [y1, y2]], weights)
 
     blocks = [own, b1, y0, b2, b3, y1, y2]
@@ -335,7 +334,7 @@
     add = lambda *terms: sum(t.astype(F32) for t in terms).astype(BF16)
     s1 = add(p1, r1)
     s2 = add(p2, r2)
-    s3 = after(add(p3, r3), keep)
+    s3 = add(p3, r3)
     d_tokens = add(
         p0,
         r0,

time: 168 us -> 149 us (0.89)
  waiting for transfers between devices: 68.2 us -> 54.8 us
  other arithmetic: 3.91 us -> 2.07 us
  local copies, waits for them, and re-layouts: 5.79 us -> 4.05 us
    ppermute x23, waiting for transfers between devices: 64.6 us -> 46.8 us  [dense_body(): move = lambda a, pairs: lax.ppermute(a, 'expert', pairs)]
    ppermute x2, waiting for transfers between devices: 3.66 us -> 7.93 us  [dense_body(): across = lambda a: lax.ppermute(a, 'dp', [(0, 1), (1, 0)])]
    ppermute x23, starting transfers between devices: 29.4 us -> 27.3 us  [dense_body(): move = lambda a, pairs: lax.ppermute(a, 'expert', pairs)]
    unnamed x46 -> x36, local copies, waits for them, and re-layouts: 5.79 us -> 4.05 us
  transfers between devices with their start and end apart: 25 -> 25, of which waited for: 9 -> 9; matrix products, arithmetic and copies ran while one was open for 2% -> 1% of each run, Pallas kernels for 16% -> 33%
where the time goes in v4:
time: 149 us
  Pallas kernels  55.1 us (37%)
  waiting for transfers between devices  54.8 us (37%)
  starting transfers between devices  31.8 us (21%)
  local copies, waits for them, and re-layouts  4.05 us (3%)
  other arithmetic  2.07 us (1%)
    ppermute x23, waiting for transfers between devices, dense_body(): move = lambda a, pairs: lax.ppermute(a, 'expert', pairs)  46.8 us
    ppermute x23, starting transfers between devices, dense_body(): move = lambda a, pairs: lax.ppermute(a, 'expert', pairs)  27.3 us
    pallas_call x3, Pallas kernels, rows_call(): pl.pallas_call(functools.partial(rows_kernel, experts, count, len(groups)...  25.3 us
    pallas_call x4, Pallas kernels, half_call(): pl.pallas_call(functools.partial(half_kernel, len(blocks), len(scaled), l...  21.4 us
    ppermute x2, waiting for transfers between devices, dense_body(): across = lambda a: lax.ppermute(a, 'dp', [(0, 1), (1, 0)])  7.93 us
    ppermute x2, starting transfers between devices, dense_body(): across = lambda a: lax.ppermute(a, 'dp', [(0, 1), (1, 0)])  4.48 us
    unnamed x36, local copies, waits for them, and re-layouts  4.05 us
    pallas_call x1, Pallas kernels, finish(): pl.pallas_call(finish_kernel, out_shape=[sds((size, hidden_units), F32),...  3.95 us
  transfers between devices with their start and end apart: 25, of which 9 were waited for; matrix products, arithmetic and copies ran while one was open for 1% of the time, Pallas kernels for 33%

profile of v4, /device:TPU:0, one launch (start us, length us, event | category | flops | bytes accessed | tf_op | source)
XLA Modules:
  0.0 148.7 jit_solution(16041372929872645484)
XLA Ops:
  0.6 2.4 %shard_map.103.refs_3_.refs_4_.refs_2_ = bf16[512,1152]{1,0:T(8,128)(2,1)} custom-call(bf16[512,384]{1,0:T(8,128)(2,1)} %bitcast.11, bf16[512,384]{1,0:T(8,128)(2,1)} %bitcast.12, bf16[384,512]{1,0:T(8,128)(2,1)} %bitcast.13), custom_call_target="tpu_custom_call" | custom-call | bytes 4718592 | tf_op jit(solution)/shard_map/pallas_call | solution.py:82
  3.1 2.9 %collective-permute-start.2 = (bf16[512,1152]{1,0:T(8,128)(2,1)}, bf16[512,1152]{1,0:T(8,128)(2,1)}, u32[]{:S(2)}, u32[]{:S(2)}) collective-permute-start(bf16[512,1152]{1,0:T(8,128)(2,1)} %shard_map.103.refs_3_.refs_4_.refs_2_), channel_id=1, source_target_pairs={{0,16},{16,0},{1,17},{17,1},{2,18},{18,2},{3,19},{19,3},{4,20},{20... | collective-permute-start | bytes 3538952 | tf_op jit(solution)/shard_map/ppermute | solution.py:288
  6.0 2.0 %shard_map.102.refs_0_ = bf16[128,2176]{1,0:T(8,128)(2,1)} custom-call(bf16[128,1024]{1,0:T(8,128)(2,1)} %tokens.1, bf16[128,1024]{1,0:T(8,128)(2,1)} %d_output.1, f32[8,128]{1,0:T(8,128)} %bitcast.14, s32[8,128]{1,0:T(8,128)} %bitcast.15), custom_call_target="tpu_custom_call" | custom-call | bytes 1572864 | tf_op jit(solution)/shard_map/pallas_call | solution.py:63
  8.0 1.6 %collective-permute-start = (bf16[128,2176]{1,0:T(8,128)(2,1)}, bf16[128,2176]{1,0:T(8,128)(2,1)S(1)}, u32[]{:S(2)}, u32[]{:S(2)}) collective-permute-start(bf16[128,2176]{1,0:T(8,128)(2,1)} %shard_map.102.refs_0_), channel_id=1, source_target_pairs={{0,4},{1,5},{2,6},{3,7},{4,0},{5,1},{6,2},{7,3},{8,12},{9,13},{10,... | collective-permute-start | bytes 1671176 | tf_op jit(solution)/shard_map/ppermute | solution.py:287
  10.3 1.6 %collective-permute-start.1 = (bf16[128,2176]{1,0:T(8,128)(2,1)}, bf16[128,2176]{1,0:T(8,128)(2,1)S(1)}, u32[]{:S(2)}, u32[]{:S(2)}) collective-permute-start(bf16[128,2176]{1,0:T(8,128)(2,1)} %shard_map.102.refs_0_), channel_id=1, source_target_pairs={{0,2},{1,3},{2,0},{3,1},{4,6},{5,7},{6,4},{7,5},{8,10},{9,11},{10,... | collective-permute-start | bytes 1671176 | tf_op jit(solution)/shard_map/ppermute | solution.py:287
  11.8 10.4 %collective-permute-done.refs_1_ = bf16[128,2176]{1,0:T(8,128)(2,1)S(1)} collective-permute-done((bf16[128,2176]{1,0:T(8,128)(2,1)}, bf16[128,2176]{1,0:T(8,128)(2,1)S(1)}, u32[]{:S(2)}, u32[]{:S(2)}) %collective-permute-start) | collective-permute-done | bytes 557088 | tf_op jit(solution)/shard_map/ppermute | solution.py:287
  23.0 1.3 collective-permute-start.8
  24.4 7.9 %collective-permute-done.2.refs_4_.refs_5_.refs_3_ = bf16[512,1152]{1,0:T(8,128)(2,1)} collective-permute-done((bf16[512,1152]{1,0:T(8,128)(2,1)}, bf16[512,1152]{1,0:T(8,128)(2,1)}, u32[]{:S(2)}, u32[]{:S(2)}) %collective-permute-start.2) | collective-permute-done | bytes 1179680 | tf_op jit(solution)/shard_map/ppermute | solution.py:288
  32.9 1.8 %collective-permute-start.9 = (bf16[128,2176]{1,0:T(8,128)(2,1)S(1)}, bf16[128,2176]{1,0:T(8,128)(2,1)S(1)}, u32[]{:S(2)}, u32[]{:S(2)}) collective-permute-start(bf16[128,2176]{1,0:T(8,128)(2,1)S(1)} %collective-permute-done.refs_1_), channel_id=1, source_target_pairs={{0,2},{1,3},{2,0},{3,1},{4,6},{5,7},{6,4},{7,5},{8,10},{9,11},{10,... | collective-permute-start | bytes 1671176 | tf_op jit(solution)/shard_map/ppermute | solution.py:287
  36.0 4.3 %collective-permute-done.8 = bf16[128,2176]{1,0:T(8,128)(2,1)S(1)} collective-permute-done((bf16[128,2176]{1,0:T(8,128)(2,1)S(1)}, bf16[128,2176]{1,0:T(8,128)(2,1)S(1)}, u32[]{:S(2)}, u32[]{:S(2)}) %collective-permute-start.8) | collective-permute-done | bytes 557088 | tf_op jit(solution)/shard_map/ppermute | solution.py:287
  40.4 7.6 %collective-permute-done.9.refs_2_.refs_5_ = bf16[128,2176]{1,0:T(8,128)(2,1)S(1)} collective-permute-done((bf16[128,2176]{1,0:T(8,128)(2,1)S(1)}, bf16[128,2176]{1,0:T(8,128)(2,1)S(1)}, u32[]{:S(2)}, u32[]{:S(2)}) %collective-permute-start.9) | collective-permute-done | bytes 557088 | tf_op jit(solution)/shard_map/ppermute | solution.py:287
  48.0 1.7 %collective-permute-start.10 = (bf16[128,2176]{1,0:T(8,128)(2,1)S(1)}, bf16[128,2176]{1,0:T(8,128)(2,1)S(1)}, u32[]{:S(2)}, u32[]{:S(2)}) collective-permute-start(bf16[128,2176]{1,0:T(8,128)(2,1)S(1)} %broadcast_select_fusion.refs_0_.refs_3_), channel_id=1, source_target_pairs={{0,2},{1,3},{2,0},{3,1},{4,6},{5,7},{6,4},{7,5},{8,10},{9,11},{10,... | collective-permute-start | bytes 1671176 | tf_op jit(solution)/shard_map/ppermute | solution.py:287
  49.7 9.0 %shard_map.104 = (bf16[128,1024]{1,0:T(8,128)(2,1)}, bf16[128,1024]{1,0:T(8,128)(2,1)}, bf16[128,1024]{1,0:T(8,128)(2,1)}, bf16[384,1024]{1,0:T(8,128)(2,1)}, bf...) custom-call(s32[2]{0:T(128)} %pad_add_fusion.scal, ...), custom_call_target="tpu_custom_call" | custom-call | flops 10871635968 | bytes 1048576 | tf_op jit(solution)/shard_map/pallas_call | solution.py:166
  58.9 3.4 %collective-permute-done.10.refs_3_.refs_6_ = bf16[128,2176]{1,0:T(8,128)(2,1)S(1)} collective-permute-done((bf16[128,2176]{1,0:T(8,128)(2,1)S(1)}, bf16[128,2176]{1,0:T(8,128)(2,1)S(1)}, u32[]{:S(2)}, u32[]{:S(2)}) %collective-permute-start.10) | collective-permute-done | bytes 557088 | tf_op jit(solution)/shard_map/ppermute | solution.py:287
  62.3 1.7 %collective-permute-start.11 = (bf16[128,2176]{1,0:T(8,128)(2,1)S(1)}, bf16[128,2176]{1,0:T(8,128)(2,1)S(1)}, u32[]{:S(2)}, u32[]{:S(2)}) collective-permute-start(bf16[128,2176]{1,0:T(8,128)(2,1)S(1)} %broadcast_select_fusion.1.refs_1_.refs_4_), channel_id=1, source_target_pairs={{0,2},{1,3},{2,0},{3,1},{4,6},{5,7},{6,4},{7,5},{8,10},{9,11},{10,... | collective-permute-start | bytes 1671176 | tf_op jit(solution)/shard_map/ppermute | solution.py:287
  64.0 11.1 %shard_map.105 = (bf16[128,1024]{1,0:T(8,128)(2,1)}, bf16[128,1024]{1,0:T(8,128)(2,1)}, bf16[256,1024]{1,0:T(8,128)(2,1)}, bf16[512,1024]{1,0:T(8,128)(2,1)}, bf...) custom-call(s32[2]{0:T(128)} %pad_add_fusion.scal, bf16[128,2176]{1,0:T(8,128)(2,1)} %copy-done, ...), custom_call_target="tpu_custom_call" | custom-call | flops 14495514624 | bytes 1048576 | tf_op jit(solution)/shard_map/pallas_call | solution.py:166
  75.1 4.8 %shard_map.106 = bf16[512,1152]{1,0:T(8,128)(2,1)} custom-call(s32[1]{0:T(128)} %bitcast.7.side, bf16[128,2176]{1,0:T(8,128)(2,1)} %shard_map.102.refs_0_, bf16[128,2176]{1,0:T(8,128)(2,1)} %copy-done.2, bf16[128,2176]{1,0:T(8,128)(2,1)} %copy-done.3, bf16[128,2176]{1,0:T(8,128)(2,1)} %copy-done, bf16[128,2176]{1,0:T(8,128)(2,1)} %copy-done.1, ...), custom_call_target="tpu_custom_call" | custom-call | flops 1024 | bytes 1024 | tf_op jit(solution)/shard_map/pallas_call | solution.py:206
  81.2 2.3 %collective-permute-done.17.refs_1_.refs_8_ = bf16[128,2176]{1,0:T(8,128)(2,1)S(1)} collective-permute-done((bf16[128,2176]{1,0:T(8,128)(2,1)S(1)}, bf16[128,2176]{1,0:T(8,128)(2,1)S(1)}, u32[]{:S(2)}, u32[]{:S(2)}) %collective-permute-start.17) | collective-permute-done | bytes 557088 | tf_op jit(solution)/shard_map/ppermute | solution.py:287
  84.3 5.2 %shard_map.107 = (bf16[128,1024]{1,0:T(8,128)(2,1)}, bf16[128,1024]{1,0:T(8,128)(2,1)}, bf16[256,1024]{1,0:T(8,128)(2,1)}, bf16[256,1152]{1,0:T(8,128)(2,1)}) custom-call(s32[2]{0:T(128)} %pad_add_fusion.scal, bf16[128,2176]{1,0:T(8,128)(2,1)} %copy-done.6, bf16[128,2176]{1,0:T(8,128)(2,1)} %copy-done.7, ...), custom_call_target="tpu_custom_call" | custom-call | flops 3623878656 | bytes 1048576 | tf_op jit(solution)/shard_map/pallas_call | solution.py:166
  91.6 6.0 %shard_map.108 = bf16[512,1152]{1,0:T(8,128)(2,1)} custom-call(s32[1]{0:T(128)} %bitcast.7.side, bf16[128,2176]{1,0:T(8,128)(2,1)} %shard_map.102.refs_0_, bf16[128,2176]{1,0:T(8,128)(2,1)} %copy-done.2, bf16[128,2176]{1,0:T(8,128)(2,1)} %copy-done.3, bf16[128,2176]{1,0:T(8,128)(2,1)} %copy-done, bf16[128,2176]{1,0:T(8,128)(2,1)} %copy-done.1, ...), custom_call_target="tpu_custom_call" | custom-call | flops 1024 | bytes 1024 | tf_op jit(solution)/shard_map/pallas_call | solution.py:206
  97.7 1.5 %collective-permute-start.24 = (bf16[512,1152]{1,0:T(8,128)(2,1)}, bf16[512,1152]{1,0:T(8,128)(2,1)S(1)}, u32[]{:S(2)}, u32[]{:S(2)}) collective-permute-start(bf16[512,1152]{1,0:T(8,128)(2,1)} %shard_map.108), channel_id=1, source_target_pairs={{0,16},{16,0},{1,17},{17,1},{2,18},{18,2},{3,19},{19,3},{4,20},{20... | collective-permute-start | bytes 3538952 | tf_op jit(solution)/shard_map/ppermute | solution.py:288
  99.2 4.8 %shard_map.109 = bf16[512,1152]{1,0:T(8,128)(2,1)} custom-call(s32[1]{0:T(128)} %bitcast.side, bf16[128,2176]{1,0:T(8,128)(2,1)} %shard_map.102.refs_0_, bf16[128,2176]{1,0:T(8,128)(2,1)} %copy-done.2, bf16[128,2176]{1,0:T(8,128)(2,1)} %copy-done.3, bf16[128,2176]{1,0:T(8,128)(2,1)} %copy-done, bf16[128,2176]{1,0:T(8,128)(2,1)} %copy-done.1, ...), custom_call_target="tpu_custom_call" | custom-call | flops 1024 | bytes 1024 | tf_op jit(solution)/shard_map/pallas_call | solution.py:206
  104.1 1.3 collective-permute-start.19
  105.6 1.6 %collective-permute-start.14 = (bf16[128,1024]{1,0:T(8,128)(2,1)S(1)}, bf16[128,1024]{1,0:T(8,128)(2,1)S(1)}, u32[]{:S(2)}, u32[]{:S(2)}) collective-permute-start(bf16[128,1024]{1,0:T(8,128)(2,1)S(1)} %get-tuple-element.64), channel_id=1, source_target_pairs={{0,4},{1,5},{2,6},{3,7},{4,0},{5,1},{6,2},{7,3},{8,12},{9,13},{10,... | collective-permute-start | bytes 786440 | tf_op jit(solution)/shard_map/ppermute | solution.py:287
  107.9 5.0 %collective-permute-done.19 = bf16[128,1024]{1,0:T(8,128)(2,1)S(1)} collective-permute-done((bf16[128,1024]{1,0:T(8,128)(2,1)S(1)}, bf16[128,1024]{1,0:T(8,128)(2,1)S(1)}, u32[]{:S(2)}, u32[]{:S(2)}) %collective-permute-start.19) | collective-permute-done | bytes 262176 | tf_op jit(solution)/shard_map/ppermute | solution.py:287
  112.9 4.5 %collective-permute-start.16 = (bf16[128,1024]{1,0:T(8,128)(2,1)S(1)}, bf16[128,1024]{1,0:T(8,128)(2,1)S(1)}, u32[]{:S(2)}, u32[]{:S(2)}) collective-permute-start(bf16[128,1024]{1,0:T(8,128)(2,1)S(1)} %get-tuple-element.65), channel_id=1, source_target_pairs={{0,8},{1,9},{2,10},{3,11},{12,4},{13,5},{14,6},{15,7},{16,24},{17,... | collective-permute-start | bytes 786440 | tf_op jit(solution)/shard_map/ppermute | solution.py:287
  117.5 1.3 collective-permute-start.20
  118.8 3.3 %collective-permute-start.21 = (bf16[128,1024]{1,0:T(8,128)(2,1)S(1)}, bf16[128,1024]{1,0:T(8,128)(2,1)S(1)}, u32[]{:S(2)}, u32[]{:S(2)}) collective-permute-start(bf16[128,1024]{1,0:T(8,128)(2,1)S(1)} %add_convert_fusion.1), channel_id=1, source_target_pairs={{0,12},{1,13},{2,14},{3,15},{12,0},{13,1},{14,2},{15,3},{16,28},{1... | collective-permute-start | bytes 786440 | tf_op jit(solution)/shard_map/ppermute | solution.py:287
  122.0 2.0 %collective-permute-done.16 = bf16[128,1024]{1,0:T(8,128)(2,1)S(1)} collective-permute-done((bf16[128,1024]{1,0:T(8,128)(2,1)S(1)}, bf16[128,1024]{1,0:T(8,128)(2,1)S(1)}, u32[]{:S(2)}, u32[]{:S(2)}) %collective-permute-start.16) | collective-permute-done | bytes 262176 | tf_op jit(solution)/shard_map/ppermute | solution.py:287
  124.0 11.8 %collective-permute-done.20 = bf16[128,1024]{1,0:T(8,128)(2,1)S(1)} collective-permute-done((bf16[128,1024]{1,0:T(8,128)(2,1)S(1)}, bf16[128,1024]{1,0:T(8,128)(2,1)S(1)}, u32[]{:S(2)}, u32[]{:S(2)}) %collective-permute-start.20) | collective-permute-done | bytes 262176 | tf_op jit(solution)/shard_map/ppermute | solution.py:287
  137.9 5.8 %shard_map.110.keep = bf16[512,1152]{1,0:T(8,128)(2,1)} custom-call(s32[1]{0:T(128)} %bitcast.side, bf16[128,2176]{1,0:T(8,128)(2,1)} %shard_map.102.refs_0_, bf16[128,2176]{1,0:T(8,128)(2,1)} %copy-done.2, bf16[128,2176]{1,0:T(8,128)(2,1)} %copy-done.3, bf16[128,2176]{1,0:T(8,128)(2,1)} %copy-done, bf16[128,2176]{1,0:T(8,128)(2,1)} %copy-done.1, ...), custom_call_target="tpu_custom_call" | custom-call | flops 1024 | bytes 1024 | tf_op jit(solution)/shard_map/pallas_call | solution.py:206
  144.8 3.9 %shard_map.111 = (f32[512,384]{1,0:T(8,128)}, f32[512,384]{1,0:T(8,128)}, f32[384,512]{1,0:T(8,128)}) custom-call(bf16[512,1152]{1,0:T(8,128)(2,1)} %shard_map.110.keep, bf16[512,1152]{1,0:T(8,128)(2,1)} %copy-done.10), custom_call_target="tpu_custom_call" | custom-call | flops 1024 | bytes 1024 | tf_op jit(solution)/shard_map/pallas_call | solution.py:234
  (71 shorter events, 11.9 us)
Async XLA Ops:
  3.1 29.2 %collective-permute-start.2 = (bf16[512,1152]{1,0:T(8,128)(2,1)}, bf16[512,1152]{1,0:T(8,128)(2,1)}, u32[]{:S(2)}, u32[]{:S(2)}) collective-permute-start(bf16[512,1152]{1,0:T(8,128)(2,1)} %shard_map.103.refs_3_.refs_4_.refs_2_), channel_id=1, source_target_pairs={{0,16},{16,0},{1,17},{17,1},{2,18},{18,2},{3,19},{19,3},{4,20},{20... | collective-permute-start | bytes 3538952 | tf_op jit(solution)/shard_map/ppermute | solution.py:288
  8.0 14.3 %collective-permute-start = (bf16[128,2176]{1,0:T(8,128)(2,1)}, bf16[128,2176]{1,0:T(8,128)(2,1)S(1)}, u32[]{:S(2)}, u32[]{:S(2)}) collective-permute-start(bf16[128,2176]{1,0:T(8,128)(2,1)} %shard_map.102.refs_0_), channel_id=1, source_target_pairs={{0,4},{1,5},{2,6},{3,7},{4,0},{5,1},{6,2},{7,3},{8,12},{9,13},{10,... | collective-permute-start | bytes 1671176 | tf_op jit(solution)/shard_map/ppermute | solution.py:287
  9.6 13.4 %collective-permute-start.7 = (bf16[128,2176]{1,0:T(8,128)(2,1)}, bf16[128,2176]{1,0:T(8,128)(2,1)S(1)}, u32[]{:S(2)}, u32[]{:S(2)}) collective-permute-start(bf16[128,2176]{1,0:T(8,128)(2,1)} %shard_map.102.refs_0_), channel_id=1, source_target_pairs={{4,8},{5,9},{6,10},{7,11},{8,4},{9,5},{10,6},{11,7},{20,24},{21,25... | collective-permute-start | bytes 1671176 | tf_op jit(solution)/shard_map/ppermute | solution.py:287
  10.3 22.7 %collective-permute-start.1 = (bf16[128,2176]{1,0:T(8,128)(2,1)}, bf16[128,2176]{1,0:T(8,128)(2,1)S(1)}, u32[]{:S(2)}, u32[]{:S(2)}) collective-permute-start(bf16[128,2176]{1,0:T(8,128)(2,1)} %shard_map.102.refs_0_), channel_id=1, source_target_pairs={{0,2},{1,3},{2,0},{3,1},{4,6},{5,7},{6,4},{7,5},{8,10},{9,11},{10,... | collective-permute-start | bytes 1671176 | tf_op jit(solution)/shard_map/ppermute | solution.py:287
  22.3 27.4 %copy-start.2 = (bf16[128,2176]{1,0:T(8,128)(2,1)}, bf16[128,2176]{1,0:T(8,128)(2,1)S(1)}, u32[]{:S(2)}) copy-start(bf16[128,2176]{1,0:T(8,128)(2,1)S(1)} %collective-permute-done.refs_1_) | copy-start | bytes 1671172
  22.3 12.4 %collective-permute-start.5 = (bf16[128,2176]{1,0:T(8,128)(2,1)S(1)}, bf16[128,2176]{1,0:T(8,128)(2,1)S(1)}, u32[]{:S(2)}, u32[]{:S(2)}) collective-permute-start(bf16[128,2176]{1,0:T(8,128)(2,1)S(1)} %collective-permute-done.refs_1_), channel_id=1, source_target_pairs={{4,8},{5,9},{6,10},{7,11},{8,4},{9,5},{10,6},{11,7},{20,24},{21,25... | collective-permute-start | bytes 1671176 | tf_op jit(solution)/shard_map/ppermute | solution.py:287
  23.0 17.3 %collective-permute-start.8 = (bf16[128,2176]{1,0:T(8,128)(2,1)S(1)}, bf16[128,2176]{1,0:T(8,128)(2,1)S(1)}, u32[]{:S(2)}, u32[]{:S(2)}) collective-permute-start(bf16[128,2176]{1,0:T(8,128)(2,1)S(1)} %collective-permute-done.7), channel_id=1, source_target_pairs={{4,0},{5,1},{6,2},{7,3},{8,12},{9,13},{10,14},{11,15},{20,16},{21,... | collective-permute-start | bytes 1671176 | tf_op jit(solution)/shard_map/ppermute | solution.py:287
  24.3 25.4 %collective-permute-start.3 = (bf16[512,1152]{1,0:T(8,128)(2,1)}, bf16[512,1152]{1,0:T(8,128)(2,1)}, u32[]{:S(2)}, u32[]{:S(2)}) collective-permute-start(bf16[512,1152]{1,0:T(8,128)(2,1)} %shard_map.103.refs_3_.refs_4_.refs_2_), channel_id=1, source_target_pairs={{0,1},{1,0},{2,3},{3,2},{4,5},{5,4},{6,7},{7,6},{8,9},{9,8},{10,11... | collective-permute-start | bytes 3538952 | tf_op jit(solution)/shard_map/ppermute | solution.py:287
  32.3 17.4 %collective-permute-start.4 = (bf16[512,1152]{1,0:T(8,128)(2,1)}, bf16[512,1152]{1,0:T(8,128)(2,1)}, u32[]{:S(2)}, u32[]{:S(2)}) collective-permute-start(bf16[512,1152]{1,0:T(8,128)(2,1)} %collective-permute-done.2.refs_4_.refs_5_.refs_3_), channel_id=1, source_target_pairs={{0,1},{1,0},{2,3},{3,2},{4,5},{5,4},{6,7},{7,6},{8,9},{9,8},{10,11... | collective-permute-start | bytes 3538952 | tf_op jit(solution)/shard_map/ppermute | solution.py:287
  32.9 16.8 %copy-start.3 = (bf16[128,2176]{1,0:T(8,128)(2,1)}, bf16[128,2176]{1,0:T(8,128)(2,1)S(1)}, u32[]{:S(2)}) copy-start(bf16[128,2176]{1,0:T(8,128)(2,1)S(1)} %collective-permute-done.1.refs_2_) | copy-start | bytes 1671172
  32.9 15.1 %collective-permute-start.9 = (bf16[128,2176]{1,0:T(8,128)(2,1)S(1)}, bf16[128,2176]{1,0:T(8,128)(2,1)S(1)}, u32[]{:S(2)}, u32[]{:S(2)}) collective-permute-start(bf16[128,2176]{1,0:T(8,128)(2,1)S(1)} %collective-permute-done.refs_1_), channel_id=1, source_target_pairs={{0,2},{1,3},{2,0},{3,1},{4,6},{5,7},{6,4},{7,5},{8,10},{9,11},{10,... | collective-permute-start | bytes 1671176 | tf_op jit(solution)/shard_map/ppermute | solution.py:287
  34.7 24.1 %collective-permute-start.6 = (bf16[128,2176]{1,0:T(8,128)(2,1)S(1)}, bf16[128,2176]{1,0:T(8,128)(2,1)S(1)}, u32[]{:S(2)}, u32[]{:S(2)}) collective-permute-start(bf16[128,2176]{1,0:T(8,128)(2,1)S(1)} %collective-permute-done.5), channel_id=1, source_target_pairs={{4,0},{5,1},{6,2},{7,3},{8,12},{9,13},{10,14},{11,15},{20,16},{21,... | collective-permute-start | bytes 1671176 | tf_op jit(solution)/shard_map/ppermute | solution.py:287
  40.4 18.4 %copy-start = (bf16[128,2176]{1,0:T(8,128)(2,1)}, bf16[128,2176]{1,0:T(8,128)(2,1)S(1)}, u32[]{:S(2)}) copy-start(bf16[128,2176]{1,0:T(8,128)(2,1)S(1)} %broadcast_select_fusion.refs_0_.refs_3_) | copy-start | bytes 1671172
  48.0 10.8 %copy-start.4 = (bf16[128,2176]{1,0:T(8,128)(2,1)}, bf16[128,2176]{1,0:T(8,128)(2,1)S(1)}, u32[]{:S(2)}) copy-start(bf16[128,2176]{1,0:T(8,128)(2,1)S(1)} %collective-permute-done.9.refs_2_.refs_5_) | copy-start | bytes 1671172
  48.0 14.3 %collective-permute-start.10 = (bf16[128,2176]{1,0:T(8,128)(2,1)S(1)}, bf16[128,2176]{1,0:T(8,128)(2,1)S(1)}, u32[]{:S(2)}, u32[]{:S(2)}) collective-permute-start(bf16[128,2176]{1,0:T(8,128)(2,1)S(1)} %broadcast_select_fusion.refs_0_.refs_3_), channel_id=1, source_target_pairs={{0,2},{1,3},{2,0},{3,1},{4,6},{5,7},{6,4},{7,5},{8,10},{9,11},{10,... | collective-permute-start | bytes 1671176 | tf_op jit(solution)/shard_map/ppermute | solution.py:287
  62.3 17.6 %collective-permute-start.11 = (bf16[128,2176]{1,0:T(8,128)(2,1)S(1)}, bf16[128,2176]{1,0:T(8,128)(2,1)S(1)}, u32[]{:S(2)}, u32[]{:S(2)}) collective-permute-start(bf16[128,2176]{1,0:T(8,128)(2,1)S(1)} %broadcast_select_fusion.1.refs_1_.refs_4_), channel_id=1, source_target_pairs={{0,2},{1,3},{2,0},{3,1},{4,6},{5,7},{6,4},{7,5},{8,10},{9,11},{10,... | collective-permute-start | bytes 1671176 | tf_op jit(solution)/shard_map/ppermute | solution.py:287
  79.9 10.7 %collective-permute-start.22 = (bf16[512,1152]{1,0:T(8,128)(2,1)}, bf16[512,1152]{1,0:T(8,128)(2,1)S(1)}, u32[]{:S(2)}, u32[]{:S(2)}) collective-permute-start(bf16[512,1152]{1,0:T(8,128)(2,1)} %shard_map.106), channel_id=1, source_target_pairs={{0,1},{1,0},{2,3},{3,2},{4,5},{5,4},{6,7},{7,6},{8,9},{9,8},{10,11... | collective-permute-start | bytes 3538952 | tf_op jit(solution)/shard_map/ppermute | solution.py:287
  79.9 3.6 %collective-permute-start.17 = (bf16[128,2176]{1,0:T(8,128)(2,1)S(1)}, bf16[128,2176]{1,0:T(8,128)(2,1)S(1)}, u32[]{:S(2)}, u32[]{:S(2)}) collective-permute-start(bf16[128,2176]{1,0:T(8,128)(2,1)S(1)} %collective-permute-done.11.refs_0_.refs_7_), channel_id=1, source_target_pairs={{0,1},{1,0},{2,3},{3,2},{4,5},{5,4},{6,7},{7,6},{8,9},{9,8},{10,11... | collective-permute-start | bytes 1671176 | tf_op jit(solution)/shard_map/ppermute | solution.py:287
  80.4 9.4 %copy-start.17 = (bf16[128,1024]{1,0:T(8,128)(2,1)S(1)}, bf16[128,1024]{1,0:T(8,128)(2,1)}, u32[]{:S(2)}) copy-start(bf16[128,1024]{1,0:T(8,128)(2,1)} %get-tuple-element.46) | copy-start | bytes 786436
  80.4 23.7 %collective-permute-start.13 = (bf16[256,1024]{1,0:T(8,128)(2,1)S(1)}, bf16[256,1024]{1,0:T(8,128)(2,1)S(1)}, u32[]{:S(2)}, u32[]{:S(2)}) collective-permute-start(bf16[256,1024]{1,0:T(8,128)(2,1)S(1)} %copy-done.16), channel_id=1, source_target_pairs={{0,2},{1,3},{2,0},{3,1},{4,6},{5,7},{6,4},{7,5},{8,10},{9,11},{10,... | collective-permute-start | bytes 1572872 | tf_op jit(solution)/shard_map/ppermute | solution.py:287
  89.6 14.4 %collective-permute-start.18 = (bf16[128,1024]{1,0:T(8,128)(2,1)}, bf16[128,1024]{1,0:T(8,128)(2,1)S(1)}, u32[]{:S(2)}, u32[]{:S(2)}) collective-permute-start(bf16[128,1024]{1,0:T(8,128)(2,1)} %get-tuple-element.52), channel_id=1, source_target_pairs={{0,1},{1,0},{2,3},{3,2},{4,5},{5,4},{6,7},{7,6},{8,9},{9,8},{10,11... | collective-permute-start | bytes 786440 | tf_op jit(solution)/shard_map/ppermute | solution.py:287
  89.8 14.3 %collective-permute-start.12 = (bf16[128,1024]{1,0:T(8,128)(2,1)S(1)}, bf16[128,1024]{1,0:T(8,128)(2,1)S(1)}, u32[]{:S(2)}, u32[]{:S(2)}) collective-permute-start(bf16[128,1024]{1,0:T(8,128)(2,1)S(1)} %copy-done.17), channel_id=1, source_target_pairs={{0,2},{1,3},{2,0},{3,1},{4,6},{5,7},{6,4},{7,5},{8,10},{9,11},{10,... | collective-permute-start | bytes 786440 | tf_op jit(solution)/shard_map/ppermute | solution.py:287
  97.7 46.0 %collective-permute-start.24 = (bf16[512,1152]{1,0:T(8,128)(2,1)}, bf16[512,1152]{1,0:T(8,128)(2,1)S(1)}, u32[]{:S(2)}, u32[]{:S(2)}) collective-permute-start(bf16[512,1152]{1,0:T(8,128)(2,1)} %shard_map.108), channel_id=1, source_target_pairs={{0,16},{16,0},{1,17},{17,1},{2,18},{18,2},{3,19},{19,3},{4,20},{20... | collective-permute-start | bytes 3538952 | tf_op jit(solution)/shard_map/ppermute | solution.py:288
  104.0 32.8 %collective-permute-start.23 = (bf16[512,1152]{1,0:T(8,128)(2,1)}, bf16[512,1152]{1,0:T(8,128)(2,1)S(1)}, u32[]{:S(2)}, u32[]{:S(2)}) collective-permute-start(bf16[512,1152]{1,0:T(8,128)(2,1)} %shard_map.109), channel_id=1, source_target_pairs={{0,1},{1,0},{2,3},{3,2},{4,5},{5,4},{6,7},{7,6},{8,9},{9,8},{10,11... | collective-permute-start | bytes 3538952 | tf_op jit(solution)/shard_map/ppermute | solution.py:287
  104.0 13.4 %copy-start.11 = (bf16[128,1024]{1,0:T(8,128)(2,1)S(1)}, bf16[128,1024]{1,0:T(8,128)(2,1)}, u32[]{:S(2)}) copy-start(bf16[128,1024]{1,0:T(8,128)(2,1)} %get-tuple-element.50) | copy-start | bytes 786436
  104.1 8.8 %collective-permute-start.19 = (bf16[128,1024]{1,0:T(8,128)(2,1)S(1)}, bf16[128,1024]{1,0:T(8,128)(2,1)S(1)}, u32[]{:S(2)}, u32[]{:S(2)}) collective-permute-start(bf16[128,1024]{1,0:T(8,128)(2,1)S(1)} %add_convert_fusion.2), channel_id=1, source_target_pairs={{0,2},{1,3},{2,0},{3,1},{4,6},{5,7},{6,4},{7,5},{8,10},{9,11},{10,... | collective-permute-start | bytes 786440 | tf_op jit(solution)/shard_map/ppermute | solution.py:287
  105.4 30.4 %copy-start.15 = (bf16[128,1024]{1,0:T(8,128)(2,1)S(1)}, bf16[128,1024]{1,0:T(8,128)(2,1)}, u32[]{:S(2)}) copy-start(bf16[128,1024]{1,0:T(8,128)(2,1)} %get-tuple-element.34) | copy-start | bytes 786436
  105.6 11.9 %collective-permute-start.14 = (bf16[128,1024]{1,0:T(8,128)(2,1)S(1)}, bf16[128,1024]{1,0:T(8,128)(2,1)S(1)}, u32[]{:S(2)}, u32[]{:S(2)}) collective-permute-start(bf16[128,1024]{1,0:T(8,128)(2,1)S(1)} %get-tuple-element.64), channel_id=1, source_target_pairs={{0,4},{1,5},{2,6},{3,7},{4,0},{5,1},{6,2},{7,3},{8,12},{9,13},{10,... | collective-permute-start | bytes 786440 | tf_op jit(solution)/shard_map/ppermute | solution.py:287
  107.2 11.5 %collective-permute-start.15 = (bf16[128,1024]{1,0:T(8,128)(2,1)S(1)}, bf16[128,1024]{1,0:T(8,128)(2,1)S(1)}, u32[]{:S(2)}, u32[]{:S(2)}) collective-permute-start(bf16[128,1024]{1,0:T(8,128)(2,1)S(1)} %get-tuple-element.65), channel_id=1, source_target_pairs={{4,8},{5,9},{6,10},{7,11},{8,4},{9,5},{10,6},{11,7},{20,24},{21,25... | collective-permute-start | bytes 786440 | tf_op jit(solution)/shard_map/ppermute | solution.py:287
  112.9 11.1 %collective-permute-start.16 = (bf16[128,1024]{1,0:T(8,128)(2,1)S(1)}, bf16[128,1024]{1,0:T(8,128)(2,1)S(1)}, u32[]{:S(2)}, u32[]{:S(2)}) collective-permute-start(bf16[128,1024]{1,0:T(8,128)(2,1)S(1)} %get-tuple-element.65), channel_id=1, source_target_pairs={{0,8},{1,9},{2,10},{3,11},{12,4},{13,5},{14,6},{15,7},{16,24},{17,... | collective-permute-start | bytes 786440 | tf_op jit(solution)/shard_map/ppermute | solution.py:287
  117.5 18.3 %collective-permute-start.20 = (bf16[128,1024]{1,0:T(8,128)(2,1)S(1)}, bf16[128,1024]{1,0:T(8,128)(2,1)S(1)}, u32[]{:S(2)}, u32[]{:S(2)}) collective-permute-start(bf16[128,1024]{1,0:T(8,128)(2,1)S(1)} %add_convert_fusion.1), channel_id=1, source_target_pairs={{4,12},{5,13},{6,14},{7,15},{8,0},{9,1},{10,2},{11,3},{20,28},{21,... | collective-permute-start | bytes 786440 | tf_op jit(solution)/shard_map/ppermute | solution.py:287
  118.8 17.0 %collective-permute-start.21 = (bf16[128,1024]{1,0:T(8,128)(2,1)S(1)}, bf16[128,1024]{1,0:T(8,128)(2,1)S(1)}, u32[]{:S(2)}, u32[]{:S(2)}) collective-permute-start(bf16[128,1024]{1,0:T(8,128)(2,1)S(1)} %add_convert_fusion.1), channel_id=1, source_target_pairs={{0,12},{1,13},{2,14},{3,15},{12,0},{13,1},{14,2},{15,3},{16,28},{1... | collective-permute-start | bytes 786440 | tf_op jit(solution)/shard_map/ppermute | solution.py:287
  (11 other events, 41.6 us)

commit v5 on v4

--- a/solution.py
+++ b/solution.py
@@ -89,13 +89,13 @@
     )(gate, up, down)
 
 
-def rows_kernel(experts, count, merged, scal, *refs):
+def rows_kernel(experts, count, merged, joined, scal, *refs):
     refs = list(refs)
     blocks = [refs.pop(0) for _ in range(count)]
-    sets = (len(refs) - 3 - merged) // 2
+    sets = 4
     raw = [refs.pop(0) for _ in range(sets)]
     out_rows = [refs.pop(0) for _ in range(merged)]
-    kept = [refs.pop(0) for _ in range(sets)]
+    kept = [refs.pop(0) for _ in range(3 if joined else 4)]
     held, total, sems = refs
     part, expert = scal[0], scal[1]
     size = raw[0].shape[0]
@@ -111,7 +111,8 @@
     lane = lax.broadcasted_iota(jnp.int32, parts.shape, 1)
     toks = [jnp.concatenate([b[:, pl.ds(at, size)] for b in blocks], axis=0) for at in sides]
     for which in range(sets // 2):
-        scaled_out, grads_out = kept[2 * which], kept[2 * which + 1]
+        grads_out = kept[2 * which]
+        scaled_out, scaled_at = (grads_out, 3 * hidden_units) if joined and which == 1 else (kept[2 * which + 1], 0)
         for c in copies[2 * which : 2 * which + 2]:
             c.wait()
         wanted = expert if which == 0 else expert + 1 - 2 * lax.rem(expert, 2)
@@ -124,7 +125,9 @@
             grad_at = pl.multiple_of(width + at, size)
             grad = jnp.concatenate([b[:, pl.ds(grad_at, size)] for b in blocks], axis=0)
             scaled = (weight * grad.astype(F32)).astype(BF16)
-            scaled_out[:, pl.ds(at, size)] = scaled
+            scaled_out[:, pl.ds(pl.multiple_of(scaled_at + at, LANES), size)] = scaled
+            if joined and which == 1:
+                grads_out[:, pl.ds(pl.multiple_of(3 * hidden_units + width + at, LANES), size)] = toks[side]
             p = dot(toks[side], held[2 * which + side, :, :both], ((1,), (0,)))
             h = dot(scaled, held[2 * which + side, :, both:], ((1,), (0,)))
             preact = p if side == 0 else preact + p
@@ -137,7 +140,7 @@
         d_up = (d_hidden * silu).astype(BF16)
         grads_out[:, :hidden_units] = d_gate
         grads_out[:, hidden_units:both] = d_up
-        grads_out[:, both:] = (silu * up_pre).astype(BF16)
+        grads_out[:, both : both + hidden_units] = (silu * up_pre).astype(BF16)
         d_preact = jnp.concatenate([d_gate, d_up], axis=1)
         for side in range(2):
             at = sides[side]
@@ -154,7 +157,7 @@
                     row += out.shape[0]
 
 
-def rows_call(experts, scal, groups, weights):
+def rows_call(experts, scal, groups, weights, joined=False):
     blocks = [b for group in groups for b in group]
     count, sets = len(blocks), len(weights)
     rows = blocks[0].shape[0]
@@ -162,9 +165,10 @@
     total = count * rows
     sds = jax.ShapeDtypeStruct
     out = [sds((len(group) * rows, 2 * size), BF16) for group in groups]
-    out += [sds((total, 2 * size), BF16), sds((total, stacked), BF16)] * (sets // 2)
+    out += [sds((total, stacked), BF16), sds((total, 2 * size), BF16)]
+    out += [sds((total, stacked + 4 * size), BF16)] if joined else out[-2:]
     return pl.pallas_call(
-        functools.partial(rows_kernel, experts, count, len(groups)),
+        functools.partial(rows_kernel, experts, count, len(groups), joined),
         out_shape=out,
         in_specs=[smem()] + [vmem()] * count + [hbm()] * sets,
         out_specs=[vmem()] * len(out),
@@ -173,48 +177,63 @@
             pltpu.VMEM((total, 2 * size), F32),
             pltpu.SemaphoreType.DMA((sets,)),
         ],
-        cost_estimate=cost(24 * total * size * stacked * sets // 2, 1 << 20),
+        cost_estimate=cost(24 * total * size * stacked * sets // 2 * (10 if joined else 1), 1 << 20),
         compiler_params=params(),
     )(scal, *blocks, *weights)
 
 
-def half_kernel(count, groups, adds, side, *refs):
-    blocks = refs[:count]
-    scaled = refs[count : count + groups]
-    grads = refs[count + groups : count + 2 * groups]
-    out = refs[-1]
-    both = 2 * (out.shape[1] // 3)
-    tok = jnp.concatenate([b[...] for b in blocks], axis=0)
-    grad = jnp.concatenate([s[...] for s in scaled], axis=0)
-    made = jnp.concatenate([g[...] for g in grads], axis=0)
-    gate_up = dot(tok, made[:, :both], ((0,), (0,)))
-    down = dot(grad, made[:, both:], ((0,), (0,)))
-    if adds:
-        more = refs[count + 2 * groups]
-        gate_up = gate_up + more[:, :both].astype(F32)
-        down = down + more[:, both:].astype(F32)
-    out[:, :both] = gate_up.astype(BF16)
-    out[:, both:] = down.astype(BF16)
-
-
-def half_call(side, blocks, scaled, grads, more=None):
+def half_kernel(count, groups, joined, adds, sides, *refs):
+    refs = list(refs)
+    side = sides[pl.program_id(0)]
+    toks = [refs.pop(0) for _ in range(count)]
+    scaled = [refs.pop(0) for _ in range(groups)]
+    made = [refs.pop(0) for _ in range(groups)]
+    last = refs.pop(0) if joined else None
+    more = refs.pop(0) if adds else None
+    out = refs.pop(0)
+    size, stacked = out.shape
+    both = stacked // 3 * 2
+    for kind in range(2):
+        rows = [r[...] for r in (toks if kind == 0 else scaled)]
+        span = slice(0, both) if kind == 0 else slice(both, stacked)
+        cols = [g[:, span] for g in made]
+        if joined:
+            cols.append(last[:, span])
+            first = stacked + (2 * size if kind == 0 else 0)
+            rows.append(last[:, pl.ds(pl.multiple_of(first + side * size, LANES), size)])
+        new = dot(jnp.concatenate(rows, axis=0), jnp.concatenate(cols, axis=0), ((0,), (0,)))
+        if adds:
+            new = new + more[:, span].astype(F32)
+        out[:, span] = new.astype(BF16)
+
+
+def half_call(sides, blocks, kept, last=None, more=None):
+    grads, scaled = [k[0] for k in kept], [k[1] for k in kept]
     size = scaled[0].shape[1] // 2
     stacked = grads[0].shape[1]
-    half = lambda a: pl.BlockSpec((a.shape[0], size), lambda i, s: (0, s[0]))
+    half = lambda a: pl.BlockSpec((a.shape[0], size), lambda i, s: (0, s[i]))
     whole = lambda a: pl.BlockSpec(a.shape, lambda i, s: (0, 0))
-    extra = [] if more is None else [more]
+    operands = [*blocks, *scaled, *grads]
+    specs = [half(a) for a in (*blocks, *scaled)] + [whole(g) for g in grads]
+    if last is not None:
+        operands.append(last)
+        specs.append(whole(last))
+    if more is not None:
+        operands.append(more)
+        specs.append(pl.BlockSpec((size, stacked), lambda i, s: (s[i], 0)))
+    count = sides.shape[0]
     return pl.pallas_call(
-        functools.partial(half_kernel, len(blocks), len(scaled), len(extra)),
-        out_shape=jax.ShapeDtypeStruct((size, stacked), BF16),
+        functools.partial(half_kernel, len(blocks), len(kept), last is not None, more is not None),
+        out_shape=jax.ShapeDtypeStruct((count * size, stacked), BF16),
         grid_spec=pltpu.PrefetchScalarGridSpec(
             num_scalar_prefetch=1,
-            grid=(1,),
-            in_specs=[half(b) for b in blocks] + [half(s) for s in scaled] + [whole(g) for g in [*grads, *extra]],
-            out_specs=pl.BlockSpec((size, stacked), lambda i, s: (0, 0)),
+            grid=(count,),
+            in_specs=specs,
+            out_specs=pl.BlockSpec((size, stacked), lambda i, s: (i, 0)),
         ),
         cost_estimate=cost(1024, 1024),
         compiler_params=params(),
-    )(side, *blocks, *scaled, *grads, *extra)
+    )(sides, *operands)
 
 
 def finish_kernel(keep, from_part, d_gate, d_up, d_down):
@@ -283,54 +302,51 @@
     scal = jnp.stack([part, expert]).astype(jnp.int32)
     mine = part[None].astype(jnp.int32)
     other = (1 - part)[None].astype(jnp.int32)
+    sides = jnp.arange(2, dtype=jnp.int32)
 
     move = lambda a, pairs: lax.ppermute(a, "expert", pairs)
     across = lambda a: lax.ppermute(a, "dp", [(0, 1), (1, 0)])
 
     swap = lambda a: move(a, SWAP_CORE)
-    w_own = pack_weights(gate_weight[0], up_weight[0], down_weight[0])
+    own = pack(experts, tokens, d_output, combine, routes)
+    w_own = pack_weights(after(gate_weight[0], own), up_weight[0], down_weight[0])
     w_part = across(w_own)
-    own = pack(experts, tokens, d_output, combine, routes)
 
     b1 = move(own, OUTER)
     f1 = move(own, INNER)
     y0 = move(own, SWAP_Y)
-    w_core = swap(w_own)
     f2 = move(b1, INNER)
     y1 = move(after(b1, y0), SWAP_Y)
     g1 = move(f1, OUTWARD)
     b2 = jnp.where(inner, f1, g1)
-    y2 = move(after(b2, y1, w_part), SWAP_Y)
-    w_both = swap(w_part)
+    y2 = move(after(b2, y1, f2), SWAP_Y)
+    g2 = move(f2, OUTWARD)
+
+    w_core = swap(after(w_own, y1, f2))
+    w_both = swap(after(w_part, y1, f2))
     weights = [w_own, w_part, w_core, w_both]
-    g2 = move(f2, OUTWARD)
     p0, p1, q0, *kept_a = rows_call(experts, scal, [[own], [b1], [y0]], weights)
     b3 = jnp.where(inner, f2, after(g2, p0))
     y3 = move(after(b3, y2), SWAP_Y)
-    p2, p3, q12, *kept_b = rows_call(experts, scal, [[b2], [b3], [y1, y2]], weights)
+    p2, p3, q1, *kept_b = rows_call(experts, scal, [[b2], [b3], [y1]], weights)
+    q2, *kept_c = rows_call(experts, scal, [[after(y2, p2)]], weights)
 
     blocks = [own, b1, y0, b2, b3, y1, y2]
-    kept = [kept_a, kept_b]
-    others = lambda side, first: half_call(side, [first] + blocks[1:], [k[2] for k in kept], [k[3] for k in kept])
-    to_core = others(other, own)
-    y3 = after(y3, p2, to_core)
-    r12 = move(after(q12, y3), SWAP_Y)
-    r0 = move(after(q0, y3), SWAP_Y)
-
-    cy3 = swap(y3)
-    last, pair, scaled_c, grads_c = rows_call(experts, scal, [[y3], [cy3]], weights[:2])
-    q3 = last.astype(F32) + swap(pair).astype(F32)
-    all_blocks = blocks + [y3, cy3]
-    mine_of = lambda side, more: half_call(
-        side, all_blocks, [k[0] for k in kept] + [scaled_c], [k[1] for k in kept] + [grads_c], more
-    )
-    send = mine_of(other, swap(to_core))
+    kept = [kept_a, kept_b, kept_c]
+    to_core = half_call(sides, blocks, [k[2:] for k in kept])
+    y3 = after(y3, q2, to_core)
+    r0, r1, r2 = (move(after(q, y3), SWAP_Y) for q in (q0, q1, q2))
+
+    q3, *kept_d, joined = rows_call(experts, scal, [[y3]], weights, joined=True)
+    last = swap(joined)
+    r3 = move(after(q3, r0), SWAP_Y)
+    all_blocks = blocks + [y3]
+    all_kept = [k[:2] for k in kept] + [kept_d]
+    got = swap(to_core)
+    send = half_call(other, all_blocks, all_kept, last, got)
     from_part = across(send)
-    keep = mine_of(mine, swap(others(mine, after(own, send))))
-
-    rows = own.shape[0]
-    r1, r2 = r12[:rows], r12[rows:]
-    r3 = move(after(q3.astype(BF16), r0, r12), SWAP_Y)
+    keep = half_call(after(mine, send), all_blocks, all_kept, last, got)
+
     add = lambda *terms: sum(t.astype(F32) for t in terms).astype(BF16)
     s1 = add(p1, r1)
     s2 = add(p2, r2)

time: 149 us -> 147 us (0.987)
  waiting for transfers between devices: 54.8 us -> 50.2 us
  Pallas kernels: 55.1 us -> 56.9 us
  other arithmetic: 2.07 us -> 3.86 us
    ppermute x2, waiting for transfers between devices: 7.93 us -> 0.01 us  [dense_body(): across = lambda a: lax.ppermute(a, 'dp', [(0, 1), (1, 0)])]
    pallas_call x3 -> x4, Pallas kernels: 25.3 us -> 29.3 us  [rows_call(): pl.pallas_call(functools.partial(rows_kernel, experts, count, len(groups)...]
    ppermute x23 -> x22, waiting for transfers between devices: 46.8 us -> 50.2 us  [dense_body(): move = lambda a, pairs: lax.ppermute(a, 'expert', pairs)]
    pallas_call x4 -> x3, Pallas kernels: 21.4 us -> 19.2 us  [half_call(): pl.pallas_call(functools.partial(half_kernel, len(blocks), len(kept), las...]
    convert_element_type x3 -> x4, other arithmetic: 1.26 us -> 3.15 us  [dense_body(): add = lambda *terms: sum((t.astype(F32) for t in terms)).astype(BF16)]
    unnamed x36 -> x30, local copies, waits for them, and re-layouts: 4.05 us -> 3.53 us
    ppermute x23 -> x22, starting transfers between devices: 27.3 us -> 27.4 us  [dense_body(): move = lambda a, pairs: lax.ppermute(a, 'expert', pairs)]
  transfers between devices with their start and end apart: 25 -> 24, of which waited for: 9 -> 8; matrix products, arithmetic and copies ran while one was open for 1% -> 3% of each run, Pallas kernels for 33% -> 33%
where the time goes in v5:
time: 147 us
  Pallas kernels  56.9 us (39%)
  waiting for transfers between devices  50.2 us (34%)
  starting transfers between devices  30.8 us (21%)
  local copies, waits for them, and re-layouts  4.09 us (3%)
  other arithmetic  3.86 us (3%)
    ppermute x22, waiting for transfers between devices, dense_body(): move = lambda a, pairs: lax.ppermute(a, 'expert', pairs)  50.2 us
    pallas_call x4, Pallas kernels, rows_call(): pl.pallas_call(functools.partial(rows_kernel, experts, count, len(groups)...  29.3 us
    ppermute x22, starting transfers between devices, dense_body(): move = lambda a, pairs: lax.ppermute(a, 'expert', pairs)  27.4 us
    pallas_call x3, Pallas kernels, half_call(): pl.pallas_call(functools.partial(half_kernel, len(blocks), len(kept), las...  19.2 us
    pallas_call x1, Pallas kernels, finish(): pl.pallas_call(finish_kernel, out_shape=[sds((size, hidden_units), F32),...  3.95 us
    unnamed x30, local copies, waits for them, and re-layouts  3.53 us
    ppermute x2, starting transfers between devices, dense_body(): across = lambda a: lax.ppermute(a, 'dp', [(0, 1), (1, 0)])  3.43 us
    convert_element_type x4, other arithmetic, dense_body(): add = lambda *terms: sum((t.astype(F32) for t in terms)).astype(BF16)  3.15 us
  transfers between devices with their start and end apart: 24, of which 8 were waited for; matrix products, arithmetic and copies ran while one was open for 3% of the time, Pallas kernels for 33%

profile of v5, /device:TPU:0, one launch (start us, length us, event | category | flops | bytes accessed | tf_op | source)
XLA Modules:
  0.0 146.9 jit_solution(11450035867996638444)
XLA Ops:
  0.6 2.0 %shard_map.102.refs_0_ = bf16[128,2176]{1,0:T(8,128)(2,1)} custom-call(bf16[128,1024]{1,0:T(8,128)(2,1)} %tokens.1, bf16[128,1024]{1,0:T(8,128)(2,1)} %d_output.1, f32[8,128]{1,0:T(8,128)} %bitcast.14, s32[8,128]{1,0:T(8,128)} %bitcast.15), custom_call_target="tpu_custom_call" | custom-call | bytes 1572864 | tf_op jit(solution)/shard_map/pallas_call | solution.py:63
  2.6 2.5 %shard_map.103.refs_3_.refs_1_ = bf16[512,1152]{1,0:T(8,128)(2,1)} custom-call(bf16[512,384]{1,0:T(8,128)(2,1)} %bitcast.11, bf16[512,384]{1,0:T(8,128)(2,1)} %bitcast.12, bf16[384,512]{1,0:T(8,128)(2,1)} %bitcast.13), custom_call_target="tpu_custom_call" | custom-call | bytes 4718592 | tf_op jit(solution)/shard_map/pallas_call | solution.py:82
  5.1 2.9 %collective-permute-start.2 = (bf16[512,1152]{1,0:T(8,128)(2,1)}, bf16[512,1152]{1,0:T(8,128)(2,1)}, u32[]{:S(2)}, u32[]{:S(2)}) collective-permute-start(bf16[512,1152]{1,0:T(8,128)(2,1)} %shard_map.103.refs_3_.refs_1_), channel_id=1, source_target_pairs={{0,16},{16,0},{1,17},{17,1},{2,18},{18,2},{3,19},{19,3},{4,20},{20... | collective-permute-start | bytes 3538952 | tf_op jit(solution)/shard_map/ppermute | solution.py:308
  8.0 1.6 %collective-permute-start = (bf16[128,2176]{1,0:T(8,128)(2,1)S(1)}, bf16[128,2176]{1,0:T(8,128)(2,1)S(1)}, u32[]{:S(2)}, u32[]{:S(2)}) collective-permute-start(bf16[128,2176]{1,0:T(8,128)(2,1)S(1)} %copy-done.3), channel_id=1, source_target_pairs={{0,4},{1,5},{2,6},{3,7},{4,0},{5,1},{6,2},{7,3},{8,12},{9,13},{10,... | collective-permute-start | bytes 1671176 | tf_op jit(solution)/shard_map/ppermute | solution.py:307
  9.6 1.5 %collective-permute-start.1 = (bf16[128,2176]{1,0:T(8,128)(2,1)S(1)}, bf16[128,2176]{1,0:T(8,128)(2,1)S(1)}, u32[]{:S(2)}, u32[]{:S(2)}) collective-permute-start(bf16[128,2176]{1,0:T(8,128)(2,1)S(1)} %copy-done.3), channel_id=1, source_target_pairs={{0,2},{1,3},{2,0},{3,1},{4,6},{5,7},{6,4},{7,5},{8,10},{9,11},{10,... | collective-permute-start | bytes 1671176 | tf_op jit(solution)/shard_map/ppermute | solution.py:307
  11.8 10.3 %collective-permute-done.refs_1_ = bf16[128,2176]{1,0:T(8,128)(2,1)S(1)} collective-permute-done((bf16[128,2176]{1,0:T(8,128)(2,1)S(1)}, bf16[128,2176]{1,0:T(8,128)(2,1)S(1)}, u32[]{:S(2)}, u32[]{:S(2)}) %collective-permute-start) | collective-permute-done | bytes 557088 | tf_op jit(solution)/shard_map/ppermute | solution.py:307
  22.1 1.3 collective-permute-done.1.refs_2_
  23.4 1.5 %collective-permute-start.3 = (bf16[128,2176]{1,0:T(8,128)(2,1)S(1)}, bf16[128,2176]{1,0:T(8,128)(2,1)S(1)}, u32[]{:S(2)}, u32[]{:S(2)}) collective-permute-start(bf16[128,2176]{1,0:T(8,128)(2,1)S(1)} %collective-permute-done.refs_1_), channel_id=1, source_target_pairs={{0,2},{1,3},{2,0},{3,1},{4,6},{5,7},{6,4},{7,5},{8,10},{9,11},{10,... | collective-permute-start | bytes 1671176 | tf_op jit(solution)/shard_map/ppermute | solution.py:307
  25.6 1.3 collective-permute-start.9
  26.9 9.5 %collective-permute-done.3.refs_2_.refs_5_ = bf16[128,2176]{1,0:T(8,128)(2,1)S(1)} collective-permute-done((bf16[128,2176]{1,0:T(8,128)(2,1)S(1)}, bf16[128,2176]{1,0:T(8,128)(2,1)S(1)}, u32[]{:S(2)}, u32[]{:S(2)}) %collective-permute-start.3) | collective-permute-done | bytes 557088 | tf_op jit(solution)/shard_map/ppermute | solution.py:307
  37.5 4.4 %collective-permute-done.9 = bf16[128,2176]{1,0:T(8,128)(2,1)S(1)} collective-permute-done((bf16[128,2176]{1,0:T(8,128)(2,1)S(1)}, bf16[128,2176]{1,0:T(8,128)(2,1)S(1)}, u32[]{:S(2)}, u32[]{:S(2)}) %collective-permute-start.9) | collective-permute-done | bytes 557088 | tf_op jit(solution)/shard_map/ppermute | solution.py:307
  42.6 1.3 collective-permute-start.7
  43.9 8.9 %shard_map.104 = (bf16[128,1024]{1,0:T(8,128)(2,1)}, bf16[128,1024]{1,0:T(8,128)(2,1)}, bf16[128,1024]{1,0:T(8,128)(2,1)}, bf16[384,1152]{1,0:T(8,128)(2,1)}, bf...) custom-call(s32[2]{0:T(128)} %pad_add_fusion.scal, ...), custom_call_target="tpu_custom_call" | custom-call | flops 10871635968 | bytes 1048576 | tf_op jit(solution)/shard_map/pallas_call | solution.py:170
  52.9 3.6 %collective-permute-done.7 = bf16[128,2176]{1,0:T(8,128)(2,1)S(1)} collective-permute-done((bf16[128,2176]{1,0:T(8,128)(2,1)S(1)}, bf16[128,2176]{1,0:T(8,128)(2,1)S(1)}, u32[]{:S(2)}, u32[]{:S(2)}) %collective-permute-start.7) | collective-permute-done | bytes 557088 | tf_op jit(solution)/shard_map/ppermute | solution.py:307
  56.6 1.6 %collective-permute-start.11 = (bf16[128,2176]{1,0:T(8,128)(2,1)S(1)}, bf16[128,2176]{1,0:T(8,128)(2,1)S(1)}, u32[]{:S(2)}, u32[]{:S(2)}) collective-permute-start(bf16[128,2176]{1,0:T(8,128)(2,1)S(1)} %broadcast_select_fusion.1.refs_1_.refs_4_), channel_id=1, source_target_pairs={{0,2},{1,3},{2,0},{3,1},{4,6},{5,7},{6,4},{7,5},{8,10},{9,11},{10,... | collective-permute-start | bytes 1671176 | tf_op jit(solution)/shard_map/ppermute | solution.py:307
  58.2 8.9 %shard_map.105 = (bf16[128,1024]{1,0:T(8,128)(2,1)}, bf16[128,1024]{1,0:T(8,128)(2,1)}, bf16[128,1024]{1,0:T(8,128)(2,1)}, bf16[384,1152]{1,0:T(8,128)(2,1)}, bf...) custom-call(s32[2]{0:T(128)} %pad_add_fusion.scal, bf16[128,2176]{1,0:T(8,128)(2,1)} %copy-done.1, ...), custom_call_target="tpu_custom_call" | custom-call | flops 10871635968 | bytes 1048576 | tf_op jit(solution)/shard_map/pallas_call | solution.py:170
  67.1 5.6 %shard_map.106 = (bf16[128,1024]{1,0:T(8,128)(2,1)}, bf16[128,1152]{1,0:T(8,128)(2,1)}, bf16[128,1024]{1,0:T(8,128)(2,1)}, bf16[128,1152]{1,0:T(8,128)(2,1)}, bf16[128,1024]{1,0:T(8,128)(2,1)}) custom-call(s32[2]{0:T(128)} %pad_add_fusion.scal, bf16[128,2176]{1,0:T(8,128)(2,1)} %copy-done.7, bf16[512,1152]{1,0:T(8,128)(2,1)} %shard_map.103.refs_3_.refs_1_, ...), custom_call_target="tpu_custom_call" | custom-call | flops 3623878656 | bytes 1048576 | tf_op jit(solution)/shard_map/pallas_call | solution.py:170
  73.3 7.4 %shard_map.107 = bf16[1024,1152]{1,0:T(8,128)(2,1)} custom-call(s32[2]{0:T(128)} %iota.3.sides, bf16[128,2176]{1,0:T(8,128)(2,1)} %shard_map.102.refs_0_, bf16[128,2176]{1,0:T(8,128)(2,1)} %copy-done.4, bf16[128,2176]{1,0:T(8,128)(2,1)} %copy-done.5, bf16[128,2176]{1,0:T(8,128)(2,1)} %copy-done.1, bf16[128,2176]{1,0:T(8,128)(2,1)} %copy-done.2, ...), custom_call_target="tpu_custom_call" | custom-call | flops 1024 | bytes 1024 | tf_op jit(solution)/shard_map/pallas_call | solution.py:225
  81.5 5.8 %shard_map.108 = (bf16[128,1024]{1,0:T(8,128)(2,1)}, bf16[128,1152]{1,0:T(8,128)(2,1)}, bf16[128,1024]{1,0:T(8,128)(2,1)}, bf16[128,3200]{1,0:T(8,128)(2,1)}) custom-call(s32[2]{0:T(128)} %pad_add_fusion.scal, bf16[128,2176]{1,0:T(8,128)(2,1)} %copy-done.9, bf16[512,1152]{1,0:T(8,128)(2,1)} %shard_map.103.refs_3_.refs_1_, ...), custom_call_target="tpu_custom_call" | custom-call | flops 36238786560 | bytes 1048576 | tf_op jit(solution)/shard_map/pallas_call | solution.py:170
  88.6 1.3 collective-permute-start.13
  90.7 6.7 %collective-permute-done.12 = bf16[128,1024]{1,0:T(8,128)(2,1)} collective-permute-done((bf16[128,1024]{1,0:T(8,128)(2,1)}, bf16[128,1024]{1,0:T(8,128)(2,1)}, u32[]{:S(2)}, u32[]{:S(2)}) %collective-permute-start.12) | collective-permute-done | bytes 262176 | tf_op jit(solution)/shard_map/ppermute | solution.py:307
  99.8 5.9 %shard_map.109 = bf16[512,1152]{1,0:T(8,128)(2,1)} custom-call(s32[1]{0:T(128)} %bitcast.7.sides, bf16[128,2176]{1,0:T(8,128)(2,1)} %shard_map.102.refs_0_, bf16[128,2176]{1,0:T(8,128)(2,1)} %copy-done.4, bf16[128,2176]{1,0:T(8,128)(2,1)} %copy-done.5, bf16[128,2176]{1,0:T(8,128)(2,1)} %copy-done.1, bf16[128,2176]{1,0:T(8,128)(2,1)} %copy-done.2, ...), custom_call_target="tpu_custom_call" | custom-call | flops 1024 | bytes 1024 | tf_op jit(solution)/shard_map/pallas_call | solution.py:225
  106.2 1.1 add_convert_fusion.3
  107.4 1.1 collective-permute-done.15
  109.3 5.5 %collective-permute-start.17 = (bf16[128,1024]{1,0:T(8,128)(2,1)S(1)}, bf16[128,1024]{1,0:T(8,128)(2,1)S(1)}, u32[]{:S(2)}, u32[]{:S(2)}) collective-permute-start(bf16[128,1024]{1,0:T(8,128)(2,1)S(1)} %add_convert_fusion.2), channel_id=1, source_target_pairs={{0,8},{1,9},{2,10},{3,11},{12,4},{13,5},{14,6},{15,7},{16,24},{17,... | collective-permute-start | bytes 786440 | tf_op jit(solution)/shard_map/ppermute | solution.py:307
  114.9 1.3 collective-permute-start.19
  116.2 4.5 %collective-permute-start.20 = (bf16[128,1024]{1,0:T(8,128)(2,1)S(1)}, bf16[128,1024]{1,0:T(8,128)(2,1)S(1)}, u32[]{:S(2)}, u32[]{:S(2)}) collective-permute-start(bf16[128,1024]{1,0:T(8,128)(2,1)S(1)} %add_convert_fusion.1), channel_id=1, source_target_pairs={{0,12},{1,13},{2,14},{3,15},{12,0},{13,1},{14,2},{15,3},{16,28},{1... | collective-permute-start | bytes 786440 | tf_op jit(solution)/shard_map/ppermute | solution.py:307
  120.8 13.3 %collective-permute-done.19 = bf16[128,1024]{1,0:T(8,128)(2,1)S(1)} collective-permute-done((bf16[128,1024]{1,0:T(8,128)(2,1)S(1)}, bf16[128,1024]{1,0:T(8,128)(2,1)S(1)}, u32[]{:S(2)}, u32[]{:S(2)}) %collective-permute-start.19) | collective-permute-done | bytes 262176 | tf_op jit(solution)/shard_map/ppermute | solution.py:307
  134.1 2.0 %add_convert_fusion = bf16[128,1024]{1,0:T(8,128)(2,1)} fusion(bf16[128,1024]{1,0:T(8,128)(2,1)S(1)} %collective-permute-done.20, bf16[128,1024]{1,0:T(8,128)(2,1)S(1)} %collective-permute-done.19, bf16[128,1024]{1,0:T(8,128)(2,1)S(1)} %collective-permute-done.17, bf16[128,1024]{1,0:T(8,128)(2,1)S(1)} %collective-permute-done.16, ...), kind=kLoop, calls=%fused_computation.2 | loop fusion | flops 1835008 | bytes 2097152 | tf_op jit(solution)/shard_map/convert_element_type | solution.py:350
  136.0 5.9 %shard_map.110.keep = bf16[512,1152]{1,0:T(8,128)(2,1)} custom-call(s32[1]{0:T(128)} %bitcast.sides, bf16[128,2176]{1,0:T(8,128)(2,1)} %shard_map.102.refs_0_, bf16[128,2176]{1,0:T(8,128)(2,1)} %copy-done.4, bf16[128,2176]{1,0:T(8,128)(2,1)} %copy-done.5, bf16[128,2176]{1,0:T(8,128)(2,1)} %copy-done.1, bf16[128,2176]{1,0:T(8,128)(2,1)} %copy-done.2, ...), custom_call_target="tpu_custom_call" | custom-call | flops 1024 | bytes 1024 | tf_op jit(solution)/shard_map/pallas_call | solution.py:225
  141.9 1.0 copy-done.10
  142.9 3.9 %shard_map.111 = (f32[512,384]{1,0:T(8,128)}, f32[512,384]{1,0:T(8,128)}, f32[384,512]{1,0:T(8,128)}) custom-call(bf16[512,1152]{1,0:T(8,128)(2,1)} %shard_map.110.keep, bf16[512,1152]{1,0:T(8,128)(2,1)} %copy-done.10), custom_call_target="tpu_custom_call" | custom-call | flops 1024 | bytes 1024 | tf_op jit(solution)/shard_map/pallas_call | solution.py:253
  (64 shorter events, 10.4 us)
Async XLA Ops:
  5.1 31.3 %collective-permute-start.2 = (bf16[512,1152]{1,0:T(8,128)(2,1)}, bf16[512,1152]{1,0:T(8,128)(2,1)}, u32[]{:S(2)}, u32[]{:S(2)}) collective-permute-start(bf16[512,1152]{1,0:T(8,128)(2,1)} %shard_map.103.refs_3_.refs_1_), channel_id=1, source_target_pairs={{0,16},{16,0},{1,17},{17,1},{2,18},{18,2},{3,19},{19,3},{4,20},{20... | collective-permute-start | bytes 3538952 | tf_op jit(solution)/shard_map/ppermute | solution.py:308
  8.0 14.1 %collective-permute-start = (bf16[128,2176]{1,0:T(8,128)(2,1)S(1)}, bf16[128,2176]{1,0:T(8,128)(2,1)S(1)}, u32[]{:S(2)}, u32[]{:S(2)}) collective-permute-start(bf16[128,2176]{1,0:T(8,128)(2,1)S(1)} %copy-done.3), channel_id=1, source_target_pairs={{0,4},{1,5},{2,6},{3,7},{4,0},{5,1},{6,2},{7,3},{8,12},{9,13},{10,... | collective-permute-start | bytes 1671176 | tf_op jit(solution)/shard_map/ppermute | solution.py:307
  9.6 13.8 %collective-permute-start.1 = (bf16[128,2176]{1,0:T(8,128)(2,1)S(1)}, bf16[128,2176]{1,0:T(8,128)(2,1)S(1)}, u32[]{:S(2)}, u32[]{:S(2)}) collective-permute-start(bf16[128,2176]{1,0:T(8,128)(2,1)S(1)} %copy-done.3), channel_id=1, source_target_pairs={{0,2},{1,3},{2,0},{3,1},{4,6},{5,7},{6,4},{7,5},{8,10},{9,11},{10,... | collective-permute-start | bytes 1671176 | tf_op jit(solution)/shard_map/ppermute | solution.py:307
  11.1 14.5 %collective-permute-start.8 = (bf16[128,2176]{1,0:T(8,128)(2,1)S(1)}, bf16[128,2176]{1,0:T(8,128)(2,1)S(1)}, u32[]{:S(2)}, u32[]{:S(2)}) collective-permute-start(bf16[128,2176]{1,0:T(8,128)(2,1)S(1)} %copy-done.3), channel_id=1, source_target_pairs={{4,8},{5,9},{6,10},{7,11},{8,4},{9,5},{10,6},{11,7},{20,24},{21,25... | collective-permute-start | bytes 1671176 | tf_op jit(solution)/shard_map/ppermute | solution.py:307
  22.1 21.8 %copy-start.4 = (bf16[128,2176]{1,0:T(8,128)(2,1)}, bf16[128,2176]{1,0:T(8,128)(2,1)S(1)}, u32[]{:S(2)}) copy-start(bf16[128,2176]{1,0:T(8,128)(2,1)S(1)} %collective-permute-done.refs_1_) | copy-start | bytes 1671172
  23.4 20.5 %copy-start.5 = (bf16[128,2176]{1,0:T(8,128)(2,1)}, bf16[128,2176]{1,0:T(8,128)(2,1)S(1)}, u32[]{:S(2)}) copy-start(bf16[128,2176]{1,0:T(8,128)(2,1)S(1)} %collective-permute-done.1.refs_2_) | copy-start | bytes 1671172
  23.4 13.0 %collective-permute-start.3 = (bf16[128,2176]{1,0:T(8,128)(2,1)S(1)}, bf16[128,2176]{1,0:T(8,128)(2,1)S(1)}, u32[]{:S(2)}, u32[]{:S(2)}) collective-permute-start(bf16[128,2176]{1,0:T(8,128)(2,1)S(1)} %collective-permute-done.refs_1_), channel_id=1, source_target_pairs={{0,2},{1,3},{2,0},{3,1},{4,6},{5,7},{6,4},{7,5},{8,10},{9,11},{10,... | collective-permute-start | bytes 1671176 | tf_op jit(solution)/shard_map/ppermute | solution.py:307
  24.9 11.5 %collective-permute-start.4 = (bf16[128,2176]{1,0:T(8,128)(2,1)S(1)}, bf16[128,2176]{1,0:T(8,128)(2,1)S(1)}, u32[]{:S(2)}, u32[]{:S(2)}) collective-permute-start(bf16[128,2176]{1,0:T(8,128)(2,1)S(1)} %collective-permute-done.refs_1_), channel_id=1, source_target_pairs={{4,8},{5,9},{6,10},{7,11},{8,4},{9,5},{10,6},{11,7},{20,24},{21,25... | collective-permute-start | bytes 1671176 | tf_op jit(solution)/shard_map/ppermute | solution.py:307
  25.6 16.3 %collective-permute-start.9 = (bf16[128,2176]{1,0:T(8,128)(2,1)S(1)}, bf16[128,2176]{1,0:T(8,128)(2,1)S(1)}, u32[]{:S(2)}, u32[]{:S(2)}) collective-permute-start(bf16[128,2176]{1,0:T(8,128)(2,1)S(1)} %collective-permute-done.8), channel_id=1, source_target_pairs={{4,0},{5,1},{6,2},{7,3},{8,12},{9,13},{10,14},{11,15},{20,16},{21,... | collective-permute-start | bytes 1671176 | tf_op jit(solution)/shard_map/ppermute | solution.py:307
  36.4 16.5 %copy-start.6 = (bf16[128,2176]{1,0:T(8,128)(2,1)}, bf16[128,2176]{1,0:T(8,128)(2,1)S(1)}, u32[]{:S(2)}) copy-start(bf16[128,2176]{1,0:T(8,128)(2,1)S(1)} %collective-permute-done.3.refs_2_.refs_5_) | copy-start | bytes 1671172
  36.4 7.5 %collective-permute-start.5 = (bf16[512,1152]{1,0:T(8,128)(2,1)}, bf16[512,1152]{1,0:T(8,128)(2,1)}, u32[]{:S(2)}, u32[]{:S(2)}) collective-permute-start(bf16[512,1152]{1,0:T(8,128)(2,1)} %shard_map.103.refs_3_.refs_1_), channel_id=1, source_target_pairs={{0,1},{1,0},{2,3},{3,2},{4,5},{5,4},{6,7},{7,6},{8,9},{9,8},{10,11... | collective-permute-start | bytes 3538952 | tf_op jit(solution)/shard_map/ppermute | solution.py:307
  36.4 7.5 %collective-permute-start.6 = (bf16[512,1152]{1,0:T(8,128)(2,1)}, bf16[512,1152]{1,0:T(8,128)(2,1)}, u32[]{:S(2)}, u32[]{:S(2)}) collective-permute-start(bf16[512,1152]{1,0:T(8,128)(2,1)} %collective-permute-done.2.refs_4_.refs_2_), channel_id=1, source_target_pairs={{0,1},{1,0},{2,3},{3,2},{4,5},{5,4},{6,7},{7,6},{8,9},{9,8},{10,11... | collective-permute-start | bytes 3538952 | tf_op jit(solution)/shard_map/ppermute | solution.py:307
  42.0 10.9 %copy-start.1 = (bf16[128,2176]{1,0:T(8,128)(2,1)}, bf16[128,2176]{1,0:T(8,128)(2,1)S(1)}, u32[]{:S(2)}) copy-start(bf16[128,2176]{1,0:T(8,128)(2,1)S(1)} %broadcast_select_fusion.refs_0_.refs_3_) | copy-start | bytes 1671172
  42.0 14.5 %collective-permute-start.10 = (bf16[128,2176]{1,0:T(8,128)(2,1)S(1)}, bf16[128,2176]{1,0:T(8,128)(2,1)S(1)}, u32[]{:S(2)}, u32[]{:S(2)}) collective-permute-start(bf16[128,2176]{1,0:T(8,128)(2,1)S(1)} %broadcast_select_fusion.refs_0_.refs_3_), channel_id=1, source_target_pairs={{0,2},{1,3},{2,0},{3,1},{4,6},{5,7},{6,4},{7,5},{8,10},{9,11},{10,... | collective-permute-start | bytes 1671176 | tf_op jit(solution)/shard_map/ppermute | solution.py:307
  42.6 13.9 %collective-permute-start.7 = (bf16[128,2176]{1,0:T(8,128)(2,1)S(1)}, bf16[128,2176]{1,0:T(8,128)(2,1)S(1)}, u32[]{:S(2)}, u32[]{:S(2)}) collective-permute-start(bf16[128,2176]{1,0:T(8,128)(2,1)S(1)} %collective-permute-done.4), channel_id=1, source_target_pairs={{4,0},{5,1},{6,2},{7,3},{8,12},{9,13},{10,14},{11,15},{20,16},{21,... | collective-permute-start | bytes 1671176 | tf_op jit(solution)/shard_map/ppermute | solution.py:307
  56.6 10.5 %copy-start.7 = (bf16[128,2176]{1,0:T(8,128)(2,1)}, bf16[128,2176]{1,0:T(8,128)(2,1)S(1)}, u32[]{:S(2)}) copy-start(bf16[128,2176]{1,0:T(8,128)(2,1)S(1)} %collective-permute-done.10.refs_0_.refs_6_) | copy-start | bytes 1671172
  56.6 24.1 %collective-permute-start.11 = (bf16[128,2176]{1,0:T(8,128)(2,1)S(1)}, bf16[128,2176]{1,0:T(8,128)(2,1)S(1)}, u32[]{:S(2)}, u32[]{:S(2)}) collective-permute-start(bf16[128,2176]{1,0:T(8,128)(2,1)S(1)} %broadcast_select_fusion.1.refs_1_.refs_4_), channel_id=1, source_target_pairs={{0,2},{1,3},{2,0},{3,1},{4,6},{5,7},{6,4},{7,5},{8,10},{9,11},{10,... | collective-permute-start | bytes 1671176 | tf_op jit(solution)/shard_map/ppermute | solution.py:307
  80.6 17.5 %collective-permute-start.22 = (bf16[1024,1152]{1,0:T(8,128)(2,1)}, bf16[1024,1152]{1,0:T(8,128)(2,1)S(1)}, u32[]{:S(2)}, u32[]{:S(2)}) collective-permute-start(bf16[1024,1152]{1,0:T(8,128)(2,1)} %shard_map.107), channel_id=1, source_target_pairs={{0,1},{1,0},{2,3},{3,2},{4,5},{5,4},{6,7},{7,6},{8,9},{9,8},{10,11... | collective-permute-start | bytes 7077896 | tf_op jit(solution)/shard_map/ppermute | solution.py:307
  87.4 10.7 %collective-permute-start.21 = (bf16[128,3200]{1,0:T(8,128)(2,1)}, bf16[128,3200]{1,0:T(8,128)(2,1)S(1)}, u32[]{:S(2)}, u32[]{:S(2)}) collective-permute-start(bf16[128,3200]{1,0:T(8,128)(2,1)} %get-tuple-element.79), channel_id=1, source_target_pairs={{0,1},{1,0},{2,3},{3,2},{4,5},{5,4},{6,7},{7,6},{8,9},{9,8},{10,11... | collective-permute-start | bytes 2457608 | tf_op jit(solution)/shard_map/ppermute | solution.py:307
  87.9 9.5 %collective-permute-start.12 = (bf16[128,1024]{1,0:T(8,128)(2,1)}, bf16[128,1024]{1,0:T(8,128)(2,1)}, u32[]{:S(2)}, u32[]{:S(2)}) collective-permute-start(bf16[128,1024]{1,0:T(8,128)(2,1)} %get-tuple-element.63), channel_id=1, source_target_pairs={{0,2},{1,3},{2,0},{3,1},{4,6},{5,7},{6,4},{7,5},{8,10},{9,11},{10,... | collective-permute-start | bytes 786440 | tf_op jit(solution)/shard_map/ppermute | solution.py:307
  88.6 17.6 %collective-permute-start.13 = (bf16[128,1024]{1,0:T(8,128)(2,1)}, bf16[128,1024]{1,0:T(8,128)(2,1)}, u32[]{:S(2)}, u32[]{:S(2)}) collective-permute-start(bf16[128,1024]{1,0:T(8,128)(2,1)} %get-tuple-element.66), channel_id=1, source_target_pairs={{0,2},{1,3},{2,0},{3,1},{4,6},{5,7},{6,4},{7,5},{8,10},{9,11},{10,... | collective-permute-start | bytes 786440 | tf_op jit(solution)/shard_map/ppermute | solution.py:307
  90.0 18.6 %collective-permute-start.15 = (bf16[128,1024]{1,0:T(8,128)(2,1)}, bf16[128,1024]{1,0:T(8,128)(2,1)S(1)}, u32[]{:S(2)}, u32[]{:S(2)}) collective-permute-start(bf16[128,1024]{1,0:T(8,128)(2,1)} %get-tuple-element.67), channel_id=1, source_target_pairs={{0,2},{1,3},{2,0},{3,1},{4,6},{5,7},{6,4},{7,5},{8,10},{9,11},{10,... | collective-permute-start | bytes 786440 | tf_op jit(solution)/shard_map/ppermute | solution.py:307
  97.4 17.4 %collective-permute-start.18 = (bf16[128,1024]{1,0:T(8,128)(2,1)}, bf16[128,1024]{1,0:T(8,128)(2,1)S(1)}, u32[]{:S(2)}, u32[]{:S(2)}) collective-permute-start(bf16[128,1024]{1,0:T(8,128)(2,1)} %get-tuple-element.70), channel_id=1, source_target_pairs={{0,2},{1,3},{2,0},{3,1},{4,6},{5,7},{6,4},{7,5},{8,10},{9,11},{10,... | collective-permute-start | bytes 786440 | tf_op jit(solution)/shard_map/ppermute | solution.py:307
  99.8 8.7 %copy-start.13 = (bf16[128,1024]{1,0:T(8,128)(2,1)S(1)}, bf16[128,1024]{1,0:T(8,128)(2,1)}, u32[]{:S(2)}) copy-start(bf16[128,1024]{1,0:T(8,128)(2,1)} %get-tuple-element.53) | copy-start | bytes 786436
  105.7 9.1 %copy-start.11 = (bf16[128,1024]{1,0:T(8,128)(2,1)S(1)}, bf16[128,1024]{1,0:T(8,128)(2,1)}, u32[]{:S(2)}) copy-start(bf16[128,1024]{1,0:T(8,128)(2,1)} %get-tuple-element.68) | copy-start | bytes 786436
  105.7 36.1 %collective-permute-start.23 = (bf16[512,1152]{1,0:T(8,128)(2,1)}, bf16[512,1152]{1,0:T(8,128)(2,1)S(1)}, u32[]{:S(2)}, u32[]{:S(2)}) collective-permute-start(bf16[512,1152]{1,0:T(8,128)(2,1)} %shard_map.109), channel_id=1, source_target_pairs={{0,16},{16,0},{1,17},{17,1},{2,18},{18,2},{3,19},{19,3},{4,20},{20... | collective-permute-start | bytes 3538952 | tf_op jit(solution)/shard_map/ppermute | solution.py:308
  106.2 27.8 %copy-start.14 = (bf16[128,1024]{1,0:T(8,128)(2,1)S(1)}, bf16[128,1024]{1,0:T(8,128)(2,1)}, u32[]{:S(2)}) copy-start(bf16[128,1024]{1,0:T(8,128)(2,1)} %get-tuple-element.48) | copy-start | bytes 786436
  107.3 8.9 %collective-permute-start.14 = (bf16[128,1024]{1,0:T(8,128)(2,1)S(1)}, bf16[128,1024]{1,0:T(8,128)(2,1)S(1)}, u32[]{:S(2)}, u32[]{:S(2)}) collective-permute-start(bf16[128,1024]{1,0:T(8,128)(2,1)S(1)} %add_convert_fusion.3), channel_id=1, source_target_pairs={{0,4},{1,5},{2,6},{3,7},{4,0},{5,1},{6,2},{7,3},{8,12},{9,13},{10,... | collective-permute-start | bytes 786440 | tf_op jit(solution)/shard_map/ppermute | solution.py:307
  108.6 12.1 %collective-permute-start.16 = (bf16[128,1024]{1,0:T(8,128)(2,1)S(1)}, bf16[128,1024]{1,0:T(8,128)(2,1)S(1)}, u32[]{:S(2)}, u32[]{:S(2)}) collective-permute-start(bf16[128,1024]{1,0:T(8,128)(2,1)S(1)} %add_convert_fusion.2), channel_id=1, source_target_pairs={{4,8},{5,9},{6,10},{7,11},{8,4},{9,5},{10,6},{11,7},{20,24},{21,25... | collective-permute-start | bytes 786440 | tf_op jit(solution)/shard_map/ppermute | solution.py:307
  109.3 11.5 %collective-permute-start.17 = (bf16[128,1024]{1,0:T(8,128)(2,1)S(1)}, bf16[128,1024]{1,0:T(8,128)(2,1)S(1)}, u32[]{:S(2)}, u32[]{:S(2)}) collective-permute-start(bf16[128,1024]{1,0:T(8,128)(2,1)S(1)} %add_convert_fusion.2), channel_id=1, source_target_pairs={{0,8},{1,9},{2,10},{3,11},{12,4},{13,5},{14,6},{15,7},{16,24},{17,... | collective-permute-start | bytes 786440 | tf_op jit(solution)/shard_map/ppermute | solution.py:307
  114.9 19.2 %collective-permute-start.19 = (bf16[128,1024]{1,0:T(8,128)(2,1)S(1)}, bf16[128,1024]{1,0:T(8,128)(2,1)S(1)}, u32[]{:S(2)}, u32[]{:S(2)}) collective-permute-start(bf16[128,1024]{1,0:T(8,128)(2,1)S(1)} %add_convert_fusion.1), channel_id=1, source_target_pairs={{4,12},{5,13},{6,14},{7,15},{8,0},{9,1},{10,2},{11,3},{20,28},{21,... | collective-permute-start | bytes 786440 | tf_op jit(solution)/shard_map/ppermute | solution.py:307
  116.2 17.8 %collective-permute-start.20 = (bf16[128,1024]{1,0:T(8,128)(2,1)S(1)}, bf16[128,1024]{1,0:T(8,128)(2,1)S(1)}, u32[]{:S(2)}, u32[]{:S(2)}) collective-permute-start(bf16[128,1024]{1,0:T(8,128)(2,1)S(1)} %add_convert_fusion.1), channel_id=1, source_target_pairs={{0,12},{1,13},{2,14},{3,15},{12,0},{13,1},{14,2},{15,3},{16,28},{1... | collective-permute-start | bytes 786440 | tf_op jit(solution)/shard_map/ppermute | solution.py:307
  (7 other events, 18.0 us)

commit v6 on v5

--- a/solution.py
+++ b/solution.py
@@ -207,7 +207,7 @@
         out[:, span] = new.astype(BF16)
 
 
-def half_call(sides, blocks, kept, last=None, more=None):
+def half_call(sides, blocks, kept, last=None, more=None, weight=0):
     grads, scaled = [k[0] for k in kept], [k[1] for k in kept]
     size = scaled[0].shape[1] // 2
     stacked = grads[0].shape[1]
@@ -220,7 +220,7 @@
         specs.append(whole(last))
     if more is not None:
         operands.append(more)
-        specs.append(pl.BlockSpec((size, stacked), lambda i, s: (s[i], 0)))
+        specs.append(pl.BlockSpec((size, stacked), lambda i, s: (i, 0)))
     count = sides.shape[0]
     return pl.pallas_call(
         functools.partial(half_kernel, len(blocks), len(kept), last is not None, more is not None),
@@ -231,7 +231,7 @@
             in_specs=specs,
             out_specs=pl.BlockSpec((size, stacked), lambda i, s: (i, 0)),
         ),
-        cost_estimate=cost(1024, 1024),
+        cost_estimate=cost(8 * weight * size * stacked * 1024 + 1024, 1024),
         compiler_params=params(),
     )(sides, *operands)
 
@@ -302,7 +302,6 @@
     scal = jnp.stack([part, expert]).astype(jnp.int32)
     mine = part[None].astype(jnp.int32)
     other = (1 - part)[None].astype(jnp.int32)
-    sides = jnp.arange(2, dtype=jnp.int32)
 
     move = lambda a, pairs: lax.ppermute(a, "expert", pairs)
     across = lambda a: lax.ppermute(a, "dp", [(0, 1), (1, 0)])
@@ -325,34 +324,37 @@
     w_core = swap(after(w_own, y1, f2))
     w_both = swap(after(w_part, y1, f2))
     weights = [w_own, w_part, w_core, w_both]
-    p0, p1, q0, *kept_a = rows_call(experts, scal, [[own], [b1], [y0]], weights)
+    p0, p1, p2, q0, *kept_a = rows_call(experts, scal, [[own], [b1], [b2], [y0]], weights)
     b3 = jnp.where(inner, f2, after(g2, p0))
     y3 = move(after(b3, y2), SWAP_Y)
-    p2, p3, q1, *kept_b = rows_call(experts, scal, [[b2], [b3], [y1]], weights)
-    q2, *kept_c = rows_call(experts, scal, [[after(y2, p2)]], weights)
-
-    blocks = [own, b1, y0, b2, b3, y1, y2]
-    kept = [kept_a, kept_b, kept_c]
-    to_core = half_call(sides, blocks, [k[2:] for k in kept])
-    y3 = after(y3, q2, to_core)
-    r0, r1, r2 = (move(after(q, y3), SWAP_Y) for q in (q0, q1, q2))
+    p3, q12, *kept_b = rows_call(experts, scal, [[b3], [y1, y2]], weights)
+
+    blocks = [own, b1, b2, y0, b3, y1, y2]
+    kept = [kept_a, kept_b]
+    others = lambda side, first: half_call(side, [first] + blocks[1:], [k[2:] for k in kept])
+    to_core = others(other, own)
+    y3 = after(y3, q12, to_core)
+    r12 = move(after(q12, y3), SWAP_Y)
+    rows = own.shape[0]
+    r1, r2 = r12[:rows], r12[rows:]
 
     q3, *kept_d, joined = rows_call(experts, scal, [[y3]], weights, joined=True)
     last = swap(joined)
-    r3 = move(after(q3, r0), SWAP_Y)
+    r3 = move(after(q3, r12), SWAP_Y)
+    r0 = move(after(q0, r3), SWAP_Y)
     all_blocks = blocks + [y3]
     all_kept = [k[:2] for k in kept] + [kept_d]
-    got = swap(to_core)
-    send = half_call(other, all_blocks, all_kept, last, got)
+    send = half_call(other, all_blocks, all_kept, last, swap(to_core), weight=1)
     from_part = across(send)
-    keep = half_call(after(mine, send), all_blocks, all_kept, last, got)
+    from_core = swap(others(mine, after(own, send, r12)))
+    keep = half_call(after(mine, send), all_blocks, all_kept, last, from_core)
 
     add = lambda *terms: sum(t.astype(F32) for t in terms).astype(BF16)
     s1 = add(p1, r1)
     s2 = add(p2, r2)
     s3 = add(p3, r3)
     d_tokens = add(
-        p0,
+        after(p0, keep),
         r0,
         move(s1, OUTER),
         move(s2, INNER),
@@ -360,7 +362,7 @@
         move(s3, SKIP_TO_OUTER),
         move(s3, ENDS),
     )
-    d_gate, d_up, d_down = finish(keep, from_part)
+    d_gate, d_up, d_down = finish(keep, after(from_part, d_tokens))
     return (d_tokens, d_gate[None], d_up[None], d_down[None])
 
 

time: 147 us -> 137 us (0.932)
  waiting for transfers between devices: 50.2 us -> 46.8 us
  starting transfers between devices: 30.8 us -> 28.3 us
  other arithmetic: 3.86 us -> 1.96 us
    pallas_call x4 -> x3, Pallas kernels: 29.3 us -> 25.7 us  [rows_call(): pl.pallas_call(functools.partial(rows_kernel, experts, count, len(groups)...]
    ppermute x22, waiting for transfers between devices: 50.2 us -> 46.8 us  [dense_body(): move = lambda a, pairs: lax.ppermute(a, 'expert', pairs)]
    ppermute x22, starting transfers between devices: 27.4 us -> 24.8 us  [dense_body(): move = lambda a, pairs: lax.ppermute(a, 'expert', pairs)]
    pallas_call x3 -> x4, Pallas kernels: 19.2 us -> 21.6 us  [half_call(): pl.pallas_call(functools.partial(half_kernel, len(blocks), len(kept), las...]
    convert_element_type x4 -> x3, other arithmetic: 3.15 us -> 1.26 us  [dense_body(): add = lambda *terms: sum((t.astype(F32) for t in terms)).astype(BF16)]
    unnamed x30 -> x40, local copies, waits for them, and re-layouts: 3.53 us -> 3.11 us
  transfers between devices with their start and end apart: 24 -> 24, of which waited for: 8 -> 11; matrix products, arithmetic and copies ran while one was open for 3% -> 1% of each run, Pallas kernels for 33% -> 31%
where the time goes in v6:
time: 137 us
  Pallas kernels  55.7 us (41%)
  waiting for transfers between devices  46.8 us (34%)
  starting transfers between devices  28.3 us (21%)
  local copies, waits for them, and re-layouts  3.11 us (2%)
  other arithmetic  1.96 us (1%)
    ppermute x22, waiting for transfers between devices, dense_body(): move = lambda a, pairs: lax.ppermute(a, 'expert', pairs)  46.8 us
    pallas_call x3, Pallas kernels, rows_call(): pl.pallas_call(functools.partial(rows_kernel, experts, count, len(groups)...  25.7 us
    ppermute x22, starting transfers between devices, dense_body(): move = lambda a, pairs: lax.ppermute(a, 'expert', pairs)  24.8 us
    pallas_call x4, Pallas kernels, half_call(): pl.pallas_call(functools.partial(half_kernel, len(blocks), len(kept), las...  21.6 us
    pallas_call x1, Pallas kernels, finish(): pl.pallas_call(finish_kernel, out_shape=[sds((size, hidden_units), F32),...  3.95 us
    ppermute x2, starting transfers between devices, dense_body(): across = lambda a: lax.ppermute(a, 'dp', [(0, 1), (1, 0)])  3.5 us
    unnamed x40, local copies, waits for them, and re-layouts  3.11 us
  transfers between devices with their start and end apart: 24, of which 11 were waited for; matrix products, arithmetic and copies ran while one was open for 1% of the time, Pallas kernels for 31%

profile of v6, /device:TPU:0, one launch (start us, length us, event | category | flops | bytes accessed | tf_op | source)
XLA Modules:
  0.0 136.8 jit_solution(8781557942540873828)
XLA Ops:
  0.6 2.0 %shard_map.102.refs_0_ = bf16[128,2176]{1,0:T(8,128)(2,1)} custom-call(bf16[128,1024]{1,0:T(8,128)(2,1)} %tokens.1, bf16[128,1024]{1,0:T(8,128)(2,1)} %d_output.1, f32[8,128]{1,0:T(8,128)} %bitcast.14, s32[8,128]{1,0:T(8,128)} %bitcast.15), custom_call_target="tpu_custom_call" | custom-call | bytes 1572864 | tf_op jit(solution)/shard_map/pallas_call | solution.py:63
  2.6 2.5 %shard_map.103.refs_4_.refs_3_.refs_1_ = bf16[512,1152]{1,0:T(8,128)(2,1)} custom-call(bf16[512,384]{1,0:T(8,128)(2,1)} %bitcast.11, bf16[512,384]{1,0:T(8,128)(2,1)} %bitcast.12, bf16[384,512]{1,0:T(8,128)(2,1)} %bitcast.13), custom_call_target="tpu_custom_call" | custom-call | bytes 4718592 | tf_op jit(solution)/shard_map/pallas_call | solution.py:82
  5.1 2.9 %collective-permute-start.4 = (bf16[512,1152]{1,0:T(8,128)(2,1)}, bf16[512,1152]{1,0:T(8,128)(2,1)}, u32[]{:S(2)}, u32[]{:S(2)}) collective-permute-start(bf16[512,1152]{1,0:T(8,128)(2,1)} %shard_map.103.refs_4_.refs_3_.refs_1_), channel_id=1, source_target_pairs={{0,16},{16,0},{1,17},{17,1},{2,18},{18,2},{3,19},{19,3},{4,20},{20... | collective-permute-start | bytes 3538952 | tf_op jit(solution)/shard_map/ppermute | solution.py:307
  8.0 1.5 %collective-permute-start.3 = (bf16[128,2176]{1,0:T(8,128)(2,1)S(1)}, bf16[128,2176]{1,0:T(8,128)(2,1)S(1)}, u32[]{:S(2)}, u32[]{:S(2)}) collective-permute-start(bf16[128,2176]{1,0:T(8,128)(2,1)S(1)} %copy-done.2), channel_id=1, source_target_pairs={{0,2},{1,3},{2,0},{3,1},{4,6},{5,7},{6,4},{7,5},{8,10},{9,11},{10,... | collective-permute-start | bytes 1671176 | tf_op jit(solution)/shard_map/ppermute | solution.py:306
  9.5 1.6 %collective-permute-start = (bf16[128,2176]{1,0:T(8,128)(2,1)S(1)}, bf16[128,2176]{1,0:T(8,128)(2,1)S(1)}, u32[]{:S(2)}, u32[]{:S(2)}) collective-permute-start(bf16[128,2176]{1,0:T(8,128)(2,1)S(1)} %copy-done.2), channel_id=1, source_target_pairs={{0,4},{1,5},{2,6},{3,7},{4,0},{5,1},{6,2},{7,3},{8,12},{9,13},{10,... | collective-permute-start | bytes 1671176 | tf_op jit(solution)/shard_map/ppermute | solution.py:306
  11.8 10.3 %collective-permute-done.3.refs_3_ = bf16[128,2176]{1,0:T(8,128)(2,1)S(1)} collective-permute-done((bf16[128,2176]{1,0:T(8,128)(2,1)S(1)}, bf16[128,2176]{1,0:T(8,128)(2,1)S(1)}, u32[]{:S(2)}, u32[]{:S(2)}) %collective-permute-start.3) | collective-permute-done | bytes 557088 | tf_op jit(solution)/shard_map/ppermute | solution.py:306
  22.1 1.2 collective-permute-done.refs_1_
  24.6 1.3 collective-permute-start.2
  25.9 10.5 %collective-permute-done.5.refs_1_.refs_5_ = bf16[128,2176]{1,0:T(8,128)(2,1)S(1)} collective-permute-done((bf16[128,2176]{1,0:T(8,128)(2,1)S(1)}, bf16[128,2176]{1,0:T(8,128)(2,1)S(1)}, u32[]{:S(2)}, u32[]{:S(2)}) %collective-permute-start.5) | collective-permute-done | bytes 557088 | tf_op jit(solution)/shard_map/ppermute | solution.py:306
  37.4 3.6 %collective-permute-done.2 = bf16[128,2176]{1,0:T(8,128)(2,1)S(1)} collective-permute-done((bf16[128,2176]{1,0:T(8,128)(2,1)S(1)}, bf16[128,2176]{1,0:T(8,128)(2,1)S(1)}, u32[]{:S(2)}, u32[]{:S(2)}) %collective-permute-start.2) | collective-permute-done | bytes 557088 | tf_op jit(solution)/shard_map/ppermute | solution.py:306
  41.1 1.4 %collective-permute-start.10 = (bf16[128,2176]{1,0:T(8,128)(2,1)S(1)}, bf16[128,2176]{1,0:T(8,128)(2,1)S(1)}, u32[]{:S(2)}, u32[]{:S(2)}) collective-permute-start(bf16[128,2176]{1,0:T(8,128)(2,1)S(1)} %broadcast_select_fusion.1.refs_2_), channel_id=1, source_target_pairs={{0,2},{1,3},{2,0},{3,1},{4,6},{5,7},{6,4},{7,5},{8,10},{9,11},{10,... | collective-permute-start | bytes 1671176 | tf_op jit(solution)/shard_map/ppermute | solution.py:306
  42.6 1.3 collective-permute-start.9
  43.9 10.8 %shard_map.104 = (bf16[128,1024]{1,0:T(8,128)(2,1)}, bf16[128,1024]{1,0:T(8,128)(2,1)}, bf16[128,1024]{1,0:T(8,128)(2,1)}, bf16[128,1024]{1,0:T(8,128)(2,1)}, bf...) custom-call(s32[2]{0:T(128)} %pad_add_fusion.scal, ...), custom_call_target="tpu_custom_call" | custom-call | flops 14495514624 | bytes 1048576 | tf_op jit(solution)/shard_map/pallas_call | solution.py:170
  54.7 1.9 %collective-permute-done.9 = bf16[128,2176]{1,0:T(8,128)(2,1)S(1)} collective-permute-done((bf16[128,2176]{1,0:T(8,128)(2,1)S(1)}, bf16[128,2176]{1,0:T(8,128)(2,1)S(1)}, u32[]{:S(2)}, u32[]{:S(2)}) %collective-permute-start.9) | collective-permute-done | bytes 557088 | tf_op jit(solution)/shard_map/ppermute | solution.py:306
  57.6 9.0 %shard_map.105 = (bf16[128,1024]{1,0:T(8,128)(2,1)}, bf16[256,1024]{1,0:T(8,128)(2,1)}, bf16[384,1152]{1,0:T(8,128)(2,1)}, bf16[384,1024]{1,0:T(8,128)(2,1)}, bf...) custom-call(s32[2]{0:T(128)} %pad_add_fusion.scal, bf16[128,2176]{1,0:T(8,128)(2,1)} %copy-done.1, ...), custom_call_target="tpu_custom_call" | custom-call | flops 10871635968 | bytes 1048576 | tf_op jit(solution)/shard_map/pallas_call | solution.py:170
  66.7 4.9 %shard_map.106 = bf16[512,1152]{1,0:T(8,128)(2,1)} custom-call(s32[1]{0:T(128)} %bitcast.7.sides, bf16[128,2176]{1,0:T(8,128)(2,1)} %shard_map.102.refs_0_, bf16[128,2176]{1,0:T(8,128)(2,1)} %copy-done.4, bf16[128,2176]{1,0:T(8,128)(2,1)} %copy-done, bf16[128,2176]{1,0:T(8,128)(2,1)} %copy-done.3, bf16[128,2176]{1,0:T(8,128)(2,1)} %copy-done.1, ...), custom_call_target="tpu_custom_call" | custom-call | flops 1024 | bytes 1024 | tf_op jit(solution)/shard_map/pallas_call | solution.py:225
  72.4 5.9 %shard_map.107 = (bf16[128,1024]{1,0:T(8,128)(2,1)}, bf16[128,1152]{1,0:T(8,128)(2,1)}, bf16[128,1024]{1,0:T(8,128)(2,1)}, bf16[128,3200]{1,0:T(8,128)(2,1)}) custom-call(s32[2]{0:T(128)} %pad_add_fusion.scal, bf16[128,2176]{1,0:T(8,128)(2,1)} %copy-done.10, bf16[512,1152]{1,0:T(8,128)(2,1)} %shard_map.103.refs_4_.refs_3_.refs_1_, ...), custom_call_target="tpu_custom_call" | custom-call | flops 36238786560 | bytes 1048576 | tf_op jit(solution)/shard_map/pallas_call | solution.py:170
  78.8 1.1 collective-permute-start.14
  79.9 1.0 collective-permute-done.12.refs_14_
  81.9 6.1 %shard_map.108 = bf16[512,1152]{1,0:T(8,128)(2,1)} custom-call(s32[1]{0:T(128)} %bitcast.7.sides, bf16[128,2176]{1,0:T(8,128)(2,1)} %shard_map.102.refs_0_, bf16[128,2176]{1,0:T(8,128)(2,1)} %copy-done.4, bf16[128,2176]{1,0:T(8,128)(2,1)} %copy-done, bf16[128,2176]{1,0:T(8,128)(2,1)} %copy-done.3, bf16[128,2176]{1,0:T(8,128)(2,1)} %copy-done.1, ...), custom_call_target="tpu_custom_call" | custom-call | flops 4831839232 | bytes 1024 | tf_op jit(solution)/shard_map/pallas_call | solution.py:225
  88.1 4.7 %collective-permute-done.14 = bf16[256,1024]{1,0:T(8,128)(2,1)S(1)} collective-permute-done((bf16[256,1024]{1,0:T(8,128)(2,1)S(1)}, bf16[256,1024]{1,0:T(8,128)(2,1)S(1)}, u32[]{:S(2)}, u32[]{:S(2)}) %collective-permute-start.14) | collective-permute-done | bytes 524320 | tf_op jit(solution)/shard_map/ppermute | solution.py:306
  92.7 4.7 %shard_map.109 = bf16[512,1152]{1,0:T(8,128)(2,1)} custom-call(s32[1]{0:T(128)} %bitcast.sides, bf16[128,2176]{1,0:T(8,128)(2,1)} %shard_map.102.refs_0_, bf16[128,2176]{1,0:T(8,128)(2,1)} %copy-done.4, bf16[128,2176]{1,0:T(8,128)(2,1)} %copy-done, bf16[128,2176]{1,0:T(8,128)(2,1)} %copy-done.3, bf16[128,2176]{1,0:T(8,128)(2,1)} %copy-done.1, ...), custom_call_target="tpu_custom_call" | custom-call | flops 1024 | bytes 1024 | tf_op jit(solution)/shard_map/pallas_call | solution.py:225
  98.1 1.1 collective-permute-start.16
  100.2 4.2 %collective-permute-start.20 = (bf16[128,1024]{1,0:T(8,128)(2,1)S(1)}, bf16[128,1024]{1,0:T(8,128)(2,1)S(1)}, u32[]{:S(2)}, u32[]{:S(2)}) collective-permute-start(bf16[128,1024]{1,0:T(8,128)(2,1)S(1)} %get-tuple-element.77), channel_id=1, source_target_pairs={{0,8},{1,9},{2,10},{3,11},{12,4},{13,5},{14,6},{15,7},{16,24},{17,... | collective-permute-start | bytes 786440 | tf_op jit(solution)/shard_map/ppermute | solution.py:306
  104.4 2.0 %collective-permute-done.16 = bf16[128,1024]{1,0:T(8,128)(2,1)S(1)} collective-permute-done((bf16[128,1024]{1,0:T(8,128)(2,1)S(1)}, bf16[128,1024]{1,0:T(8,128)(2,1)S(1)}, u32[]{:S(2)}, u32[]{:S(2)}) %collective-permute-start.16) | collective-permute-done | bytes 262176 | tf_op jit(solution)/shard_map/ppermute | solution.py:306
  108.5 3.1 %collective-permute-done.20 = bf16[128,1024]{1,0:T(8,128)(2,1)S(1)} collective-permute-done((bf16[128,1024]{1,0:T(8,128)(2,1)S(1)}, bf16[128,1024]{1,0:T(8,128)(2,1)S(1)}, u32[]{:S(2)}, u32[]{:S(2)}) %collective-permute-start.20) | collective-permute-done | bytes 262176 | tf_op jit(solution)/shard_map/ppermute | solution.py:306
  111.5 3.9 %collective-permute-start.22 = (bf16[128,1024]{1,0:T(8,128)(2,1)S(1)}, bf16[128,1024]{1,0:T(8,128)(2,1)S(1)}, u32[]{:S(2)}, u32[]{:S(2)}) collective-permute-start(bf16[128,1024]{1,0:T(8,128)(2,1)S(1)} %add_convert_fusion.1), channel_id=1, source_target_pairs={{0,12},{1,13},{2,14},{3,15},{12,0},{13,1},{14,2},{15,3},{16,28},{1... | collective-permute-start | bytes 786440 | tf_op jit(solution)/shard_map/ppermute | solution.py:306
  115.4 1.3 collective-permute-start.21
  116.7 5.9 %shard_map.110.keep = bf16[512,1152]{1,0:T(8,128)(2,1)} custom-call(s32[1]{0:T(128)} %bitcast.sides, bf16[128,2176]{1,0:T(8,128)(2,1)} %shard_map.102.refs_0_, bf16[128,2176]{1,0:T(8,128)(2,1)} %copy-done.4, bf16[128,2176]{1,0:T(8,128)(2,1)} %copy-done, bf16[128,2176]{1,0:T(8,128)(2,1)} %copy-done.3, bf16[128,2176]{1,0:T(8,128)(2,1)} %copy-done.1, ...), custom_call_target="tpu_custom_call" | custom-call | flops 1024 | bytes 1024 | tf_op jit(solution)/shard_map/pallas_call | solution.py:225
  122.7 8.1 %collective-permute-done.21 = bf16[128,1024]{1,0:T(8,128)(2,1)S(1)} collective-permute-done((bf16[128,1024]{1,0:T(8,128)(2,1)S(1)}, bf16[128,1024]{1,0:T(8,128)(2,1)S(1)}, u32[]{:S(2)}, u32[]{:S(2)}) %collective-permute-start.21) | collective-permute-done | bytes 262176 | tf_op jit(solution)/shard_map/ppermute | solution.py:306
  131.8 1.0 copy-done.8
  132.8 3.9 %shard_map.111 = (f32[512,384]{1,0:T(8,128)}, f32[512,384]{1,0:T(8,128)}, f32[384,512]{1,0:T(8,128)}) custom-call(bf16[512,1152]{1,0:T(8,128)(2,1)} %shard_map.110.keep, bf16[512,1152]{1,0:T(8,128)(2,1)} %copy-done.8), custom_call_target="tpu_custom_call" | custom-call | flops 1024 | bytes 1024 | tf_op jit(solution)/shard_map/pallas_call | solution.py:253
  (72 shorter events, 11.1 us)
Async XLA Ops:
  5.1 31.3 %collective-permute-start.4 = (bf16[512,1152]{1,0:T(8,128)(2,1)}, bf16[512,1152]{1,0:T(8,128)(2,1)}, u32[]{:S(2)}, u32[]{:S(2)}) collective-permute-start(bf16[512,1152]{1,0:T(8,128)(2,1)} %shard_map.103.refs_4_.refs_3_.refs_1_), channel_id=1, source_target_pairs={{0,16},{16,0},{1,17},{17,1},{2,18},{18,2},{3,19},{19,3},{4,20},{20... | collective-permute-start | bytes 3538952 | tf_op jit(solution)/shard_map/ppermute | solution.py:307
  8.0 14.1 %collective-permute-start.3 = (bf16[128,2176]{1,0:T(8,128)(2,1)S(1)}, bf16[128,2176]{1,0:T(8,128)(2,1)S(1)}, u32[]{:S(2)}, u32[]{:S(2)}) collective-permute-start(bf16[128,2176]{1,0:T(8,128)(2,1)S(1)} %copy-done.2), channel_id=1, source_target_pairs={{0,2},{1,3},{2,0},{3,1},{4,6},{5,7},{6,4},{7,5},{8,10},{9,11},{10,... | collective-permute-start | bytes 1671176 | tf_op jit(solution)/shard_map/ppermute | solution.py:306
  9.5 13.8 %collective-permute-start = (bf16[128,2176]{1,0:T(8,128)(2,1)S(1)}, bf16[128,2176]{1,0:T(8,128)(2,1)S(1)}, u32[]{:S(2)}, u32[]{:S(2)}) collective-permute-start(bf16[128,2176]{1,0:T(8,128)(2,1)S(1)} %copy-done.2), channel_id=1, source_target_pairs={{0,4},{1,5},{2,6},{3,7},{4,0},{5,1},{6,2},{7,3},{8,12},{9,13},{10,... | collective-permute-start | bytes 1671176 | tf_op jit(solution)/shard_map/ppermute | solution.py:306
  11.1 13.4 %collective-permute-start.1 = (bf16[128,2176]{1,0:T(8,128)(2,1)S(1)}, bf16[128,2176]{1,0:T(8,128)(2,1)S(1)}, u32[]{:S(2)}, u32[]{:S(2)}) collective-permute-start(bf16[128,2176]{1,0:T(8,128)(2,1)S(1)} %copy-done.2), channel_id=1, source_target_pairs={{4,8},{5,9},{6,10},{7,11},{8,4},{9,5},{10,6},{11,7},{20,24},{21,25... | collective-permute-start | bytes 1671176 | tf_op jit(solution)/shard_map/ppermute | solution.py:306
  22.1 21.7 %copy-start.3 = (bf16[128,2176]{1,0:T(8,128)(2,1)}, bf16[128,2176]{1,0:T(8,128)(2,1)S(1)}, u32[]{:S(2)}) copy-start(bf16[128,2176]{1,0:T(8,128)(2,1)S(1)} %collective-permute-done.3.refs_3_) | copy-start | bytes 1671172
  23.4 20.5 %copy-start.4 = (bf16[128,2176]{1,0:T(8,128)(2,1)}, bf16[128,2176]{1,0:T(8,128)(2,1)S(1)}, u32[]{:S(2)}) copy-start(bf16[128,2176]{1,0:T(8,128)(2,1)S(1)} %collective-permute-done.refs_1_) | copy-start | bytes 1671172
  23.4 13.0 %collective-permute-start.5 = (bf16[128,2176]{1,0:T(8,128)(2,1)S(1)}, bf16[128,2176]{1,0:T(8,128)(2,1)S(1)}, u32[]{:S(2)}, u32[]{:S(2)}) collective-permute-start(bf16[128,2176]{1,0:T(8,128)(2,1)S(1)} %collective-permute-done.refs_1_), channel_id=1, source_target_pairs={{0,2},{1,3},{2,0},{3,1},{4,6},{5,7},{6,4},{7,5},{8,10},{9,11},{10,... | collective-permute-start | bytes 1671176 | tf_op jit(solution)/shard_map/ppermute | solution.py:306
  23.9 12.5 %collective-permute-start.6 = (bf16[128,2176]{1,0:T(8,128)(2,1)S(1)}, bf16[128,2176]{1,0:T(8,128)(2,1)S(1)}, u32[]{:S(2)}, u32[]{:S(2)}) collective-permute-start(bf16[128,2176]{1,0:T(8,128)(2,1)S(1)} %collective-permute-done.refs_1_), channel_id=1, source_target_pairs={{4,8},{5,9},{6,10},{7,11},{8,4},{9,5},{10,6},{11,7},{20,24},{21,25... | collective-permute-start | bytes 1671176 | tf_op jit(solution)/shard_map/ppermute | solution.py:306
  24.6 16.5 %collective-permute-start.2 = (bf16[128,2176]{1,0:T(8,128)(2,1)S(1)}, bf16[128,2176]{1,0:T(8,128)(2,1)S(1)}, u32[]{:S(2)}, u32[]{:S(2)}) collective-permute-start(bf16[128,2176]{1,0:T(8,128)(2,1)S(1)} %collective-permute-done.1), channel_id=1, source_target_pairs={{4,0},{5,1},{6,2},{7,3},{8,12},{9,13},{10,14},{11,15},{20,16},{21,... | collective-permute-start | bytes 1671176 | tf_op jit(solution)/shard_map/ppermute | solution.py:306
  36.3 18.3 %copy-start.5 = (bf16[128,2176]{1,0:T(8,128)(2,1)}, bf16[128,2176]{1,0:T(8,128)(2,1)S(1)}, u32[]{:S(2)}) copy-start(bf16[128,2176]{1,0:T(8,128)(2,1)S(1)} %collective-permute-done.5.refs_1_.refs_5_) | copy-start | bytes 1671172
  36.3 7.5 %collective-permute-start.7 = (bf16[512,1152]{1,0:T(8,128)(2,1)}, bf16[512,1152]{1,0:T(8,128)(2,1)}, u32[]{:S(2)}, u32[]{:S(2)}) collective-permute-start(bf16[512,1152]{1,0:T(8,128)(2,1)} %shard_map.103.refs_4_.refs_3_.refs_1_), channel_id=1, source_target_pairs={{0,1},{1,0},{2,3},{3,2},{4,5},{5,4},{6,7},{7,6},{8,9},{9,8},{10,11... | collective-permute-start | bytes 3538952 | tf_op jit(solution)/shard_map/ppermute | solution.py:306
  36.4 7.5 %collective-permute-start.8 = (bf16[512,1152]{1,0:T(8,128)(2,1)}, bf16[512,1152]{1,0:T(8,128)(2,1)}, u32[]{:S(2)}, u32[]{:S(2)}) collective-permute-start(bf16[512,1152]{1,0:T(8,128)(2,1)} %collective-permute-done.4.refs_5_.refs_4_.refs_2_), channel_id=1, source_target_pairs={{0,1},{1,0},{2,3},{3,2},{4,5},{5,4},{6,7},{7,6},{8,9},{9,8},{10,11... | collective-permute-start | bytes 3538952 | tf_op jit(solution)/shard_map/ppermute | solution.py:306
  41.1 15.5 %collective-permute-start.10 = (bf16[128,2176]{1,0:T(8,128)(2,1)S(1)}, bf16[128,2176]{1,0:T(8,128)(2,1)S(1)}, u32[]{:S(2)}, u32[]{:S(2)}) collective-permute-start(bf16[128,2176]{1,0:T(8,128)(2,1)S(1)} %broadcast_select_fusion.1.refs_2_), channel_id=1, source_target_pairs={{0,2},{1,3},{2,0},{3,1},{4,6},{5,7},{6,4},{7,5},{8,10},{9,11},{10,... | collective-permute-start | bytes 1671176 | tf_op jit(solution)/shard_map/ppermute | solution.py:306
  42.6 14.0 %collective-permute-start.9 = (bf16[128,2176]{1,0:T(8,128)(2,1)S(1)}, bf16[128,2176]{1,0:T(8,128)(2,1)S(1)}, u32[]{:S(2)}, u32[]{:S(2)}) collective-permute-start(bf16[128,2176]{1,0:T(8,128)(2,1)S(1)} %collective-permute-done.6), channel_id=1, source_target_pairs={{4,0},{5,1},{6,2},{7,3},{8,12},{9,13},{10,14},{11,15},{20,16},{21,... | collective-permute-start | bytes 1671176 | tf_op jit(solution)/shard_map/ppermute | solution.py:306
  56.7 14.9 %collective-permute-start.11 = (bf16[128,2176]{1,0:T(8,128)(2,1)S(1)}, bf16[128,2176]{1,0:T(8,128)(2,1)S(1)}, u32[]{:S(2)}, u32[]{:S(2)}) collective-permute-start(bf16[128,2176]{1,0:T(8,128)(2,1)S(1)} %broadcast_select_fusion.refs_0_.refs_4_), channel_id=1, source_target_pairs={{0,2},{1,3},{2,0},{3,1},{4,6},{5,7},{6,4},{7,5},{8,10},{9,11},{10,... | collective-permute-start | bytes 1671176 | tf_op jit(solution)/shard_map/ppermute | solution.py:306
  71.5 8.4 %collective-permute-start.13 = (bf16[512,1152]{1,0:T(8,128)(2,1)}, bf16[512,1152]{1,0:T(8,128)(2,1)S(1)}, u32[]{:S(2)}, u32[]{:S(2)}) collective-permute-start(bf16[512,1152]{1,0:T(8,128)(2,1)} %shard_map.106), channel_id=1, source_target_pairs={{0,1},{1,0},{2,3},{3,2},{4,5},{5,4},{6,7},{7,6},{8,9},{9,8},{10,11... | collective-permute-start | bytes 3538952 | tf_op jit(solution)/shard_map/ppermute | solution.py:306
  78.2 2.7 %collective-permute-start.12 = (bf16[128,3200]{1,0:T(8,128)(2,1)}, bf16[128,3200]{1,0:T(8,128)(2,1)S(1)}, u32[]{:S(2)}, u32[]{:S(2)}) collective-permute-start(bf16[128,3200]{1,0:T(8,128)(2,1)} %get-tuple-element.60), channel_id=1, source_target_pairs={{0,1},{1,0},{2,3},{3,2},{4,5},{5,4},{6,7},{7,6},{8,9},{9,8},{10,11... | collective-permute-start | bytes 2457608 | tf_op jit(solution)/shard_map/ppermute | solution.py:306
  78.8 13.9 %collective-permute-start.14 = (bf16[256,1024]{1,0:T(8,128)(2,1)S(1)}, bf16[256,1024]{1,0:T(8,128)(2,1)S(1)}, u32[]{:S(2)}, u32[]{:S(2)}) collective-permute-start(bf16[256,1024]{1,0:T(8,128)(2,1)S(1)} %copy-done.17), channel_id=1, source_target_pairs={{0,2},{1,3},{2,0},{3,1},{4,6},{5,7},{6,4},{7,5},{8,10},{9,11},{10,... | collective-permute-start | bytes 1572872 | tf_op jit(solution)/shard_map/ppermute | solution.py:306
  88.0 10.0 %copy-start.19 = (bf16[128,1024]{1,0:T(8,128)(2,1)S(1)}, bf16[128,1024]{1,0:T(8,128)(2,1)}, u32[]{:S(2)}) copy-start(bf16[128,1024]{1,0:T(8,128)(2,1)} %get-tuple-element.67) | copy-start | bytes 786436
  88.0 11.2 %copy-start.12 = (bf16[128,1024]{1,0:T(8,128)(2,1)S(1)}, bf16[128,1024]{1,0:T(8,128)(2,1)}, u32[]{:S(2)}) copy-start(bf16[128,1024]{1,0:T(8,128)(2,1)} %get-tuple-element.69) | copy-start | bytes 786436
  88.0 11.2 %copy-start.13 = (bf16[128,1024]{1,0:T(8,128)(2,1)S(1)}, bf16[128,1024]{1,0:T(8,128)(2,1)}, u32[]{:S(2)}) copy-start(bf16[128,1024]{1,0:T(8,128)(2,1)} %get-tuple-element.70) | copy-start | bytes 786436
  97.5 9.6 %copy-start.11 = (bf16[128,1024]{1,0:T(8,128)(2,1)S(1)}, bf16[128,1024]{1,0:T(8,128)(2,1)}, u32[]{:S(2)}) copy-start(bf16[128,1024]{1,0:T(8,128)(2,1)} %get-tuple-element.71) | copy-start | bytes 786436
  97.5 17.9 %collective-permute-start.15 = (bf16[512,1152]{1,0:T(8,128)(2,1)}, bf16[512,1152]{1,0:T(8,128)(2,1)S(1)}, u32[]{:S(2)}, u32[]{:S(2)}) collective-permute-start(bf16[512,1152]{1,0:T(8,128)(2,1)} %shard_map.109), channel_id=1, source_target_pairs={{0,1},{1,0},{2,3},{3,2},{4,5},{5,4},{6,7},{7,6},{8,9},{9,8},{10,11... | collective-permute-start | bytes 3538952 | tf_op jit(solution)/shard_map/ppermute | solution.py:306
  97.5 34.3 %collective-permute-start.23 = (bf16[512,1152]{1,0:T(8,128)(2,1)S(1)}, bf16[512,1152]{1,0:T(8,128)(2,1)S(1)}, u32[]{:S(2)}, u32[]{:S(2)}) collective-permute-start(bf16[512,1152]{1,0:T(8,128)(2,1)S(1)} %copy-done.15), channel_id=1, source_target_pairs={{0,16},{16,0},{1,17},{17,1},{2,18},{18,2},{3,19},{19,3},{4,20},{20... | collective-permute-start | bytes 3538952 | tf_op jit(solution)/shard_map/ppermute | solution.py:307
  98.1 8.4 %collective-permute-start.16 = (bf16[128,1024]{1,0:T(8,128)(2,1)S(1)}, bf16[128,1024]{1,0:T(8,128)(2,1)S(1)}, u32[]{:S(2)}, u32[]{:S(2)}) collective-permute-start(bf16[128,1024]{1,0:T(8,128)(2,1)S(1)} %copy-done.19), channel_id=1, source_target_pairs={{0,2},{1,3},{2,0},{3,1},{4,6},{5,7},{6,4},{7,5},{8,10},{9,11},{10,... | collective-permute-start | bytes 786440 | tf_op jit(solution)/shard_map/ppermute | solution.py:306
  99.4 8.2 %collective-permute-start.18 = (bf16[128,1024]{1,0:T(8,128)(2,1)S(1)}, bf16[128,1024]{1,0:T(8,128)(2,1)S(1)}, u32[]{:S(2)}, u32[]{:S(2)}) collective-permute-start(bf16[128,1024]{1,0:T(8,128)(2,1)S(1)} %get-tuple-element.76), channel_id=1, source_target_pairs={{0,4},{1,5},{2,6},{3,7},{4,0},{5,1},{6,2},{7,3},{8,12},{9,13},{10,... | collective-permute-start | bytes 786440 | tf_op jit(solution)/shard_map/ppermute | solution.py:306
  100.2 11.3 %collective-permute-start.20 = (bf16[128,1024]{1,0:T(8,128)(2,1)S(1)}, bf16[128,1024]{1,0:T(8,128)(2,1)S(1)}, u32[]{:S(2)}, u32[]{:S(2)}) collective-permute-start(bf16[128,1024]{1,0:T(8,128)(2,1)S(1)} %get-tuple-element.77), channel_id=1, source_target_pairs={{0,8},{1,9},{2,10},{3,11},{12,4},{13,5},{14,6},{15,7},{16,24},{17,... | collective-permute-start | bytes 786440 | tf_op jit(solution)/shard_map/ppermute | solution.py:306
  106.4 16.2 %collective-permute-start.19 = (bf16[128,1024]{1,0:T(8,128)(2,1)S(1)}, bf16[128,1024]{1,0:T(8,128)(2,1)S(1)}, u32[]{:S(2)}, u32[]{:S(2)}) collective-permute-start(bf16[128,1024]{1,0:T(8,128)(2,1)S(1)} %get-tuple-element.77), channel_id=1, source_target_pairs={{4,8},{5,9},{6,10},{7,11},{8,4},{9,5},{10,6},{11,7},{20,24},{21,25... | collective-permute-start | bytes 786440 | tf_op jit(solution)/shard_map/ppermute | solution.py:306
  107.2 23.6 %copy-start.14 = (bf16[128,1024]{1,0:T(8,128)(2,1)S(1)}, bf16[128,1024]{1,0:T(8,128)(2,1)}, u32[]{:S(2)}) copy-start(bf16[128,1024]{1,0:T(8,128)(2,1)} %get-tuple-element.64) | copy-start | bytes 786436
  107.6 15.1 %collective-permute-start.17 = (bf16[128,1024]{1,0:T(8,128)(2,1)S(1)}, bf16[128,1024]{1,0:T(8,128)(2,1)S(1)}, u32[]{:S(2)}, u32[]{:S(2)}) collective-permute-start(bf16[128,1024]{1,0:T(8,128)(2,1)S(1)} %copy-done.18), channel_id=1, source_target_pairs={{0,2},{1,3},{2,0},{3,1},{4,6},{5,7},{6,4},{7,5},{8,10},{9,11},{10,... | collective-permute-start | bytes 786440 | tf_op jit(solution)/shard_map/ppermute | solution.py:306
  111.5 11.1 %collective-permute-start.22 = (bf16[128,1024]{1,0:T(8,128)(2,1)S(1)}, bf16[128,1024]{1,0:T(8,128)(2,1)S(1)}, u32[]{:S(2)}, u32[]{:S(2)}) collective-permute-start(bf16[128,1024]{1,0:T(8,128)(2,1)S(1)} %add_convert_fusion.1), channel_id=1, source_target_pairs={{0,12},{1,13},{2,14},{3,15},{12,0},{13,1},{14,2},{15,3},{16,28},{1... | collective-permute-start | bytes 786440 | tf_op jit(solution)/shard_map/ppermute | solution.py:306
  115.4 15.3 %collective-permute-start.21 = (bf16[128,1024]{1,0:T(8,128)(2,1)S(1)}, bf16[128,1024]{1,0:T(8,128)(2,1)S(1)}, u32[]{:S(2)}, u32[]{:S(2)}) collective-permute-start(bf16[128,1024]{1,0:T(8,128)(2,1)S(1)} %add_convert_fusion.1), channel_id=1, source_target_pairs={{4,12},{5,13},{6,14},{7,15},{8,0},{9,1},{10,2},{11,3},{20,28},{21,... | collective-permute-start | bytes 786440 | tf_op jit(solution)/shard_map/ppermute | solution.py:306
  (12 other events, 39.5 us)

commit v7 on v6

--- a/solution.py
+++ b/solution.py
@@ -207,7 +207,7 @@
         out[:, span] = new.astype(BF16)
 
 
-def half_call(sides, blocks, kept, last=None, more=None, weight=0):
+def half_call(sides, blocks, kept, last=None, more=None, at=0, weight=0):
     grads, scaled = [k[0] for k in kept], [k[1] for k in kept]
     size = scaled[0].shape[1] // 2
     stacked = grads[0].shape[1]
@@ -220,7 +220,7 @@
         specs.append(whole(last))
     if more is not None:
         operands.append(more)
-        specs.append(pl.BlockSpec((size, stacked), lambda i, s: (i, 0)))
+        specs.append(pl.BlockSpec((size, stacked), lambda i, s: (at, 0)))
     count = sides.shape[0]
     return pl.pallas_call(
         functools.partial(half_kernel, len(blocks), len(kept), last is not None, more is not None),
@@ -331,8 +331,7 @@
 
     blocks = [own, b1, b2, y0, b3, y1, y2]
     kept = [kept_a, kept_b]
-    others = lambda side, first: half_call(side, [first] + blocks[1:], [k[2:] for k in kept])
-    to_core = others(other, own)
+    to_core = half_call(jnp.concatenate([other, mine]), blocks, [k[2:] for k in kept])
     y3 = after(y3, q12, to_core)
     r12 = move(after(q12, y3), SWAP_Y)
     rows = own.shape[0]
@@ -344,10 +343,10 @@
     r0 = move(after(q0, r3), SWAP_Y)
     all_blocks = blocks + [y3]
     all_kept = [k[:2] for k in kept] + [kept_d]
-    send = half_call(other, all_blocks, all_kept, last, swap(to_core), weight=1)
+    got = swap(to_core)
+    send = half_call(other, all_blocks, all_kept, last, got, weight=1)
     from_part = across(send)
-    from_core = swap(others(mine, after(own, send, r12)))
-    keep = half_call(after(mine, send), all_blocks, all_kept, last, from_core)
+    keep = half_call(after(mine, send), all_blocks, all_kept, last, got, at=1)
 
     add = lambda *terms: sum(t.astype(F32) for t in terms).astype(BF16)
     s1 = add(p1, r1)

time: 137 us -> 132 us (0.964)
  waiting for transfers between devices: 46.8 us -> 38.6 us
  starting transfers between devices: 28.3 us -> 31.6 us
  Pallas kernels: 55.7 us -> 53.3 us
    ppermute x22 -> x21, waiting for transfers between devices: 46.8 us -> 38.6 us  [dense_body(): move = lambda a, pairs: lax.ppermute(a, 'expert', pairs)]
    ppermute x22 -> x21, starting transfers between devices: 24.8 us -> 28.1 us  [dense_body(): move = lambda a, pairs: lax.ppermute(a, 'expert', pairs)]
    pallas_call x4 -> x3, Pallas kernels: 21.6 us -> 19.3 us  [half_call(): pl.pallas_call(functools.partial(half_kernel, len(blocks), len(kept), las...]
    unnamed x40 -> x36, local copies, waits for them, and re-layouts: 3.11 us -> 3.57 us
  transfers between devices with their start and end apart: 24 -> 23, of which waited for: 11 -> 8; matrix products, arithmetic and copies ran while one was open for 1% -> 2% of each run, Pallas kernels for 31% -> 34%
where the time goes in v7:
time: 132 us; the launch traced here: 131 us
  Pallas kernels  53.3 us (40%)
  waiting for transfers between devices  38.6 us (29%)
  starting transfers between devices  31.6 us (24%)
  local copies, waits for them, and re-layouts  3.57 us (3%)
  other arithmetic  2.63 us (2%)
    ppermute x21, waiting for transfers between devices, dense_body(): move = lambda a, pairs: lax.ppermute(a, 'expert', pairs)  38.6 us
    ppermute x21, starting transfers between devices, dense_body(): move = lambda a, pairs: lax.ppermute(a, 'expert', pairs)  28.1 us
    pallas_call x3, Pallas kernels, rows_call(): pl.pallas_call(functools.partial(rows_kernel, experts, count, len(groups)...  25.7 us
    pallas_call x3, Pallas kernels, half_call(): pl.pallas_call(functools.partial(half_kernel, len(blocks), len(kept), las...  19.3 us
    pallas_call x1, Pallas kernels, finish(): pl.pallas_call(finish_kernel, out_shape=[sds((size, hidden_units), F32),...  3.95 us
    unnamed x36, local copies, waits for them, and re-layouts  3.57 us
    ppermute x2, starting transfers between devices, dense_body(): across = lambda a: lax.ppermute(a, 'dp', [(0, 1), (1, 0)])  3.52 us
  transfers between devices with their start and end apart: 23, of which 8 were waited for; matrix products, arithmetic and copies ran while one was open for 2% of the time, Pallas kernels for 34%

profile of v7, /device:TPU:0, one launch (start us, length us, event | category | flops | bytes accessed | tf_op | source)
XLA Modules:
  0.0 130.7 jit_solution(16052829720393260317)
XLA Ops:
  0.6 2.0 %shard_map.102.refs_0_ = bf16[128,2176]{1,0:T(8,128)(2,1)} custom-call(bf16[128,1024]{1,0:T(8,128)(2,1)} %tokens.1, bf16[128,1024]{1,0:T(8,128)(2,1)} %d_output.1, f32[8,128]{1,0:T(8,128)} %bitcast.14, s32[8,128]{1,0:T(8,128)} %bitcast.15), custom_call_target="tpu_custom_call" | custom-call | bytes 1572864 | tf_op jit(solution)/shard_map/pallas_call | solution.py:63
  2.6 2.5 %shard_map.103.refs_4_.refs_3_.refs_1_ = bf16[512,1152]{1,0:T(8,128)(2,1)} custom-call(bf16[512,384]{1,0:T(8,128)(2,1)} %bitcast.11, bf16[512,384]{1,0:T(8,128)(2,1)} %bitcast.12, bf16[384,512]{1,0:T(8,128)(2,1)} %bitcast.13), custom_call_target="tpu_custom_call" | custom-call | bytes 4718592 | tf_op jit(solution)/shard_map/pallas_call | solution.py:82
  5.1 2.9 %collective-permute-start.4 = (bf16[512,1152]{1,0:T(8,128)(2,1)}, bf16[512,1152]{1,0:T(8,128)(2,1)}, u32[]{:S(2)}, u32[]{:S(2)}) collective-permute-start(bf16[512,1152]{1,0:T(8,128)(2,1)} %shard_map.103.refs_4_.refs_3_.refs_1_), channel_id=1, source_target_pairs={{0,16},{16,0},{1,17},{17,1},{2,18},{18,2},{3,19},{19,3},{4,20},{20... | collective-permute-start | bytes 3538952 | tf_op jit(solution)/shard_map/ppermute | solution.py:307
  8.0 1.6 %collective-permute-start = (bf16[128,2176]{1,0:T(8,128)(2,1)S(1)}, bf16[128,2176]{1,0:T(8,128)(2,1)S(1)}, u32[]{:S(2)}, u32[]{:S(2)}) collective-permute-start(bf16[128,2176]{1,0:T(8,128)(2,1)S(1)} %copy-done.2), channel_id=1, source_target_pairs={{0,4},{1,5},{2,6},{3,7},{4,0},{5,1},{6,2},{7,3},{8,12},{9,13},{10,... | collective-permute-start | bytes 1671176 | tf_op jit(solution)/shard_map/ppermute | solution.py:306
  9.6 1.5 %collective-permute-start.3 = (bf16[128,2176]{1,0:T(8,128)(2,1)S(1)}, bf16[128,2176]{1,0:T(8,128)(2,1)S(1)}, u32[]{:S(2)}, u32[]{:S(2)}) collective-permute-start(bf16[128,2176]{1,0:T(8,128)(2,1)S(1)} %copy-done.2), channel_id=1, source_target_pairs={{0,2},{1,3},{2,0},{3,1},{4,6},{5,7},{6,4},{7,5},{8,10},{9,11},{10,... | collective-permute-start | bytes 1671176 | tf_op jit(solution)/shard_map/ppermute | solution.py:306
  11.8 10.3 %collective-permute-done.refs_1_ = bf16[128,2176]{1,0:T(8,128)(2,1)S(1)} collective-permute-done((bf16[128,2176]{1,0:T(8,128)(2,1)S(1)}, bf16[128,2176]{1,0:T(8,128)(2,1)S(1)}, u32[]{:S(2)}, u32[]{:S(2)}) %collective-permute-start) | collective-permute-done | bytes 557088 | tf_op jit(solution)/shard_map/ppermute | solution.py:306
  22.1 1.3 collective-permute-done.3.refs_3_
  23.4 1.5 %collective-permute-start.5 = (bf16[128,2176]{1,0:T(8,128)(2,1)S(1)}, bf16[128,2176]{1,0:T(8,128)(2,1)S(1)}, u32[]{:S(2)}, u32[]{:S(2)}) collective-permute-start(bf16[128,2176]{1,0:T(8,128)(2,1)S(1)} %collective-permute-done.refs_1_), channel_id=1, source_target_pairs={{0,2},{1,3},{2,0},{3,1},{4,6},{5,7},{6,4},{7,5},{8,10},{9,11},{10,... | collective-permute-start | bytes 1671176 | tf_op jit(solution)/shard_map/ppermute | solution.py:306
  25.6 1.3 collective-permute-start.2
  26.9 9.5 %collective-permute-done.5.refs_1_.refs_5_ = bf16[128,2176]{1,0:T(8,128)(2,1)S(1)} collective-permute-done((bf16[128,2176]{1,0:T(8,128)(2,1)S(1)}, bf16[128,2176]{1,0:T(8,128)(2,1)S(1)}, u32[]{:S(2)}, u32[]{:S(2)}) %collective-permute-start.5) | collective-permute-done | bytes 557088 | tf_op jit(solution)/shard_map/ppermute | solution.py:306
  38.2 3.8 %collective-permute-done.2 = bf16[128,2176]{1,0:T(8,128)(2,1)S(1)} collective-permute-done((bf16[128,2176]{1,0:T(8,128)(2,1)S(1)}, bf16[128,2176]{1,0:T(8,128)(2,1)S(1)}, u32[]{:S(2)}, u32[]{:S(2)}) %collective-permute-start.2) | collective-permute-done | bytes 557088 | tf_op jit(solution)/shard_map/ppermute | solution.py:306
  42.6 1.3 collective-permute-start.9
  43.9 10.8 %shard_map.104 = (bf16[128,1024]{1,0:T(8,128)(2,1)}, bf16[128,1024]{1,0:T(8,128)(2,1)}, bf16[128,1024]{1,0:T(8,128)(2,1)}, bf16[128,1024]{1,0:T(8,128)(2,1)}, bf...) custom-call(s32[2]{0:T(128)} %pad_add_fusion.scal, ...), custom_call_target="tpu_custom_call" | custom-call | flops 14495514624 | bytes 1048576 | tf_op jit(solution)/shard_map/pallas_call | solution.py:170
  54.7 2.4 %collective-permute-done.9 = bf16[128,2176]{1,0:T(8,128)(2,1)S(1)} collective-permute-done((bf16[128,2176]{1,0:T(8,128)(2,1)S(1)}, bf16[128,2176]{1,0:T(8,128)(2,1)S(1)}, u32[]{:S(2)}, u32[]{:S(2)}) %collective-permute-start.9) | collective-permute-done | bytes 557088 | tf_op jit(solution)/shard_map/ppermute | solution.py:306
  57.2 1.6 %collective-permute-start.11 = (bf16[128,2176]{1,0:T(8,128)(2,1)S(1)}, bf16[128,2176]{1,0:T(8,128)(2,1)S(1)}, u32[]{:S(2)}, u32[]{:S(2)}) collective-permute-start(bf16[128,2176]{1,0:T(8,128)(2,1)S(1)} %broadcast_select_fusion.refs_0_.refs_4_), channel_id=1, source_target_pairs={{0,2},{1,3},{2,0},{3,1},{4,6},{5,7},{6,4},{7,5},{8,10},{9,11},{10,... | collective-permute-start | bytes 1671176 | tf_op jit(solution)/shard_map/ppermute | solution.py:306
  58.8 9.1 %shard_map.105 = (bf16[128,1024]{1,0:T(8,128)(2,1)}, bf16[256,1024]{1,0:T(8,128)(2,1)}, bf16[384,1152]{1,0:T(8,128)(2,1)}, bf16[384,1024]{1,0:T(8,128)(2,1)}, bf...) custom-call(s32[2]{0:T(128)} %pad_add_fusion.scal, bf16[128,2176]{1,0:T(8,128)(2,1)} %copy-done.1, ...), custom_call_target="tpu_custom_call" | custom-call | flops 10871635968 | bytes 1048576 | tf_op jit(solution)/shard_map/pallas_call | solution.py:170
  67.9 7.4 %shard_map.106 = bf16[1024,1152]{1,0:T(8,128)(2,1)} custom-call(s32[2]{0:T(128)} %pad_add_fusion.1.sides, bf16[128,2176]{1,0:T(8,128)(2,1)} %shard_map.102.refs_0_, bf16[128,2176]{1,0:T(8,128)(2,1)} %copy-done.4, bf16[128,2176]{1,0:T(8,128)(2,1)} %copy-done, bf16[128,2176]{1,0:T(8,128)(2,1)} %copy-done.5, bf16[128,2176]{1,0:T(8,128)(2,1)} %copy-done.1, ...), custom_call_target="tpu_custom_call" | custom-call | flops 1024 | bytes 1024 | tf_op jit(solution)/shard_map/pallas_call | solution.py:225
  76.1 5.9 %shard_map.107 = (bf16[128,1024]{1,0:T(8,128)(2,1)}, bf16[128,1152]{1,0:T(8,128)(2,1)}, bf16[128,1024]{1,0:T(8,128)(2,1)}, bf16[128,3200]{1,0:T(8,128)(2,1)}) custom-call(s32[2]{0:T(128)} %pad_add_fusion.scal, bf16[128,2176]{1,0:T(8,128)(2,1)} %copy-done.10, bf16[512,1152]{1,0:T(8,128)(2,1)} %shard_map.103.refs_4_.refs_3_.refs_1_, ...), custom_call_target="tpu_custom_call" | custom-call | flops 36238786560 | bytes 1048576 | tf_op jit(solution)/shard_map/pallas_call | solution.py:170
  82.6 0.9 collective-permute-start.14
  83.5 1.3 collective-permute-done.12.refs_14_
  86.4 5.9 %shard_map.108 = bf16[512,1152]{1,0:T(8,128)(2,1)} custom-call(s32[1]{0:T(128)} %bitcast.7.sides, bf16[128,2176]{1,0:T(8,128)(2,1)} %shard_map.102.refs_0_, bf16[128,2176]{1,0:T(8,128)(2,1)} %copy-done.4, bf16[128,2176]{1,0:T(8,128)(2,1)} %copy-done, bf16[128,2176]{1,0:T(8,128)(2,1)} %copy-done.5, bf16[128,2176]{1,0:T(8,128)(2,1)} %copy-done.1, ...), custom_call_target="tpu_custom_call" | custom-call | flops 4831839232 | bytes 1024 | tf_op jit(solution)/shard_map/pallas_call | solution.py:225
  92.9 3.5 %collective-permute-done.14 = bf16[256,1024]{1,0:T(8,128)(2,1)S(1)} collective-permute-done((bf16[256,1024]{1,0:T(8,128)(2,1)S(1)}, bf16[256,1024]{1,0:T(8,128)(2,1)S(1)}, u32[]{:S(2)}, u32[]{:S(2)}) %collective-permute-start.14) | collective-permute-done | bytes 524320 | tf_op jit(solution)/shard_map/ppermute | solution.py:306
  96.5 0.9 collective-permute-start.15
  98.6 6.3 %collective-permute-start.19 = (bf16[128,1024]{1,0:T(8,128)(2,1)S(1)}, bf16[128,1024]{1,0:T(8,128)(2,1)S(1)}, u32[]{:S(2)}, u32[]{:S(2)}) collective-permute-start(bf16[128,1024]{1,0:T(8,128)(2,1)S(1)} %get-tuple-element.75), channel_id=1, source_target_pairs={{0,8},{1,9},{2,10},{3,11},{12,4},{13,5},{14,6},{15,7},{16,24},{17,... | collective-permute-start | bytes 786440 | tf_op jit(solution)/shard_map/ppermute | solution.py:306
  105.0 1.2 collective-permute-start.16
  106.3 1.4 %collective-permute-start.20 = (bf16[128,1024]{1,0:T(8,128)(2,1)S(1)}, bf16[128,1024]{1,0:T(8,128)(2,1)S(1)}, u32[]{:S(2)}, u32[]{:S(2)}) collective-permute-start(bf16[128,1024]{1,0:T(8,128)(2,1)S(1)} %add_convert_fusion.1), channel_id=1, source_target_pairs={{4,12},{5,13},{6,14},{7,15},{8,0},{9,1},{10,2},{11,3},{20,28},{21,... | collective-permute-start | bytes 786440 | tf_op jit(solution)/shard_map/ppermute | solution.py:306
  107.7 4.5 %collective-permute-start.21 = (bf16[128,1024]{1,0:T(8,128)(2,1)S(1)}, bf16[128,1024]{1,0:T(8,128)(2,1)S(1)}, u32[]{:S(2)}, u32[]{:S(2)}) collective-permute-start(bf16[128,1024]{1,0:T(8,128)(2,1)S(1)} %add_convert_fusion.1), channel_id=1, source_target_pairs={{0,12},{1,13},{2,14},{3,15},{12,0},{13,1},{14,2},{15,3},{16,28},{1... | collective-permute-start | bytes 786440 | tf_op jit(solution)/shard_map/ppermute | solution.py:306
  112.3 5.9 %shard_map.109.keep = bf16[512,1152]{1,0:T(8,128)(2,1)} custom-call(s32[1]{0:T(128)} %bitcast.sides, bf16[128,2176]{1,0:T(8,128)(2,1)} %shard_map.102.refs_0_, bf16[128,2176]{1,0:T(8,128)(2,1)} %copy-done.4, bf16[128,2176]{1,0:T(8,128)(2,1)} %copy-done, bf16[128,2176]{1,0:T(8,128)(2,1)} %copy-done.5, bf16[128,2176]{1,0:T(8,128)(2,1)} %copy-done.1, ...), custom_call_target="tpu_custom_call" | custom-call | flops 1024 | bytes 1024 | tf_op jit(solution)/shard_map/pallas_call | solution.py:225
  118.2 6.5 %collective-permute-done.20 = bf16[128,1024]{1,0:T(8,128)(2,1)S(1)} collective-permute-done((bf16[128,1024]{1,0:T(8,128)(2,1)S(1)}, bf16[128,1024]{1,0:T(8,128)(2,1)S(1)}, u32[]{:S(2)}, u32[]{:S(2)}) %collective-permute-start.20) | collective-permute-done | bytes 262176 | tf_op jit(solution)/shard_map/ppermute | solution.py:306
  124.7 1.0 add_convert_fusion
  125.8 1.0 copy-done.8
  126.8 3.9 %shard_map.110 = (f32[512,384]{1,0:T(8,128)}, f32[512,384]{1,0:T(8,128)}, f32[384,512]{1,0:T(8,128)}) custom-call(bf16[512,1152]{1,0:T(8,128)(2,1)} %shard_map.109.keep, bf16[512,1152]{1,0:T(8,128)(2,1)} %copy-done.8), custom_call_target="tpu_custom_call" | custom-call | flops 1024 | bytes 1024 | tf_op jit(solution)/shard_map/pallas_call | solution.py:253
  (66 shorter events, 8.8 us)
Async XLA Ops:
  5.1 31.3 %collective-permute-start.4 = (bf16[512,1152]{1,0:T(8,128)(2,1)}, bf16[512,1152]{1,0:T(8,128)(2,1)}, u32[]{:S(2)}, u32[]{:S(2)}) collective-permute-start(bf16[512,1152]{1,0:T(8,128)(2,1)} %shard_map.103.refs_4_.refs_3_.refs_1_), channel_id=1, source_target_pairs={{0,16},{16,0},{1,17},{17,1},{2,18},{18,2},{3,19},{19,3},{4,20},{20... | collective-permute-start | bytes 3538952 | tf_op jit(solution)/shard_map/ppermute | solution.py:307
  8.0 14.1 %collective-permute-start = (bf16[128,2176]{1,0:T(8,128)(2,1)S(1)}, bf16[128,2176]{1,0:T(8,128)(2,1)S(1)}, u32[]{:S(2)}, u32[]{:S(2)}) collective-permute-start(bf16[128,2176]{1,0:T(8,128)(2,1)S(1)} %copy-done.2), channel_id=1, source_target_pairs={{0,4},{1,5},{2,6},{3,7},{4,0},{5,1},{6,2},{7,3},{8,12},{9,13},{10,... | collective-permute-start | bytes 1671176 | tf_op jit(solution)/shard_map/ppermute | solution.py:306
  9.6 13.8 %collective-permute-start.3 = (bf16[128,2176]{1,0:T(8,128)(2,1)S(1)}, bf16[128,2176]{1,0:T(8,128)(2,1)S(1)}, u32[]{:S(2)}, u32[]{:S(2)}) collective-permute-start(bf16[128,2176]{1,0:T(8,128)(2,1)S(1)} %copy-done.2), channel_id=1, source_target_pairs={{0,2},{1,3},{2,0},{3,1},{4,6},{5,7},{6,4},{7,5},{8,10},{9,11},{10,... | collective-permute-start | bytes 1671176 | tf_op jit(solution)/shard_map/ppermute | solution.py:306
  11.1 14.5 %collective-permute-start.1 = (bf16[128,2176]{1,0:T(8,128)(2,1)S(1)}, bf16[128,2176]{1,0:T(8,128)(2,1)S(1)}, u32[]{:S(2)}, u32[]{:S(2)}) collective-permute-start(bf16[128,2176]{1,0:T(8,128)(2,1)S(1)} %copy-done.2), channel_id=1, source_target_pairs={{4,8},{5,9},{6,10},{7,11},{8,4},{9,5},{10,6},{11,7},{20,24},{21,25... | collective-permute-start | bytes 1671176 | tf_op jit(solution)/shard_map/ppermute | solution.py:306
  22.1 21.8 %copy-start.4 = (bf16[128,2176]{1,0:T(8,128)(2,1)}, bf16[128,2176]{1,0:T(8,128)(2,1)S(1)}, u32[]{:S(2)}) copy-start(bf16[128,2176]{1,0:T(8,128)(2,1)S(1)} %collective-permute-done.refs_1_) | copy-start | bytes 1671172
  23.4 20.5 %copy-start.5 = (bf16[128,2176]{1,0:T(8,128)(2,1)}, bf16[128,2176]{1,0:T(8,128)(2,1)S(1)}, u32[]{:S(2)}) copy-start(bf16[128,2176]{1,0:T(8,128)(2,1)S(1)} %collective-permute-done.3.refs_3_) | copy-start | bytes 1671172
  23.4 13.0 %collective-permute-start.5 = (bf16[128,2176]{1,0:T(8,128)(2,1)S(1)}, bf16[128,2176]{1,0:T(8,128)(2,1)S(1)}, u32[]{:S(2)}, u32[]{:S(2)}) collective-permute-start(bf16[128,2176]{1,0:T(8,128)(2,1)S(1)} %collective-permute-done.refs_1_), channel_id=1, source_target_pairs={{0,2},{1,3},{2,0},{3,1},{4,6},{5,7},{6,4},{7,5},{8,10},{9,11},{10,... | collective-permute-start | bytes 1671176 | tf_op jit(solution)/shard_map/ppermute | solution.py:306
  24.9 11.5 %collective-permute-start.6 = (bf16[128,2176]{1,0:T(8,128)(2,1)S(1)}, bf16[128,2176]{1,0:T(8,128)(2,1)S(1)}, u32[]{:S(2)}, u32[]{:S(2)}) collective-permute-start(bf16[128,2176]{1,0:T(8,128)(2,1)S(1)} %collective-permute-done.refs_1_), channel_id=1, source_target_pairs={{4,8},{5,9},{6,10},{7,11},{8,4},{9,5},{10,6},{11,7},{20,24},{21,25... | collective-permute-start | bytes 1671176 | tf_op jit(solution)/shard_map/ppermute | solution.py:306
  25.6 16.3 %collective-permute-start.2 = (bf16[128,2176]{1,0:T(8,128)(2,1)S(1)}, bf16[128,2176]{1,0:T(8,128)(2,1)S(1)}, u32[]{:S(2)}, u32[]{:S(2)}) collective-permute-start(bf16[128,2176]{1,0:T(8,128)(2,1)S(1)} %collective-permute-done.1), channel_id=1, source_target_pairs={{4,0},{5,1},{6,2},{7,3},{8,12},{9,13},{10,14},{11,15},{20,16},{21,... | collective-permute-start | bytes 1671176 | tf_op jit(solution)/shard_map/ppermute | solution.py:306
  36.4 18.3 %copy-start.6 = (bf16[128,2176]{1,0:T(8,128)(2,1)}, bf16[128,2176]{1,0:T(8,128)(2,1)S(1)}, u32[]{:S(2)}) copy-start(bf16[128,2176]{1,0:T(8,128)(2,1)S(1)} %collective-permute-done.5.refs_1_.refs_5_) | copy-start | bytes 1671172
  36.4 7.5 %collective-permute-start.7 = (bf16[512,1152]{1,0:T(8,128)(2,1)}, bf16[512,1152]{1,0:T(8,128)(2,1)}, u32[]{:S(2)}, u32[]{:S(2)}) collective-permute-start(bf16[512,1152]{1,0:T(8,128)(2,1)} %shard_map.103.refs_4_.refs_3_.refs_1_), channel_id=1, source_target_pairs={{0,1},{1,0},{2,3},{3,2},{4,5},{5,4},{6,7},{7,6},{8,9},{9,8},{10,11... | collective-permute-start | bytes 3538952 | tf_op jit(solution)/shard_map/ppermute | solution.py:306
  36.4 7.5 %collective-permute-start.8 = (bf16[512,1152]{1,0:T(8,128)(2,1)}, bf16[512,1152]{1,0:T(8,128)(2,1)}, u32[]{:S(2)}, u32[]{:S(2)}) collective-permute-start(bf16[512,1152]{1,0:T(8,128)(2,1)} %collective-permute-done.4.refs_5_.refs_4_.refs_2_), channel_id=1, source_target_pairs={{0,1},{1,0},{2,3},{3,2},{4,5},{5,4},{6,7},{7,6},{8,9},{9,8},{10,11... | collective-permute-start | bytes 3538952 | tf_op jit(solution)/shard_map/ppermute | solution.py:306
  42.0 15.2 %collective-permute-start.10 = (bf16[128,2176]{1,0:T(8,128)(2,1)S(1)}, bf16[128,2176]{1,0:T(8,128)(2,1)S(1)}, u32[]{:S(2)}, u32[]{:S(2)}) collective-permute-start(bf16[128,2176]{1,0:T(8,128)(2,1)S(1)} %broadcast_select_fusion.1.refs_2_), channel_id=1, source_target_pairs={{0,2},{1,3},{2,0},{3,1},{4,6},{5,7},{6,4},{7,5},{8,10},{9,11},{10,... | collective-permute-start | bytes 1671176 | tf_op jit(solution)/shard_map/ppermute | solution.py:306
  42.6 14.5 %collective-permute-start.9 = (bf16[128,2176]{1,0:T(8,128)(2,1)S(1)}, bf16[128,2176]{1,0:T(8,128)(2,1)S(1)}, u32[]{:S(2)}, u32[]{:S(2)}) collective-permute-start(bf16[128,2176]{1,0:T(8,128)(2,1)S(1)} %collective-permute-done.6), channel_id=1, source_target_pairs={{4,0},{5,1},{6,2},{7,3},{8,12},{9,13},{10,14},{11,15},{20,16},{21,... | collective-permute-start | bytes 1671176 | tf_op jit(solution)/shard_map/ppermute | solution.py:306
  57.2 18.1 %collective-permute-start.11 = (bf16[128,2176]{1,0:T(8,128)(2,1)S(1)}, bf16[128,2176]{1,0:T(8,128)(2,1)S(1)}, u32[]{:S(2)}, u32[]{:S(2)}) collective-permute-start(bf16[128,2176]{1,0:T(8,128)(2,1)S(1)} %broadcast_select_fusion.refs_0_.refs_4_), channel_id=1, source_target_pairs={{0,2},{1,3},{2,0},{3,1},{4,6},{5,7},{6,4},{7,5},{8,10},{9,11},{10,... | collective-permute-start | bytes 1671176 | tf_op jit(solution)/shard_map/ppermute | solution.py:306
  75.3 9.5 %collective-permute-start.13 = (bf16[1024,1152]{1,0:T(8,128)(2,1)}, bf16[1024,1152]{1,0:T(8,128)(2,1)S(1)}, u32[]{:S(2)}, u32[]{:S(2)}) collective-permute-start(bf16[1024,1152]{1,0:T(8,128)(2,1)} %shard_map.106), channel_id=1, source_target_pairs={{0,1},{1,0},{2,3},{3,2},{4,5},{5,4},{6,7},{7,6},{8,9},{9,8},{10,11... | collective-permute-start | bytes 7077896 | tf_op jit(solution)/shard_map/ppermute | solution.py:306
  82.0 2.7 %collective-permute-start.12 = (bf16[128,3200]{1,0:T(8,128)(2,1)}, bf16[128,3200]{1,0:T(8,128)(2,1)S(1)}, u32[]{:S(2)}, u32[]{:S(2)}) collective-permute-start(bf16[128,3200]{1,0:T(8,128)(2,1)} %get-tuple-element.59), channel_id=1, source_target_pairs={{0,1},{1,0},{2,3},{3,2},{4,5},{5,4},{6,7},{7,6},{8,9},{9,8},{10,11... | collective-permute-start | bytes 2457608 | tf_op jit(solution)/shard_map/ppermute | solution.py:306
  82.6 13.9 %collective-permute-start.14 = (bf16[256,1024]{1,0:T(8,128)(2,1)S(1)}, bf16[256,1024]{1,0:T(8,128)(2,1)S(1)}, u32[]{:S(2)}, u32[]{:S(2)}) collective-permute-start(bf16[256,1024]{1,0:T(8,128)(2,1)S(1)} %copy-done.15), channel_id=1, source_target_pairs={{0,2},{1,3},{2,0},{3,1},{4,6},{5,7},{6,4},{7,5},{8,10},{9,11},{10,... | collective-permute-start | bytes 1572872 | tf_op jit(solution)/shard_map/ppermute | solution.py:306
  86.4 10.1 %copy-start.17 = (bf16[128,1024]{1,0:T(8,128)(2,1)S(1)}, bf16[128,1024]{1,0:T(8,128)(2,1)}, u32[]{:S(2)}) copy-start(bf16[128,1024]{1,0:T(8,128)(2,1)} %get-tuple-element.65) | copy-start | bytes 786436
  86.4 11.0 %copy-start.12 = (bf16[128,1024]{1,0:T(8,128)(2,1)S(1)}, bf16[128,1024]{1,0:T(8,128)(2,1)}, u32[]{:S(2)}) copy-start(bf16[128,1024]{1,0:T(8,128)(2,1)} %get-tuple-element.67) | copy-start | bytes 786436
  86.4 11.0 %copy-start.13 = (bf16[128,1024]{1,0:T(8,128)(2,1)S(1)}, bf16[128,1024]{1,0:T(8,128)(2,1)}, u32[]{:S(2)}) copy-start(bf16[128,1024]{1,0:T(8,128)(2,1)} %get-tuple-element.68) | copy-start | bytes 786436
  92.3 12.6 %copy-start.16 = (bf16[128,1024]{1,0:T(8,128)(2,1)S(1)}, bf16[128,1024]{1,0:T(8,128)(2,1)}, u32[]{:S(2)}) copy-start(bf16[128,1024]{1,0:T(8,128)(2,1)} %get-tuple-element.66) | copy-start | bytes 786436
  92.4 13.8 %copy-start.11 = (bf16[128,1024]{1,0:T(8,128)(2,1)S(1)}, bf16[128,1024]{1,0:T(8,128)(2,1)}, u32[]{:S(2)}) copy-start(bf16[128,1024]{1,0:T(8,128)(2,1)} %get-tuple-element.69) | copy-start | bytes 786436
  92.4 33.4 %collective-permute-start.22 = (bf16[512,1152]{1,0:T(8,128)(2,1)}, bf16[512,1152]{1,0:T(8,128)(2,1)S(1)}, u32[]{:S(2)}, u32[]{:S(2)}) collective-permute-start(bf16[512,1152]{1,0:T(8,128)(2,1)} %shard_map.108), channel_id=1, source_target_pairs={{0,16},{16,0},{1,17},{17,1},{2,18},{18,2},{3,19},{19,3},{4,20},{20... | collective-permute-start | bytes 3538952 | tf_op jit(solution)/shard_map/ppermute | solution.py:307
  96.5 8.5 %collective-permute-start.15 = (bf16[128,1024]{1,0:T(8,128)(2,1)S(1)}, bf16[128,1024]{1,0:T(8,128)(2,1)S(1)}, u32[]{:S(2)}, u32[]{:S(2)}) collective-permute-start(bf16[128,1024]{1,0:T(8,128)(2,1)S(1)} %copy-done.17), channel_id=1, source_target_pairs={{0,2},{1,3},{2,0},{3,1},{4,6},{5,7},{6,4},{7,5},{8,10},{9,11},{10,... | collective-permute-start | bytes 786440 | tf_op jit(solution)/shard_map/ppermute | solution.py:306
  97.6 8.7 %collective-permute-start.17 = (bf16[128,1024]{1,0:T(8,128)(2,1)S(1)}, bf16[128,1024]{1,0:T(8,128)(2,1)S(1)}, u32[]{:S(2)}, u32[]{:S(2)}) collective-permute-start(bf16[128,1024]{1,0:T(8,128)(2,1)S(1)} %get-tuple-element.74), channel_id=1, source_target_pairs={{0,4},{1,5},{2,6},{3,7},{4,0},{5,1},{6,2},{7,3},{8,12},{9,13},{10,... | collective-permute-start | bytes 786440 | tf_op jit(solution)/shard_map/ppermute | solution.py:306
  97.9 9.8 %collective-permute-start.18 = (bf16[128,1024]{1,0:T(8,128)(2,1)S(1)}, bf16[128,1024]{1,0:T(8,128)(2,1)S(1)}, u32[]{:S(2)}, u32[]{:S(2)}) collective-permute-start(bf16[128,1024]{1,0:T(8,128)(2,1)S(1)} %get-tuple-element.75), channel_id=1, source_target_pairs={{4,8},{5,9},{6,10},{7,11},{8,4},{9,5},{10,6},{11,7},{20,24},{21,25... | collective-permute-start | bytes 786440 | tf_op jit(solution)/shard_map/ppermute | solution.py:306
  98.6 19.6 %collective-permute-start.19 = (bf16[128,1024]{1,0:T(8,128)(2,1)S(1)}, bf16[128,1024]{1,0:T(8,128)(2,1)S(1)}, u32[]{:S(2)}, u32[]{:S(2)}) collective-permute-start(bf16[128,1024]{1,0:T(8,128)(2,1)S(1)} %get-tuple-element.75), channel_id=1, source_target_pairs={{0,8},{1,9},{2,10},{3,11},{12,4},{13,5},{14,6},{15,7},{16,24},{17,... | collective-permute-start | bytes 786440 | tf_op jit(solution)/shard_map/ppermute | solution.py:306
  105.0 13.2 %collective-permute-start.16 = (bf16[128,1024]{1,0:T(8,128)(2,1)S(1)}, bf16[128,1024]{1,0:T(8,128)(2,1)S(1)}, u32[]{:S(2)}, u32[]{:S(2)}) collective-permute-start(bf16[128,1024]{1,0:T(8,128)(2,1)S(1)} %copy-done.16), channel_id=1, source_target_pairs={{0,2},{1,3},{2,0},{3,1},{4,6},{5,7},{6,4},{7,5},{8,10},{9,11},{10,... | collective-permute-start | bytes 786440 | tf_op jit(solution)/shard_map/ppermute | solution.py:306
  106.3 18.5 %copy-start.14 = (bf16[128,1024]{1,0:T(8,128)(2,1)S(1)}, bf16[128,1024]{1,0:T(8,128)(2,1)}, u32[]{:S(2)}) copy-start(bf16[128,1024]{1,0:T(8,128)(2,1)} %get-tuple-element.61) | copy-start | bytes 786436
  106.3 18.5 %collective-permute-start.20 = (bf16[128,1024]{1,0:T(8,128)(2,1)S(1)}, bf16[128,1024]{1,0:T(8,128)(2,1)S(1)}, u32[]{:S(2)}, u32[]{:S(2)}) collective-permute-start(bf16[128,1024]{1,0:T(8,128)(2,1)S(1)} %add_convert_fusion.1), channel_id=1, source_target_pairs={{4,12},{5,13},{6,14},{7,15},{8,0},{9,1},{10,2},{11,3},{20,28},{21,... | collective-permute-start | bytes 786440 | tf_op jit(solution)/shard_map/ppermute | solution.py:306
  107.7 17.0 %collective-permute-start.21 = (bf16[128,1024]{1,0:T(8,128)(2,1)S(1)}, bf16[128,1024]{1,0:T(8,128)(2,1)S(1)}, u32[]{:S(2)}, u32[]{:S(2)}) collective-permute-start(bf16[128,1024]{1,0:T(8,128)(2,1)S(1)} %add_convert_fusion.1), channel_id=1, source_target_pairs={{0,12},{1,13},{2,14},{3,15},{12,0},{13,1},{14,2},{15,3},{16,28},{1... | collective-permute-start | bytes 786440 | tf_op jit(solution)/shard_map/ppermute | solution.py:306
  (9 other events, 21.4 us)

commit v8 on v7

--- a/solution.py
+++ b/solution.py
@@ -84,36 +84,46 @@
         out_shape=jax.ShapeDtypeStruct((size, 3 * hidden_units), BF16),
         in_specs=[vmem()] * 3,
         out_specs=vmem(),
-        cost_estimate=cost(0, 6 * size * hidden_units * 4),
+        cost_estimate=cost(0, 6 * size * hidden_units * 40),
         compiler_params=params(),
     )(gate, up, down)
 
 
-def rows_kernel(experts, count, merged, joined, scal, *refs):
+def rows_kernel(experts, count, sizes, joined, scal, *refs):
     refs = list(refs)
     blocks = [refs.pop(0) for _ in range(count)]
-    sets = 4
-    raw = [refs.pop(0) for _ in range(sets)]
-    out_rows = [refs.pop(0) for _ in range(merged)]
+    raw = [refs.pop(0) for _ in range(4)]
+    out_rows = [refs.pop(0) for _ in sizes]
     kept = [refs.pop(0) for _ in range(3 if joined else 4)]
-    held, total, sems = refs
+    block, held, grads, scaled, total, d_rows, in_sems, out_sems = refs
     part, expert = scal[0], scal[1]
-    size = raw[0].shape[0]
-    hidden_units = raw[0].shape[1] // 3
+    size, stacked = raw[0].shape
+    hidden_units = stacked // 3
     both = 2 * hidden_units
     width = 2 * size
     rows = blocks[0].shape[0]
-    copies = [pltpu.make_async_copy(raw[i], held.at[i], sems.at[i]) for i in range(sets)]
-    for c in copies:
+    arrivals = [
+        pltpu.make_async_copy(b, block.at[pl.ds(i * rows, rows), :], in_sems.at[i]) for i, b in enumerate(blocks)
+    ]
+    weights = [pltpu.make_async_copy(raw[i], held.at[i], in_sems.at[count + i]) for i in range(4)]
+    for c in arrivals + weights:
         c.start()
+    leaving = []
+
+    def leave(source, target):
+        copy = pltpu.make_async_copy(source, target, out_sems.at[len(leaving)])
+        copy.start()
+        leaving.append(copy)
+
+    for c in arrivals:
+        c.wait()
+    if joined:
+        leave(block.at[:, pl.ds(0, width)], kept[2].at[:, pl.ds(stacked + width, width)])
     sides = [pl.multiple_of(part * size, size), pl.multiple_of((1 - part) * size, size)]
-    parts = jnp.concatenate([b[:, 2 * width :] for b in blocks], axis=0).astype(F32)
+    parts = block[:, 2 * width :].astype(F32)
     lane = lax.broadcasted_iota(jnp.int32, parts.shape, 1)
-    toks = [jnp.concatenate([b[:, pl.ds(at, size)] for b in blocks], axis=0) for at in sides]
-    for which in range(sets // 2):
-        grads_out = kept[2 * which]
-        scaled_out, scaled_at = (grads_out, 3 * hidden_units) if joined and which == 1 else (kept[2 * which + 1], 0)
-        for c in copies[2 * which : 2 * which + 2]:
+    for which in range(2):
+        for c in weights[2 * which : 2 * which + 2]:
             c.wait()
         wanted = expert if which == 0 else expert + 1 - 2 * lax.rem(expert, 2)
         mine = (lax.rem(lane, experts) == wanted) & (lane < 3 * experts)
@@ -122,115 +132,171 @@
         d_hidden = None
         for side in range(2):
             at = sides[side]
-            grad_at = pl.multiple_of(width + at, size)
-            grad = jnp.concatenate([b[:, pl.ds(grad_at, size)] for b in blocks], axis=0)
-            scaled = (weight * grad.astype(F32)).astype(BF16)
-            scaled_out[:, pl.ds(pl.multiple_of(scaled_at + at, LANES), size)] = scaled
-            if joined and which == 1:
-                grads_out[:, pl.ds(pl.multiple_of(3 * hidden_units + width + at, LANES), size)] = toks[side]
-            p = dot(toks[side], held[2 * which + side, :, :both], ((1,), (0,)))
-            h = dot(scaled, held[2 * which + side, :, both:], ((1,), (0,)))
+            grad = block[:, pl.ds(pl.multiple_of(width + at, size), size)]
+            scaled_half = (weight * grad.astype(F32)).astype(BF16)
+            scaled[which, :, pl.ds(at, size)] = scaled_half
+            p = dot(block[:, pl.ds(at, size)], held[2 * which + side, :, :both], ((1,), (0,)))
+            h = dot(scaled_half, held[2 * which + side, :, both:], ((1,), (0,)))
             preact = p if side == 0 else preact + p
             d_hidden = h if side == 0 else d_hidden + h
+        if joined and which == 1:
+            leave(scaled.at[1], kept[2].at[:, pl.ds(stacked, width)])
+        else:
+            leave(scaled.at[which], kept[2 * which + 1])
         gate_pre = preact[:, :hidden_units]
         up_pre = preact[:, hidden_units:]
         sig = jax.nn.sigmoid(gate_pre)
         silu = gate_pre * sig
         d_gate = (d_hidden * up_pre * sig * (1.0 + gate_pre * (1.0 - sig))).astype(BF16)
         d_up = (d_hidden * silu).astype(BF16)
-        grads_out[:, :hidden_units] = d_gate
-        grads_out[:, hidden_units:both] = d_up
-        grads_out[:, both : both + hidden_units] = (silu * up_pre).astype(BF16)
+        grads[which, :, :hidden_units] = d_gate
+        grads[which, :, hidden_units:both] = d_up
+        grads[which, :, both:] = (silu * up_pre).astype(BF16)
+        if joined and which == 1:
+            leave(grads.at[1], kept[2].at[:, pl.ds(0, stacked)])
+        else:
+            leave(grads.at[which], kept[2 * which])
         d_preact = jnp.concatenate([d_gate, d_up], axis=1)
         for side in range(2):
             at = sides[side]
-            d_rows = dot(d_preact, held[2 * which + side, :, :both], ((1,), (1,)))
-            if which > 0:
-                d_rows = d_rows + total[:, pl.ds(at, size)]
-            if which + 1 < sets // 2:
-                total[:, pl.ds(at, size)] = d_rows
+            new = dot(d_preact, held[2 * which + side, :, :both], ((1,), (1,)))
+            if which == 0:
+                total[:, pl.ds(at, size)] = new
             else:
-                d_rows = d_rows.astype(BF16)
-                row = 0
-                for out in out_rows:
-                    out[:, pl.ds(at, size)] = d_rows[row : row + out.shape[0]]
-                    row += out.shape[0]
+                d_rows[:, pl.ds(at, size)] = (new + total[:, pl.ds(at, size)]).astype(BF16)
+    row = 0
+    for out, n in zip(out_rows, sizes):
+        leave(d_rows.at[pl.ds(row, n), :], out)
+        row += n
+    for c in leaving:
+        c.wait()
 
 
 def rows_call(experts, scal, groups, weights, joined=False):
     blocks = [b for group in groups for b in group]
-    count, sets = len(blocks), len(weights)
+    count = len(blocks)
     rows = blocks[0].shape[0]
     size, stacked = weights[0].shape
     total = count * rows
+    sizes = [len(group) * rows for group in groups]
     sds = jax.ShapeDtypeStruct
-    out = [sds((len(group) * rows, 2 * size), BF16) for group in groups]
+    out = [sds((n, 2 * size), BF16) for n in sizes]
     out += [sds((total, stacked), BF16), sds((total, 2 * size), BF16)]
     out += [sds((total, stacked + 4 * size), BF16)] if joined else out[-2:]
     return pl.pallas_call(
-        functools.partial(rows_kernel, experts, count, len(groups), joined),
+        functools.partial(rows_kernel, experts, count, sizes, joined),
         out_shape=out,
-        in_specs=[smem()] + [vmem()] * count + [hbm()] * sets,
-        out_specs=[vmem()] * len(out),
+        in_specs=[smem()] + [hbm()] * (count + 4),
+        out_specs=[hbm()] * len(out),
         scratch_shapes=[
-            pltpu.VMEM((sets, size, stacked), BF16),
+            pltpu.VMEM((total, blocks[0].shape[1]), BF16),
+            pltpu.VMEM((4, size, stacked), BF16),
+            pltpu.VMEM((2, total, stacked), BF16),
+            pltpu.VMEM((2, total, 2 * size), BF16),
             pltpu.VMEM((total, 2 * size), F32),
-            pltpu.SemaphoreType.DMA((sets,)),
+            pltpu.VMEM((total, 2 * size), BF16),
+            pltpu.SemaphoreType.DMA((count + 4,)),
+            pltpu.SemaphoreType.DMA((len(groups) + 5,)),
         ],
-        cost_estimate=cost(24 * total * size * stacked * sets // 2 * (10 if joined else 1), 1 << 20),
+        cost_estimate=cost(24 * total * size * stacked * 2 * (10 if joined else 1), 1 << 20),
         compiler_params=params(),
     )(scal, *blocks, *weights)
 
 
-def half_kernel(count, groups, joined, adds, sides, *refs):
+def half_kernel(count, groups, joined, adds, at, sides, *refs):
     refs = list(refs)
-    side = sides[pl.program_id(0)]
-    toks = [refs.pop(0) for _ in range(count)]
+    blocks = [refs.pop(0) for _ in range(count)]
     scaled = [refs.pop(0) for _ in range(groups)]
-    made = [refs.pop(0) for _ in range(groups)]
+    grads = [refs.pop(0) for _ in range(groups)]
     last = refs.pop(0) if joined else None
     more = refs.pop(0) if adds else None
-    out = refs.pop(0)
-    size, stacked = out.shape
+    out, lefts, made, extra, done, sems, out_sems = refs
+    size, stacked = done.shape[1:]
     both = stacked // 3 * 2
-    for kind in range(2):
-        rows = [r[...] for r in (toks if kind == 0 else scaled)]
-        span = slice(0, both) if kind == 0 else slice(both, stacked)
-        cols = [g[:, span] for g in made]
+    rows = blocks[0].shape[0]
+    steps = done.shape[0]
+    started = []
+
+    def start(source, target):
+        copy = pltpu.make_async_copy(source, target, sems.at[len(started)])
+        copy.start()
+        started.append(copy)
+        return copy
+
+    loads = [[[], []] for _ in range(steps)]
+    offsets = [pl.multiple_of(sides[i] * size, size) for i in range(steps)]
+    row = 0
+    for i, b in enumerate(blocks):
+        loads[0][0].append(start(b.at[:, pl.ds(offsets[0], size)], lefts.at[0, 0, pl.ds(row, rows), :]))
+        row += rows
+    if joined:
+        first = pl.multiple_of(stacked + 2 * size + offsets[0], LANES)
+        loads[0][0].append(start(last.at[:, pl.ds(first, size)], lefts.at[0, 0, pl.ds(row, rows), :]))
+    row = 0
+    for g in grads:
+        loads[0][0].append(start(g, made.at[pl.ds(row, g.shape[0]), :]))
+        row += g.shape[0]
+    if joined:
+        loads[0][0].append(start(last.at[:, pl.ds(0, stacked)], made.at[pl.ds(row, rows), :]))
+    if adds:
+        loads[0][0].append(start(more.at[pl.ds(at * size, size), :], extra))
+    for step in range(steps):
+        if step > 0:
+            for i, b in enumerate(blocks):
+                loads[step][0].append(
+                    start(b.at[:, pl.ds(offsets[step], size)], lefts.at[step, 0, pl.ds(i * rows, rows), :])
+                )
+        row = 0
+        for x in scaled:
+            n = x.shape[0]
+            loads[step][1].append(start(x.at[:, pl.ds(offsets[step], size)], lefts.at[step, 1, pl.ds(row, n), :]))
+            row += n
         if joined:
-            cols.append(last[:, span])
-            first = stacked + (2 * size if kind == 0 else 0)
-            rows.append(last[:, pl.ds(pl.multiple_of(first + side * size, LANES), size)])
-        new = dot(jnp.concatenate(rows, axis=0), jnp.concatenate(cols, axis=0), ((0,), (0,)))
-        if adds:
-            new = new + more[:, span].astype(F32)
-        out[:, span] = new.astype(BF16)
+            first = pl.multiple_of(stacked + offsets[step], LANES)
+            loads[step][1].append(start(last.at[:, pl.ds(first, size)], lefts.at[step, 1, pl.ds(row, rows), :]))
+    leaving = []
+    for step in range(steps):
+        for kind in range(2):
+            for c in loads[step][kind]:
+                c.wait()
+            first, wide = (0, both) if kind == 0 else (both, stacked - both)
+            new = dot(lefts[step, kind], made[:, first : first + wide], ((0,), (0,)))
+            if adds:
+                new = new + extra[:, first : first + wide].astype(F32)
+            done[step, :, first : first + wide] = new.astype(BF16)
+            copy = pltpu.make_async_copy(
+                done.at[step, :, pl.ds(first, wide)],
+                out.at[pl.ds(step * size, size), pl.ds(first, wide)],
+                out_sems.at[len(leaving)],
+            )
+            copy.start()
+            leaving.append(copy)
+    for c in leaving:
+        c.wait()
 
 
 def half_call(sides, blocks, kept, last=None, more=None, at=0, weight=0):
     grads, scaled = [k[0] for k in kept], [k[1] for k in kept]
     size = scaled[0].shape[1] // 2
     stacked = grads[0].shape[1]
-    half = lambda a: pl.BlockSpec((a.shape[0], size), lambda i, s: (0, s[i]))
-    whole = lambda a: pl.BlockSpec(a.shape, lambda i, s: (0, 0))
-    operands = [*blocks, *scaled, *grads]
-    specs = [half(a) for a in (*blocks, *scaled)] + [whole(g) for g in grads]
-    if last is not None:
-        operands.append(last)
-        specs.append(whole(last))
-    if more is not None:
-        operands.append(more)
-        specs.append(pl.BlockSpec((size, stacked), lambda i, s: (at, 0)))
-    count = sides.shape[0]
+    rows = blocks[0].shape[0]
+    extra = [a for a in (last, more) if a is not None]
+    operands = [*blocks, *scaled, *grads, *extra]
+    steps = sides.shape[0]
+    total = (len(blocks) + (last is not None)) * rows
     return pl.pallas_call(
-        functools.partial(half_kernel, len(blocks), len(kept), last is not None, more is not None),
-        out_shape=jax.ShapeDtypeStruct((count * size, stacked), BF16),
-        grid_spec=pltpu.PrefetchScalarGridSpec(
-            num_scalar_prefetch=1,
-            grid=(count,),
-            in_specs=specs,
-            out_specs=pl.BlockSpec((size, stacked), lambda i, s: (i, 0)),
-        ),
+        functools.partial(half_kernel, len(blocks), len(kept), last is not None, more is not None, at),
+        out_shape=jax.ShapeDtypeStruct((steps * size, stacked), BF16),
+        in_specs=[smem()] + [hbm()] * len(operands),
+        out_specs=hbm(),
+        scratch_shapes=[
+            pltpu.VMEM((steps, 2, total, size), BF16),
+            pltpu.VMEM((total, stacked), BF16),
+            pltpu.VMEM((size, stacked), BF16),
+            pltpu.VMEM((steps, size, stacked), BF16),
+            pltpu.SemaphoreType.DMA((steps * (len(blocks) + len(kept) + 2) + len(kept) + 2,)),
+            pltpu.SemaphoreType.DMA((2 * steps,)),
+        ],
         cost_estimate=cost(8 * weight * size * stacked * 1024 + 1024, 1024),
         compiler_params=params(),
     )(sides, *operands)
@@ -308,12 +374,12 @@
 
     swap = lambda a: move(a, SWAP_CORE)
     own = pack(experts, tokens, d_output, combine, routes)
-    w_own = pack_weights(after(gate_weight[0], own), up_weight[0], down_weight[0])
-    w_part = across(w_own)
 
     b1 = move(own, OUTER)
     f1 = move(own, INNER)
     y0 = move(own, SWAP_Y)
+    w_own = pack_weights(after(gate_weight[0], own), up_weight[0], down_weight[0])
+    w_part = across(w_own)
     f2 = move(b1, INNER)
     y1 = move(after(b1, y0), SWAP_Y)
     g1 = move(f1, OUTWARD)

time: 132 us -> 132 us (level)
    pallas_call x3, Pallas kernels: 25.7 us -> 24.2 us  [rows_call(): pl.pallas_call(functools.partial(rows_kernel, experts, count, sizes, join...]
  transfers between devices with their start and end apart: 23 -> 23, of which waited for: 8 -> 8; matrix products, arithmetic and copies ran while one was open for 2% -> 2% of each run, Pallas kernels for 34% -> 33%
where the time goes in v8:
time: 132 us; the launch traced here: 130 us
  Pallas kernels  52 us (39%)
  waiting for transfers between devices  39.5 us (30%)
  starting transfers between devices  31.7 us (24%)
  local copies, waits for them, and re-layouts  3.57 us (3%)
  other arithmetic  2.63 us (2%)
    ppermute x21, waiting for transfers between devices, dense_body(): move = lambda a, pairs: lax.ppermute(a, 'expert', pairs)  39.5 us
    ppermute x21, starting transfers between devices, dense_body(): move = lambda a, pairs: lax.ppermute(a, 'expert', pairs)  28.1 us
    pallas_call x3, Pallas kernels, rows_call(): pl.pallas_call(functools.partial(rows_kernel, experts, count, sizes, join...  24.2 us
    pallas_call x3, Pallas kernels, half_call(): pl.pallas_call(functools.partial(half_kernel, len(blocks), len(kept), las...  19.4 us
    pallas_call x1, Pallas kernels, finish(): pl.pallas_call(finish_kernel, out_shape=[sds((size, hidden_units), F32),...  3.95 us
    unnamed x36, local copies, waits for them, and re-layouts  3.57 us
    ppermute x2, starting transfers between devices, dense_body(): across = lambda a: lax.ppermute(a, 'dp', [(0, 1), (1, 0)])  3.52 us
  transfers between devices with their start and end apart: 23, of which 8 were waited for; matrix products, arithmetic and copies ran while one was open for 2% of the time, Pallas kernels for 33%

profile of v8, /device:TPU:0, one launch (start us, length us, event | category | flops | bytes accessed | tf_op | source)
XLA Modules:
  0.0 130.4 jit_solution(6477625945833266862)
XLA Ops:
  0.6 2.0 %shard_map.102.refs_0_ = bf16[128,2176]{1,0:T(8,128)(2,1)} custom-call(bf16[128,1024]{1,0:T(8,128)(2,1)} %tokens.1, bf16[128,1024]{1,0:T(8,128)(2,1)} %d_output.1, f32[8,128]{1,0:T(8,128)} %bitcast.14, s32[8,128]{1,0:T(8,128)} %bitcast.15), custom_call_target="tpu_custom_call" | custom-call | bytes 1572864 | tf_op jit(solution)/shard_map/pallas_call | solution.py:63
  2.6 2.5 %shard_map.103.refs_4_.refs_3_.refs_1_ = bf16[512,1152]{1,0:T(8,128)(2,1)} custom-call(bf16[512,384]{1,0:T(8,128)(2,1)} %bitcast.11, bf16[512,384]{1,0:T(8,128)(2,1)} %bitcast.12, bf16[384,512]{1,0:T(8,128)(2,1)} %bitcast.13), custom_call_target="tpu_custom_call" | custom-call | bytes 47185920 | tf_op jit(solution)/shard_map/pallas_call | solution.py:82
  5.1 2.9 %collective-permute-start.4 = (bf16[512,1152]{1,0:T(8,128)(2,1)}, bf16[512,1152]{1,0:T(8,128)(2,1)}, u32[]{:S(2)}, u32[]{:S(2)}) collective-permute-start(bf16[512,1152]{1,0:T(8,128)(2,1)} %shard_map.103.refs_4_.refs_3_.refs_1_), channel_id=1, source_target_pairs={{0,16},{16,0},{1,17},{17,1},{2,18},{18,2},{3,19},{19,3},{4,20},{20... | collective-permute-start | bytes 3538952 | tf_op jit(solution)/shard_map/ppermute | solution.py:373
  8.0 1.6 %collective-permute-start = (bf16[128,2176]{1,0:T(8,128)(2,1)S(1)}, bf16[128,2176]{1,0:T(8,128)(2,1)S(1)}, u32[]{:S(2)}, u32[]{:S(2)}) collective-permute-start(bf16[128,2176]{1,0:T(8,128)(2,1)S(1)} %copy-done.2), channel_id=1, source_target_pairs={{0,4},{1,5},{2,6},{3,7},{4,0},{5,1},{6,2},{7,3},{8,12},{9,13},{10,... | collective-permute-start | bytes 1671176 | tf_op jit(solution)/shard_map/ppermute | solution.py:372
  9.6 1.5 %collective-permute-start.3 = (bf16[128,2176]{1,0:T(8,128)(2,1)S(1)}, bf16[128,2176]{1,0:T(8,128)(2,1)S(1)}, u32[]{:S(2)}, u32[]{:S(2)}) collective-permute-start(bf16[128,2176]{1,0:T(8,128)(2,1)S(1)} %copy-done.2), channel_id=1, source_target_pairs={{0,2},{1,3},{2,0},{3,1},{4,6},{5,7},{6,4},{7,5},{8,10},{9,11},{10,... | collective-permute-start | bytes 1671176 | tf_op jit(solution)/shard_map/ppermute | solution.py:372
  11.8 10.3 %collective-permute-done.refs_1_ = bf16[128,2176]{1,0:T(8,128)(2,1)S(1)} collective-permute-done((bf16[128,2176]{1,0:T(8,128)(2,1)S(1)}, bf16[128,2176]{1,0:T(8,128)(2,1)S(1)}, u32[]{:S(2)}, u32[]{:S(2)}) %collective-permute-start) | collective-permute-done | bytes 557088 | tf_op jit(solution)/shard_map/ppermute | solution.py:372
  22.1 1.3 collective-permute-done.3.refs_3_
  23.4 1.5 %collective-permute-start.5 = (bf16[128,2176]{1,0:T(8,128)(2,1)S(1)}, bf16[128,2176]{1,0:T(8,128)(2,1)S(1)}, u32[]{:S(2)}, u32[]{:S(2)}) collective-permute-start(bf16[128,2176]{1,0:T(8,128)(2,1)S(1)} %collective-permute-done.refs_1_), channel_id=1, source_target_pairs={{0,2},{1,3},{2,0},{3,1},{4,6},{5,7},{6,4},{7,5},{8,10},{9,11},{10,... | collective-permute-start | bytes 1671176 | tf_op jit(solution)/shard_map/ppermute | solution.py:372
  25.6 1.3 collective-permute-start.2
  26.9 9.5 %collective-permute-done.5.refs_1_.refs_5_ = bf16[128,2176]{1,0:T(8,128)(2,1)S(1)} collective-permute-done((bf16[128,2176]{1,0:T(8,128)(2,1)S(1)}, bf16[128,2176]{1,0:T(8,128)(2,1)S(1)}, u32[]{:S(2)}, u32[]{:S(2)}) %collective-permute-start.5) | collective-permute-done | bytes 557088 | tf_op jit(solution)/shard_map/ppermute | solution.py:372
  38.2 3.8 %collective-permute-done.2 = bf16[128,2176]{1,0:T(8,128)(2,1)S(1)} collective-permute-done((bf16[128,2176]{1,0:T(8,128)(2,1)S(1)}, bf16[128,2176]{1,0:T(8,128)(2,1)S(1)}, u32[]{:S(2)}, u32[]{:S(2)}) %collective-permute-start.2) | collective-permute-done | bytes 557088 | tf_op jit(solution)/shard_map/ppermute | solution.py:372
  42.6 1.3 collective-permute-start.9
  43.9 10.1 %shard_map.104 = (bf16[128,1024]{1,0:T(8,128)(2,1)}, bf16[128,1024]{1,0:T(8,128)(2,1)}, bf16[128,1024]{1,0:T(8,128)(2,1)}, bf16[128,1024]{1,0:T(8,128)(2,1)}, bf...) custom-call(s32[2]{0:T(128)} %pad_add_fusion.scal, ...), custom_call_target="tpu_custom_call" | custom-call | flops 14495514624 | bytes 1048576 | tf_op jit(solution)/shard_map/pallas_call | solution.py:186
  54.0 3.1 %collective-permute-done.9 = bf16[128,2176]{1,0:T(8,128)(2,1)S(1)} collective-permute-done((bf16[128,2176]{1,0:T(8,128)(2,1)S(1)}, bf16[128,2176]{1,0:T(8,128)(2,1)S(1)}, u32[]{:S(2)}, u32[]{:S(2)}) %collective-permute-start.9) | collective-permute-done | bytes 557088 | tf_op jit(solution)/shard_map/ppermute | solution.py:372
  57.2 1.6 %collective-permute-start.11 = (bf16[128,2176]{1,0:T(8,128)(2,1)S(1)}, bf16[128,2176]{1,0:T(8,128)(2,1)S(1)}, u32[]{:S(2)}, u32[]{:S(2)}) collective-permute-start(bf16[128,2176]{1,0:T(8,128)(2,1)S(1)} %broadcast_select_fusion.refs_0_.refs_4_), channel_id=1, source_target_pairs={{0,2},{1,3},{2,0},{3,1},{4,6},{5,7},{6,4},{7,5},{8,10},{9,11},{10,... | collective-permute-start | bytes 1671176 | tf_op jit(solution)/shard_map/ppermute | solution.py:372
  58.8 8.4 %shard_map.105 = (bf16[128,1024]{1,0:T(8,128)(2,1)}, bf16[256,1024]{1,0:T(8,128)(2,1)}, bf16[384,1152]{1,0:T(8,128)(2,1)}, bf16[384,1024]{1,0:T(8,128)(2,1)}, bf...) custom-call(s32[2]{0:T(128)} %pad_add_fusion.scal, bf16[128,2176]{1,0:T(8,128)(2,1)} %copy-done.1, ...), custom_call_target="tpu_custom_call" | custom-call | flops 10871635968 | bytes 1048576 | tf_op jit(solution)/shard_map/pallas_call | solution.py:186
  67.2 7.8 %shard_map.106 = bf16[1024,1152]{1,0:T(8,128)(2,1)} custom-call(s32[2]{0:T(128)} %pad_add_fusion.1.sides, bf16[128,2176]{1,0:T(8,128)(2,1)} %shard_map.102.refs_0_, bf16[128,2176]{1,0:T(8,128)(2,1)} %copy-done.4, bf16[128,2176]{1,0:T(8,128)(2,1)} %copy-done, bf16[128,2176]{1,0:T(8,128)(2,1)} %copy-done.5, bf16[128,2176]{1,0:T(8,128)(2,1)} %copy-done.1, ...), custom_call_target="tpu_custom_call" | custom-call | flops 1024 | bytes 1024 | tf_op jit(solution)/shard_map/pallas_call | solution.py:287
  75.9 5.8 %shard_map.107 = (bf16[128,1024]{1,0:T(8,128)(2,1)}, bf16[128,1152]{1,0:T(8,128)(2,1)}, bf16[128,1024]{1,0:T(8,128)(2,1)}, bf16[128,3200]{1,0:T(8,128)(2,1)}) custom-call(s32[2]{0:T(128)} %pad_add_fusion.scal, bf16[128,2176]{1,0:T(8,128)(2,1)} %copy-done.10, bf16[512,1152]{1,0:T(8,128)(2,1)} %shard_map.103.refs_4_.refs_3_.refs_1_, ...), custom_call_target="tpu_custom_call" | custom-call | flops 36238786560 | bytes 1048576 | tf_op jit(solution)/shard_map/pallas_call | solution.py:186
  82.3 0.9 collective-permute-start.14
  83.1 1.3 collective-permute-done.12.refs_14_
  86.1 5.8 %shard_map.108 = bf16[512,1152]{1,0:T(8,128)(2,1)} custom-call(s32[1]{0:T(128)} %bitcast.7.sides, bf16[128,2176]{1,0:T(8,128)(2,1)} %shard_map.102.refs_0_, bf16[128,2176]{1,0:T(8,128)(2,1)} %copy-done.4, bf16[128,2176]{1,0:T(8,128)(2,1)} %copy-done, bf16[128,2176]{1,0:T(8,128)(2,1)} %copy-done.5, bf16[128,2176]{1,0:T(8,128)(2,1)} %copy-done.1, ...), custom_call_target="tpu_custom_call" | custom-call | flops 4831839232 | bytes 1024 | tf_op jit(solution)/shard_map/pallas_call | solution.py:287
  92.5 3.6 %collective-permute-done.14 = bf16[256,1024]{1,0:T(8,128)(2,1)S(1)} collective-permute-done((bf16[256,1024]{1,0:T(8,128)(2,1)S(1)}, bf16[256,1024]{1,0:T(8,128)(2,1)S(1)}, u32[]{:S(2)}, u32[]{:S(2)}) %collective-permute-start.14) | collective-permute-done | bytes 524320 | tf_op jit(solution)/shard_map/ppermute | solution.py:372
  96.2 0.9 collective-permute-start.15
  98.0 6.6 %collective-permute-start.19 = (bf16[128,1024]{1,0:T(8,128)(2,1)S(1)}, bf16[128,1024]{1,0:T(8,128)(2,1)S(1)}, u32[]{:S(2)}, u32[]{:S(2)}) collective-permute-start(bf16[128,1024]{1,0:T(8,128)(2,1)S(1)} %get-tuple-element.75), channel_id=1, source_target_pairs={{0,8},{1,9},{2,10},{3,11},{12,4},{13,5},{14,6},{15,7},{16,24},{17,... | collective-permute-start | bytes 786440 | tf_op jit(solution)/shard_map/ppermute | solution.py:372
  104.7 1.2 collective-permute-start.16
  106.0 1.4 %collective-permute-start.20 = (bf16[128,1024]{1,0:T(8,128)(2,1)S(1)}, bf16[128,1024]{1,0:T(8,128)(2,1)S(1)}, u32[]{:S(2)}, u32[]{:S(2)}) collective-permute-start(bf16[128,1024]{1,0:T(8,128)(2,1)S(1)} %add_convert_fusion.1), channel_id=1, source_target_pairs={{4,12},{5,13},{6,14},{7,15},{8,0},{9,1},{10,2},{11,3},{20,28},{21,... | collective-permute-start | bytes 786440 | tf_op jit(solution)/shard_map/ppermute | solution.py:372
  107.4 4.5 %collective-permute-start.21 = (bf16[128,1024]{1,0:T(8,128)(2,1)S(1)}, bf16[128,1024]{1,0:T(8,128)(2,1)S(1)}, u32[]{:S(2)}, u32[]{:S(2)}) collective-permute-start(bf16[128,1024]{1,0:T(8,128)(2,1)S(1)} %add_convert_fusion.1), channel_id=1, source_target_pairs={{0,12},{1,13},{2,14},{3,15},{12,0},{13,1},{14,2},{15,3},{16,28},{1... | collective-permute-start | bytes 786440 | tf_op jit(solution)/shard_map/ppermute | solution.py:372
  111.9 5.8 %shard_map.109.keep = bf16[512,1152]{1,0:T(8,128)(2,1)} custom-call(s32[1]{0:T(128)} %bitcast.sides, bf16[128,2176]{1,0:T(8,128)(2,1)} %shard_map.102.refs_0_, bf16[128,2176]{1,0:T(8,128)(2,1)} %copy-done.4, bf16[128,2176]{1,0:T(8,128)(2,1)} %copy-done, bf16[128,2176]{1,0:T(8,128)(2,1)} %copy-done.5, bf16[128,2176]{1,0:T(8,128)(2,1)} %copy-done.1, ...), custom_call_target="tpu_custom_call" | custom-call | flops 1024 | bytes 1024 | tf_op jit(solution)/shard_map/pallas_call | solution.py:287
  117.8 6.7 %collective-permute-done.20 = bf16[128,1024]{1,0:T(8,128)(2,1)S(1)} collective-permute-done((bf16[128,1024]{1,0:T(8,128)(2,1)S(1)}, bf16[128,1024]{1,0:T(8,128)(2,1)S(1)}, u32[]{:S(2)}, u32[]{:S(2)}) %collective-permute-start.20) | collective-permute-done | bytes 262176 | tf_op jit(solution)/shard_map/ppermute | solution.py:372
  124.4 1.0 add_convert_fusion
  125.4 1.0 copy-done.8
  126.5 3.9 %shard_map.110 = (f32[512,384]{1,0:T(8,128)}, f32[512,384]{1,0:T(8,128)}, f32[384,512]{1,0:T(8,128)}) custom-call(bf16[512,1152]{1,0:T(8,128)(2,1)} %shard_map.109.keep, bf16[512,1152]{1,0:T(8,128)(2,1)} %copy-done.8), custom_call_target="tpu_custom_call" | custom-call | flops 1024 | bytes 1024 | tf_op jit(solution)/shard_map/pallas_call | solution.py:319
  (66 shorter events, 8.6 us)
Async XLA Ops:
  5.1 31.3 %collective-permute-start.4 = (bf16[512,1152]{1,0:T(8,128)(2,1)}, bf16[512,1152]{1,0:T(8,128)(2,1)}, u32[]{:S(2)}, u32[]{:S(2)}) collective-permute-start(bf16[512,1152]{1,0:T(8,128)(2,1)} %shard_map.103.refs_4_.refs_3_.refs_1_), channel_id=1, source_target_pairs={{0,16},{16,0},{1,17},{17,1},{2,18},{18,2},{3,19},{19,3},{4,20},{20... | collective-permute-start | bytes 3538952 | tf_op jit(solution)/shard_map/ppermute | solution.py:373
  8.0 14.1 %collective-permute-start = (bf16[128,2176]{1,0:T(8,128)(2,1)S(1)}, bf16[128,2176]{1,0:T(8,128)(2,1)S(1)}, u32[]{:S(2)}, u32[]{:S(2)}) collective-permute-start(bf16[128,2176]{1,0:T(8,128)(2,1)S(1)} %copy-done.2), channel_id=1, source_target_pairs={{0,4},{1,5},{2,6},{3,7},{4,0},{5,1},{6,2},{7,3},{8,12},{9,13},{10,... | collective-permute-start | bytes 1671176 | tf_op jit(solution)/shard_map/ppermute | solution.py:372
  9.6 13.8 %collective-permute-start.3 = (bf16[128,2176]{1,0:T(8,128)(2,1)S(1)}, bf16[128,2176]{1,0:T(8,128)(2,1)S(1)}, u32[]{:S(2)}, u32[]{:S(2)}) collective-permute-start(bf16[128,2176]{1,0:T(8,128)(2,1)S(1)} %copy-done.2), channel_id=1, source_target_pairs={{0,2},{1,3},{2,0},{3,1},{4,6},{5,7},{6,4},{7,5},{8,10},{9,11},{10,... | collective-permute-start | bytes 1671176 | tf_op jit(solution)/shard_map/ppermute | solution.py:372
  11.1 14.5 %collective-permute-start.1 = (bf16[128,2176]{1,0:T(8,128)(2,1)S(1)}, bf16[128,2176]{1,0:T(8,128)(2,1)S(1)}, u32[]{:S(2)}, u32[]{:S(2)}) collective-permute-start(bf16[128,2176]{1,0:T(8,128)(2,1)S(1)} %copy-done.2), channel_id=1, source_target_pairs={{4,8},{5,9},{6,10},{7,11},{8,4},{9,5},{10,6},{11,7},{20,24},{21,25... | collective-permute-start | bytes 1671176 | tf_op jit(solution)/shard_map/ppermute | solution.py:372
  22.1 21.8 %copy-start.4 = (bf16[128,2176]{1,0:T(8,128)(2,1)}, bf16[128,2176]{1,0:T(8,128)(2,1)S(1)}, u32[]{:S(2)}) copy-start(bf16[128,2176]{1,0:T(8,128)(2,1)S(1)} %collective-permute-done.refs_1_) | copy-start | bytes 1671172
  23.4 20.5 %copy-start.5 = (bf16[128,2176]{1,0:T(8,128)(2,1)}, bf16[128,2176]{1,0:T(8,128)(2,1)S(1)}, u32[]{:S(2)}) copy-start(bf16[128,2176]{1,0:T(8,128)(2,1)S(1)} %collective-permute-done.3.refs_3_) | copy-start | bytes 1671172
  23.4 13.0 %collective-permute-start.5 = (bf16[128,2176]{1,0:T(8,128)(2,1)S(1)}, bf16[128,2176]{1,0:T(8,128)(2,1)S(1)}, u32[]{:S(2)}, u32[]{:S(2)}) collective-permute-start(bf16[128,2176]{1,0:T(8,128)(2,1)S(1)} %collective-permute-done.refs_1_), channel_id=1, source_target_pairs={{0,2},{1,3},{2,0},{3,1},{4,6},{5,7},{6,4},{7,5},{8,10},{9,11},{10,... | collective-permute-start | bytes 1671176 | tf_op jit(solution)/shard_map/ppermute | solution.py:372
  24.9 11.5 %collective-permute-start.6 = (bf16[128,2176]{1,0:T(8,128)(2,1)S(1)}, bf16[128,2176]{1,0:T(8,128)(2,1)S(1)}, u32[]{:S(2)}, u32[]{:S(2)}) collective-permute-start(bf16[128,2176]{1,0:T(8,128)(2,1)S(1)} %collective-permute-done.refs_1_), channel_id=1, source_target_pairs={{4,8},{5,9},{6,10},{7,11},{8,4},{9,5},{10,6},{11,7},{20,24},{21,25... | collective-permute-start | bytes 1671176 | tf_op jit(solution)/shard_map/ppermute | solution.py:372
  25.6 16.3 %collective-permute-start.2 = (bf16[128,2176]{1,0:T(8,128)(2,1)S(1)}, bf16[128,2176]{1,0:T(8,128)(2,1)S(1)}, u32[]{:S(2)}, u32[]{:S(2)}) collective-permute-start(bf16[128,2176]{1,0:T(8,128)(2,1)S(1)} %collective-permute-done.1), channel_id=1, source_target_pairs={{4,0},{5,1},{6,2},{7,3},{8,12},{9,13},{10,14},{11,15},{20,16},{21,... | collective-permute-start | bytes 1671176 | tf_op jit(solution)/shard_map/ppermute | solution.py:372
  36.4 17.6 %copy-start.6 = (bf16[128,2176]{1,0:T(8,128)(2,1)}, bf16[128,2176]{1,0:T(8,128)(2,1)S(1)}, u32[]{:S(2)}) copy-start(bf16[128,2176]{1,0:T(8,128)(2,1)S(1)} %collective-permute-done.5.refs_1_.refs_5_) | copy-start | bytes 1671172
  36.4 7.5 %collective-permute-start.7 = (bf16[512,1152]{1,0:T(8,128)(2,1)}, bf16[512,1152]{1,0:T(8,128)(2,1)}, u32[]{:S(2)}, u32[]{:S(2)}) collective-permute-start(bf16[512,1152]{1,0:T(8,128)(2,1)} %shard_map.103.refs_4_.refs_3_.refs_1_), channel_id=1, source_target_pairs={{0,1},{1,0},{2,3},{3,2},{4,5},{5,4},{6,7},{7,6},{8,9},{9,8},{10,11... | collective-permute-start | bytes 3538952 | tf_op jit(solution)/shard_map/ppermute | solution.py:372
  36.4 7.5 %collective-permute-start.8 = (bf16[512,1152]{1,0:T(8,128)(2,1)}, bf16[512,1152]{1,0:T(8,128)(2,1)}, u32[]{:S(2)}, u32[]{:S(2)}) collective-permute-start(bf16[512,1152]{1,0:T(8,128)(2,1)} %collective-permute-done.4.refs_5_.refs_4_.refs_2_), channel_id=1, source_target_pairs={{0,1},{1,0},{2,3},{3,2},{4,5},{5,4},{6,7},{7,6},{8,9},{9,8},{10,11... | collective-permute-start | bytes 3538952 | tf_op jit(solution)/shard_map/ppermute | solution.py:372
  42.0 15.2 %collective-permute-start.10 = (bf16[128,2176]{1,0:T(8,128)(2,1)S(1)}, bf16[128,2176]{1,0:T(8,128)(2,1)S(1)}, u32[]{:S(2)}, u32[]{:S(2)}) collective-permute-start(bf16[128,2176]{1,0:T(8,128)(2,1)S(1)} %broadcast_select_fusion.1.refs_2_), channel_id=1, source_target_pairs={{0,2},{1,3},{2,0},{3,1},{4,6},{5,7},{6,4},{7,5},{8,10},{9,11},{10,... | collective-permute-start | bytes 1671176 | tf_op jit(solution)/shard_map/ppermute | solution.py:372
  42.6 14.5 %collective-permute-start.9 = (bf16[128,2176]{1,0:T(8,128)(2,1)S(1)}, bf16[128,2176]{1,0:T(8,128)(2,1)S(1)}, u32[]{:S(2)}, u32[]{:S(2)}) collective-permute-start(bf16[128,2176]{1,0:T(8,128)(2,1)S(1)} %collective-permute-done.6), channel_id=1, source_target_pairs={{4,0},{5,1},{6,2},{7,3},{8,12},{9,13},{10,14},{11,15},{20,16},{21,... | collective-permute-start | bytes 1671176 | tf_op jit(solution)/shard_map/ppermute | solution.py:372
  57.2 17.9 %collective-permute-start.11 = (bf16[128,2176]{1,0:T(8,128)(2,1)S(1)}, bf16[128,2176]{1,0:T(8,128)(2,1)S(1)}, u32[]{:S(2)}, u32[]{:S(2)}) collective-permute-start(bf16[128,2176]{1,0:T(8,128)(2,1)S(1)} %broadcast_select_fusion.refs_0_.refs_4_), channel_id=1, source_target_pairs={{0,2},{1,3},{2,0},{3,1},{4,6},{5,7},{6,4},{7,5},{8,10},{9,11},{10,... | collective-permute-start | bytes 1671176 | tf_op jit(solution)/shard_map/ppermute | solution.py:372
  75.0 9.4 %collective-permute-start.13 = (bf16[1024,1152]{1,0:T(8,128)(2,1)}, bf16[1024,1152]{1,0:T(8,128)(2,1)S(1)}, u32[]{:S(2)}, u32[]{:S(2)}) collective-permute-start(bf16[1024,1152]{1,0:T(8,128)(2,1)} %shard_map.106), channel_id=1, source_target_pairs={{0,1},{1,0},{2,3},{3,2},{4,5},{5,4},{6,7},{7,6},{8,9},{9,8},{10,11... | collective-permute-start | bytes 7077896 | tf_op jit(solution)/shard_map/ppermute | solution.py:372
  81.7 2.7 %collective-permute-start.12 = (bf16[128,3200]{1,0:T(8,128)(2,1)}, bf16[128,3200]{1,0:T(8,128)(2,1)S(1)}, u32[]{:S(2)}, u32[]{:S(2)}) collective-permute-start(bf16[128,3200]{1,0:T(8,128)(2,1)} %get-tuple-element.59), channel_id=1, source_target_pairs={{0,1},{1,0},{2,3},{3,2},{4,5},{5,4},{6,7},{7,6},{8,9},{9,8},{10,11... | collective-permute-start | bytes 2457608 | tf_op jit(solution)/shard_map/ppermute | solution.py:372
  82.3 13.9 %collective-permute-start.14 = (bf16[256,1024]{1,0:T(8,128)(2,1)S(1)}, bf16[256,1024]{1,0:T(8,128)(2,1)S(1)}, u32[]{:S(2)}, u32[]{:S(2)}) collective-permute-start(bf16[256,1024]{1,0:T(8,128)(2,1)S(1)} %copy-done.15), channel_id=1, source_target_pairs={{0,2},{1,3},{2,0},{3,1},{4,6},{5,7},{6,4},{7,5},{8,10},{9,11},{10,... | collective-permute-start | bytes 1572872 | tf_op jit(solution)/shard_map/ppermute | solution.py:372
  86.1 10.1 %copy-start.17 = (bf16[128,1024]{1,0:T(8,128)(2,1)S(1)}, bf16[128,1024]{1,0:T(8,128)(2,1)}, u32[]{:S(2)}) copy-start(bf16[128,1024]{1,0:T(8,128)(2,1)} %get-tuple-element.65) | copy-start | bytes 786436
  86.1 11.0 %copy-start.12 = (bf16[128,1024]{1,0:T(8,128)(2,1)S(1)}, bf16[128,1024]{1,0:T(8,128)(2,1)}, u32[]{:S(2)}) copy-start(bf16[128,1024]{1,0:T(8,128)(2,1)} %get-tuple-element.67) | copy-start | bytes 786436
  86.1 11.0 %copy-start.13 = (bf16[128,1024]{1,0:T(8,128)(2,1)S(1)}, bf16[128,1024]{1,0:T(8,128)(2,1)}, u32[]{:S(2)}) copy-start(bf16[128,1024]{1,0:T(8,128)(2,1)} %get-tuple-element.68) | copy-start | bytes 786436
  91.9 12.7 %copy-start.16 = (bf16[128,1024]{1,0:T(8,128)(2,1)S(1)}, bf16[128,1024]{1,0:T(8,128)(2,1)}, u32[]{:S(2)}) copy-start(bf16[128,1024]{1,0:T(8,128)(2,1)} %get-tuple-element.66) | copy-start | bytes 786436
  91.9 13.9 %copy-start.11 = (bf16[128,1024]{1,0:T(8,128)(2,1)S(1)}, bf16[128,1024]{1,0:T(8,128)(2,1)}, u32[]{:S(2)}) copy-start(bf16[128,1024]{1,0:T(8,128)(2,1)} %get-tuple-element.69) | copy-start | bytes 786436
  92.0 33.5 %collective-permute-start.22 = (bf16[512,1152]{1,0:T(8,128)(2,1)}, bf16[512,1152]{1,0:T(8,128)(2,1)S(1)}, u32[]{:S(2)}, u32[]{:S(2)}) collective-permute-start(bf16[512,1152]{1,0:T(8,128)(2,1)} %shard_map.108), channel_id=1, source_target_pairs={{0,16},{16,0},{1,17},{17,1},{2,18},{18,2},{3,19},{19,3},{4,20},{20... | collective-permute-start | bytes 3538952 | tf_op jit(solution)/shard_map/ppermute | solution.py:373
  96.2 8.5 %collective-permute-start.15 = (bf16[128,1024]{1,0:T(8,128)(2,1)S(1)}, bf16[128,1024]{1,0:T(8,128)(2,1)S(1)}, u32[]{:S(2)}, u32[]{:S(2)}) collective-permute-start(bf16[128,1024]{1,0:T(8,128)(2,1)S(1)} %copy-done.17), channel_id=1, source_target_pairs={{0,2},{1,3},{2,0},{3,1},{4,6},{5,7},{6,4},{7,5},{8,10},{9,11},{10,... | collective-permute-start | bytes 786440 | tf_op jit(solution)/shard_map/ppermute | solution.py:372
  97.3 8.7 %collective-permute-start.17 = (bf16[128,1024]{1,0:T(8,128)(2,1)S(1)}, bf16[128,1024]{1,0:T(8,128)(2,1)S(1)}, u32[]{:S(2)}, u32[]{:S(2)}) collective-permute-start(bf16[128,1024]{1,0:T(8,128)(2,1)S(1)} %get-tuple-element.74), channel_id=1, source_target_pairs={{0,4},{1,5},{2,6},{3,7},{4,0},{5,1},{6,2},{7,3},{8,12},{9,13},{10,... | collective-permute-start | bytes 786440 | tf_op jit(solution)/shard_map/ppermute | solution.py:372
  97.3 10.1 %collective-permute-start.18 = (bf16[128,1024]{1,0:T(8,128)(2,1)S(1)}, bf16[128,1024]{1,0:T(8,128)(2,1)S(1)}, u32[]{:S(2)}, u32[]{:S(2)}) collective-permute-start(bf16[128,1024]{1,0:T(8,128)(2,1)S(1)} %get-tuple-element.75), channel_id=1, source_target_pairs={{4,8},{5,9},{6,10},{7,11},{8,4},{9,5},{10,6},{11,7},{20,24},{21,25... | collective-permute-start | bytes 786440 | tf_op jit(solution)/shard_map/ppermute | solution.py:372
  98.0 19.7 %collective-permute-start.19 = (bf16[128,1024]{1,0:T(8,128)(2,1)S(1)}, bf16[128,1024]{1,0:T(8,128)(2,1)S(1)}, u32[]{:S(2)}, u32[]{:S(2)}) collective-permute-start(bf16[128,1024]{1,0:T(8,128)(2,1)S(1)} %get-tuple-element.75), channel_id=1, source_target_pairs={{0,8},{1,9},{2,10},{3,11},{12,4},{13,5},{14,6},{15,7},{16,24},{17,... | collective-permute-start | bytes 786440 | tf_op jit(solution)/shard_map/ppermute | solution.py:372
  104.7 13.1 %collective-permute-start.16 = (bf16[128,1024]{1,0:T(8,128)(2,1)S(1)}, bf16[128,1024]{1,0:T(8,128)(2,1)S(1)}, u32[]{:S(2)}, u32[]{:S(2)}) collective-permute-start(bf16[128,1024]{1,0:T(8,128)(2,1)S(1)} %copy-done.16), channel_id=1, source_target_pairs={{0,2},{1,3},{2,0},{3,1},{4,6},{5,7},{6,4},{7,5},{8,10},{9,11},{10,... | collective-permute-start | bytes 786440 | tf_op jit(solution)/shard_map/ppermute | solution.py:372
  105.9 18.5 %copy-start.14 = (bf16[128,1024]{1,0:T(8,128)(2,1)S(1)}, bf16[128,1024]{1,0:T(8,128)(2,1)}, u32[]{:S(2)}) copy-start(bf16[128,1024]{1,0:T(8,128)(2,1)} %get-tuple-element.61) | copy-start | bytes 786436
  106.0 18.5 %collective-permute-start.20 = (bf16[128,1024]{1,0:T(8,128)(2,1)S(1)}, bf16[128,1024]{1,0:T(8,128)(2,1)S(1)}, u32[]{:S(2)}, u32[]{:S(2)}) collective-permute-start(bf16[128,1024]{1,0:T(8,128)(2,1)S(1)} %add_convert_fusion.1), channel_id=1, source_target_pairs={{4,12},{5,13},{6,14},{7,15},{8,0},{9,1},{10,2},{11,3},{20,28},{21,... | collective-permute-start | bytes 786440 | tf_op jit(solution)/shard_map/ppermute | solution.py:372
  107.4 17.0 %collective-permute-start.21 = (bf16[128,1024]{1,0:T(8,128)(2,1)S(1)}, bf16[128,1024]{1,0:T(8,128)(2,1)S(1)}, u32[]{:S(2)}, u32[]{:S(2)}) collective-permute-start(bf16[128,1024]{1,0:T(8,128)(2,1)S(1)} %add_convert_fusion.1), channel_id=1, source_target_pairs={{0,12},{1,13},{2,14},{3,15},{12,0},{13,1},{14,2},{15,3},{16,28},{1... | collective-permute-start | bytes 786440 | tf_op jit(solution)/shard_map/ppermute | solution.py:372
  (9 other events, 21.3 us)

commit v9 on v8

--- a/solution.py
+++ b/solution.py
@@ -95,7 +95,7 @@
     raw = [refs.pop(0) for _ in range(4)]
     out_rows = [refs.pop(0) for _ in sizes]
     kept = [refs.pop(0) for _ in range(3 if joined else 4)]
-    block, held, grads, scaled, total, d_rows, in_sems, out_sems = refs
+    block, held, grads, scaled, d_rows, in_sems, out_sems = refs
     part, expert = scal[0], scal[1]
     size, stacked = raw[0].shape
     hidden_units = stacked // 3
@@ -122,6 +122,7 @@
     sides = [pl.multiple_of(part * size, size), pl.multiple_of((1 - part) * size, size)]
     parts = block[:, 2 * width :].astype(F32)
     lane = lax.broadcasted_iota(jnp.int32, parts.shape, 1)
+    first = []
     for which in range(2):
         for c in weights[2 * which : 2 * which + 2]:
             c.wait()
@@ -139,10 +140,12 @@
             h = dot(scaled_half, held[2 * which + side, :, both:], ((1,), (0,)))
             preact = p if side == 0 else preact + p
             d_hidden = h if side == 0 else d_hidden + h
-        if joined and which == 1:
-            leave(scaled.at[1], kept[2].at[:, pl.ds(stacked, width)])
-        else:
-            leave(scaled.at[which], kept[2 * which + 1])
+        first.append((preact, d_hidden))
+    leave(scaled.at[0], kept[1])
+    leave(scaled.at[1], kept[2].at[:, pl.ds(stacked, width)] if joined else kept[3])
+    second = []
+    for which in range(2):
+        preact, d_hidden = first[which]
         gate_pre = preact[:, :hidden_units]
         up_pre = preact[:, hidden_units:]
         sig = jax.nn.sigmoid(gate_pre)
@@ -152,18 +155,12 @@
         grads[which, :, :hidden_units] = d_gate
         grads[which, :, hidden_units:both] = d_up
         grads[which, :, both:] = (silu * up_pre).astype(BF16)
-        if joined and which == 1:
-            leave(grads.at[1], kept[2].at[:, pl.ds(0, stacked)])
-        else:
-            leave(grads.at[which], kept[2 * which])
         d_preact = jnp.concatenate([d_gate, d_up], axis=1)
-        for side in range(2):
-            at = sides[side]
-            new = dot(d_preact, held[2 * which + side, :, :both], ((1,), (1,)))
-            if which == 0:
-                total[:, pl.ds(at, size)] = new
-            else:
-                d_rows[:, pl.ds(at, size)] = (new + total[:, pl.ds(at, size)]).astype(BF16)
+        second.append([dot(d_preact, held[2 * which + side, :, :both], ((1,), (1,))) for side in range(2)])
+    leave(grads.at[0], kept[0])
+    leave(grads.at[1], kept[2].at[:, pl.ds(0, stacked)] if joined else kept[2])
+    for side in range(2):
+        d_rows[:, pl.ds(sides[side], size)] = (second[0][side] + second[1][side]).astype(BF16)
     row = 0
     for out, n in zip(out_rows, sizes):
         leave(d_rows.at[pl.ds(row, n), :], out)
@@ -193,7 +190,6 @@
             pltpu.VMEM((4, size, stacked), BF16),
             pltpu.VMEM((2, total, stacked), BF16),
             pltpu.VMEM((2, total, 2 * size), BF16),
-            pltpu.VMEM((total, 2 * size), F32),
             pltpu.VMEM((total, 2 * size), BF16),
             pltpu.SemaphoreType.DMA((count + 4,)),
             pltpu.SemaphoreType.DMA((len(groups) + 5,)),
@@ -350,9 +346,8 @@
 OUTER = along_z({0: 1, 1: 0, 2: 3, 3: 2})
 INNER = along_z({1: 2, 2: 1})
 OUTWARD = along_z({1: 0, 2: 3})
-SKIP_TO_INNER = along_z({0: 2, 3: 1})
+INWARD = along_z({0: 1, 3: 2})
 SKIP_TO_OUTER = along_z({1: 3, 2: 0})
-ENDS = along_z({0: 3, 3: 0})
 
 
 def after(value, *others):
@@ -405,29 +400,23 @@
 
     q3, *kept_d, joined = rows_call(experts, scal, [[y3]], weights, joined=True)
     last = swap(joined)
-    r3 = move(after(q3, r12), SWAP_Y)
-    r0 = move(after(q0, r3), SWAP_Y)
     all_blocks = blocks + [y3]
     all_kept = [k[:2] for k in kept] + [kept_d]
     got = swap(to_core)
     send = half_call(other, all_blocks, all_kept, last, got, weight=1)
     from_part = across(send)
+    r3 = move(after(q3, send), SWAP_Y)
+    r0 = move(after(q0, r3), SWAP_Y)
     keep = half_call(after(mine, send), all_blocks, all_kept, last, got, at=1)
 
     add = lambda *terms: sum(t.astype(F32) for t in terms).astype(BF16)
     s1 = add(p1, r1)
     s2 = add(p2, r2)
+    s2 = add(s2, move(s2, INWARD))
     s3 = add(p3, r3)
-    d_tokens = add(
-        after(p0, keep),
-        r0,
-        move(s1, OUTER),
-        move(s2, INNER),
-        move(s2, SKIP_TO_INNER),
-        move(s3, SKIP_TO_OUTER),
-        move(s3, ENDS),
-    )
-    d_gate, d_up, d_down = finish(keep, after(from_part, d_tokens))
+    s3 = add(s3, move(s3, INWARD))
+    d_gate, d_up, d_down = finish(keep, after(from_part, s2))
+    d_tokens = add(after(p0, d_gate), r0, move(s1, OUTER), move(s2, INNER), move(s3, SKIP_TO_OUTER))
     return (d_tokens, d_gate[None], d_up[None], d_down[None])
 
 

time: 132 us -> 128 us (0.970)
  starting transfers between devices: 31.7 us -> 23.4 us
  waiting for transfers between devices: 39.5 us -> 44.5 us
    ppermute x21, starting transfers between devices: 28.1 us -> 19.9 us  [dense_body(): move = lambda a, pairs: lax.ppermute(a, 'expert', pairs)]
    ppermute x2, waiting for transfers between devices: 0.01 us -> 3.85 us  [dense_body(): across = lambda a: lax.ppermute(a, 'dp', [(0, 1), (1, 0)])]
  transfers between devices with their start and end apart: 23 -> 23, of which waited for: 8 -> 10; matrix products, arithmetic and copies ran while one was open for 2% -> 1% of each run, Pallas kernels for 33% -> 38%
where the time goes in v9:
time: 128 us; the launch traced here: 127 us
  Pallas kernels  52.2 us (41%)
  waiting for transfers between devices  44.5 us (35%)
  starting transfers between devices  23.4 us (18%)
  local copies, waits for them, and re-layouts  3.57 us (3%)
  other arithmetic  2.68 us (2%)
    ppermute x21, waiting for transfers between devices, dense_body(): move = lambda a, pairs: lax.ppermute(a, 'expert', pairs)  40.6 us
    pallas_call x3, Pallas kernels, rows_call(): pl.pallas_call(functools.partial(rows_kernel, experts, count, sizes, join...  24.4 us
    ppermute x21, starting transfers between devices, dense_body(): move = lambda a, pairs: lax.ppermute(a, 'expert', pairs)  19.9 us
    pallas_call x3, Pallas kernels, half_call(): pl.pallas_call(functools.partial(half_kernel, len(blocks), len(kept), las...  19.4 us
    pallas_call x1, Pallas kernels, finish(): pl.pallas_call(finish_kernel, out_shape=[sds((size, hidden_units), F32),...  3.95 us
    ppermute x2, waiting for transfers between devices, dense_body(): across = lambda a: lax.ppermute(a, 'dp', [(0, 1), (1, 0)])  3.85 us
    unnamed x36, local copies, waits for them, and re-layouts  3.57 us
    ppermute x2, starting transfers between devices, dense_body(): across = lambda a: lax.ppermute(a, 'dp', [(0, 1), (1, 0)])  3.46 us
  transfers between devices with their start and end apart: 23, of which 10 were waited for; matrix products, arithmetic and copies ran while one was open for 1% of the time, Pallas kernels for 38%

profile of v9, /device:TPU:0, one launch (start us, length us, event | category | flops | bytes accessed | tf_op | source)
XLA Modules:
  0.0 127.3 jit_solution(9853255755365246016)
XLA Ops:
  0.6 2.0 %shard_map.102.refs_0_ = bf16[128,2176]{1,0:T(8,128)(2,1)} custom-call(bf16[128,1024]{1,0:T(8,128)(2,1)} %tokens.1, bf16[128,1024]{1,0:T(8,128)(2,1)} %d_output.1, f32[8,128]{1,0:T(8,128)} %bitcast.14, s32[8,128]{1,0:T(8,128)} %bitcast.15), custom_call_target="tpu_custom_call" | custom-call | bytes 1572864 | tf_op jit(solution)/shard_map/pallas_call | solution.py:63
  2.6 2.5 %shard_map.103.refs_4_.refs_3_.refs_1_ = bf16[512,1152]{1,0:T(8,128)(2,1)} custom-call(bf16[512,384]{1,0:T(8,128)(2,1)} %bitcast.11, bf16[512,384]{1,0:T(8,128)(2,1)} %bitcast.12, bf16[384,512]{1,0:T(8,128)(2,1)} %bitcast.13), custom_call_target="tpu_custom_call" | custom-call | bytes 47185920 | tf_op jit(solution)/shard_map/pallas_call | solution.py:82
  5.1 2.9 %collective-permute-start.4 = (bf16[512,1152]{1,0:T(8,128)(2,1)}, bf16[512,1152]{1,0:T(8,128)(2,1)}, u32[]{:S(2)}, u32[]{:S(2)}) collective-permute-start(bf16[512,1152]{1,0:T(8,128)(2,1)} %shard_map.103.refs_4_.refs_3_.refs_1_), channel_id=1, source_target_pairs={{0,16},{16,0},{1,17},{17,1},{2,18},{18,2},{3,19},{19,3},{4,20},{20... | collective-permute-start | bytes 3538952 | tf_op jit(solution)/shard_map/ppermute | solution.py:368
  8.0 1.6 %collective-permute-start = (bf16[128,2176]{1,0:T(8,128)(2,1)S(1)}, bf16[128,2176]{1,0:T(8,128)(2,1)S(1)}, u32[]{:S(2)}, u32[]{:S(2)}) collective-permute-start(bf16[128,2176]{1,0:T(8,128)(2,1)S(1)} %copy-done.2), channel_id=1, source_target_pairs={{0,4},{1,5},{2,6},{3,7},{4,0},{5,1},{6,2},{7,3},{8,12},{9,13},{10,... | collective-permute-start | bytes 1671176 | tf_op jit(solution)/shard_map/ppermute | solution.py:367
  9.6 1.5 %collective-permute-start.3 = (bf16[128,2176]{1,0:T(8,128)(2,1)S(1)}, bf16[128,2176]{1,0:T(8,128)(2,1)S(1)}, u32[]{:S(2)}, u32[]{:S(2)}) collective-permute-start(bf16[128,2176]{1,0:T(8,128)(2,1)S(1)} %copy-done.2), channel_id=1, source_target_pairs={{0,2},{1,3},{2,0},{3,1},{4,6},{5,7},{6,4},{7,5},{8,10},{9,11},{10,... | collective-permute-start | bytes 1671176 | tf_op jit(solution)/shard_map/ppermute | solution.py:367
  11.8 10.3 %collective-permute-done.refs_1_ = bf16[128,2176]{1,0:T(8,128)(2,1)S(1)} collective-permute-done((bf16[128,2176]{1,0:T(8,128)(2,1)S(1)}, bf16[128,2176]{1,0:T(8,128)(2,1)S(1)}, u32[]{:S(2)}, u32[]{:S(2)}) %collective-permute-start) | collective-permute-done | bytes 557088 | tf_op jit(solution)/shard_map/ppermute | solution.py:367
  22.1 1.3 %collective-permute-done.3.refs_3_ = bf16[128,2176]{1,0:T(8,128)(2,1)S(1)} collective-permute-done((bf16[128,2176]{1,0:T(8,128)(2,1)S(1)}, bf16[128,2176]{1,0:T(8,128)(2,1)S(1)}, u32[]{:S(2)}, u32[]{:S(2)}) %collective-permute-start.3) | collective-permute-done | bytes 557088 | tf_op jit(solution)/shard_map/ppermute | solution.py:367
  23.4 1.5 %collective-permute-start.5 = (bf16[128,2176]{1,0:T(8,128)(2,1)S(1)}, bf16[128,2176]{1,0:T(8,128)(2,1)S(1)}, u32[]{:S(2)}, u32[]{:S(2)}) collective-permute-start(bf16[128,2176]{1,0:T(8,128)(2,1)S(1)} %collective-permute-done.refs_1_), channel_id=1, source_target_pairs={{0,2},{1,3},{2,0},{3,1},{4,6},{5,7},{6,4},{7,5},{8,10},{9,11},{10,... | collective-permute-start | bytes 1671176 | tf_op jit(solution)/shard_map/ppermute | solution.py:367
  25.6 1.3 %collective-permute-start.2 = (bf16[128,2176]{1,0:T(8,128)(2,1)S(1)}, bf16[128,2176]{1,0:T(8,128)(2,1)S(1)}, u32[]{:S(2)}, u32[]{:S(2)}) collective-permute-start(bf16[128,2176]{1,0:T(8,128)(2,1)S(1)} %collective-permute-done.1), channel_id=1, source_target_pairs={{4,0},{5,1},{6,2},{7,3},{8,12},{9,13},{10,14},{11,15},{20,16},{21,... | collective-permute-start | bytes 1671176 | tf_op jit(solution)/shard_map/ppermute | solution.py:367
  26.9 9.5 %collective-permute-done.5.refs_1_.refs_5_ = bf16[128,2176]{1,0:T(8,128)(2,1)S(1)} collective-permute-done((bf16[128,2176]{1,0:T(8,128)(2,1)S(1)}, bf16[128,2176]{1,0:T(8,128)(2,1)S(1)}, u32[]{:S(2)}, u32[]{:S(2)}) %collective-permute-start.5) | collective-permute-done | bytes 557088 | tf_op jit(solution)/shard_map/ppermute | solution.py:367
  38.2 3.8 %collective-permute-done.2 = bf16[128,2176]{1,0:T(8,128)(2,1)S(1)} collective-permute-done((bf16[128,2176]{1,0:T(8,128)(2,1)S(1)}, bf16[128,2176]{1,0:T(8,128)(2,1)S(1)}, u32[]{:S(2)}, u32[]{:S(2)}) %collective-permute-start.2) | collective-permute-done | bytes 557088 | tf_op jit(solution)/shard_map/ppermute | solution.py:367
  42.6 1.3 %collective-permute-start.9 = (bf16[128,2176]{1,0:T(8,128)(2,1)S(1)}, bf16[128,2176]{1,0:T(8,128)(2,1)S(1)}, u32[]{:S(2)}, u32[]{:S(2)}) collective-permute-start(bf16[128,2176]{1,0:T(8,128)(2,1)S(1)} %collective-permute-done.6), channel_id=1, source_target_pairs={{4,0},{5,1},{6,2},{7,3},{8,12},{9,13},{10,14},{11,15},{20,16},{21,... | collective-permute-start | bytes 1671176 | tf_op jit(solution)/shard_map/ppermute | solution.py:367
  43.9 9.9 %shard_map.104 = (bf16[128,1024]{1,0:T(8,128)(2,1)}, bf16[128,1024]{1,0:T(8,128)(2,1)}, bf16[128,1024]{1,0:T(8,128)(2,1)}, bf16[128,1024]{1,0:T(8,128)(2,1)}, bf...) custom-call(s32[2]{0:T(128)} %pad_add_fusion.scal, ...), custom_call_target="tpu_custom_call" | custom-call | flops 14495514624 | bytes 1048576 | tf_op jit(solution)/shard_map/pallas_call | solution.py:183
  53.9 3.2 %collective-permute-done.9 = bf16[128,2176]{1,0:T(8,128)(2,1)S(1)} collective-permute-done((bf16[128,2176]{1,0:T(8,128)(2,1)S(1)}, bf16[128,2176]{1,0:T(8,128)(2,1)S(1)}, u32[]{:S(2)}, u32[]{:S(2)}) %collective-permute-start.9) | collective-permute-done | bytes 557088 | tf_op jit(solution)/shard_map/ppermute | solution.py:367
  57.2 1.6 %collective-permute-start.11 = (bf16[128,2176]{1,0:T(8,128)(2,1)S(1)}, bf16[128,2176]{1,0:T(8,128)(2,1)S(1)}, u32[]{:S(2)}, u32[]{:S(2)}) collective-permute-start(bf16[128,2176]{1,0:T(8,128)(2,1)S(1)} %broadcast_select_fusion.refs_0_.refs_4_), channel_id=1, source_target_pairs={{0,2},{1,3},{2,0},{3,1},{4,6},{5,7},{6,4},{7,5},{8,10},{9,11},{10,... | collective-permute-start | bytes 1671176 | tf_op jit(solution)/shard_map/ppermute | solution.py:367
  58.8 8.4 %shard_map.105 = (bf16[128,1024]{1,0:T(8,128)(2,1)}, bf16[256,1024]{1,0:T(8,128)(2,1)}, bf16[384,1152]{1,0:T(8,128)(2,1)}, bf16[384,1024]{1,0:T(8,128)(2,1)}, bf...) custom-call(s32[2]{0:T(128)} %pad_add_fusion.scal, bf16[128,2176]{1,0:T(8,128)(2,1)} %copy-done.1, ...), custom_call_target="tpu_custom_call" | custom-call | flops 10871635968 | bytes 1048576 | tf_op jit(solution)/shard_map/pallas_call | solution.py:183
  67.3 7.8 %shard_map.106 = bf16[1024,1152]{1,0:T(8,128)(2,1)} custom-call(s32[2]{0:T(128)} %pad_add_fusion.1.sides, bf16[128,2176]{1,0:T(8,128)(2,1)} %shard_map.102.refs_0_, bf16[128,2176]{1,0:T(8,128)(2,1)} %copy-done.4, bf16[128,2176]{1,0:T(8,128)(2,1)} %copy-done, bf16[128,2176]{1,0:T(8,128)(2,1)} %copy-done.5, bf16[128,2176]{1,0:T(8,128)(2,1)} %copy-done.1, ...), custom_call_target="tpu_custom_call" | custom-call | flops 1024 | bytes 1024 | tf_op jit(solution)/shard_map/pallas_call | solution.py:283
  76.0 6.0 %shard_map.107 = (bf16[128,1024]{1,0:T(8,128)(2,1)}, bf16[128,1152]{1,0:T(8,128)(2,1)}, bf16[128,1024]{1,0:T(8,128)(2,1)}, bf16[128,3200]{1,0:T(8,128)(2,1)}) custom-call(s32[2]{0:T(128)} %pad_add_fusion.scal, bf16[128,2176]{1,0:T(8,128)(2,1)} %copy-done.10, bf16[512,1152]{1,0:T(8,128)(2,1)} %shard_map.103.refs_4_.refs_3_.refs_1_, ...), custom_call_target="tpu_custom_call" | custom-call | flops 36238786560 | bytes 1048576 | tf_op jit(solution)/shard_map/pallas_call | solution.py:183
  83.4 1.3 collective-permute-done.12.refs_14_
  86.4 5.8 %shard_map.108 = bf16[512,1152]{1,0:T(8,128)(2,1)} custom-call(s32[1]{0:T(128)} %bitcast.7.sides, bf16[128,2176]{1,0:T(8,128)(2,1)} %shard_map.102.refs_0_, bf16[128,2176]{1,0:T(8,128)(2,1)} %copy-done.4, bf16[128,2176]{1,0:T(8,128)(2,1)} %copy-done, bf16[128,2176]{1,0:T(8,128)(2,1)} %copy-done.5, bf16[128,2176]{1,0:T(8,128)(2,1)} %copy-done.1, ...), custom_call_target="tpu_custom_call" | custom-call | flops 4831839232 | bytes 1024 | tf_op jit(solution)/shard_map/pallas_call | solution.py:283
  92.2 1.0 collective-permute-start.17
  93.7 3.6 %collective-permute-done.15 = bf16[256,1024]{1,0:T(8,128)(2,1)S(1)} collective-permute-done((bf16[256,1024]{1,0:T(8,128)(2,1)S(1)}, bf16[256,1024]{1,0:T(8,128)(2,1)S(1)}, u32[]{:S(2)}, u32[]{:S(2)}) %collective-permute-start.15) | collective-permute-done | bytes 524320 | tf_op jit(solution)/shard_map/ppermute | solution.py:367
  97.5 1.6 %collective-permute-start.16 = (bf16[128,1024]{1,0:T(8,128)(2,1)S(1)}, bf16[128,1024]{1,0:T(8,128)(2,1)S(1)}, u32[]{:S(2)}, u32[]{:S(2)}) collective-permute-start(bf16[128,1024]{1,0:T(8,128)(2,1)S(1)} %get-tuple-element.75), channel_id=1, source_target_pairs={{0,4},{1,5},{2,6},{3,7},{12,8},{13,9},{14,10},{15,11},{16,20},{17,... | collective-permute-start | bytes 786440 | tf_op jit(solution)/shard_map/ppermute | solution.py:367
  99.1 2.9 %collective-permute-done.17 = bf16[128,1024]{1,0:T(8,128)(2,1)S(1)} collective-permute-done((bf16[128,1024]{1,0:T(8,128)(2,1)S(1)}, bf16[128,1024]{1,0:T(8,128)(2,1)S(1)}, u32[]{:S(2)}, u32[]{:S(2)}) %collective-permute-start.17) | collective-permute-done | bytes 262176 | tf_op jit(solution)/shard_map/ppermute | solution.py:367
  102.1 1.5 %collective-permute-start.21 = (bf16[128,1024]{1,0:T(8,128)(2,1)S(1)}, bf16[128,1024]{1,0:T(8,128)(2,1)S(1)}, u32[]{:S(2)}, u32[]{:S(2)}) collective-permute-start(bf16[128,1024]{1,0:T(8,128)(2,1)S(1)} %add_convert_fusion.2), channel_id=1, source_target_pairs={{0,4},{1,5},{2,6},{3,7},{12,8},{13,9},{14,10},{15,11},{16,20},{17,... | collective-permute-start | bytes 786440 | tf_op jit(solution)/shard_map/ppermute | solution.py:367
  104.5 1.1 collective-permute-start.18
  105.6 4.8 %collective-permute-done.21 = bf16[128,1024]{1,0:T(8,128)(2,1)S(1)} collective-permute-done((bf16[128,1024]{1,0:T(8,128)(2,1)S(1)}, bf16[128,1024]{1,0:T(8,128)(2,1)S(1)}, u32[]{:S(2)}, u32[]{:S(2)}) %collective-permute-start.21) | collective-permute-done | bytes 262176 | tf_op jit(solution)/shard_map/ppermute | solution.py:367
  110.4 1.3 %collective-permute-start.22 = (bf16[128,1024]{1,0:T(8,128)(2,1)S(1)}, bf16[128,1024]{1,0:T(8,128)(2,1)S(1)}, u32[]{:S(2)}, u32[]{:S(2)}) collective-permute-start(bf16[128,1024]{1,0:T(8,128)(2,1)S(1)} %add_convert_fusion.1), channel_id=1, source_target_pairs={{4,12},{5,13},{6,14},{7,15},{8,0},{9,1},{10,2},{11,3},{20,28},{21,... | collective-permute-start | bytes 786440 | tf_op jit(solution)/shard_map/ppermute | solution.py:367
  111.7 5.8 %shard_map.109.keep = bf16[512,1152]{1,0:T(8,128)(2,1)} custom-call(s32[1]{0:T(128)} %bitcast.sides, bf16[128,2176]{1,0:T(8,128)(2,1)} %shard_map.102.refs_0_, bf16[128,2176]{1,0:T(8,128)(2,1)} %copy-done.4, bf16[128,2176]{1,0:T(8,128)(2,1)} %copy-done, bf16[128,2176]{1,0:T(8,128)(2,1)} %copy-done.5, bf16[128,2176]{1,0:T(8,128)(2,1)} %copy-done.1, ...), custom_call_target="tpu_custom_call" | custom-call | flops 1024 | bytes 1024 | tf_op jit(solution)/shard_map/pallas_call | solution.py:283
  117.5 3.8 %collective-permute-done.14.from_part = bf16[512,1152]{1,0:T(8,128)(2,1)S(1)} collective-permute-done((bf16[512,1152]{1,0:T(8,128)(2,1)}, bf16[512,1152]{1,0:T(8,128)(2,1)S(1)}, u32[]{:S(2)}, u32[]{:S(2)}) %collective-permute-start.14) | collective-permute-done | bytes 1179680 | tf_op jit(solution)/shard_map/ppermute | solution.py:368
  121.4 1.0 copy-done.8
  122.4 3.9 %shard_map.110 = (f32[512,384]{1,0:T(8,128)}, f32[512,384]{1,0:T(8,128)}, f32[384,512]{1,0:T(8,128)}) custom-call(bf16[512,1152]{1,0:T(8,128)(2,1)} %shard_map.109.keep, bf16[512,1152]{1,0:T(8,128)(2,1)} %copy-done.8), custom_call_target="tpu_custom_call" | custom-call | flops 1024 | bytes 1024 | tf_op jit(solution)/shard_map/pallas_call | solution.py:315
  (68 shorter events, 10.5 us)
Async XLA Ops:
  5.1 31.3 %collective-permute-start.4 = (bf16[512,1152]{1,0:T(8,128)(2,1)}, bf16[512,1152]{1,0:T(8,128)(2,1)}, u32[]{:S(2)}, u32[]{:S(2)}) collective-permute-start(bf16[512,1152]{1,0:T(8,128)(2,1)} %shard_map.103.refs_4_.refs_3_.refs_1_), channel_id=1, source_target_pairs={{0,16},{16,0},{1,17},{17,1},{2,18},{18,2},{3,19},{19,3},{4,20},{20... | collective-permute-start | bytes 3538952 | tf_op jit(solution)/shard_map/ppermute | solution.py:368
  8.0 14.1 %collective-permute-start = (bf16[128,2176]{1,0:T(8,128)(2,1)S(1)}, bf16[128,2176]{1,0:T(8,128)(2,1)S(1)}, u32[]{:S(2)}, u32[]{:S(2)}) collective-permute-start(bf16[128,2176]{1,0:T(8,128)(2,1)S(1)} %copy-done.2), channel_id=1, source_target_pairs={{0,4},{1,5},{2,6},{3,7},{4,0},{5,1},{6,2},{7,3},{8,12},{9,13},{10,... | collective-permute-start | bytes 1671176 | tf_op jit(solution)/shard_map/ppermute | solution.py:367
  9.6 13.8 %collective-permute-start.3 = (bf16[128,2176]{1,0:T(8,128)(2,1)S(1)}, bf16[128,2176]{1,0:T(8,128)(2,1)S(1)}, u32[]{:S(2)}, u32[]{:S(2)}) collective-permute-start(bf16[128,2176]{1,0:T(8,128)(2,1)S(1)} %copy-done.2), channel_id=1, source_target_pairs={{0,2},{1,3},{2,0},{3,1},{4,6},{5,7},{6,4},{7,5},{8,10},{9,11},{10,... | collective-permute-start | bytes 1671176 | tf_op jit(solution)/shard_map/ppermute | solution.py:367
  11.1 14.5 %collective-permute-start.1 = (bf16[128,2176]{1,0:T(8,128)(2,1)S(1)}, bf16[128,2176]{1,0:T(8,128)(2,1)S(1)}, u32[]{:S(2)}, u32[]{:S(2)}) collective-permute-start(bf16[128,2176]{1,0:T(8,128)(2,1)S(1)} %copy-done.2), channel_id=1, source_target_pairs={{4,8},{5,9},{6,10},{7,11},{8,4},{9,5},{10,6},{11,7},{20,24},{21,25... | collective-permute-start | bytes 1671176 | tf_op jit(solution)/shard_map/ppermute | solution.py:367
  22.1 21.8 %copy-start.4 = (bf16[128,2176]{1,0:T(8,128)(2,1)}, bf16[128,2176]{1,0:T(8,128)(2,1)S(1)}, u32[]{:S(2)}) copy-start(bf16[128,2176]{1,0:T(8,128)(2,1)S(1)} %collective-permute-done.refs_1_) | copy-start | bytes 1671172
  23.4 20.5 %copy-start.5 = (bf16[128,2176]{1,0:T(8,128)(2,1)}, bf16[128,2176]{1,0:T(8,128)(2,1)S(1)}, u32[]{:S(2)}) copy-start(bf16[128,2176]{1,0:T(8,128)(2,1)S(1)} %collective-permute-done.3.refs_3_) | copy-start | bytes 1671172
  23.4 13.0 %collective-permute-start.5 = (bf16[128,2176]{1,0:T(8,128)(2,1)S(1)}, bf16[128,2176]{1,0:T(8,128)(2,1)S(1)}, u32[]{:S(2)}, u32[]{:S(2)}) collective-permute-start(bf16[128,2176]{1,0:T(8,128)(2,1)S(1)} %collective-permute-done.refs_1_), channel_id=1, source_target_pairs={{0,2},{1,3},{2,0},{3,1},{4,6},{5,7},{6,4},{7,5},{8,10},{9,11},{10,... | collective-permute-start | bytes 1671176 | tf_op jit(solution)/shard_map/ppermute | solution.py:367
  24.9 11.5 %collective-permute-start.6 = (bf16[128,2176]{1,0:T(8,128)(2,1)S(1)}, bf16[128,2176]{1,0:T(8,128)(2,1)S(1)}, u32[]{:S(2)}, u32[]{:S(2)}) collective-permute-start(bf16[128,2176]{1,0:T(8,128)(2,1)S(1)} %collective-permute-done.refs_1_), channel_id=1, source_target_pairs={{4,8},{5,9},{6,10},{7,11},{8,4},{9,5},{10,6},{11,7},{20,24},{21,25... | collective-permute-start | bytes 1671176 | tf_op jit(solution)/shard_map/ppermute | solution.py:367
  25.6 16.3 %collective-permute-start.2 = (bf16[128,2176]{1,0:T(8,128)(2,1)S(1)}, bf16[128,2176]{1,0:T(8,128)(2,1)S(1)}, u32[]{:S(2)}, u32[]{:S(2)}) collective-permute-start(bf16[128,2176]{1,0:T(8,128)(2,1)S(1)} %collective-permute-done.1), channel_id=1, source_target_pairs={{4,0},{5,1},{6,2},{7,3},{8,12},{9,13},{10,14},{11,15},{20,16},{21,... | collective-permute-start | bytes 1671176 | tf_op jit(solution)/shard_map/ppermute | solution.py:367
  36.4 17.5 %copy-start.6 = (bf16[128,2176]{1,0:T(8,128)(2,1)}, bf16[128,2176]{1,0:T(8,128)(2,1)S(1)}, u32[]{:S(2)}) copy-start(bf16[128,2176]{1,0:T(8,128)(2,1)S(1)} %collective-permute-done.5.refs_1_.refs_5_) | copy-start | bytes 1671172
  36.4 7.5 %collective-permute-start.7 = (bf16[512,1152]{1,0:T(8,128)(2,1)}, bf16[512,1152]{1,0:T(8,128)(2,1)}, u32[]{:S(2)}, u32[]{:S(2)}) collective-permute-start(bf16[512,1152]{1,0:T(8,128)(2,1)} %shard_map.103.refs_4_.refs_3_.refs_1_), channel_id=1, source_target_pairs={{0,1},{1,0},{2,3},{3,2},{4,5},{5,4},{6,7},{7,6},{8,9},{9,8},{10,11... | collective-permute-start | bytes 3538952 | tf_op jit(solution)/shard_map/ppermute | solution.py:367
  36.4 7.5 %collective-permute-start.8 = (bf16[512,1152]{1,0:T(8,128)(2,1)}, bf16[512,1152]{1,0:T(8,128)(2,1)}, u32[]{:S(2)}, u32[]{:S(2)}) collective-permute-start(bf16[512,1152]{1,0:T(8,128)(2,1)} %collective-permute-done.4.refs_5_.refs_4_.refs_2_), channel_id=1, source_target_pairs={{0,1},{1,0},{2,3},{3,2},{4,5},{5,4},{6,7},{7,6},{8,9},{9,8},{10,11... | collective-permute-start | bytes 3538952 | tf_op jit(solution)/shard_map/ppermute | solution.py:367
  42.0 15.2 %collective-permute-start.10 = (bf16[128,2176]{1,0:T(8,128)(2,1)S(1)}, bf16[128,2176]{1,0:T(8,128)(2,1)S(1)}, u32[]{:S(2)}, u32[]{:S(2)}) collective-permute-start(bf16[128,2176]{1,0:T(8,128)(2,1)S(1)} %broadcast_select_fusion.1.refs_2_), channel_id=1, source_target_pairs={{0,2},{1,3},{2,0},{3,1},{4,6},{5,7},{6,4},{7,5},{8,10},{9,11},{10,... | collective-permute-start | bytes 1671176 | tf_op jit(solution)/shard_map/ppermute | solution.py:367
  42.6 14.5 %collective-permute-start.9 = (bf16[128,2176]{1,0:T(8,128)(2,1)S(1)}, bf16[128,2176]{1,0:T(8,128)(2,1)S(1)}, u32[]{:S(2)}, u32[]{:S(2)}) collective-permute-start(bf16[128,2176]{1,0:T(8,128)(2,1)S(1)} %collective-permute-done.6), channel_id=1, source_target_pairs={{4,0},{5,1},{6,2},{7,3},{8,12},{9,13},{10,14},{11,15},{20,16},{21,... | collective-permute-start | bytes 1671176 | tf_op jit(solution)/shard_map/ppermute | solution.py:367
  57.2 18.0 %collective-permute-start.11 = (bf16[128,2176]{1,0:T(8,128)(2,1)S(1)}, bf16[128,2176]{1,0:T(8,128)(2,1)S(1)}, u32[]{:S(2)}, u32[]{:S(2)}) collective-permute-start(bf16[128,2176]{1,0:T(8,128)(2,1)S(1)} %broadcast_select_fusion.refs_0_.refs_4_), channel_id=1, source_target_pairs={{0,2},{1,3},{2,0},{3,1},{4,6},{5,7},{6,4},{7,5},{8,10},{9,11},{10,... | collective-permute-start | bytes 1671176 | tf_op jit(solution)/shard_map/ppermute | solution.py:367
  75.1 9.6 %collective-permute-start.13 = (bf16[1024,1152]{1,0:T(8,128)(2,1)}, bf16[1024,1152]{1,0:T(8,128)(2,1)S(1)}, u32[]{:S(2)}, u32[]{:S(2)}) collective-permute-start(bf16[1024,1152]{1,0:T(8,128)(2,1)} %shard_map.106), channel_id=1, source_target_pairs={{0,1},{1,0},{2,3},{3,2},{4,5},{5,4},{6,7},{7,6},{8,9},{9,8},{10,11... | collective-permute-start | bytes 7077896 | tf_op jit(solution)/shard_map/ppermute | solution.py:367
  76.0 6.5 %copy-start.15 = (bf16[256,1024]{1,0:T(8,128)(2,1)S(1)}, bf16[256,1024]{1,0:T(8,128)(2,1)}, u32[]{:S(2)}) copy-start(bf16[256,1024]{1,0:T(8,128)(2,1)} %get-tuple-element.62) | copy-start | bytes 1572868
  82.0 2.7 %collective-permute-start.12 = (bf16[128,3200]{1,0:T(8,128)(2,1)}, bf16[128,3200]{1,0:T(8,128)(2,1)S(1)}, u32[]{:S(2)}, u32[]{:S(2)}) collective-permute-start(bf16[128,3200]{1,0:T(8,128)(2,1)} %get-tuple-element.59), channel_id=1, source_target_pairs={{0,1},{1,0},{2,3},{3,2},{4,5},{5,4},{6,7},{7,6},{8,9},{9,8},{10,11... | collective-permute-start | bytes 2457608 | tf_op jit(solution)/shard_map/ppermute | solution.py:367
  82.5 14.8 %collective-permute-start.15 = (bf16[256,1024]{1,0:T(8,128)(2,1)S(1)}, bf16[256,1024]{1,0:T(8,128)(2,1)S(1)}, u32[]{:S(2)}, u32[]{:S(2)}) collective-permute-start(bf16[256,1024]{1,0:T(8,128)(2,1)S(1)} %copy-done.15), channel_id=1, source_target_pairs={{0,2},{1,3},{2,0},{3,1},{4,6},{5,7},{6,4},{7,5},{8,10},{9,11},{10,... | collective-permute-start | bytes 1572872 | tf_op jit(solution)/shard_map/ppermute | solution.py:367
  86.4 10.9 %copy-start.13 = (bf16[128,1024]{1,0:T(8,128)(2,1)S(1)}, bf16[128,1024]{1,0:T(8,128)(2,1)}, u32[]{:S(2)}) copy-start(bf16[128,1024]{1,0:T(8,128)(2,1)} %get-tuple-element.70) | copy-start | bytes 786436
  86.4 10.9 %copy-start.14 = (bf16[128,1024]{1,0:T(8,128)(2,1)S(1)}, bf16[128,1024]{1,0:T(8,128)(2,1)}, u32[]{:S(2)}) copy-start(bf16[128,1024]{1,0:T(8,128)(2,1)} %get-tuple-element.61) | copy-start | bytes 786436
  92.2 9.9 %copy-start.11 = (bf16[128,1024]{1,0:T(8,128)(2,1)S(1)}, bf16[128,1024]{1,0:T(8,128)(2,1)}, u32[]{:S(2)}) copy-start(bf16[128,1024]{1,0:T(8,128)(2,1)} %get-tuple-element.71) | copy-start | bytes 786436
  92.2 9.8 %collective-permute-start.17 = (bf16[128,1024]{1,0:T(8,128)(2,1)S(1)}, bf16[128,1024]{1,0:T(8,128)(2,1)S(1)}, u32[]{:S(2)}, u32[]{:S(2)}) collective-permute-start(bf16[128,1024]{1,0:T(8,128)(2,1)S(1)} %copy-done.17), channel_id=1, source_target_pairs={{0,2},{1,3},{2,0},{3,1},{4,6},{5,7},{6,4},{7,5},{8,10},{9,11},{10,... | collective-permute-start | bytes 786440 | tf_op jit(solution)/shard_map/ppermute | solution.py:367
  93.2 28.2 %collective-permute-start.14 = (bf16[512,1152]{1,0:T(8,128)(2,1)}, bf16[512,1152]{1,0:T(8,128)(2,1)S(1)}, u32[]{:S(2)}, u32[]{:S(2)}) collective-permute-start(bf16[512,1152]{1,0:T(8,128)(2,1)} %shard_map.108), channel_id=1, source_target_pairs={{0,16},{16,0},{1,17},{17,1},{2,18},{18,2},{3,19},{19,3},{4,20},{20... | collective-permute-start | bytes 3538952 | tf_op jit(solution)/shard_map/ppermute | solution.py:368
  97.5 7.0 %copy-start.16 = (bf16[128,1024]{1,0:T(8,128)(2,1)S(1)}, bf16[128,1024]{1,0:T(8,128)(2,1)}, u32[]{:S(2)}) copy-start(bf16[128,1024]{1,0:T(8,128)(2,1)} %get-tuple-element.69) | copy-start | bytes 786436
  97.5 6.2 %collective-permute-start.16 = (bf16[128,1024]{1,0:T(8,128)(2,1)S(1)}, bf16[128,1024]{1,0:T(8,128)(2,1)S(1)}, u32[]{:S(2)}, u32[]{:S(2)}) collective-permute-start(bf16[128,1024]{1,0:T(8,128)(2,1)S(1)} %get-tuple-element.75), channel_id=1, source_target_pairs={{0,4},{1,5},{2,6},{3,7},{12,8},{13,9},{14,10},{15,11},{16,20},{17,... | collective-permute-start | bytes 786440 | tf_op jit(solution)/shard_map/ppermute | solution.py:367
  102.1 8.2 %collective-permute-start.21 = (bf16[128,1024]{1,0:T(8,128)(2,1)S(1)}, bf16[128,1024]{1,0:T(8,128)(2,1)S(1)}, u32[]{:S(2)}, u32[]{:S(2)}) collective-permute-start(bf16[128,1024]{1,0:T(8,128)(2,1)S(1)} %add_convert_fusion.2), channel_id=1, source_target_pairs={{0,4},{1,5},{2,6},{3,7},{12,8},{13,9},{14,10},{15,11},{16,20},{17,... | collective-permute-start | bytes 786440 | tf_op jit(solution)/shard_map/ppermute | solution.py:367
  103.6 22.7 %collective-permute-start.19 = (bf16[128,1024]{1,0:T(8,128)(2,1)S(1)}, bf16[128,1024]{1,0:T(8,128)(2,1)S(1)}, u32[]{:S(2)}, u32[]{:S(2)}) collective-permute-start(bf16[128,1024]{1,0:T(8,128)(2,1)S(1)} %get-tuple-element.74), channel_id=1, source_target_pairs={{0,4},{1,5},{2,6},{3,7},{4,0},{5,1},{6,2},{7,3},{8,12},{9,13},{10,... | collective-permute-start | bytes 786440 | tf_op jit(solution)/shard_map/ppermute | solution.py:367
  103.8 22.6 %collective-permute-start.20 = (bf16[128,1024]{1,0:T(8,128)(2,1)S(1)}, bf16[128,1024]{1,0:T(8,128)(2,1)S(1)}, u32[]{:S(2)}, u32[]{:S(2)}) collective-permute-start(bf16[128,1024]{1,0:T(8,128)(2,1)S(1)} %add_convert_fusion.4), channel_id=1, source_target_pairs={{4,8},{5,9},{6,10},{7,11},{8,4},{9,5},{10,6},{11,7},{20,24},{21,25... | collective-permute-start | bytes 786440 | tf_op jit(solution)/shard_map/ppermute | solution.py:367
  104.5 21.9 %collective-permute-start.18 = (bf16[128,1024]{1,0:T(8,128)(2,1)S(1)}, bf16[128,1024]{1,0:T(8,128)(2,1)S(1)}, u32[]{:S(2)}, u32[]{:S(2)}) collective-permute-start(bf16[128,1024]{1,0:T(8,128)(2,1)S(1)} %copy-done.16), channel_id=1, source_target_pairs={{0,2},{1,3},{2,0},{3,1},{4,6},{5,7},{6,4},{7,5},{8,10},{9,11},{10,... | collective-permute-start | bytes 786440 | tf_op jit(solution)/shard_map/ppermute | solution.py:367
  110.4 16.0 %collective-permute-start.22 = (bf16[128,1024]{1,0:T(8,128)(2,1)S(1)}, bf16[128,1024]{1,0:T(8,128)(2,1)S(1)}, u32[]{:S(2)}, u32[]{:S(2)}) collective-permute-start(bf16[128,1024]{1,0:T(8,128)(2,1)S(1)} %add_convert_fusion.1), channel_id=1, source_target_pairs={{4,12},{5,13},{6,14},{7,15},{8,0},{9,1},{10,2},{11,3},{20,28},{21,... | collective-permute-start | bytes 786440 | tf_op jit(solution)/shard_map/ppermute | solution.py:367
  117.5 8.9 %copy-start.12 = (bf16[128,1024]{1,0:T(8,128)(2,1)S(1)}, bf16[128,1024]{1,0:T(8,128)(2,1)}, u32[]{:S(2)}) copy-start(bf16[128,1024]{1,0:T(8,128)(2,1)} %get-tuple-element.65) | copy-start | bytes 786436
  (9 other events, 20.8 us)

commit v10 on v9

--- a/solution.py
+++ b/solution.py
@@ -37,10 +37,22 @@
     return lax.dot_general(a, b, (dims, ((), ())), preferred_element_type=F32)
 
 
-def pack_kernel(experts, tokens, d_output, combine, routes, out):
+def pack_kernel(experts, tokens, d_output, combine, routes, gate, up, down, out, w_out, parts, turned, sems):
     rows, width = tokens.shape
-    out[:, :width] = tokens[...]
-    out[:, width : 2 * width] = d_output[...]
+    hidden_units = gate.shape[1]
+    copies = []
+
+    def start(source, target):
+        copy = pltpu.make_async_copy(source, target, sems.at[len(copies)])
+        copy.start()
+        copies.append(copy)
+
+    start(tokens, out.at[:, pl.ds(0, width)])
+    start(d_output, out.at[:, pl.ds(width, width)])
+    start(gate, w_out.at[:, pl.ds(0, hidden_units)])
+    start(up, w_out.at[:, pl.ds(hidden_units, hidden_units)])
+    turned[...] = down[...].T
+    start(turned, w_out.at[:, pl.ds(2 * hidden_units, hidden_units)])
     line = lax.broadcasted_iota(jnp.int32, (LANES, rows), 0)
     expert = lax.rem(line, experts)
     dense = jnp.zeros((LANES, rows), F32)
@@ -50,43 +62,36 @@
     rest = dense - high
     middle = rest.astype(BF16).astype(F32)
     low = rest - middle
-    parts = jnp.where(
+    whole = jnp.where(
         line < experts,
         high,
         jnp.where(line < 2 * experts, middle, jnp.where(line < 3 * experts, low, 0.0)),
     )
-    out[:, 2 * width :] = parts.T.astype(BF16)
-
-
-def pack(experts, tokens, d_output, combine, routes):
+    parts[...] = whole.T.astype(BF16)
+    start(parts, out.at[:, pl.ds(2 * width, LANES)])
+    for c in copies:
+        c.wait()
+
+
+def pack(experts, tokens, d_output, combine, routes, gate, up, down):
     rows, width = tokens.shape
+    size, hidden_units = gate.shape
     return pl.pallas_call(
         functools.partial(pack_kernel, experts),
-        out_shape=jax.ShapeDtypeStruct((rows, 2 * width + LANES), BF16),
-        in_specs=[vmem()] * 4,
-        out_specs=vmem(),
-        cost_estimate=cost(0, 3 * rows * width * 2 * 2),
+        out_shape=[
+            jax.ShapeDtypeStruct((rows, 2 * width + LANES), BF16),
+            jax.ShapeDtypeStruct((size, 3 * hidden_units), BF16),
+        ],
+        in_specs=[hbm(), hbm(), vmem(), vmem(), hbm(), hbm(), vmem()],
+        out_specs=[hbm(), hbm()],
+        scratch_shapes=[
+            pltpu.VMEM((rows, LANES), BF16),
+            pltpu.VMEM((size, hidden_units), BF16),
+            pltpu.SemaphoreType.DMA((6,)),
+        ],
+        cost_estimate=cost(0, 1 << 20),
         compiler_params=params(),
-    )(tokens, d_output, combine.T, routes.T)
-
-
-def pack_weights_kernel(gate, up, down, out):
-    hidden_units = gate.shape[1]
-    out[:, :hidden_units] = gate[...]
-    out[:, hidden_units : 2 * hidden_units] = up[...]
-    out[:, 2 * hidden_units :] = down[...].T
-
-
-def pack_weights(gate, up, down):
-    size, hidden_units = gate.shape
-    return pl.pallas_call(
-        pack_weights_kernel,
-        out_shape=jax.ShapeDtypeStruct((size, 3 * hidden_units), BF16),
-        in_specs=[vmem()] * 3,
-        out_specs=vmem(),
-        cost_estimate=cost(0, 6 * size * hidden_units * 40),
-        compiler_params=params(),
-    )(gate, up, down)
+    )(tokens, d_output, combine.T, routes.T, gate, up, down)
 
 
 def rows_kernel(experts, count, sizes, joined, scal, *refs):
@@ -298,31 +303,6 @@
     )(sides, *operands)
 
 
-def finish_kernel(keep, from_part, d_gate, d_up, d_down):
-    hidden_units = d_gate.shape[1]
-    whole = keep[...].astype(F32) + from_part[...].astype(F32)
-    d_gate[...] = whole[:, :hidden_units]
-    d_up[...] = whole[:, hidden_units : 2 * hidden_units]
-    d_down[...] = whole[:, 2 * hidden_units :].T
-
-
-def finish(keep, from_part):
-    size, stacked = keep.shape
-    hidden_units = stacked // 3
-    sds = jax.ShapeDtypeStruct
-    step = size // 4
-    piece = lambda n: pl.BlockSpec((step, n), lambda i: (i, 0))
-    return pl.pallas_call(
-        finish_kernel,
-        out_shape=[sds((size, hidden_units), F32), sds((size, hidden_units), F32), sds((hidden_units, size), F32)],
-        grid=(size // step,),
-        in_specs=[piece(stacked)] * 2,
-        out_specs=[piece(hidden_units), piece(hidden_units), pl.BlockSpec((hidden_units, step), lambda i: (0, i))],
-        cost_estimate=cost(1024, 1024),
-        compiler_params=params(),
-    )(keep, from_part)
-
-
 Z, Y, CORES = 4, 2, 2
 
 
@@ -368,13 +348,12 @@
     across = lambda a: lax.ppermute(a, "dp", [(0, 1), (1, 0)])
 
     swap = lambda a: move(a, SWAP_CORE)
-    own = pack(experts, tokens, d_output, combine, routes)
+    own, w_own = pack(experts, tokens, d_output, combine, routes, gate_weight[0], up_weight[0], down_weight[0])
+    w_part = across(w_own)
 
     b1 = move(own, OUTER)
     f1 = move(own, INNER)
     y0 = move(own, SWAP_Y)
-    w_own = pack_weights(after(gate_weight[0], own), up_weight[0], down_weight[0])
-    w_part = across(w_own)
     f2 = move(b1, INNER)
     y1 = move(after(b1, y0), SWAP_Y)
     g1 = move(f1, OUTWARD)
@@ -415,8 +394,11 @@
     s2 = add(s2, move(s2, INWARD))
     s3 = add(p3, r3)
     s3 = add(s3, move(s3, INWARD))
-    d_gate, d_up, d_down = finish(keep, after(from_part, s2))
-    d_tokens = add(after(p0, d_gate), r0, move(s1, OUTER), move(s2, INNER), move(s3, SKIP_TO_OUTER))
+    d_weights = keep.astype(F32) + after(from_part, s2).astype(F32)
+    hidden_units = gate_weight.shape[2]
+    d_gate, d_up = d_weights[:, :hidden_units], d_weights[:, hidden_units : 2 * hidden_units]
+    d_down = d_weights[:, 2 * hidden_units :].T
+    d_tokens = add(after(p0, d_weights), r0, move(s1, OUTER), move(s2, INNER), move(s3, SKIP_TO_OUTER))
     return (d_tokens, d_gate[None], d_up[None], d_down[None])
 
 

time: 128 us -> 164 us (1.28)
  Pallas kernels: 52.2 us -> 85.8 us
    pallas_call x3 -> x1, Pallas kernels: 8.39 us -> 41.9 us  [pack(): pl.pallas_call(functools.partial(pack_kernel, experts), out_shape=[jax.Sh...]
    ppermute x21, waiting for transfers between devices: 40.6 us -> 36.3 us  [dense_body(): move = lambda a, pairs: lax.ppermute(a, 'expert', pairs)]
    ppermute x2, waiting for transfers between devices: 3.85 us -> 7.85 us  [dense_body(): across = lambda a: lax.ppermute(a, 'dp', [(0, 1), (1, 0)])]
    unnamed x36 -> x33, local copies, waits for them, and re-layouts: 3.57 us -> 3.66 us
  transfers between devices with their start and end apart: 23 -> 23, of which waited for: 10 -> 9; matrix products, arithmetic and copies ran while one was open for 1% -> 3% of each run, Pallas kernels for 38% -> 27%
where the time goes in v10:
time: 164 us; the launch traced here: 163 us
  Pallas kernels  85.8 us (52%)
  waiting for transfers between devices  44.1 us (27%)
  starting transfers between devices  23.4 us (14%)
  local copies, waits for them, and re-layouts  4.96 us (3%)
  other arithmetic  4.14 us (3%)
    pallas_call x1, Pallas kernels, pack(): pl.pallas_call(functools.partial(pack_kernel, experts), out_shape=[jax.Sh...  41.9 us
    ppermute x21, waiting for transfers between devices, dense_body(): move = lambda a, pairs: lax.ppermute(a, 'expert', pairs)  36.3 us
    pallas_call x3, Pallas kernels, rows_call(): pl.pallas_call(functools.partial(rows_kernel, experts, count, sizes, join...  24.4 us
    ppermute x21, starting transfers between devices, dense_body(): move = lambda a, pairs: lax.ppermute(a, 'expert', pairs)  19.8 us
    pallas_call x3, Pallas kernels, half_call(): pl.pallas_call(functools.partial(half_kernel, len(blocks), len(kept), las...  19.5 us
    ppermute x2, waiting for transfers between devices, dense_body(): across = lambda a: lax.ppermute(a, 'dp', [(0, 1), (1, 0)])  7.85 us
    unnamed x33, local copies, waits for them, and re-layouts  3.66 us
    ppermute x2, starting transfers between devices, dense_body(): across = lambda a: lax.ppermute(a, 'dp', [(0, 1), (1, 0)])  3.6 us
  transfers between devices with their start and end apart: 23, of which 9 were waited for; matrix products, arithmetic and copies ran while one was open for 3% of the time, Pallas kernels for 27%

profile of v10, /device:TPU:0, one launch (start us, length us, event | category | flops | bytes accessed | tf_op | source)
XLA Modules:
  0.0 163.4 jit_solution(3892775950073572035)
XLA Ops:
  0.6 41.9 %shard_map.102 = (bf16[128,2176]{1,0:T(8,128)(2,1)}, bf16[512,1152]{1,0:T(8,128)(2,1)}) custom-call(bf16[128,1024]{1,0:T(8,128)(2,1)} %tokens.1, bf16[128,1024]{1,0:T(8,128)(2,1)} %d_output.1, f32[8,128]{1,0:T(8,128)} %bitcast.19, s32[8,128]{1,0:T(8,128)} %bitcast.20, bf16[512,384]{1,0:T(8,128)(2,1)} %bitcast.16, bf16[512,384]{1,0:T(8,128)(2,1)} %bitcast.17, ...), custom_call_target="tpu_custom_call" | custom-call | bytes 1048576 | tf_op jit(solution)/shard_map/pallas_call | solution.py:79
  42.5 3.0 %collective-permute-start.4 = (bf16[512,1152]{1,0:T(8,128)(2,1)}, bf16[512,1152]{1,0:T(8,128)(2,1)}, u32[]{:S(2)}, u32[]{:S(2)}) collective-permute-start(bf16[512,1152]{1,0:T(8,128)(2,1)} %get-tuple-element.40.refs_4_.refs_3_.refs_1_), channel_id=1, source_target_pairs={{0,16},{16,0},{1,17},{17,1},{2,18},{18,2},{3,19},{19,3},{4,20},{20... | collective-permute-start | bytes 3538952 | tf_op jit(solution)/shard_map/ppermute | solution.py:348
  45.5 1.6 collective-permute-start
  47.1 1.5 collective-permute-start.3
  49.3 10.5 %collective-permute-done.refs_1_ = bf16[128,2176]{1,0:T(8,128)(2,1)S(1)} collective-permute-done((bf16[128,2176]{1,0:T(8,128)(2,1)}, bf16[128,2176]{1,0:T(8,128)(2,1)S(1)}, u32[]{:S(2)}, u32[]{:S(2)}) %collective-permute-start) | collective-permute-done | bytes 557088 | tf_op jit(solution)/shard_map/ppermute | solution.py:347
  59.8 1.3 collective-permute-done.3.refs_3_
  61.1 1.5 collective-permute-start.5
  63.4 1.3 collective-permute-start.2
  64.7 9.5 %collective-permute-done.5.refs_1_.refs_5_ = bf16[128,2176]{1,0:T(8,128)(2,1)S(1)} collective-permute-done((bf16[128,2176]{1,0:T(8,128)(2,1)S(1)}, bf16[128,2176]{1,0:T(8,128)(2,1)S(1)}, u32[]{:S(2)}, u32[]{:S(2)}) %collective-permute-start.5) | collective-permute-done | bytes 557088 | tf_op jit(solution)/shard_map/ppermute | solution.py:347
  75.8 3.8 %collective-permute-done.2 = bf16[128,2176]{1,0:T(8,128)(2,1)S(1)} collective-permute-done((bf16[128,2176]{1,0:T(8,128)(2,1)S(1)}, bf16[128,2176]{1,0:T(8,128)(2,1)S(1)}, u32[]{:S(2)}, u32[]{:S(2)}) %collective-permute-start.2) | collective-permute-done | bytes 557088 | tf_op jit(solution)/shard_map/ppermute | solution.py:347
  80.3 1.3 collective-permute-start.9
  81.7 10.0 %shard_map.103 = (bf16[128,1024]{1,0:T(8,128)(2,1)}, bf16[128,1024]{1,0:T(8,128)(2,1)}, bf16[128,1024]{1,0:T(8,128)(2,1)}, bf16[128,1024]{1,0:T(8,128)(2,1)}, bf...) custom-call(s32[2]{0:T(128)} %pad_add_fusion.scal, ...), custom_call_target="tpu_custom_call" | custom-call | flops 14495514624 | bytes 1048576 | tf_op jit(solution)/shard_map/pallas_call | solution.py:188
  91.6 3.2 %collective-permute-done.9 = bf16[128,2176]{1,0:T(8,128)(2,1)S(1)} collective-permute-done((bf16[128,2176]{1,0:T(8,128)(2,1)S(1)}, bf16[128,2176]{1,0:T(8,128)(2,1)S(1)}, u32[]{:S(2)}, u32[]{:S(2)}) %collective-permute-start.9) | collective-permute-done | bytes 557088 | tf_op jit(solution)/shard_map/ppermute | solution.py:347
  94.9 1.6 collective-permute-start.11
  96.5 8.5 %shard_map.104 = (bf16[128,1024]{1,0:T(8,128)(2,1)}, bf16[256,1024]{1,0:T(8,128)(2,1)}, bf16[384,1152]{1,0:T(8,128)(2,1)}, bf16[384,1024]{1,0:T(8,128)(2,1)}, bf...) custom-call(s32[2]{0:T(128)} %pad_add_fusion.scal, bf16[128,2176]{1,0:T(8,128)(2,1)} %copy-done.1, ...), custom_call_target="tpu_custom_call" | custom-call | flops 10871635968 | bytes 1048576 | tf_op jit(solution)/shard_map/pallas_call | solution.py:188
  105.0 7.8 %shard_map.105 = bf16[1024,1152]{1,0:T(8,128)(2,1)} custom-call(s32[2]{0:T(128)} %pad_add_fusion.1.sides, bf16[128,2176]{1,0:T(8,128)(2,1)} %get-tuple-element.37.refs_0_, bf16[128,2176]{1,0:T(8,128)(2,1)} %copy-done.3, bf16[128,2176]{1,0:T(8,128)(2,1)} %copy-done, bf16[128,2176]{1,0:T(8,128)(2,1)} %copy-done.4, bf16[128,2176]{1,0:T(8,128)(2,1)} %copy-done.1, ...), custom_call_target="tpu_custom_call" | custom-call | flops 1024 | bytes 1024 | tf_op jit(solution)/shard_map/pallas_call | solution.py:288
  113.7 6.0 %shard_map.106 = (bf16[128,1024]{1,0:T(8,128)(2,1)}, bf16[128,1152]{1,0:T(8,128)(2,1)}, bf16[128,1024]{1,0:T(8,128)(2,1)}, bf16[128,3200]{1,0:T(8,128)(2,1)}) custom-call(s32[2]{0:T(128)} %pad_add_fusion.scal, bf16[128,2176]{1,0:T(8,128)(2,1)} %copy-done.8, bf16[512,1152]{1,0:T(8,128)(2,1)} %get-tuple-element.40.refs_4_.refs_3_.refs_1_, ...), custom_call_target="tpu_custom_call" | custom-call | flops 36238786560 | bytes 1048576 | tf_op jit(solution)/shard_map/pallas_call | solution.py:188
  121.1 1.3 collective-permute-done.12.refs_14_
  124.1 5.8 %shard_map.107 = bf16[512,1152]{1,0:T(8,128)(2,1)} custom-call(s32[1]{0:T(128)} %bitcast.7.sides, bf16[128,2176]{1,0:T(8,128)(2,1)} %get-tuple-element.37.refs_0_, bf16[128,2176]{1,0:T(8,128)(2,1)} %copy-done.3, bf16[128,2176]{1,0:T(8,128)(2,1)} %copy-done, bf16[128,2176]{1,0:T(8,128)(2,1)} %copy-done.4, bf16[128,2176]{1,0:T(8,128)(2,1)} %copy-done.1, ...), custom_call_target="tpu_custom_call" | custom-call | flops 4831839232 | bytes 1024 | tf_op jit(solution)/shard_map/pallas_call | solution.py:288
  130.5 0.9 collective-permute-start.17
  131.5 3.6 %collective-permute-done.15 = bf16[256,1024]{1,0:T(8,128)(2,1)S(1)} collective-permute-done((bf16[256,1024]{1,0:T(8,128)(2,1)S(1)}, bf16[256,1024]{1,0:T(8,128)(2,1)S(1)}, u32[]{:S(2)}, u32[]{:S(2)}) %collective-permute-start.15) | collective-permute-done | bytes 524320 | tf_op jit(solution)/shard_map/ppermute | solution.py:347
  135.2 1.5 collective-permute-start.16
  136.7 3.1 %collective-permute-done.17 = bf16[128,1024]{1,0:T(8,128)(2,1)S(1)} collective-permute-done((bf16[128,1024]{1,0:T(8,128)(2,1)S(1)}, bf16[128,1024]{1,0:T(8,128)(2,1)S(1)}, u32[]{:S(2)}, u32[]{:S(2)}) %collective-permute-start.17) | collective-permute-done | bytes 262176 | tf_op jit(solution)/shard_map/ppermute | solution.py:347
  139.9 1.5 collective-permute-start.21
  142.3 5.8 %shard_map.108 = bf16[512,1152]{1,0:T(8,128)(2,1)} custom-call(s32[1]{0:T(128)} %bitcast.sides, bf16[128,2176]{1,0:T(8,128)(2,1)} %get-tuple-element.37.refs_0_, bf16[128,2176]{1,0:T(8,128)(2,1)} %copy-done.3, bf16[128,2176]{1,0:T(8,128)(2,1)} %copy-done, bf16[128,2176]{1,0:T(8,128)(2,1)} %copy-done.4, bf16[128,2176]{1,0:T(8,128)(2,1)} %copy-done.1, ...), custom_call_target="tpu_custom_call" | custom-call | flops 1024 | bytes 1024 | tf_op jit(solution)/shard_map/pallas_call | solution.py:288
  148.1 1.1 collective-permute-start.18
  149.3 1.3 collective-permute-start.22
  150.6 7.9 %collective-permute-done.14 = bf16[512,1152]{1,0:T(8,128)(2,1)S(1)} collective-permute-done((bf16[512,1152]{1,0:T(8,128)(2,1)}, bf16[512,1152]{1,0:T(8,128)(2,1)S(1)}, u32[]{:S(2)}, u32[]{:S(2)}) %collective-permute-start.14) | collective-permute-done | bytes 1179680 | tf_op jit(solution)/shard_map/ppermute | solution.py:348
  158.5 1.5 convert_add_fusion
  160.0 1.3 slice_bitcast_fusion
  161.3 1.1 copy.11
  162.5 0.9 add_convert_fusion
  (65 shorter events, 9.7 us)
Async XLA Ops:
  42.5 31.6 %collective-permute-start.4 = (bf16[512,1152]{1,0:T(8,128)(2,1)}, bf16[512,1152]{1,0:T(8,128)(2,1)}, u32[]{:S(2)}, u32[]{:S(2)}) collective-permute-start(bf16[512,1152]{1,0:T(8,128)(2,1)} %get-tuple-element.40.refs_4_.refs_3_.refs_1_), channel_id=1, source_target_pairs={{0,16},{16,0},{1,17},{17,1},{2,18},{18,2},{3,19},{19,3},{4,20},{20... | collective-permute-start | bytes 3538952 | tf_op jit(solution)/shard_map/ppermute | solution.py:348
  45.5 14.3 %collective-permute-start = (bf16[128,2176]{1,0:T(8,128)(2,1)}, bf16[128,2176]{1,0:T(8,128)(2,1)S(1)}, u32[]{:S(2)}, u32[]{:S(2)}) collective-permute-start(bf16[128,2176]{1,0:T(8,128)(2,1)} %get-tuple-element.37.refs_0_), channel_id=1, source_target_pairs={{0,4},{1,5},{2,6},{3,7},{4,0},{5,1},{6,2},{7,3},{8,12},{9,13},{10,... | collective-permute-start | bytes 1671176 | tf_op jit(solution)/shard_map/ppermute | solution.py:347
  47.1 14.0 %collective-permute-start.3 = (bf16[128,2176]{1,0:T(8,128)(2,1)}, bf16[128,2176]{1,0:T(8,128)(2,1)S(1)}, u32[]{:S(2)}, u32[]{:S(2)}) collective-permute-start(bf16[128,2176]{1,0:T(8,128)(2,1)} %get-tuple-element.37.refs_0_), channel_id=1, source_target_pairs={{0,2},{1,3},{2,0},{3,1},{4,6},{5,7},{6,4},{7,5},{8,10},{9,11},{10,... | collective-permute-start | bytes 1671176 | tf_op jit(solution)/shard_map/ppermute | solution.py:347
  48.6 14.7 %collective-permute-start.1 = (bf16[128,2176]{1,0:T(8,128)(2,1)}, bf16[128,2176]{1,0:T(8,128)(2,1)S(1)}, u32[]{:S(2)}, u32[]{:S(2)}) collective-permute-start(bf16[128,2176]{1,0:T(8,128)(2,1)} %get-tuple-element.37.refs_0_), channel_id=1, source_target_pairs={{4,8},{5,9},{6,10},{7,11},{8,4},{9,5},{10,6},{11,7},{20,24},{21,25... | collective-permute-start | bytes 1671176 | tf_op jit(solution)/shard_map/ppermute | solution.py:347
  59.8 21.8 %copy-start.3 = (bf16[128,2176]{1,0:T(8,128)(2,1)}, bf16[128,2176]{1,0:T(8,128)(2,1)S(1)}, u32[]{:S(2)}) copy-start(bf16[128,2176]{1,0:T(8,128)(2,1)S(1)} %collective-permute-done.refs_1_) | copy-start | bytes 1671172
  61.1 20.5 %copy-start.4 = (bf16[128,2176]{1,0:T(8,128)(2,1)}, bf16[128,2176]{1,0:T(8,128)(2,1)S(1)}, u32[]{:S(2)}) copy-start(bf16[128,2176]{1,0:T(8,128)(2,1)S(1)} %collective-permute-done.3.refs_3_) | copy-start | bytes 1671172
  61.1 13.0 %collective-permute-start.5 = (bf16[128,2176]{1,0:T(8,128)(2,1)S(1)}, bf16[128,2176]{1,0:T(8,128)(2,1)S(1)}, u32[]{:S(2)}, u32[]{:S(2)}) collective-permute-start(bf16[128,2176]{1,0:T(8,128)(2,1)S(1)} %collective-permute-done.refs_1_), channel_id=1, source_target_pairs={{0,2},{1,3},{2,0},{3,1},{4,6},{5,7},{6,4},{7,5},{8,10},{9,11},{10,... | collective-permute-start | bytes 1671176 | tf_op jit(solution)/shard_map/ppermute | solution.py:347
  62.7 11.5 %collective-permute-start.6 = (bf16[128,2176]{1,0:T(8,128)(2,1)S(1)}, bf16[128,2176]{1,0:T(8,128)(2,1)S(1)}, u32[]{:S(2)}, u32[]{:S(2)}) collective-permute-start(bf16[128,2176]{1,0:T(8,128)(2,1)S(1)} %collective-permute-done.refs_1_), channel_id=1, source_target_pairs={{4,8},{5,9},{6,10},{7,11},{8,4},{9,5},{10,6},{11,7},{20,24},{21,25... | collective-permute-start | bytes 1671176 | tf_op jit(solution)/shard_map/ppermute | solution.py:347
  63.4 16.3 %collective-permute-start.2 = (bf16[128,2176]{1,0:T(8,128)(2,1)S(1)}, bf16[128,2176]{1,0:T(8,128)(2,1)S(1)}, u32[]{:S(2)}, u32[]{:S(2)}) collective-permute-start(bf16[128,2176]{1,0:T(8,128)(2,1)S(1)} %collective-permute-done.1), channel_id=1, source_target_pairs={{4,0},{5,1},{6,2},{7,3},{8,12},{9,13},{10,14},{11,15},{20,16},{21,... | collective-permute-start | bytes 1671176 | tf_op jit(solution)/shard_map/ppermute | solution.py:347
  74.1 17.5 %copy-start.5 = (bf16[128,2176]{1,0:T(8,128)(2,1)}, bf16[128,2176]{1,0:T(8,128)(2,1)S(1)}, u32[]{:S(2)}) copy-start(bf16[128,2176]{1,0:T(8,128)(2,1)S(1)} %collective-permute-done.5.refs_1_.refs_5_) | copy-start | bytes 1671172
  74.1 7.5 %collective-permute-start.7 = (bf16[512,1152]{1,0:T(8,128)(2,1)}, bf16[512,1152]{1,0:T(8,128)(2,1)}, u32[]{:S(2)}, u32[]{:S(2)}) collective-permute-start(bf16[512,1152]{1,0:T(8,128)(2,1)} %get-tuple-element.40.refs_4_.refs_3_.refs_1_), channel_id=1, source_target_pairs={{0,1},{1,0},{2,3},{3,2},{4,5},{5,4},{6,7},{7,6},{8,9},{9,8},{10,11... | collective-permute-start | bytes 3538952 | tf_op jit(solution)/shard_map/ppermute | solution.py:347
  74.1 7.5 %collective-permute-start.8 = (bf16[512,1152]{1,0:T(8,128)(2,1)}, bf16[512,1152]{1,0:T(8,128)(2,1)}, u32[]{:S(2)}, u32[]{:S(2)}) collective-permute-start(bf16[512,1152]{1,0:T(8,128)(2,1)} %collective-permute-done.4.refs_5_.refs_4_.refs_2_), channel_id=1, source_target_pairs={{0,1},{1,0},{2,3},{3,2},{4,5},{5,4},{6,7},{7,6},{8,9},{9,8},{10,11... | collective-permute-start | bytes 3538952 | tf_op jit(solution)/shard_map/ppermute | solution.py:347
  79.8 15.1 %collective-permute-start.10 = (bf16[128,2176]{1,0:T(8,128)(2,1)S(1)}, bf16[128,2176]{1,0:T(8,128)(2,1)S(1)}, u32[]{:S(2)}, u32[]{:S(2)}) collective-permute-start(bf16[128,2176]{1,0:T(8,128)(2,1)S(1)} %broadcast_select_fusion.1.refs_2_), channel_id=1, source_target_pairs={{0,2},{1,3},{2,0},{3,1},{4,6},{5,7},{6,4},{7,5},{8,10},{9,11},{10,... | collective-permute-start | bytes 1671176 | tf_op jit(solution)/shard_map/ppermute | solution.py:347
  80.3 14.5 %collective-permute-start.9 = (bf16[128,2176]{1,0:T(8,128)(2,1)S(1)}, bf16[128,2176]{1,0:T(8,128)(2,1)S(1)}, u32[]{:S(2)}, u32[]{:S(2)}) collective-permute-start(bf16[128,2176]{1,0:T(8,128)(2,1)S(1)} %collective-permute-done.6), channel_id=1, source_target_pairs={{4,0},{5,1},{6,2},{7,3},{8,12},{9,13},{10,14},{11,15},{20,16},{21,... | collective-permute-start | bytes 1671176 | tf_op jit(solution)/shard_map/ppermute | solution.py:347
  94.9 18.0 %collective-permute-start.11 = (bf16[128,2176]{1,0:T(8,128)(2,1)S(1)}, bf16[128,2176]{1,0:T(8,128)(2,1)S(1)}, u32[]{:S(2)}, u32[]{:S(2)}) collective-permute-start(bf16[128,2176]{1,0:T(8,128)(2,1)S(1)} %broadcast_select_fusion.refs_0_.refs_4_), channel_id=1, source_target_pairs={{0,2},{1,3},{2,0},{3,1},{4,6},{5,7},{6,4},{7,5},{8,10},{9,11},{10,... | collective-permute-start | bytes 1671176 | tf_op jit(solution)/shard_map/ppermute | solution.py:347
  112.8 9.6 %collective-permute-start.13 = (bf16[1024,1152]{1,0:T(8,128)(2,1)}, bf16[1024,1152]{1,0:T(8,128)(2,1)S(1)}, u32[]{:S(2)}, u32[]{:S(2)}) collective-permute-start(bf16[1024,1152]{1,0:T(8,128)(2,1)} %shard_map.105), channel_id=1, source_target_pairs={{0,1},{1,0},{2,3},{3,2},{4,5},{5,4},{6,7},{7,6},{8,9},{9,8},{10,11... | collective-permute-start | bytes 7077896 | tf_op jit(solution)/shard_map/ppermute | solution.py:347
  113.7 6.5 %copy-start.13 = (bf16[256,1024]{1,0:T(8,128)(2,1)S(1)}, bf16[256,1024]{1,0:T(8,128)(2,1)}, u32[]{:S(2)}) copy-start(bf16[256,1024]{1,0:T(8,128)(2,1)} %get-tuple-element.61) | copy-start | bytes 1572868
  119.7 2.7 %collective-permute-start.12 = (bf16[128,3200]{1,0:T(8,128)(2,1)}, bf16[128,3200]{1,0:T(8,128)(2,1)S(1)}, u32[]{:S(2)}, u32[]{:S(2)}) collective-permute-start(bf16[128,3200]{1,0:T(8,128)(2,1)} %get-tuple-element.58), channel_id=1, source_target_pairs={{0,1},{1,0},{2,3},{3,2},{4,5},{5,4},{6,7},{7,6},{8,9},{9,8},{10,11... | collective-permute-start | bytes 2457608 | tf_op jit(solution)/shard_map/ppermute | solution.py:347
  120.3 14.8 %collective-permute-start.15 = (bf16[256,1024]{1,0:T(8,128)(2,1)S(1)}, bf16[256,1024]{1,0:T(8,128)(2,1)S(1)}, u32[]{:S(2)}, u32[]{:S(2)}) collective-permute-start(bf16[256,1024]{1,0:T(8,128)(2,1)S(1)} %copy-done.13), channel_id=1, source_target_pairs={{0,2},{1,3},{2,0},{3,1},{4,6},{5,7},{6,4},{7,5},{8,10},{9,11},{10,... | collective-permute-start | bytes 1572872 | tf_op jit(solution)/shard_map/ppermute | solution.py:347
  124.1 6.5 %copy-start.15 = (bf16[128,1024]{1,0:T(8,128)(2,1)S(1)}, bf16[128,1024]{1,0:T(8,128)(2,1)}, u32[]{:S(2)}) copy-start(bf16[128,1024]{1,0:T(8,128)(2,1)} %get-tuple-element.66) | copy-start | bytes 786436
  124.1 10.9 %copy-start.11 = (bf16[128,1024]{1,0:T(8,128)(2,1)S(1)}, bf16[128,1024]{1,0:T(8,128)(2,1)}, u32[]{:S(2)}) copy-start(bf16[128,1024]{1,0:T(8,128)(2,1)} %get-tuple-element.68) | copy-start | bytes 786436
  124.1 10.9 %copy-start.12 = (bf16[128,1024]{1,0:T(8,128)(2,1)S(1)}, bf16[128,1024]{1,0:T(8,128)(2,1)}, u32[]{:S(2)}) copy-start(bf16[128,1024]{1,0:T(8,128)(2,1)} %get-tuple-element.60) | copy-start | bytes 786436
  129.9 9.8 %copy-start.9 = (bf16[128,1024]{1,0:T(8,128)(2,1)S(1)}, bf16[128,1024]{1,0:T(8,128)(2,1)}, u32[]{:S(2)}) copy-start(bf16[128,1024]{1,0:T(8,128)(2,1)} %get-tuple-element.69) | copy-start | bytes 786436
  130.0 28.5 %collective-permute-start.14 = (bf16[512,1152]{1,0:T(8,128)(2,1)}, bf16[512,1152]{1,0:T(8,128)(2,1)S(1)}, u32[]{:S(2)}, u32[]{:S(2)}) collective-permute-start(bf16[512,1152]{1,0:T(8,128)(2,1)} %shard_map.107), channel_id=1, source_target_pairs={{0,16},{16,0},{1,17},{17,1},{2,18},{18,2},{3,19},{19,3},{4,20},{20... | collective-permute-start | bytes 3538952 | tf_op jit(solution)/shard_map/ppermute | solution.py:348
  130.5 9.2 %collective-permute-start.17 = (bf16[128,1024]{1,0:T(8,128)(2,1)S(1)}, bf16[128,1024]{1,0:T(8,128)(2,1)S(1)}, u32[]{:S(2)}, u32[]{:S(2)}) collective-permute-start(bf16[128,1024]{1,0:T(8,128)(2,1)S(1)} %copy-done.15), channel_id=1, source_target_pairs={{0,2},{1,3},{2,0},{3,1},{4,6},{5,7},{6,4},{7,5},{8,10},{9,11},{10,... | collective-permute-start | bytes 786440 | tf_op jit(solution)/shard_map/ppermute | solution.py:347
  135.2 6.2 %collective-permute-start.16 = (bf16[128,1024]{1,0:T(8,128)(2,1)S(1)}, bf16[128,1024]{1,0:T(8,128)(2,1)S(1)}, u32[]{:S(2)}, u32[]{:S(2)}) collective-permute-start(bf16[128,1024]{1,0:T(8,128)(2,1)S(1)} %get-tuple-element.78), channel_id=1, source_target_pairs={{0,4},{1,5},{2,6},{3,7},{12,8},{13,9},{14,10},{15,11},{16,20},{17,... | collective-permute-start | bytes 786440 | tf_op jit(solution)/shard_map/ppermute | solution.py:347
  139.9 9.4 %collective-permute-start.21 = (bf16[128,1024]{1,0:T(8,128)(2,1)S(1)}, bf16[128,1024]{1,0:T(8,128)(2,1)S(1)}, u32[]{:S(2)}, u32[]{:S(2)}) collective-permute-start(bf16[128,1024]{1,0:T(8,128)(2,1)S(1)} %add_convert_fusion.2), channel_id=1, source_target_pairs={{0,4},{1,5},{2,6},{3,7},{12,8},{13,9},{14,10},{15,11},{16,20},{17,... | collective-permute-start | bytes 786440 | tf_op jit(solution)/shard_map/ppermute | solution.py:347
  141.3 21.1 %collective-permute-start.19 = (bf16[128,1024]{1,0:T(8,128)(2,1)S(1)}, bf16[128,1024]{1,0:T(8,128)(2,1)S(1)}, u32[]{:S(2)}, u32[]{:S(2)}) collective-permute-start(bf16[128,1024]{1,0:T(8,128)(2,1)S(1)} %get-tuple-element.77), channel_id=1, source_target_pairs={{0,4},{1,5},{2,6},{3,7},{4,0},{5,1},{6,2},{7,3},{8,12},{9,13},{10,... | collective-permute-start | bytes 786440 | tf_op jit(solution)/shard_map/ppermute | solution.py:347
  141.5 6.6 %copy-start.14 = (bf16[128,1024]{1,0:T(8,128)(2,1)S(1)}, bf16[128,1024]{1,0:T(8,128)(2,1)}, u32[]{:S(2)}) copy-start(bf16[128,1024]{1,0:T(8,128)(2,1)} %get-tuple-element.67) | copy-start | bytes 786436
  141.5 20.9 %collective-permute-start.20 = (bf16[128,1024]{1,0:T(8,128)(2,1)S(1)}, bf16[128,1024]{1,0:T(8,128)(2,1)S(1)}, u32[]{:S(2)}, u32[]{:S(2)}) collective-permute-start(bf16[128,1024]{1,0:T(8,128)(2,1)S(1)} %add_convert_fusion.4), channel_id=1, source_target_pairs={{4,8},{5,9},{6,10},{7,11},{8,4},{9,5},{10,6},{11,7},{20,24},{21,25... | collective-permute-start | bytes 786440 | tf_op jit(solution)/shard_map/ppermute | solution.py:347
  148.1 14.3 %collective-permute-start.18 = (bf16[128,1024]{1,0:T(8,128)(2,1)S(1)}, bf16[128,1024]{1,0:T(8,128)(2,1)S(1)}, u32[]{:S(2)}, u32[]{:S(2)}) collective-permute-start(bf16[128,1024]{1,0:T(8,128)(2,1)S(1)} %copy-done.14), channel_id=1, source_target_pairs={{0,2},{1,3},{2,0},{3,1},{4,6},{5,7},{6,4},{7,5},{8,10},{9,11},{10,... | collective-permute-start | bytes 786440 | tf_op jit(solution)/shard_map/ppermute | solution.py:347
  149.3 13.1 %collective-permute-start.22 = (bf16[128,1024]{1,0:T(8,128)(2,1)S(1)}, bf16[128,1024]{1,0:T(8,128)(2,1)S(1)}, u32[]{:S(2)}, u32[]{:S(2)}) collective-permute-start(bf16[128,1024]{1,0:T(8,128)(2,1)S(1)} %add_convert_fusion.1), channel_id=1, source_target_pairs={{4,12},{5,13},{6,14},{7,15},{8,0},{9,1},{10,2},{11,3},{20,28},{21,... | collective-permute-start | bytes 786440 | tf_op jit(solution)/shard_map/ppermute | solution.py:347
  (7 other events, 9.7 us)

commit v11 on v10

--- a/solution.py
+++ b/solution.py
@@ -82,7 +82,7 @@
             jax.ShapeDtypeStruct((rows, 2 * width + LANES), BF16),
             jax.ShapeDtypeStruct((size, 3 * hidden_units), BF16),
         ],
-        in_specs=[hbm(), hbm(), vmem(), vmem(), hbm(), hbm(), vmem()],
+        in_specs=[vmem()] * 7,
         out_specs=[hbm(), hbm()],
         scratch_shapes=[
             pltpu.VMEM((rows, LANES), BF16),
@@ -364,18 +364,16 @@
     w_core = swap(after(w_own, y1, f2))
     w_both = swap(after(w_part, y1, f2))
     weights = [w_own, w_part, w_core, w_both]
-    p0, p1, p2, q0, *kept_a = rows_call(experts, scal, [[own], [b1], [b2], [y0]], weights)
+    p0, p1, p2, q01, *kept_a = rows_call(experts, scal, [[own], [b1], [b2], [y0, y1]], weights)
     b3 = jnp.where(inner, f2, after(g2, p0))
     y3 = move(after(b3, y2), SWAP_Y)
-    p3, q12, *kept_b = rows_call(experts, scal, [[b3], [y1, y2]], weights)
-
-    blocks = [own, b1, b2, y0, b3, y1, y2]
+    p3, q2, *kept_b = rows_call(experts, scal, [[b3], [y2]], weights)
+
+    blocks = [own, b1, b2, y0, y1, b3, y2]
     kept = [kept_a, kept_b]
     to_core = half_call(jnp.concatenate([other, mine]), blocks, [k[2:] for k in kept])
-    y3 = after(y3, q12, to_core)
-    r12 = move(after(q12, y3), SWAP_Y)
-    rows = own.shape[0]
-    r1, r2 = r12[:rows], r12[rows:]
+    y3 = after(y3, q2, to_core)
+    r2 = move(after(q2, y3), SWAP_Y)
 
     q3, *kept_d, joined = rows_call(experts, scal, [[y3]], weights, joined=True)
     last = swap(joined)
@@ -385,7 +383,9 @@
     send = half_call(other, all_blocks, all_kept, last, got, weight=1)
     from_part = across(send)
     r3 = move(after(q3, send), SWAP_Y)
-    r0 = move(after(q0, r3), SWAP_Y)
+    r01 = move(after(q01, r3), SWAP_Y)
+    rows = own.shape[0]
+    r0, r1 = r01[:rows], r01[rows:]
     keep = half_call(after(mine, send), all_blocks, all_kept, last, got, at=1)
 
     add = lambda *terms: sum(t.astype(F32) for t in terms).astype(BF16)

time: 164 us -> 124 us (0.76)
  Pallas kernels: 85.8 us -> 45.9 us
  starting transfers between devices: 23.4 us -> 28.3 us
  waiting for transfers between devices: 44.1 us -> 41.1 us
    pallas_call x1, Pallas kernels: 41.9 us -> 2.7 us  [pack(): pl.pallas_call(functools.partial(pack_kernel, experts), out_shape=[jax.Sh...]
    ppermute x21, starting transfers between devices: 19.8 us -> 24.8 us  [dense_body(): move = lambda a, pairs: lax.ppermute(a, 'expert', pairs)]
    ppermute x2, waiting for transfers between devices: 7.85 us -> 5.47 us  [dense_body(): across = lambda a: lax.ppermute(a, 'dp', [(0, 1), (1, 0)])]
    unnamed x33 -> x35, local copies, waits for them, and re-layouts: 3.66 us -> 3.67 us
  transfers between devices with their start and end apart: 23 -> 23, of which waited for: 9 -> 10; matrix products, arithmetic and copies ran while one was open for 3% -> 3% of each run, Pallas kernels for 27% -> 35%
where the time goes in v11:
time: 124 us
  Pallas kernels  45.9 us (37%)
  waiting for transfers between devices  41.1 us (33%)
  starting transfers between devices  28.3 us (23%)
  local copies, waits for them, and re-layouts  4.96 us (4%)
  other arithmetic  2.82 us (2%)
    ppermute x21, waiting for transfers between devices, dense_body(): move = lambda a, pairs: lax.ppermute(a, 'expert', pairs)  35.6 us
    ppermute x21, starting transfers between devices, dense_body(): move = lambda a, pairs: lax.ppermute(a, 'expert', pairs)  24.8 us
    pallas_call x3, Pallas kernels, rows_call(): pl.pallas_call(functools.partial(rows_kernel, experts, count, sizes, join...  23.8 us
    pallas_call x3, Pallas kernels, half_call(): pl.pallas_call(functools.partial(half_kernel, len(blocks), len(kept), las...  19.4 us
    ppermute x2, waiting for transfers between devices, dense_body(): across = lambda a: lax.ppermute(a, 'dp', [(0, 1), (1, 0)])  5.47 us
    unnamed x35, local copies, waits for them, and re-layouts  3.67 us
    ppermute x2, starting transfers between devices, dense_body(): across = lambda a: lax.ppermute(a, 'dp', [(0, 1), (1, 0)])  3.54 us
    pallas_call x1, Pallas kernels, pack(): pl.pallas_call(functools.partial(pack_kernel, experts), out_shape=[jax.Sh...  2.7 us
  transfers between devices with their start and end apart: 23, of which 10 were waited for; matrix products, arithmetic and copies ran while one was open for 3% of the time, Pallas kernels for 35%

profile of v11, /device:TPU:0, one launch (start us, length us, event | category | flops | bytes accessed | tf_op | source)
XLA Modules:
  0.0 124.1 jit_solution(10109958607085760209)
XLA Ops:
  0.6 2.7 %shard_map.102 = (bf16[128,2176]{1,0:T(8,128)(2,1)}, bf16[512,1152]{1,0:T(8,128)(2,1)}) custom-call(bf16[128,1024]{1,0:T(8,128)(2,1)} %tokens.1, bf16[128,1024]{1,0:T(8,128)(2,1)} %d_output.1, f32[8,128]{1,0:T(8,128)} %bitcast.19, s32[8,128]{1,0:T(8,128)} %bitcast.20, bf16[512,384]{1,0:T(8,128)(2,1)} %bitcast.16, bf16[512,384]{1,0:T(8,128)(2,1)} %bitcast.17, ...), custom_call_target="tpu_custom_call" | custom-call | bytes 1048576 | tf_op jit(solution)/shard_map/pallas_call | solution.py:79
  3.3 3.0 %collective-permute-start.5 = (bf16[512,1152]{1,0:T(8,128)(2,1)}, bf16[512,1152]{1,0:T(8,128)(2,1)}, u32[]{:S(2)}, u32[]{:S(2)}) collective-permute-start(bf16[512,1152]{1,0:T(8,128)(2,1)} %get-tuple-element.40.refs_5_.refs_2_.refs_1_), channel_id=1, source_target_pairs={{0,16},{16,0},{1,17},{17,1},{2,18},{18,2},{3,19},{19,3},{4,20},{20... | collective-permute-start | bytes 3538952 | tf_op jit(solution)/shard_map/ppermute | solution.py:348
  6.3 1.6 %collective-permute-start = (bf16[128,2176]{1,0:T(8,128)(2,1)}, bf16[128,2176]{1,0:T(8,128)(2,1)S(1)}, u32[]{:S(2)}, u32[]{:S(2)}) collective-permute-start(bf16[128,2176]{1,0:T(8,128)(2,1)} %get-tuple-element.37.refs_0_), channel_id=1, source_target_pairs={{0,4},{1,5},{2,6},{3,7},{4,0},{5,1},{6,2},{7,3},{8,12},{9,13},{10,... | collective-permute-start | bytes 1671176 | tf_op jit(solution)/shard_map/ppermute | solution.py:347
  7.9 1.5 %collective-permute-start.3 = (bf16[128,2176]{1,0:T(8,128)(2,1)}, bf16[128,2176]{1,0:T(8,128)(2,1)S(1)}, u32[]{:S(2)}, u32[]{:S(2)}) collective-permute-start(bf16[128,2176]{1,0:T(8,128)(2,1)} %get-tuple-element.37.refs_0_), channel_id=1, source_target_pairs={{0,2},{1,3},{2,0},{3,1},{4,6},{5,7},{6,4},{7,5},{8,10},{9,11},{10,... | collective-permute-start | bytes 1671176 | tf_op jit(solution)/shard_map/ppermute | solution.py:347
  10.1 10.5 %collective-permute-done.refs_1_ = bf16[128,2176]{1,0:T(8,128)(2,1)S(1)} collective-permute-done((bf16[128,2176]{1,0:T(8,128)(2,1)}, bf16[128,2176]{1,0:T(8,128)(2,1)S(1)}, u32[]{:S(2)}, u32[]{:S(2)}) %collective-permute-start) | collective-permute-done | bytes 557088 | tf_op jit(solution)/shard_map/ppermute | solution.py:347
  20.6 1.3 %collective-permute-done.3.refs_3_ = bf16[128,2176]{1,0:T(8,128)(2,1)S(1)} collective-permute-done((bf16[128,2176]{1,0:T(8,128)(2,1)}, bf16[128,2176]{1,0:T(8,128)(2,1)S(1)}, u32[]{:S(2)}, u32[]{:S(2)}) %collective-permute-start.3) | collective-permute-done | bytes 557088 | tf_op jit(solution)/shard_map/ppermute | solution.py:347
  21.9 1.5 %collective-permute-start.4 = (bf16[128,2176]{1,0:T(8,128)(2,1)S(1)}, bf16[128,2176]{1,0:T(8,128)(2,1)S(1)}, u32[]{:S(2)}, u32[]{:S(2)}) collective-permute-start(bf16[128,2176]{1,0:T(8,128)(2,1)S(1)} %collective-permute-done.refs_1_), channel_id=1, source_target_pairs={{0,2},{1,3},{2,0},{3,1},{4,6},{5,7},{6,4},{7,5},{8,10},{9,11},{10,... | collective-permute-start | bytes 1671176 | tf_op jit(solution)/shard_map/ppermute | solution.py:347
  24.2 1.3 %collective-permute-start.2 = (bf16[128,2176]{1,0:T(8,128)(2,1)S(1)}, bf16[128,2176]{1,0:T(8,128)(2,1)S(1)}, u32[]{:S(2)}, u32[]{:S(2)}) collective-permute-start(bf16[128,2176]{1,0:T(8,128)(2,1)S(1)} %collective-permute-done.1), channel_id=1, source_target_pairs={{4,0},{5,1},{6,2},{7,3},{8,12},{9,13},{10,14},{11,15},{20,16},{21,... | collective-permute-start | bytes 1671176 | tf_op jit(solution)/shard_map/ppermute | solution.py:347
  25.5 9.5 %collective-permute-done.4.refs_4_ = bf16[128,2176]{1,0:T(8,128)(2,1)S(1)} collective-permute-done((bf16[128,2176]{1,0:T(8,128)(2,1)S(1)}, bf16[128,2176]{1,0:T(8,128)(2,1)S(1)}, u32[]{:S(2)}, u32[]{:S(2)}) %collective-permute-start.4) | collective-permute-done | bytes 557088 | tf_op jit(solution)/shard_map/ppermute | solution.py:347
  36.6 3.9 %collective-permute-done.2 = bf16[128,2176]{1,0:T(8,128)(2,1)S(1)} collective-permute-done((bf16[128,2176]{1,0:T(8,128)(2,1)S(1)}, bf16[128,2176]{1,0:T(8,128)(2,1)S(1)}, u32[]{:S(2)}, u32[]{:S(2)}) %collective-permute-start.2) | collective-permute-done | bytes 557088 | tf_op jit(solution)/shard_map/ppermute | solution.py:347
  41.1 1.3 %collective-permute-start.9 = (bf16[128,2176]{1,0:T(8,128)(2,1)S(1)}, bf16[128,2176]{1,0:T(8,128)(2,1)S(1)}, u32[]{:S(2)}, u32[]{:S(2)}) collective-permute-start(bf16[128,2176]{1,0:T(8,128)(2,1)S(1)} %collective-permute-done.6), channel_id=1, source_target_pairs={{4,0},{5,1},{6,2},{7,3},{8,12},{9,13},{10,14},{11,15},{20,16},{21,... | collective-permute-start | bytes 1671176 | tf_op jit(solution)/shard_map/ppermute | solution.py:347
  42.5 11.5 %shard_map.103 = (bf16[128,1024]{1,0:T(8,128)(2,1)}, bf16[128,1024]{1,0:T(8,128)(2,1)}, bf16[128,1024]{1,0:T(8,128)(2,1)}, bf16[256,1024]{1,0:T(8,128)(2,1)}, bf...) custom-call(s32[2]{0:T(128)} %pad_add_fusion.scal, ...), custom_call_target="tpu_custom_call" | custom-call | flops 18119393280 | bytes 1048576 | tf_op jit(solution)/shard_map/pallas_call | solution.py:188
  54.0 1.5 %collective-permute-done.9 = bf16[128,2176]{1,0:T(8,128)(2,1)S(1)} collective-permute-done((bf16[128,2176]{1,0:T(8,128)(2,1)S(1)}, bf16[128,2176]{1,0:T(8,128)(2,1)S(1)}, u32[]{:S(2)}, u32[]{:S(2)}) %collective-permute-start.9) | collective-permute-done | bytes 557088 | tf_op jit(solution)/shard_map/ppermute | solution.py:347
  55.6 1.6 %collective-permute-start.11 = (bf16[128,2176]{1,0:T(8,128)(2,1)S(1)}, bf16[128,2176]{1,0:T(8,128)(2,1)S(1)}, u32[]{:S(2)}, u32[]{:S(2)}) collective-permute-start(bf16[128,2176]{1,0:T(8,128)(2,1)S(1)} %broadcast_select_fusion.refs_0_.refs_5_), channel_id=1, source_target_pairs={{0,2},{1,3},{2,0},{3,1},{4,6},{5,7},{6,4},{7,5},{8,10},{9,11},{10,... | collective-permute-start | bytes 1671176 | tf_op jit(solution)/shard_map/ppermute | solution.py:347
  57.2 6.2 %shard_map.104 = (bf16[128,1024]{1,0:T(8,128)(2,1)}, bf16[128,1024]{1,0:T(8,128)(2,1)}, bf16[256,1152]{1,0:T(8,128)(2,1)}, bf16[256,1024]{1,0:T(8,128)(2,1)}, bf...) custom-call(s32[2]{0:T(128)} %pad_add_fusion.scal, bf16[128,2176]{1,0:T(8,128)(2,1)} %copy-done.1, ...), custom_call_target="tpu_custom_call" | custom-call | flops 7247757312 | bytes 1048576 | tf_op jit(solution)/shard_map/pallas_call | solution.py:188
  63.5 7.8 %shard_map.105 = bf16[1024,1152]{1,0:T(8,128)(2,1)} custom-call(s32[2]{0:T(128)} %pad_add_fusion.1.sides, bf16[128,2176]{1,0:T(8,128)(2,1)} %get-tuple-element.37.refs_0_, bf16[128,2176]{1,0:T(8,128)(2,1)} %copy-done.4, bf16[128,2176]{1,0:T(8,128)(2,1)} %copy-done, bf16[128,2176]{1,0:T(8,128)(2,1)} %copy-done.5, bf16[128,2176]{1,0:T(8,128)(2,1)} %copy-done.6, ...), custom_call_target="tpu_custom_call" | custom-call | flops 1024 | bytes 1024 | tf_op jit(solution)/shard_map/pallas_call | solution.py:288
  72.2 6.0 %shard_map.106 = (bf16[128,1024]{1,0:T(8,128)(2,1)}, bf16[128,1152]{1,0:T(8,128)(2,1)}, bf16[128,1024]{1,0:T(8,128)(2,1)}, bf16[128,3200]{1,0:T(8,128)(2,1)}) custom-call(s32[2]{0:T(128)} %pad_add_fusion.scal, bf16[128,2176]{1,0:T(8,128)(2,1)} %copy-done.9, bf16[512,1152]{1,0:T(8,128)(2,1)} %get-tuple-element.40.refs_5_.refs_2_.refs_1_, ...), custom_call_target="tpu_custom_call" | custom-call | flops 36238786560 | bytes 1048576 | tf_op jit(solution)/shard_map/pallas_call | solution.py:188
  79.7 1.2 collective-permute-done.12.refs_14_
  82.6 5.8 %shard_map.107 = bf16[512,1152]{1,0:T(8,128)(2,1)} custom-call(s32[1]{0:T(128)} %bitcast.7.sides, bf16[128,2176]{1,0:T(8,128)(2,1)} %get-tuple-element.37.refs_0_, bf16[128,2176]{1,0:T(8,128)(2,1)} %copy-done.4, bf16[128,2176]{1,0:T(8,128)(2,1)} %copy-done, bf16[128,2176]{1,0:T(8,128)(2,1)} %copy-done.5, bf16[128,2176]{1,0:T(8,128)(2,1)} %copy-done.6, ...), custom_call_target="tpu_custom_call" | custom-call | flops 4831839232 | bytes 1024 | tf_op jit(solution)/shard_map/pallas_call | solution.py:288
  88.5 1.0 collective-permute-start.17
  90.1 3.1 %collective-permute-start.16 = (bf16[128,1024]{1,0:T(8,128)(2,1)S(1)}, bf16[128,1024]{1,0:T(8,128)(2,1)S(1)}, u32[]{:S(2)}, u32[]{:S(2)}) collective-permute-start(bf16[128,1024]{1,0:T(8,128)(2,1)S(1)} %add_convert_fusion.5), channel_id=1, source_target_pairs={{0,4},{1,5},{2,6},{3,7},{12,8},{13,9},{14,10},{15,11},{16,20},{17,... | collective-permute-start | bytes 786440 | tf_op jit(solution)/shard_map/ppermute | solution.py:347
  93.2 3.9 %collective-permute-done.17 = bf16[128,1024]{1,0:T(8,128)(2,1)S(1)} collective-permute-done((bf16[128,1024]{1,0:T(8,128)(2,1)S(1)}, bf16[128,1024]{1,0:T(8,128)(2,1)S(1)}, u32[]{:S(2)}, u32[]{:S(2)}) %collective-permute-start.17) | collective-permute-done | bytes 262176 | tf_op jit(solution)/shard_map/ppermute | solution.py:347
  97.1 0.9 collective-permute-start.18
  98.2 3.1 %collective-permute-start.21 = (bf16[128,1024]{1,0:T(8,128)(2,1)S(1)}, bf16[128,1024]{1,0:T(8,128)(2,1)S(1)}, u32[]{:S(2)}, u32[]{:S(2)}) collective-permute-start(bf16[128,1024]{1,0:T(8,128)(2,1)S(1)} %add_convert_fusion.2), channel_id=1, source_target_pairs={{0,4},{1,5},{2,6},{3,7},{12,8},{13,9},{14,10},{15,11},{16,20},{17,... | collective-permute-start | bytes 786440 | tf_op jit(solution)/shard_map/ppermute | solution.py:347
  102.2 5.8 %shard_map.108 = bf16[512,1152]{1,0:T(8,128)(2,1)} custom-call(s32[1]{0:T(128)} %bitcast.sides, bf16[128,2176]{1,0:T(8,128)(2,1)} %get-tuple-element.37.refs_0_, bf16[128,2176]{1,0:T(8,128)(2,1)} %copy-done.4, bf16[128,2176]{1,0:T(8,128)(2,1)} %copy-done, bf16[128,2176]{1,0:T(8,128)(2,1)} %copy-done.5, bf16[128,2176]{1,0:T(8,128)(2,1)} %copy-done.6, ...), custom_call_target="tpu_custom_call" | custom-call | flops 1024 | bytes 1024 | tf_op jit(solution)/shard_map/pallas_call | solution.py:288
  108.0 1.4 %collective-permute-start.22 = (bf16[128,1024]{1,0:T(8,128)(2,1)S(1)}, bf16[128,1024]{1,0:T(8,128)(2,1)S(1)}, u32[]{:S(2)}, u32[]{:S(2)}) collective-permute-start(bf16[128,1024]{1,0:T(8,128)(2,1)S(1)} %add_convert_fusion.1), channel_id=1, source_target_pairs={{4,12},{5,13},{6,14},{7,15},{8,0},{9,1},{10,2},{11,3},{20,28},{21,... | collective-permute-start | bytes 786440 | tf_op jit(solution)/shard_map/ppermute | solution.py:347
  109.5 1.1 collective-permute-done.18
  110.6 1.6 %collective-permute-start.19 = (bf16[128,1024]{1,0:T(8,128)(2,1)S(1)}, bf16[128,1024]{1,0:T(8,128)(2,1)S(1)}, u32[]{:S(2)}, u32[]{:S(2)}) collective-permute-start(bf16[128,1024]{1,0:T(8,128)(2,1)S(1)} %add_convert_fusion.3), channel_id=1, source_target_pairs={{0,4},{1,5},{2,6},{3,7},{4,0},{5,1},{6,2},{7,3},{8,12},{9,13},{10,... | collective-permute-start | bytes 786440 | tf_op jit(solution)/shard_map/ppermute | solution.py:347
  112.2 5.5 %collective-permute-done.14 = bf16[512,1152]{1,0:T(8,128)(2,1)S(1)} collective-permute-done((bf16[512,1152]{1,0:T(8,128)(2,1)}, bf16[512,1152]{1,0:T(8,128)(2,1)S(1)}, u32[]{:S(2)}, u32[]{:S(2)}) %collective-permute-start.14) | collective-permute-done | bytes 1179680 | tf_op jit(solution)/shard_map/ppermute | solution.py:348
  118.0 1.3 %slice_bitcast_fusion = (f32[1,384,512]{1,2,0:T(8,128)S(1)}, f32[1,512,384]{2,1,0:T(8,128)}, f32[1,512,384]{2,1,0:T(8,128)}) fusion(f32[512,1152]{1,0:T(8,128)S(1)} %convert_add_fusion), kind=kLoop, calls=%fused_computation.1 | loop fusion | bytes 4718592 | tf_op jit(solution)/shard_map/broadcast_in_dim | solution.py:402
  119.3 1.1 copy.11
  120.4 2.7 %collective-permute-done.19 = bf16[128,1024]{1,0:T(8,128)(2,1)S(1)} collective-permute-done((bf16[128,1024]{1,0:T(8,128)(2,1)S(1)}, bf16[128,1024]{1,0:T(8,128)(2,1)S(1)}, u32[]{:S(2)}, u32[]{:S(2)}) %collective-permute-start.19) | collective-permute-done | bytes 262176 | tf_op jit(solution)/shard_map/ppermute | solution.py:347
  (68 shorter events, 10.7 us)
Async XLA Ops:
  3.3 31.6 %collective-permute-start.5 = (bf16[512,1152]{1,0:T(8,128)(2,1)}, bf16[512,1152]{1,0:T(8,128)(2,1)}, u32[]{:S(2)}, u32[]{:S(2)}) collective-permute-start(bf16[512,1152]{1,0:T(8,128)(2,1)} %get-tuple-element.40.refs_5_.refs_2_.refs_1_), channel_id=1, source_target_pairs={{0,16},{16,0},{1,17},{17,1},{2,18},{18,2},{3,19},{19,3},{4,20},{20... | collective-permute-start | bytes 3538952 | tf_op jit(solution)/shard_map/ppermute | solution.py:348
  6.3 14.3 %collective-permute-start = (bf16[128,2176]{1,0:T(8,128)(2,1)}, bf16[128,2176]{1,0:T(8,128)(2,1)S(1)}, u32[]{:S(2)}, u32[]{:S(2)}) collective-permute-start(bf16[128,2176]{1,0:T(8,128)(2,1)} %get-tuple-element.37.refs_0_), channel_id=1, source_target_pairs={{0,4},{1,5},{2,6},{3,7},{4,0},{5,1},{6,2},{7,3},{8,12},{9,13},{10,... | collective-permute-start | bytes 1671176 | tf_op jit(solution)/shard_map/ppermute | solution.py:347
  7.9 14.0 %collective-permute-start.3 = (bf16[128,2176]{1,0:T(8,128)(2,1)}, bf16[128,2176]{1,0:T(8,128)(2,1)S(1)}, u32[]{:S(2)}, u32[]{:S(2)}) collective-permute-start(bf16[128,2176]{1,0:T(8,128)(2,1)} %get-tuple-element.37.refs_0_), channel_id=1, source_target_pairs={{0,2},{1,3},{2,0},{3,1},{4,6},{5,7},{6,4},{7,5},{8,10},{9,11},{10,... | collective-permute-start | bytes 1671176 | tf_op jit(solution)/shard_map/ppermute | solution.py:347
  9.4 14.7 %collective-permute-start.1 = (bf16[128,2176]{1,0:T(8,128)(2,1)}, bf16[128,2176]{1,0:T(8,128)(2,1)S(1)}, u32[]{:S(2)}, u32[]{:S(2)}) collective-permute-start(bf16[128,2176]{1,0:T(8,128)(2,1)} %get-tuple-element.37.refs_0_), channel_id=1, source_target_pairs={{4,8},{5,9},{6,10},{7,11},{8,4},{9,5},{10,6},{11,7},{20,24},{21,25... | collective-permute-start | bytes 1671176 | tf_op jit(solution)/shard_map/ppermute | solution.py:347
  20.6 21.8 %copy-start.4 = (bf16[128,2176]{1,0:T(8,128)(2,1)}, bf16[128,2176]{1,0:T(8,128)(2,1)S(1)}, u32[]{:S(2)}) copy-start(bf16[128,2176]{1,0:T(8,128)(2,1)S(1)} %collective-permute-done.refs_1_) | copy-start | bytes 1671172
  21.9 20.5 %copy-start.5 = (bf16[128,2176]{1,0:T(8,128)(2,1)}, bf16[128,2176]{1,0:T(8,128)(2,1)S(1)}, u32[]{:S(2)}) copy-start(bf16[128,2176]{1,0:T(8,128)(2,1)S(1)} %collective-permute-done.3.refs_3_) | copy-start | bytes 1671172
  21.9 13.0 %collective-permute-start.4 = (bf16[128,2176]{1,0:T(8,128)(2,1)S(1)}, bf16[128,2176]{1,0:T(8,128)(2,1)S(1)}, u32[]{:S(2)}, u32[]{:S(2)}) collective-permute-start(bf16[128,2176]{1,0:T(8,128)(2,1)S(1)} %collective-permute-done.refs_1_), channel_id=1, source_target_pairs={{0,2},{1,3},{2,0},{3,1},{4,6},{5,7},{6,4},{7,5},{8,10},{9,11},{10,... | collective-permute-start | bytes 1671176 | tf_op jit(solution)/shard_map/ppermute | solution.py:347
  23.5 11.5 %collective-permute-start.6 = (bf16[128,2176]{1,0:T(8,128)(2,1)S(1)}, bf16[128,2176]{1,0:T(8,128)(2,1)S(1)}, u32[]{:S(2)}, u32[]{:S(2)}) collective-permute-start(bf16[128,2176]{1,0:T(8,128)(2,1)S(1)} %collective-permute-done.refs_1_), channel_id=1, source_target_pairs={{4,8},{5,9},{6,10},{7,11},{8,4},{9,5},{10,6},{11,7},{20,24},{21,25... | collective-permute-start | bytes 1671176 | tf_op jit(solution)/shard_map/ppermute | solution.py:347
  24.2 16.3 %collective-permute-start.2 = (bf16[128,2176]{1,0:T(8,128)(2,1)S(1)}, bf16[128,2176]{1,0:T(8,128)(2,1)S(1)}, u32[]{:S(2)}, u32[]{:S(2)}) collective-permute-start(bf16[128,2176]{1,0:T(8,128)(2,1)S(1)} %collective-permute-done.1), channel_id=1, source_target_pairs={{4,0},{5,1},{6,2},{7,3},{8,12},{9,13},{10,14},{11,15},{20,16},{21,... | collective-permute-start | bytes 1671176 | tf_op jit(solution)/shard_map/ppermute | solution.py:347
  34.9 7.5 %copy-start.6 = (bf16[128,2176]{1,0:T(8,128)(2,1)}, bf16[128,2176]{1,0:T(8,128)(2,1)S(1)}, u32[]{:S(2)}) copy-start(bf16[128,2176]{1,0:T(8,128)(2,1)S(1)} %collective-permute-done.4.refs_4_) | copy-start | bytes 1671172
  34.9 7.5 %collective-permute-start.7 = (bf16[512,1152]{1,0:T(8,128)(2,1)}, bf16[512,1152]{1,0:T(8,128)(2,1)}, u32[]{:S(2)}, u32[]{:S(2)}) collective-permute-start(bf16[512,1152]{1,0:T(8,128)(2,1)} %get-tuple-element.40.refs_5_.refs_2_.refs_1_), channel_id=1, source_target_pairs={{0,1},{1,0},{2,3},{3,2},{4,5},{5,4},{6,7},{7,6},{8,9},{9,8},{10,11... | collective-permute-start | bytes 3538952 | tf_op jit(solution)/shard_map/ppermute | solution.py:347
  34.9 7.5 %collective-permute-start.8 = (bf16[512,1152]{1,0:T(8,128)(2,1)}, bf16[512,1152]{1,0:T(8,128)(2,1)}, u32[]{:S(2)}, u32[]{:S(2)}) collective-permute-start(bf16[512,1152]{1,0:T(8,128)(2,1)} %collective-permute-done.5.refs_6_.refs_3_.refs_2_), channel_id=1, source_target_pairs={{0,1},{1,0},{2,3},{3,2},{4,5},{5,4},{6,7},{7,6},{8,9},{9,8},{10,11... | collective-permute-start | bytes 3538952 | tf_op jit(solution)/shard_map/ppermute | solution.py:347
  40.6 15.1 %collective-permute-start.10 = (bf16[128,2176]{1,0:T(8,128)(2,1)S(1)}, bf16[128,2176]{1,0:T(8,128)(2,1)S(1)}, u32[]{:S(2)}, u32[]{:S(2)}) collective-permute-start(bf16[128,2176]{1,0:T(8,128)(2,1)S(1)} %broadcast_select_fusion.1.refs_2_), channel_id=1, source_target_pairs={{0,2},{1,3},{2,0},{3,1},{4,6},{5,7},{6,4},{7,5},{8,10},{9,11},{10,... | collective-permute-start | bytes 1671176 | tf_op jit(solution)/shard_map/ppermute | solution.py:347
  41.1 14.4 %collective-permute-start.9 = (bf16[128,2176]{1,0:T(8,128)(2,1)S(1)}, bf16[128,2176]{1,0:T(8,128)(2,1)S(1)}, u32[]{:S(2)}, u32[]{:S(2)}) collective-permute-start(bf16[128,2176]{1,0:T(8,128)(2,1)S(1)} %collective-permute-done.6), channel_id=1, source_target_pairs={{4,0},{5,1},{6,2},{7,3},{8,12},{9,13},{10,14},{11,15},{20,16},{21,... | collective-permute-start | bytes 1671176 | tf_op jit(solution)/shard_map/ppermute | solution.py:347
  55.6 15.7 %collective-permute-start.11 = (bf16[128,2176]{1,0:T(8,128)(2,1)S(1)}, bf16[128,2176]{1,0:T(8,128)(2,1)S(1)}, u32[]{:S(2)}, u32[]{:S(2)}) collective-permute-start(bf16[128,2176]{1,0:T(8,128)(2,1)S(1)} %broadcast_select_fusion.refs_0_.refs_5_), channel_id=1, source_target_pairs={{0,2},{1,3},{2,0},{3,1},{4,6},{5,7},{6,4},{7,5},{8,10},{9,11},{10,... | collective-permute-start | bytes 1671176 | tf_op jit(solution)/shard_map/ppermute | solution.py:347
  71.3 9.6 %collective-permute-start.13 = (bf16[1024,1152]{1,0:T(8,128)(2,1)}, bf16[1024,1152]{1,0:T(8,128)(2,1)S(1)}, u32[]{:S(2)}, u32[]{:S(2)}) collective-permute-start(bf16[1024,1152]{1,0:T(8,128)(2,1)} %shard_map.105), channel_id=1, source_target_pairs={{0,1},{1,0},{2,3},{3,2},{4,5},{5,4},{6,7},{7,6},{8,9},{9,8},{10,11... | collective-permute-start | bytes 7077896 | tf_op jit(solution)/shard_map/ppermute | solution.py:347
  72.2 6.6 %copy-start.15 = (bf16[128,1024]{1,0:T(8,128)(2,1)S(1)}, bf16[128,1024]{1,0:T(8,128)(2,1)}, u32[]{:S(2)}) copy-start(bf16[128,1024]{1,0:T(8,128)(2,1)} %get-tuple-element.61) | copy-start | bytes 786436
  78.2 2.7 %collective-permute-start.12 = (bf16[128,3200]{1,0:T(8,128)(2,1)}, bf16[128,3200]{1,0:T(8,128)(2,1)S(1)}, u32[]{:S(2)}, u32[]{:S(2)}) collective-permute-start(bf16[128,3200]{1,0:T(8,128)(2,1)} %get-tuple-element.58), channel_id=1, source_target_pairs={{0,1},{1,0},{2,3},{3,2},{4,5},{5,4},{6,7},{7,6},{8,9},{9,8},{10,11... | collective-permute-start | bytes 2457608 | tf_op jit(solution)/shard_map/ppermute | solution.py:347
  78.8 11.3 %collective-permute-start.15 = (bf16[128,1024]{1,0:T(8,128)(2,1)S(1)}, bf16[128,1024]{1,0:T(8,128)(2,1)S(1)}, u32[]{:S(2)}, u32[]{:S(2)}) collective-permute-start(bf16[128,1024]{1,0:T(8,128)(2,1)S(1)} %copy-done.15), channel_id=1, source_target_pairs={{0,2},{1,3},{2,0},{3,1},{4,6},{5,7},{6,4},{7,5},{8,10},{9,11},{10,... | collective-permute-start | bytes 786440 | tf_op jit(solution)/shard_map/ppermute | solution.py:347
  82.6 7.4 %copy-start.11 = (bf16[128,1024]{1,0:T(8,128)(2,1)S(1)}, bf16[128,1024]{1,0:T(8,128)(2,1)}, u32[]{:S(2)}) copy-start(bf16[128,1024]{1,0:T(8,128)(2,1)} %get-tuple-element.60) | copy-start | bytes 786436
  82.6 14.5 %copy-start.14 = (bf16[256,1024]{1,0:T(8,128)(2,1)S(1)}, bf16[256,1024]{1,0:T(8,128)(2,1)}, u32[]{:S(2)}) copy-start(bf16[256,1024]{1,0:T(8,128)(2,1)} %get-tuple-element.67) | copy-start | bytes 1572868
  82.6 15.5 %copy-start.12 = (bf16[128,1024]{1,0:T(8,128)(2,1)S(1)}, bf16[128,1024]{1,0:T(8,128)(2,1)}, u32[]{:S(2)}) copy-start(bf16[128,1024]{1,0:T(8,128)(2,1)} %get-tuple-element.69) | copy-start | bytes 786436
  88.5 8.7 %collective-permute-start.17 = (bf16[128,1024]{1,0:T(8,128)(2,1)S(1)}, bf16[128,1024]{1,0:T(8,128)(2,1)S(1)}, u32[]{:S(2)}, u32[]{:S(2)}) collective-permute-start(bf16[128,1024]{1,0:T(8,128)(2,1)S(1)} %copy-done.16), channel_id=1, source_target_pairs={{0,2},{1,3},{2,0},{3,1},{4,6},{5,7},{6,4},{7,5},{8,10},{9,11},{10,... | collective-permute-start | bytes 786440 | tf_op jit(solution)/shard_map/ppermute | solution.py:347
  89.5 28.2 %collective-permute-start.14 = (bf16[512,1152]{1,0:T(8,128)(2,1)}, bf16[512,1152]{1,0:T(8,128)(2,1)S(1)}, u32[]{:S(2)}, u32[]{:S(2)}) collective-permute-start(bf16[512,1152]{1,0:T(8,128)(2,1)} %shard_map.107), channel_id=1, source_target_pairs={{0,16},{16,0},{1,17},{17,1},{2,18},{18,2},{3,19},{19,3},{4,20},{20... | collective-permute-start | bytes 3538952 | tf_op jit(solution)/shard_map/ppermute | solution.py:348
  90.1 11.1 %collective-permute-start.16 = (bf16[128,1024]{1,0:T(8,128)(2,1)S(1)}, bf16[128,1024]{1,0:T(8,128)(2,1)S(1)}, u32[]{:S(2)}, u32[]{:S(2)}) collective-permute-start(bf16[128,1024]{1,0:T(8,128)(2,1)S(1)} %add_convert_fusion.5), channel_id=1, source_target_pairs={{0,4},{1,5},{2,6},{3,7},{12,8},{13,9},{14,10},{15,11},{16,20},{17,... | collective-permute-start | bytes 786440 | tf_op jit(solution)/shard_map/ppermute | solution.py:347
  97.1 13.4 %collective-permute-start.18 = (bf16[256,1024]{1,0:T(8,128)(2,1)S(1)}, bf16[256,1024]{1,0:T(8,128)(2,1)S(1)}, u32[]{:S(2)}, u32[]{:S(2)}) collective-permute-start(bf16[256,1024]{1,0:T(8,128)(2,1)S(1)} %copy-done.14), channel_id=1, source_target_pairs={{0,2},{1,3},{2,0},{3,1},{4,6},{5,7},{6,4},{7,5},{8,10},{9,11},{10,... | collective-permute-start | bytes 1572872 | tf_op jit(solution)/shard_map/ppermute | solution.py:347
  98.2 9.8 %collective-permute-start.21 = (bf16[128,1024]{1,0:T(8,128)(2,1)S(1)}, bf16[128,1024]{1,0:T(8,128)(2,1)S(1)}, u32[]{:S(2)}, u32[]{:S(2)}) collective-permute-start(bf16[128,1024]{1,0:T(8,128)(2,1)S(1)} %add_convert_fusion.2), channel_id=1, source_target_pairs={{0,4},{1,5},{2,6},{3,7},{12,8},{13,9},{14,10},{15,11},{16,20},{17,... | collective-permute-start | bytes 786440 | tf_op jit(solution)/shard_map/ppermute | solution.py:347
  101.3 9.2 %copy-start.10 = (bf16[128,1024]{1,0:T(8,128)(2,1)S(1)}, bf16[128,1024]{1,0:T(8,128)(2,1)}, u32[]{:S(2)}) copy-start(bf16[128,1024]{1,0:T(8,128)(2,1)} %get-tuple-element.68) | copy-start | bytes 786436
  101.3 19.1 %collective-permute-start.20 = (bf16[128,1024]{1,0:T(8,128)(2,1)S(1)}, bf16[128,1024]{1,0:T(8,128)(2,1)S(1)}, u32[]{:S(2)}, u32[]{:S(2)}) collective-permute-start(bf16[128,1024]{1,0:T(8,128)(2,1)S(1)} %add_convert_fusion.4), channel_id=1, source_target_pairs={{4,8},{5,9},{6,10},{7,11},{8,4},{9,5},{10,6},{11,7},{20,24},{21,25... | collective-permute-start | bytes 786440 | tf_op jit(solution)/shard_map/ppermute | solution.py:347
  107.9 9.7 %copy-start.2 = (bf16[512,1152]{1,0:T(8,128)(2,1)S(1)}, bf16[512,1152]{1,0:T(8,128)(2,1)}, u32[]{:S(2)}) copy-start(bf16[512,1152]{1,0:T(8,128)(2,1)} %shard_map.108) | copy-start | bytes 3538948
  108.0 12.4 %collective-permute-start.22 = (bf16[128,1024]{1,0:T(8,128)(2,1)S(1)}, bf16[128,1024]{1,0:T(8,128)(2,1)S(1)}, u32[]{:S(2)}, u32[]{:S(2)}) collective-permute-start(bf16[128,1024]{1,0:T(8,128)(2,1)S(1)} %add_convert_fusion.1), channel_id=1, source_target_pairs={{4,12},{5,13},{6,14},{7,15},{8,0},{9,1},{10,2},{11,3},{20,28},{21,... | collective-permute-start | bytes 786440 | tf_op jit(solution)/shard_map/ppermute | solution.py:347
  110.6 12.5 %collective-permute-start.19 = (bf16[128,1024]{1,0:T(8,128)(2,1)S(1)}, bf16[128,1024]{1,0:T(8,128)(2,1)S(1)}, u32[]{:S(2)}, u32[]{:S(2)}) collective-permute-start(bf16[128,1024]{1,0:T(8,128)(2,1)S(1)} %add_convert_fusion.3), channel_id=1, source_target_pairs={{0,4},{1,5},{2,6},{3,7},{4,0},{5,1},{6,2},{7,3},{8,12},{9,13},{10,... | collective-permute-start | bytes 786440 | tf_op jit(solution)/shard_map/ppermute | solution.py:347
  (8 other events, 18.3 us)

commit v12 on v11

--- a/solution.py
+++ b/solution.py
@@ -94,13 +94,16 @@
     )(tokens, d_output, combine.T, routes.T, gate, up, down)
 
 
-def rows_kernel(experts, count, sizes, joined, scal, *refs):
+def rows_kernel(experts, count, sizes, which, scal, *refs):
     refs = list(refs)
+    joined, closing = which == (1,), which == (0,)
     blocks = [refs.pop(0) for _ in range(count)]
-    raw = [refs.pop(0) for _ in range(4)]
+    raw = [refs.pop(0) for _ in range(2 * len(which))]
+    partial = refs.pop(0) if closing else None
     out_rows = [refs.pop(0) for _ in sizes]
-    kept = [refs.pop(0) for _ in range(3 if joined else 4)]
-    block, held, grads, scaled, d_rows, in_sems, out_sems = refs
+    kept = [refs.pop(0) for _ in range(1 if joined else 2 * len(which))]
+    block, held, grads, scaled, d_rows, in_sems, out_sems = refs[:7]
+    before = refs[7] if closing else None
     part, expert = scal[0], scal[1]
     size, stacked = raw[0].shape
     hidden_units = stacked // 3
@@ -110,9 +113,12 @@
     arrivals = [
         pltpu.make_async_copy(b, block.at[pl.ds(i * rows, rows), :], in_sems.at[i]) for i, b in enumerate(blocks)
     ]
-    weights = [pltpu.make_async_copy(raw[i], held.at[i], in_sems.at[count + i]) for i in range(4)]
+    weights = [pltpu.make_async_copy(w, held.at[i], in_sems.at[count + i]) for i, w in enumerate(raw)]
     for c in arrivals + weights:
         c.start()
+    if closing:
+        earlier = pltpu.make_async_copy(partial, before, in_sems.at[count + len(raw)])
+        earlier.start()
     leaving = []
 
     def leave(source, target):
@@ -123,15 +129,15 @@
     for c in arrivals:
         c.wait()
     if joined:
-        leave(block.at[:, pl.ds(0, width)], kept[2].at[:, pl.ds(stacked + width, width)])
+        leave(block.at[:, pl.ds(0, width)], kept[0].at[:, pl.ds(stacked + width, width)])
     sides = [pl.multiple_of(part * size, size), pl.multiple_of((1 - part) * size, size)]
     parts = block[:, 2 * width :].astype(F32)
     lane = lax.broadcasted_iota(jnp.int32, parts.shape, 1)
     first = []
-    for which in range(2):
-        for c in weights[2 * which : 2 * which + 2]:
+    for i, one in enumerate(which):
+        for c in weights[2 * i : 2 * i + 2]:
             c.wait()
-        wanted = expert if which == 0 else expert + 1 - 2 * lax.rem(expert, 2)
+        wanted = expert if one == 0 else expert + 1 - 2 * lax.rem(expert, 2)
         mine = (lax.rem(lane, experts) == wanted) & (lane < 3 * experts)
         weight = jnp.sum(jnp.where(mine, parts, 0.0), axis=1, keepdims=True)
         preact = None
@@ -140,32 +146,35 @@
             at = sides[side]
             grad = block[:, pl.ds(pl.multiple_of(width + at, size), size)]
             scaled_half = (weight * grad.astype(F32)).astype(BF16)
-            scaled[which, :, pl.ds(at, size)] = scaled_half
-            p = dot(block[:, pl.ds(at, size)], held[2 * which + side, :, :both], ((1,), (0,)))
-            h = dot(scaled_half, held[2 * which + side, :, both:], ((1,), (0,)))
+            scaled[i, :, pl.ds(at, size)] = scaled_half
+            p = dot(block[:, pl.ds(at, size)], held[2 * i + side, :, :both], ((1,), (0,)))
+            h = dot(scaled_half, held[2 * i + side, :, both:], ((1,), (0,)))
             preact = p if side == 0 else preact + p
             d_hidden = h if side == 0 else d_hidden + h
         first.append((preact, d_hidden))
-    leave(scaled.at[0], kept[1])
-    leave(scaled.at[1], kept[2].at[:, pl.ds(stacked, width)] if joined else kept[3])
+    for i in range(len(which)):
+        leave(scaled.at[i], kept[0].at[:, pl.ds(stacked, width)] if joined else kept[2 * i + 1])
     second = []
-    for which in range(2):
-        preact, d_hidden = first[which]
+    for i in range(len(which)):
+        preact, d_hidden = first[i]
         gate_pre = preact[:, :hidden_units]
         up_pre = preact[:, hidden_units:]
         sig = jax.nn.sigmoid(gate_pre)
         silu = gate_pre * sig
         d_gate = (d_hidden * up_pre * sig * (1.0 + gate_pre * (1.0 - sig))).astype(BF16)
         d_up = (d_hidden * silu).astype(BF16)
-        grads[which, :, :hidden_units] = d_gate
-        grads[which, :, hidden_units:both] = d_up
-        grads[which, :, both:] = (silu * up_pre).astype(BF16)
+        grads[i, :, :hidden_units] = d_gate
+        grads[i, :, hidden_units:both] = d_up
+        grads[i, :, both:] = (silu * up_pre).astype(BF16)
         d_preact = jnp.concatenate([d_gate, d_up], axis=1)
-        second.append([dot(d_preact, held[2 * which + side, :, :both], ((1,), (1,))) for side in range(2)])
-    leave(grads.at[0], kept[0])
-    leave(grads.at[1], kept[2].at[:, pl.ds(0, stacked)] if joined else kept[2])
+        second.append([dot(d_preact, held[2 * i + side, :, :both], ((1,), (1,))) for side in range(2)])
+    for i in range(len(which)):
+        leave(grads.at[i], kept[0].at[:, pl.ds(0, stacked)] if joined else kept[2 * i])
+    if closing:
+        earlier.wait()
+        second.append([before[:, pl.ds(at, size)] for at in sides])
     for side in range(2):
-        d_rows[:, pl.ds(sides[side], size)] = (second[0][side] + second[1][side]).astype(BF16)
+        d_rows[:, pl.ds(sides[side], size)] = sum(x[side] for x in second).astype(d_rows.dtype)
     row = 0
     for out, n in zip(out_rows, sizes):
         leave(d_rows.at[pl.ds(row, n), :], out)
@@ -174,34 +183,42 @@
         c.wait()
 
 
-def rows_call(experts, scal, groups, weights, joined=False):
+def rows_call(experts, scal, groups, weights, which=(0, 1), partial=None):
     blocks = [b for group in groups for b in group]
     count = len(blocks)
     rows = blocks[0].shape[0]
     size, stacked = weights[0].shape
     total = count * rows
     sizes = [len(group) * rows for group in groups]
+    joined = which == (1,)
+    kind = F32 if joined else BF16
     sds = jax.ShapeDtypeStruct
-    out = [sds((n, 2 * size), BF16) for n in sizes]
-    out += [sds((total, stacked), BF16), sds((total, 2 * size), BF16)]
-    out += [sds((total, stacked + 4 * size), BF16)] if joined else out[-2:]
+    out = [sds((n, 2 * size), kind) for n in sizes]
+    if joined:
+        out += [sds((total, stacked + 4 * size), BF16)]
+    else:
+        out += [sds((total, stacked), BF16), sds((total, 2 * size), BF16)] * len(which)
+    operands = [*blocks, *weights] + ([] if partial is None else [partial])
+    scratch = [
+        pltpu.VMEM((total, blocks[0].shape[1]), BF16),
+        pltpu.VMEM((len(weights), size, stacked), BF16),
+        pltpu.VMEM((len(which), total, stacked), BF16),
+        pltpu.VMEM((len(which), total, 2 * size), BF16),
+        pltpu.VMEM((total, 2 * size), kind),
+        pltpu.SemaphoreType.DMA((len(operands),)),
+        pltpu.SemaphoreType.DMA((len(groups) + 5,)),
+    ]
+    if partial is not None:
+        scratch.append(pltpu.VMEM(partial.shape, F32))
     return pl.pallas_call(
-        functools.partial(rows_kernel, experts, count, sizes, joined),
+        functools.partial(rows_kernel, experts, count, sizes, which),
         out_shape=out,
-        in_specs=[smem()] + [hbm()] * (count + 4),
+        in_specs=[smem()] + [hbm()] * len(operands),
         out_specs=[hbm()] * len(out),
-        scratch_shapes=[
-            pltpu.VMEM((total, blocks[0].shape[1]), BF16),
-            pltpu.VMEM((4, size, stacked), BF16),
-            pltpu.VMEM((2, total, stacked), BF16),
-            pltpu.VMEM((2, total, 2 * size), BF16),
-            pltpu.VMEM((total, 2 * size), BF16),
-            pltpu.SemaphoreType.DMA((count + 4,)),
-            pltpu.SemaphoreType.DMA((len(groups) + 5,)),
-        ],
-        cost_estimate=cost(24 * total * size * stacked * 2 * (10 if joined else 1), 1 << 20),
+        scratch_shapes=scratch,
+        cost_estimate=cost(24 * total * size * stacked * len(which) * (1 if len(which) == 2 else 10), 1 << 20),
         compiler_params=params(),
-    )(scal, *blocks, *weights)
+    )(scal, *operands)
 
 
 def half_kernel(count, groups, joined, adds, at, sides, *refs):
@@ -375,7 +392,8 @@
     y3 = after(y3, q2, to_core)
     r2 = move(after(q2, y3), SWAP_Y)
 
-    q3, *kept_d, joined = rows_call(experts, scal, [[y3]], weights, joined=True)
+    partial, joined = rows_call(experts, scal, [[y3]], weights[2:], which=(1,))
+    q3, *kept_d = rows_call(experts, scal, [[y3]], weights[:2], which=(0,), partial=partial)
     last = swap(joined)
     all_blocks = blocks + [y3]
     all_kept = [k[:2] for k in kept] + [kept_d]

time: 124 us -> 125 us (level)
  Pallas kernels: 45.9 us -> 49.1 us
  waiting for transfers between devices: 41.1 us -> 37.9 us
    ppermute x21, waiting for transfers between devices: 35.6 us -> 32.3 us  [dense_body(): move = lambda a, pairs: lax.ppermute(a, 'expert', pairs)]
    pallas_call x3 -> x4, Pallas kernels: 23.8 us -> 26.9 us  [rows_call(): pl.pallas_call(functools.partial(rows_kernel, experts, count, sizes, whic...]
  transfers between devices with their start and end apart: 23 -> 23, of which waited for: 10 -> 9; matrix products, arithmetic and copies ran while one was open for 3% -> 4% of each run, Pallas kernels for 35% -> 37%
where the time goes in v12:
time: 125 us
  Pallas kernels  49.1 us (39%)
  waiting for transfers between devices  37.9 us (30%)
  starting transfers between devices  28.9 us (23%)
  local copies, waits for them, and re-layouts  4.95 us (4%)
  other arithmetic  2.92 us (2%)
    ppermute x21, waiting for transfers between devices, dense_body(): move = lambda a, pairs: lax.ppermute(a, 'expert', pairs)  32.3 us
    pallas_call x4, Pallas kernels, rows_call(): pl.pallas_call(functools.partial(rows_kernel, experts, count, sizes, whic...  26.9 us
    ppermute x21, starting transfers between devices, dense_body(): move = lambda a, pairs: lax.ppermute(a, 'expert', pairs)  25.4 us
    pallas_call x3, Pallas kernels, half_call(): pl.pallas_call(functools.partial(half_kernel, len(blocks), len(kept), las...  19.5 us
    ppermute x2, waiting for transfers between devices, dense_body(): across = lambda a: lax.ppermute(a, 'dp', [(0, 1), (1, 0)])  5.65 us
    unnamed x35, local copies, waits for them, and re-layouts  3.66 us
    ppermute x2, starting transfers between devices, dense_body(): across = lambda a: lax.ppermute(a, 'dp', [(0, 1), (1, 0)])  3.54 us
    pallas_call x1, Pallas kernels, pack(): pl.pallas_call(functools.partial(pack_kernel, experts), out_shape=[jax.Sh...  2.7 us
  transfers between devices with their start and end apart: 23, of which 9 were waited for; matrix products, arithmetic and copies ran while one was open for 4% of the time, Pallas kernels for 37%

profile of v12, /device:TPU:0, one launch (start us, length us, event | category | flops | bytes accessed | tf_op | source)
XLA Modules:
  0.0 124.8 jit_solution(6778346619841512408)
XLA Ops:
  0.6 2.7 %shard_map.102 = (bf16[128,2176]{1,0:T(8,128)(2,1)}, bf16[512,1152]{1,0:T(8,128)(2,1)}) custom-call(bf16[128,1024]{1,0:T(8,128)(2,1)} %tokens.1, bf16[128,1024]{1,0:T(8,128)(2,1)} %d_output.1, f32[8,128]{1,0:T(8,128)} %bitcast.19, s32[8,128]{1,0:T(8,128)} %bitcast.20, bf16[512,384]{1,0:T(8,128)(2,1)} %bitcast.16, bf16[512,384]{1,0:T(8,128)(2,1)} %bitcast.17, ...), custom_call_target="tpu_custom_call" | custom-call | bytes 1048576 | tf_op jit(solution)/shard_map/pallas_call | solution.py:79
  3.3 3.0 %collective-permute-start.5 = (bf16[512,1152]{1,0:T(8,128)(2,1)}, bf16[512,1152]{1,0:T(8,128)(2,1)}, u32[]{:S(2)}, u32[]{:S(2)}) collective-permute-start(bf16[512,1152]{1,0:T(8,128)(2,1)} %get-tuple-element.41.refs_5_.refs_2_.refs_1_), channel_id=1, source_target_pairs={{0,16},{16,0},{1,17},{17,1},{2,18},{18,2},{3,19},{19,3},{4,20},{20... | collective-permute-start | bytes 3538952 | tf_op jit(solution)/shard_map/ppermute | solution.py:365
  6.3 1.6 %collective-permute-start = (bf16[128,2176]{1,0:T(8,128)(2,1)}, bf16[128,2176]{1,0:T(8,128)(2,1)S(1)}, u32[]{:S(2)}, u32[]{:S(2)}) collective-permute-start(bf16[128,2176]{1,0:T(8,128)(2,1)} %get-tuple-element.38.refs_0_), channel_id=1, source_target_pairs={{0,4},{1,5},{2,6},{3,7},{4,0},{5,1},{6,2},{7,3},{8,12},{9,13},{10,... | collective-permute-start | bytes 1671176 | tf_op jit(solution)/shard_map/ppermute | solution.py:364
  7.9 1.5 %collective-permute-start.3 = (bf16[128,2176]{1,0:T(8,128)(2,1)}, bf16[128,2176]{1,0:T(8,128)(2,1)S(1)}, u32[]{:S(2)}, u32[]{:S(2)}) collective-permute-start(bf16[128,2176]{1,0:T(8,128)(2,1)} %get-tuple-element.38.refs_0_), channel_id=1, source_target_pairs={{0,2},{1,3},{2,0},{3,1},{4,6},{5,7},{6,4},{7,5},{8,10},{9,11},{10,... | collective-permute-start | bytes 1671176 | tf_op jit(solution)/shard_map/ppermute | solution.py:364
  10.1 10.5 %collective-permute-done.refs_1_ = bf16[128,2176]{1,0:T(8,128)(2,1)S(1)} collective-permute-done((bf16[128,2176]{1,0:T(8,128)(2,1)}, bf16[128,2176]{1,0:T(8,128)(2,1)S(1)}, u32[]{:S(2)}, u32[]{:S(2)}) %collective-permute-start) | collective-permute-done | bytes 557088 | tf_op jit(solution)/shard_map/ppermute | solution.py:364
  20.6 1.3 %collective-permute-done.3.refs_3_ = bf16[128,2176]{1,0:T(8,128)(2,1)S(1)} collective-permute-done((bf16[128,2176]{1,0:T(8,128)(2,1)}, bf16[128,2176]{1,0:T(8,128)(2,1)S(1)}, u32[]{:S(2)}, u32[]{:S(2)}) %collective-permute-start.3) | collective-permute-done | bytes 557088 | tf_op jit(solution)/shard_map/ppermute | solution.py:364
  21.9 1.5 %collective-permute-start.4 = (bf16[128,2176]{1,0:T(8,128)(2,1)S(1)}, bf16[128,2176]{1,0:T(8,128)(2,1)S(1)}, u32[]{:S(2)}, u32[]{:S(2)}) collective-permute-start(bf16[128,2176]{1,0:T(8,128)(2,1)S(1)} %collective-permute-done.refs_1_), channel_id=1, source_target_pairs={{0,2},{1,3},{2,0},{3,1},{4,6},{5,7},{6,4},{7,5},{8,10},{9,11},{10,... | collective-permute-start | bytes 1671176 | tf_op jit(solution)/shard_map/ppermute | solution.py:364
  24.2 1.3 %collective-permute-start.2 = (bf16[128,2176]{1,0:T(8,128)(2,1)S(1)}, bf16[128,2176]{1,0:T(8,128)(2,1)S(1)}, u32[]{:S(2)}, u32[]{:S(2)}) collective-permute-start(bf16[128,2176]{1,0:T(8,128)(2,1)S(1)} %collective-permute-done.1), channel_id=1, source_target_pairs={{4,0},{5,1},{6,2},{7,3},{8,12},{9,13},{10,14},{11,15},{20,16},{21,... | collective-permute-start | bytes 1671176 | tf_op jit(solution)/shard_map/ppermute | solution.py:364
  25.5 9.5 %collective-permute-done.4.refs_4_ = bf16[128,2176]{1,0:T(8,128)(2,1)S(1)} collective-permute-done((bf16[128,2176]{1,0:T(8,128)(2,1)S(1)}, bf16[128,2176]{1,0:T(8,128)(2,1)S(1)}, u32[]{:S(2)}, u32[]{:S(2)}) %collective-permute-start.4) | collective-permute-done | bytes 557088 | tf_op jit(solution)/shard_map/ppermute | solution.py:364
  36.7 3.8 %collective-permute-done.2 = bf16[128,2176]{1,0:T(8,128)(2,1)S(1)} collective-permute-done((bf16[128,2176]{1,0:T(8,128)(2,1)S(1)}, bf16[128,2176]{1,0:T(8,128)(2,1)S(1)}, u32[]{:S(2)}, u32[]{:S(2)}) %collective-permute-start.2) | collective-permute-done | bytes 557088 | tf_op jit(solution)/shard_map/ppermute | solution.py:364
  41.1 1.3 %collective-permute-start.9 = (bf16[128,2176]{1,0:T(8,128)(2,1)S(1)}, bf16[128,2176]{1,0:T(8,128)(2,1)S(1)}, u32[]{:S(2)}, u32[]{:S(2)}) collective-permute-start(bf16[128,2176]{1,0:T(8,128)(2,1)S(1)} %collective-permute-done.6), channel_id=1, source_target_pairs={{4,0},{5,1},{6,2},{7,3},{8,12},{9,13},{10,14},{11,15},{20,16},{21,... | collective-permute-start | bytes 1671176 | tf_op jit(solution)/shard_map/ppermute | solution.py:364
  42.5 11.5 %shard_map.103 = (bf16[128,1024]{1,0:T(8,128)(2,1)}, bf16[128,1024]{1,0:T(8,128)(2,1)}, bf16[128,1024]{1,0:T(8,128)(2,1)}, bf16[256,1024]{1,0:T(8,128)(2,1)}, bf...) custom-call(s32[2]{0:T(128)} %pad_add_fusion.scal, ...), custom_call_target="tpu_custom_call" | custom-call | flops 18119393280 | bytes 1048576 | tf_op jit(solution)/shard_map/pallas_call | solution.py:213
  54.0 1.7 %collective-permute-done.9 = bf16[128,2176]{1,0:T(8,128)(2,1)S(1)} collective-permute-done((bf16[128,2176]{1,0:T(8,128)(2,1)S(1)}, bf16[128,2176]{1,0:T(8,128)(2,1)S(1)}, u32[]{:S(2)}, u32[]{:S(2)}) %collective-permute-start.9) | collective-permute-done | bytes 557088 | tf_op jit(solution)/shard_map/ppermute | solution.py:364
  55.8 1.6 %collective-permute-start.11 = (bf16[128,2176]{1,0:T(8,128)(2,1)S(1)}, bf16[128,2176]{1,0:T(8,128)(2,1)S(1)}, u32[]{:S(2)}, u32[]{:S(2)}) collective-permute-start(bf16[128,2176]{1,0:T(8,128)(2,1)S(1)} %broadcast_select_fusion.refs_0_.refs_5_), channel_id=1, source_target_pairs={{0,2},{1,3},{2,0},{3,1},{4,6},{5,7},{6,4},{7,5},{8,10},{9,11},{10,... | collective-permute-start | bytes 1671176 | tf_op jit(solution)/shard_map/ppermute | solution.py:364
  57.3 6.2 %shard_map.104 = (bf16[128,1024]{1,0:T(8,128)(2,1)}, bf16[128,1024]{1,0:T(8,128)(2,1)}, bf16[256,1152]{1,0:T(8,128)(2,1)}, bf16[256,1024]{1,0:T(8,128)(2,1)}, bf...) custom-call(s32[2]{0:T(128)} %pad_add_fusion.scal, bf16[128,2176]{1,0:T(8,128)(2,1)} %copy-done.1, ...), custom_call_target="tpu_custom_call" | custom-call | flops 7247757312 | bytes 1048576 | tf_op jit(solution)/shard_map/pallas_call | solution.py:213
  63.6 7.8 %shard_map.105 = bf16[1024,1152]{1,0:T(8,128)(2,1)} custom-call(s32[2]{0:T(128)} %pad_add_fusion.1.sides, bf16[128,2176]{1,0:T(8,128)(2,1)} %get-tuple-element.38.refs_0_, bf16[128,2176]{1,0:T(8,128)(2,1)} %copy-done.4, bf16[128,2176]{1,0:T(8,128)(2,1)} %copy-done, bf16[128,2176]{1,0:T(8,128)(2,1)} %copy-done.5, bf16[128,2176]{1,0:T(8,128)(2,1)} %copy-done.6, ...), custom_call_target="tpu_custom_call" | custom-call | flops 1024 | bytes 1024 | tf_op jit(solution)/shard_map/pallas_call | solution.py:305
  72.3 4.7 %shard_map.106 = (f32[128,1024]{1,0:T(8,128)}, bf16[128,3200]{1,0:T(8,128)(2,1)}) custom-call(s32[2]{0:T(128)} %pad_add_fusion.scal, bf16[128,2176]{1,0:T(8,128)(2,1)} %copy-done.9, bf16[512,1152]{1,0:T(8,128)(2,1)} %collective-permute-done.7.refs_7_.refs_4_.refs_1_, bf16[512,1152]{1,0:T(8,128)(2,1)} %collective-permute-done.8.refs_8_.refs_5_.refs_2_), custom_call_target="tpu_custom_call" | custom-call | flops 18119393280 | bytes 1048576 | tf_op jit(solution)/shard_map/pallas_call | solution.py:213
  77.5 0.9 collective-permute-start.15
  78.5 4.5 %shard_map.107 = (bf16[128,1024]{1,0:T(8,128)(2,1)}, bf16[128,1152]{1,0:T(8,128)(2,1)}, bf16[128,1024]{1,0:T(8,128)(2,1)}) custom-call(s32[2]{0:T(128)} %pad_add_fusion.scal, bf16[128,2176]{1,0:T(8,128)(2,1)} %copy-done.9, bf16[512,1152]{1,0:T(8,128)(2,1)} %get-tuple-element.41.refs_5_.refs_2_.refs_1_, ...), custom_call_target="tpu_custom_call" | custom-call | flops 18119393280 | bytes 1048576 | tf_op jit(solution)/shard_map/pallas_call | solution.py:213
  84.7 5.9 %shard_map.108 = bf16[512,1152]{1,0:T(8,128)(2,1)} custom-call(s32[1]{0:T(128)} %bitcast.7.sides, bf16[128,2176]{1,0:T(8,128)(2,1)} %get-tuple-element.38.refs_0_, bf16[128,2176]{1,0:T(8,128)(2,1)} %copy-done.4, bf16[128,2176]{1,0:T(8,128)(2,1)} %copy-done, bf16[128,2176]{1,0:T(8,128)(2,1)} %copy-done.5, bf16[128,2176]{1,0:T(8,128)(2,1)} %copy-done.6, ...), custom_call_target="tpu_custom_call" | custom-call | flops 4831839232 | bytes 1024 | tf_op jit(solution)/shard_map/pallas_call | solution.py:305
  90.6 1.1 collective-permute-start.17
  92.3 3.0 %collective-permute-start.16 = (bf16[128,1024]{1,0:T(8,128)(2,1)S(1)}, bf16[128,1024]{1,0:T(8,128)(2,1)S(1)}, u32[]{:S(2)}, u32[]{:S(2)}) collective-permute-start(bf16[128,1024]{1,0:T(8,128)(2,1)S(1)} %add_convert_fusion.5), channel_id=1, source_target_pairs={{0,4},{1,5},{2,6},{3,7},{12,8},{13,9},{14,10},{15,11},{16,20},{17,... | collective-permute-start | bytes 786440 | tf_op jit(solution)/shard_map/ppermute | solution.py:364
  95.3 3.3 %collective-permute-done.17 = bf16[128,1024]{1,0:T(8,128)(2,1)S(1)} collective-permute-done((bf16[128,1024]{1,0:T(8,128)(2,1)S(1)}, bf16[128,1024]{1,0:T(8,128)(2,1)S(1)}, u32[]{:S(2)}, u32[]{:S(2)}) %collective-permute-start.17) | collective-permute-done | bytes 262176 | tf_op jit(solution)/shard_map/ppermute | solution.py:364
  98.7 1.1 collective-permute-start.18
  99.8 3.0 %collective-permute-start.21 = (bf16[128,1024]{1,0:T(8,128)(2,1)S(1)}, bf16[128,1024]{1,0:T(8,128)(2,1)S(1)}, u32[]{:S(2)}, u32[]{:S(2)}) collective-permute-start(bf16[128,1024]{1,0:T(8,128)(2,1)S(1)} %add_convert_fusion.2), channel_id=1, source_target_pairs={{0,4},{1,5},{2,6},{3,7},{12,8},{13,9},{14,10},{15,11},{16,20},{17,... | collective-permute-start | bytes 786440 | tf_op jit(solution)/shard_map/ppermute | solution.py:364
  103.7 5.8 %shard_map.109 = bf16[512,1152]{1,0:T(8,128)(2,1)} custom-call(s32[1]{0:T(128)} %bitcast.sides, bf16[128,2176]{1,0:T(8,128)(2,1)} %get-tuple-element.38.refs_0_, bf16[128,2176]{1,0:T(8,128)(2,1)} %copy-done.4, bf16[128,2176]{1,0:T(8,128)(2,1)} %copy-done, bf16[128,2176]{1,0:T(8,128)(2,1)} %copy-done.5, bf16[128,2176]{1,0:T(8,128)(2,1)} %copy-done.6, ...), custom_call_target="tpu_custom_call" | custom-call | flops 1024 | bytes 1024 | tf_op jit(solution)/shard_map/pallas_call | solution.py:305
  109.6 1.4 %collective-permute-start.22 = (bf16[128,1024]{1,0:T(8,128)(2,1)S(1)}, bf16[128,1024]{1,0:T(8,128)(2,1)S(1)}, u32[]{:S(2)}, u32[]{:S(2)}) collective-permute-start(bf16[128,1024]{1,0:T(8,128)(2,1)S(1)} %add_convert_fusion.1), channel_id=1, source_target_pairs={{4,12},{5,13},{6,14},{7,15},{8,0},{9,1},{10,2},{11,3},{20,28},{21,... | collective-permute-start | bytes 786440 | tf_op jit(solution)/shard_map/ppermute | solution.py:364
  111.5 2.2 %collective-permute-start.19 = (bf16[128,1024]{1,0:T(8,128)(2,1)S(1)}, bf16[128,1024]{1,0:T(8,128)(2,1)S(1)}, u32[]{:S(2)}, u32[]{:S(2)}) collective-permute-start(bf16[128,1024]{1,0:T(8,128)(2,1)S(1)} %add_convert_fusion.3), channel_id=1, source_target_pairs={{0,4},{1,5},{2,6},{3,7},{4,0},{5,1},{6,2},{7,3},{8,12},{9,13},{10,... | collective-permute-start | bytes 786440 | tf_op jit(solution)/shard_map/ppermute | solution.py:364
  113.7 5.7 %collective-permute-done.14 = bf16[512,1152]{1,0:T(8,128)(2,1)S(1)} collective-permute-done((bf16[512,1152]{1,0:T(8,128)(2,1)}, bf16[512,1152]{1,0:T(8,128)(2,1)S(1)}, u32[]{:S(2)}, u32[]{:S(2)}) %collective-permute-start.14) | collective-permute-done | bytes 1179680 | tf_op jit(solution)/shard_map/ppermute | solution.py:365
  119.6 1.3 %slice_bitcast_fusion = (f32[1,384,512]{1,2,0:T(8,128)S(1)}, f32[1,512,384]{2,1,0:T(8,128)}, f32[1,512,384]{2,1,0:T(8,128)}) fusion(f32[512,1152]{1,0:T(8,128)S(1)} %convert_add_fusion), kind=kLoop, calls=%fused_computation.1 | loop fusion | bytes 4718592 | tf_op jit(solution)/shard_map/broadcast_in_dim | solution.py:420
  120.9 1.1 copy.11
  122.1 1.8 %collective-permute-done.19 = bf16[128,1024]{1,0:T(8,128)(2,1)S(1)} collective-permute-done((bf16[128,1024]{1,0:T(8,128)(2,1)S(1)}, bf16[128,1024]{1,0:T(8,128)(2,1)S(1)}, u32[]{:S(2)}, u32[]{:S(2)}) %collective-permute-start.19) | collective-permute-done | bytes 262176 | tf_op jit(solution)/shard_map/ppermute | solution.py:364
  (69 shorter events, 10.3 us)
Async XLA Ops:
  3.3 31.6 %collective-permute-start.5 = (bf16[512,1152]{1,0:T(8,128)(2,1)}, bf16[512,1152]{1,0:T(8,128)(2,1)}, u32[]{:S(2)}, u32[]{:S(2)}) collective-permute-start(bf16[512,1152]{1,0:T(8,128)(2,1)} %get-tuple-element.41.refs_5_.refs_2_.refs_1_), channel_id=1, source_target_pairs={{0,16},{16,0},{1,17},{17,1},{2,18},{18,2},{3,19},{19,3},{4,20},{20... | collective-permute-start | bytes 3538952 | tf_op jit(solution)/shard_map/ppermute | solution.py:365
  6.3 14.3 %collective-permute-start = (bf16[128,2176]{1,0:T(8,128)(2,1)}, bf16[128,2176]{1,0:T(8,128)(2,1)S(1)}, u32[]{:S(2)}, u32[]{:S(2)}) collective-permute-start(bf16[128,2176]{1,0:T(8,128)(2,1)} %get-tuple-element.38.refs_0_), channel_id=1, source_target_pairs={{0,4},{1,5},{2,6},{3,7},{4,0},{5,1},{6,2},{7,3},{8,12},{9,13},{10,... | collective-permute-start | bytes 1671176 | tf_op jit(solution)/shard_map/ppermute | solution.py:364
  7.9 14.0 %collective-permute-start.3 = (bf16[128,2176]{1,0:T(8,128)(2,1)}, bf16[128,2176]{1,0:T(8,128)(2,1)S(1)}, u32[]{:S(2)}, u32[]{:S(2)}) collective-permute-start(bf16[128,2176]{1,0:T(8,128)(2,1)} %get-tuple-element.38.refs_0_), channel_id=1, source_target_pairs={{0,2},{1,3},{2,0},{3,1},{4,6},{5,7},{6,4},{7,5},{8,10},{9,11},{10,... | collective-permute-start | bytes 1671176 | tf_op jit(solution)/shard_map/ppermute | solution.py:364
  9.4 14.7 %collective-permute-start.1 = (bf16[128,2176]{1,0:T(8,128)(2,1)}, bf16[128,2176]{1,0:T(8,128)(2,1)S(1)}, u32[]{:S(2)}, u32[]{:S(2)}) collective-permute-start(bf16[128,2176]{1,0:T(8,128)(2,1)} %get-tuple-element.38.refs_0_), channel_id=1, source_target_pairs={{4,8},{5,9},{6,10},{7,11},{8,4},{9,5},{10,6},{11,7},{20,24},{21,25... | collective-permute-start | bytes 1671176 | tf_op jit(solution)/shard_map/ppermute | solution.py:364
  20.6 21.8 %copy-start.4 = (bf16[128,2176]{1,0:T(8,128)(2,1)}, bf16[128,2176]{1,0:T(8,128)(2,1)S(1)}, u32[]{:S(2)}) copy-start(bf16[128,2176]{1,0:T(8,128)(2,1)S(1)} %collective-permute-done.refs_1_) | copy-start | bytes 1671172
  21.9 20.5 %copy-start.5 = (bf16[128,2176]{1,0:T(8,128)(2,1)}, bf16[128,2176]{1,0:T(8,128)(2,1)S(1)}, u32[]{:S(2)}) copy-start(bf16[128,2176]{1,0:T(8,128)(2,1)S(1)} %collective-permute-done.3.refs_3_) | copy-start | bytes 1671172
  21.9 13.0 %collective-permute-start.4 = (bf16[128,2176]{1,0:T(8,128)(2,1)S(1)}, bf16[128,2176]{1,0:T(8,128)(2,1)S(1)}, u32[]{:S(2)}, u32[]{:S(2)}) collective-permute-start(bf16[128,2176]{1,0:T(8,128)(2,1)S(1)} %collective-permute-done.refs_1_), channel_id=1, source_target_pairs={{0,2},{1,3},{2,0},{3,1},{4,6},{5,7},{6,4},{7,5},{8,10},{9,11},{10,... | collective-permute-start | bytes 1671176 | tf_op jit(solution)/shard_map/ppermute | solution.py:364
  23.5 11.5 %collective-permute-start.6 = (bf16[128,2176]{1,0:T(8,128)(2,1)S(1)}, bf16[128,2176]{1,0:T(8,128)(2,1)S(1)}, u32[]{:S(2)}, u32[]{:S(2)}) collective-permute-start(bf16[128,2176]{1,0:T(8,128)(2,1)S(1)} %collective-permute-done.refs_1_), channel_id=1, source_target_pairs={{4,8},{5,9},{6,10},{7,11},{8,4},{9,5},{10,6},{11,7},{20,24},{21,25... | collective-permute-start | bytes 1671176 | tf_op jit(solution)/shard_map/ppermute | solution.py:364
  24.2 16.3 %collective-permute-start.2 = (bf16[128,2176]{1,0:T(8,128)(2,1)S(1)}, bf16[128,2176]{1,0:T(8,128)(2,1)S(1)}, u32[]{:S(2)}, u32[]{:S(2)}) collective-permute-start(bf16[128,2176]{1,0:T(8,128)(2,1)S(1)} %collective-permute-done.1), channel_id=1, source_target_pairs={{4,0},{5,1},{6,2},{7,3},{8,12},{9,13},{10,14},{11,15},{20,16},{21,... | collective-permute-start | bytes 1671176 | tf_op jit(solution)/shard_map/ppermute | solution.py:364
  34.9 7.5 %copy-start.6 = (bf16[128,2176]{1,0:T(8,128)(2,1)}, bf16[128,2176]{1,0:T(8,128)(2,1)S(1)}, u32[]{:S(2)}) copy-start(bf16[128,2176]{1,0:T(8,128)(2,1)S(1)} %collective-permute-done.4.refs_4_) | copy-start | bytes 1671172
  34.9 7.5 %collective-permute-start.7 = (bf16[512,1152]{1,0:T(8,128)(2,1)}, bf16[512,1152]{1,0:T(8,128)(2,1)}, u32[]{:S(2)}, u32[]{:S(2)}) collective-permute-start(bf16[512,1152]{1,0:T(8,128)(2,1)} %get-tuple-element.41.refs_5_.refs_2_.refs_1_), channel_id=1, source_target_pairs={{0,1},{1,0},{2,3},{3,2},{4,5},{5,4},{6,7},{7,6},{8,9},{9,8},{10,11... | collective-permute-start | bytes 3538952 | tf_op jit(solution)/shard_map/ppermute | solution.py:364
  34.9 7.5 %collective-permute-start.8 = (bf16[512,1152]{1,0:T(8,128)(2,1)}, bf16[512,1152]{1,0:T(8,128)(2,1)}, u32[]{:S(2)}, u32[]{:S(2)}) collective-permute-start(bf16[512,1152]{1,0:T(8,128)(2,1)} %collective-permute-done.5.refs_6_.refs_3_.refs_2_), channel_id=1, source_target_pairs={{0,1},{1,0},{2,3},{3,2},{4,5},{5,4},{6,7},{7,6},{8,9},{9,8},{10,11... | collective-permute-start | bytes 3538952 | tf_op jit(solution)/shard_map/ppermute | solution.py:364
  40.6 15.2 %collective-permute-start.10 = (bf16[128,2176]{1,0:T(8,128)(2,1)S(1)}, bf16[128,2176]{1,0:T(8,128)(2,1)S(1)}, u32[]{:S(2)}, u32[]{:S(2)}) collective-permute-start(bf16[128,2176]{1,0:T(8,128)(2,1)S(1)} %broadcast_select_fusion.1.refs_2_), channel_id=1, source_target_pairs={{0,2},{1,3},{2,0},{3,1},{4,6},{5,7},{6,4},{7,5},{8,10},{9,11},{10,... | collective-permute-start | bytes 1671176 | tf_op jit(solution)/shard_map/ppermute | solution.py:364
  41.1 14.5 %collective-permute-start.9 = (bf16[128,2176]{1,0:T(8,128)(2,1)S(1)}, bf16[128,2176]{1,0:T(8,128)(2,1)S(1)}, u32[]{:S(2)}, u32[]{:S(2)}) collective-permute-start(bf16[128,2176]{1,0:T(8,128)(2,1)S(1)} %collective-permute-done.6), channel_id=1, source_target_pairs={{4,0},{5,1},{6,2},{7,3},{8,12},{9,13},{10,14},{11,15},{20,16},{21,... | collective-permute-start | bytes 1671176 | tf_op jit(solution)/shard_map/ppermute | solution.py:364
  55.8 15.7 %collective-permute-start.11 = (bf16[128,2176]{1,0:T(8,128)(2,1)S(1)}, bf16[128,2176]{1,0:T(8,128)(2,1)S(1)}, u32[]{:S(2)}, u32[]{:S(2)}) collective-permute-start(bf16[128,2176]{1,0:T(8,128)(2,1)S(1)} %broadcast_select_fusion.refs_0_.refs_5_), channel_id=1, source_target_pairs={{0,2},{1,3},{2,0},{3,1},{4,6},{5,7},{6,4},{7,5},{8,10},{9,11},{10,... | collective-permute-start | bytes 1671176 | tf_op jit(solution)/shard_map/ppermute | solution.py:364
  71.4 11.6 %collective-permute-start.13 = (bf16[1024,1152]{1,0:T(8,128)(2,1)}, bf16[1024,1152]{1,0:T(8,128)(2,1)S(1)}, u32[]{:S(2)}, u32[]{:S(2)}) collective-permute-start(bf16[1024,1152]{1,0:T(8,128)(2,1)} %shard_map.105), channel_id=1, source_target_pairs={{0,1},{1,0},{2,3},{3,2},{4,5},{5,4},{6,7},{7,6},{8,9},{9,8},{10,11... | collective-permute-start | bytes 7077896 | tf_op jit(solution)/shard_map/ppermute | solution.py:364
  77.0 6.0 %collective-permute-start.12 = (bf16[128,3200]{1,0:T(8,128)(2,1)}, bf16[128,3200]{1,0:T(8,128)(2,1)S(1)}, u32[]{:S(2)}, u32[]{:S(2)}) collective-permute-start(bf16[128,3200]{1,0:T(8,128)(2,1)} %get-tuple-element.60), channel_id=1, source_target_pairs={{0,1},{1,0},{2,3},{3,2},{4,5},{5,4},{6,7},{7,6},{8,9},{9,8},{10,11... | collective-permute-start | bytes 2457608 | tf_op jit(solution)/shard_map/ppermute | solution.py:364
  77.5 14.7 %collective-permute-start.15 = (bf16[128,1024]{1,0:T(8,128)(2,1)S(1)}, bf16[128,1024]{1,0:T(8,128)(2,1)S(1)}, u32[]{:S(2)}, u32[]{:S(2)}) collective-permute-start(bf16[128,1024]{1,0:T(8,128)(2,1)S(1)} %copy-done.15), channel_id=1, source_target_pairs={{0,2},{1,3},{2,0},{3,1},{4,6},{5,7},{6,4},{7,5},{8,10},{9,11},{10,... | collective-permute-start | bytes 786440 | tf_op jit(solution)/shard_map/ppermute | solution.py:364
  84.7 5.9 %copy-start.16 = (bf16[128,1024]{1,0:T(8,128)(2,1)S(1)}, bf16[128,1024]{1,0:T(8,128)(2,1)}, u32[]{:S(2)}) copy-start(bf16[128,1024]{1,0:T(8,128)(2,1)} %get-tuple-element.68) | copy-start | bytes 786436
  84.7 7.6 %copy-start.11 = (bf16[128,1024]{1,0:T(8,128)(2,1)S(1)}, bf16[128,1024]{1,0:T(8,128)(2,1)}, u32[]{:S(2)}) copy-start(bf16[128,1024]{1,0:T(8,128)(2,1)} %get-tuple-element.62) | copy-start | bytes 786436
  84.7 14.0 %copy-start.14 = (bf16[256,1024]{1,0:T(8,128)(2,1)S(1)}, bf16[256,1024]{1,0:T(8,128)(2,1)}, u32[]{:S(2)}) copy-start(bf16[256,1024]{1,0:T(8,128)(2,1)} %get-tuple-element.69) | copy-start | bytes 1572868
  84.7 15.0 %copy-start.12 = (bf16[128,1024]{1,0:T(8,128)(2,1)S(1)}, bf16[128,1024]{1,0:T(8,128)(2,1)}, u32[]{:S(2)}) copy-start(bf16[128,1024]{1,0:T(8,128)(2,1)} %get-tuple-element.71) | copy-start | bytes 786436
  90.6 8.1 %collective-permute-start.17 = (bf16[128,1024]{1,0:T(8,128)(2,1)S(1)}, bf16[128,1024]{1,0:T(8,128)(2,1)S(1)}, u32[]{:S(2)}, u32[]{:S(2)}) collective-permute-start(bf16[128,1024]{1,0:T(8,128)(2,1)S(1)} %copy-done.16), channel_id=1, source_target_pairs={{0,2},{1,3},{2,0},{3,1},{4,6},{5,7},{6,4},{7,5},{8,10},{9,11},{10,... | collective-permute-start | bytes 786440 | tf_op jit(solution)/shard_map/ppermute | solution.py:364
  91.7 27.6 %collective-permute-start.14 = (bf16[512,1152]{1,0:T(8,128)(2,1)}, bf16[512,1152]{1,0:T(8,128)(2,1)S(1)}, u32[]{:S(2)}, u32[]{:S(2)}) collective-permute-start(bf16[512,1152]{1,0:T(8,128)(2,1)} %shard_map.108), channel_id=1, source_target_pairs={{0,16},{16,0},{1,17},{17,1},{2,18},{18,2},{3,19},{19,3},{4,20},{20... | collective-permute-start | bytes 3538952 | tf_op jit(solution)/shard_map/ppermute | solution.py:365
  92.3 10.4 %collective-permute-start.16 = (bf16[128,1024]{1,0:T(8,128)(2,1)S(1)}, bf16[128,1024]{1,0:T(8,128)(2,1)S(1)}, u32[]{:S(2)}, u32[]{:S(2)}) collective-permute-start(bf16[128,1024]{1,0:T(8,128)(2,1)S(1)} %add_convert_fusion.5), channel_id=1, source_target_pairs={{0,4},{1,5},{2,6},{3,7},{12,8},{13,9},{14,10},{15,11},{16,20},{17,... | collective-permute-start | bytes 786440 | tf_op jit(solution)/shard_map/ppermute | solution.py:364
  98.7 12.8 %collective-permute-start.18 = (bf16[256,1024]{1,0:T(8,128)(2,1)S(1)}, bf16[256,1024]{1,0:T(8,128)(2,1)S(1)}, u32[]{:S(2)}, u32[]{:S(2)}) collective-permute-start(bf16[256,1024]{1,0:T(8,128)(2,1)S(1)} %copy-done.14), channel_id=1, source_target_pairs={{0,2},{1,3},{2,0},{3,1},{4,6},{5,7},{6,4},{7,5},{8,10},{9,11},{10,... | collective-permute-start | bytes 1572872 | tf_op jit(solution)/shard_map/ppermute | solution.py:364
  99.8 9.7 %collective-permute-start.21 = (bf16[128,1024]{1,0:T(8,128)(2,1)S(1)}, bf16[128,1024]{1,0:T(8,128)(2,1)S(1)}, u32[]{:S(2)}, u32[]{:S(2)}) collective-permute-start(bf16[128,1024]{1,0:T(8,128)(2,1)S(1)} %add_convert_fusion.2), channel_id=1, source_target_pairs={{0,4},{1,5},{2,6},{3,7},{12,8},{13,9},{14,10},{15,11},{16,20},{17,... | collective-permute-start | bytes 786440 | tf_op jit(solution)/shard_map/ppermute | solution.py:364
  102.9 8.5 %copy-start.10 = (bf16[128,1024]{1,0:T(8,128)(2,1)S(1)}, bf16[128,1024]{1,0:T(8,128)(2,1)}, u32[]{:S(2)}) copy-start(bf16[128,1024]{1,0:T(8,128)(2,1)} %get-tuple-element.70) | copy-start | bytes 786436
  102.9 19.2 %collective-permute-start.20 = (bf16[128,1024]{1,0:T(8,128)(2,1)S(1)}, bf16[128,1024]{1,0:T(8,128)(2,1)S(1)}, u32[]{:S(2)}, u32[]{:S(2)}) collective-permute-start(bf16[128,1024]{1,0:T(8,128)(2,1)S(1)} %add_convert_fusion.4), channel_id=1, source_target_pairs={{4,8},{5,9},{6,10},{7,11},{8,4},{9,5},{10,6},{11,7},{20,24},{21,25... | collective-permute-start | bytes 786440 | tf_op jit(solution)/shard_map/ppermute | solution.py:364
  109.5 9.8 %copy-start.2 = (bf16[512,1152]{1,0:T(8,128)(2,1)S(1)}, bf16[512,1152]{1,0:T(8,128)(2,1)}, u32[]{:S(2)}) copy-start(bf16[512,1152]{1,0:T(8,128)(2,1)} %shard_map.109) | copy-start | bytes 3538948
  109.6 12.5 %collective-permute-start.22 = (bf16[128,1024]{1,0:T(8,128)(2,1)S(1)}, bf16[128,1024]{1,0:T(8,128)(2,1)S(1)}, u32[]{:S(2)}, u32[]{:S(2)}) collective-permute-start(bf16[128,1024]{1,0:T(8,128)(2,1)S(1)} %add_convert_fusion.1), channel_id=1, source_target_pairs={{4,12},{5,13},{6,14},{7,15},{8,0},{9,1},{10,2},{11,3},{20,28},{21,... | collective-permute-start | bytes 786440 | tf_op jit(solution)/shard_map/ppermute | solution.py:364
  111.5 12.4 %collective-permute-start.19 = (bf16[128,1024]{1,0:T(8,128)(2,1)S(1)}, bf16[128,1024]{1,0:T(8,128)(2,1)S(1)}, u32[]{:S(2)}, u32[]{:S(2)}) collective-permute-start(bf16[128,1024]{1,0:T(8,128)(2,1)S(1)} %add_convert_fusion.3), channel_id=1, source_target_pairs={{0,4},{1,5},{2,6},{3,7},{4,0},{5,1},{6,2},{7,3},{8,12},{9,13},{10,... | collective-permute-start | bytes 786440 | tf_op jit(solution)/shard_map/ppermute | solution.py:364
  (8 other events, 16.8 us)

commit v13 on v12

--- a/solution.py
+++ b/solution.py
@@ -94,43 +94,58 @@
     )(tokens, d_output, combine.T, routes.T, gate, up, down)
 
 
-def rows_kernel(experts, count, sizes, which, scal, *refs):
+def rows_kernel(experts, count, sizes, which, halves, scal, *refs):
     refs = list(refs)
-    joined, closing = which == (1,), which == (0,)
     blocks = [refs.pop(0) for _ in range(count)]
     raw = [refs.pop(0) for _ in range(2 * len(which))]
-    partial = refs.pop(0) if closing else None
+    past, kinds, wanted_sides, adds = halves
+    past_blocks = [refs.pop(0) for _ in range(past)]
+    past_grads = [refs.pop(0) for _ in range(kinds)]
+    past_scaled = [refs.pop(0) for _ in range(kinds)]
+    more = refs.pop(0) if adds else None
     out_rows = [refs.pop(0) for _ in sizes]
-    kept = [refs.pop(0) for _ in range(1 if joined else 2 * len(which))]
+    kept = [refs.pop(0) for _ in range(2 * len(which))]
+    products = [refs.pop(0) for _ in wanted_sides]
     block, held, grads, scaled, d_rows, in_sems, out_sems = refs[:7]
-    before = refs[7] if closing else None
     part, expert = scal[0], scal[1]
     size, stacked = raw[0].shape
     hidden_units = stacked // 3
     both = 2 * hidden_units
     width = 2 * size
     rows = blocks[0].shape[0]
-    arrivals = [
-        pltpu.make_async_copy(b, block.at[pl.ds(i * rows, rows), :], in_sems.at[i]) for i, b in enumerate(blocks)
-    ]
-    weights = [pltpu.make_async_copy(w, held.at[i], in_sems.at[count + i]) for i, w in enumerate(raw)]
-    for c in arrivals + weights:
-        c.start()
-    if closing:
-        earlier = pltpu.make_async_copy(partial, before, in_sems.at[count + len(raw)])
-        earlier.start()
-    leaving = []
+    sides = [pl.multiple_of(part * size, size), pl.multiple_of((1 - part) * size, size)]
+    started, leaving = [], []
+
+    def start(source, target):
+        copy = pltpu.make_async_copy(source, target, in_sems.at[len(started)])
+        copy.start()
+        started.append(copy)
+        return copy
 
     def leave(source, target):
         copy = pltpu.make_async_copy(source, target, out_sems.at[len(leaving)])
         copy.start()
         leaving.append(copy)
 
+    arrivals = [start(b, block.at[pl.ds(i * rows, rows), :]) for i, b in enumerate(blocks)]
+    weights = [start(w, held.at[i]) for i, w in enumerate(raw)]
+    later = []
+    if wanted_sides:
+        lefts, made, extra, done = refs[7:]
+        row = 0
+        for g, x in zip(past_grads, past_scaled):
+            n = g.shape[0]
+            later.append(start(g, made.at[pl.ds(row, n), :]))
+            for k, side in enumerate(wanted_sides):
+                later.append(start(x.at[:, pl.ds(sides[side], size)], lefts.at[k, 1, pl.ds(row, n), :]))
+            row += n
+        for i, b in enumerate(past_blocks):
+            for k, side in enumerate(wanted_sides):
+                later.append(start(b.at[:, pl.ds(sides[side], size)], lefts.at[k, 0, pl.ds(i * rows, rows), :]))
+        if adds:
+            later.append(start(more, extra))
     for c in arrivals:
         c.wait()
-    if joined:
-        leave(block.at[:, pl.ds(0, width)], kept[0].at[:, pl.ds(stacked + width, width)])
-    sides = [pl.multiple_of(part * size, size), pl.multiple_of((1 - part) * size, size)]
     parts = block[:, 2 * width :].astype(F32)
     lane = lax.broadcasted_iota(jnp.int32, parts.shape, 1)
     first = []
@@ -153,7 +168,7 @@
             d_hidden = h if side == 0 else d_hidden + h
         first.append((preact, d_hidden))
     for i in range(len(which)):
-        leave(scaled.at[i], kept[0].at[:, pl.ds(stacked, width)] if joined else kept[2 * i + 1])
+        leave(scaled.at[i], kept[2 * i + 1])
     second = []
     for i in range(len(which)):
         preact, d_hidden = first[i]
@@ -169,49 +184,64 @@
         d_preact = jnp.concatenate([d_gate, d_up], axis=1)
         second.append([dot(d_preact, held[2 * i + side, :, :both], ((1,), (1,))) for side in range(2)])
     for i in range(len(which)):
-        leave(grads.at[i], kept[0].at[:, pl.ds(0, stacked)] if joined else kept[2 * i])
-    if closing:
-        earlier.wait()
-        second.append([before[:, pl.ds(at, size)] for at in sides])
+        leave(grads.at[i], kept[2 * i])
     for side in range(2):
-        d_rows[:, pl.ds(sides[side], size)] = sum(x[side] for x in second).astype(d_rows.dtype)
+        d_rows[:, pl.ds(sides[side], size)] = sum(x[side] for x in second).astype(BF16)
     row = 0
     for out, n in zip(out_rows, sizes):
         leave(d_rows.at[pl.ds(row, n), :], out)
         row += n
+    for c in later:
+        c.wait()
+    end = len(which) - 1
+    for k, side in enumerate(wanted_sides):
+        at = sides[side]
+        for kind, span in enumerate((slice(0, both), slice(both, stacked))):
+            now = block[:, pl.ds(at, size)] if kind == 0 else scaled[end, :, pl.ds(at, size)]
+            new = dot(lefts[k, kind], made[:, span], ((0,), (0,))) + dot(now, grads[end, :, span], ((0,), (0,)))
+            if adds:
+                new = new + extra[:, span].astype(F32)
+            done[k, :, span] = new.astype(BF16)
+        leave(done.at[k], products[k])
     for c in leaving:
         c.wait()
 
 
-def rows_call(experts, scal, groups, weights, which=(0, 1), partial=None):
+def rows_call(experts, scal, groups, weights, which=(0, 1), past=((), ()), sides=(), more=None):
     blocks = [b for group in groups for b in group]
     count = len(blocks)
     rows = blocks[0].shape[0]
     size, stacked = weights[0].shape
     total = count * rows
     sizes = [len(group) * rows for group in groups]
-    joined = which == (1,)
-    kind = F32 if joined else BF16
     sds = jax.ShapeDtypeStruct
-    out = [sds((n, 2 * size), kind) for n in sizes]
-    if joined:
-        out += [sds((total, stacked + 4 * size), BF16)]
-    else:
-        out += [sds((total, stacked), BF16), sds((total, 2 * size), BF16)] * len(which)
-    operands = [*blocks, *weights] + ([] if partial is None else [partial])
+    out = [sds((n, 2 * size), BF16) for n in sizes]
+    out += [sds((total, stacked), BF16), sds((total, 2 * size), BF16)] * len(which)
+    out += [sds((size, stacked), BF16)] * len(sides)
+    past_blocks, past_kept = past
+    operands = [*blocks, *weights, *past_blocks, *(k[0] for k in past_kept), *(k[1] for k in past_kept)]
+    if more is not None:
+        operands.append(more)
     scratch = [
         pltpu.VMEM((total, blocks[0].shape[1]), BF16),
         pltpu.VMEM((len(weights), size, stacked), BF16),
         pltpu.VMEM((len(which), total, stacked), BF16),
         pltpu.VMEM((len(which), total, 2 * size), BF16),
-        pltpu.VMEM((total, 2 * size), kind),
-        pltpu.SemaphoreType.DMA((len(operands),)),
-        pltpu.SemaphoreType.DMA((len(groups) + 5,)),
+        pltpu.VMEM((total, 2 * size), BF16),
+        pltpu.SemaphoreType.DMA((len(operands) + len(sides) * (len(past_blocks) + len(past_kept)),)),
+        pltpu.SemaphoreType.DMA((len(out),)),
     ]
-    if partial is not None:
-        scratch.append(pltpu.VMEM(partial.shape, F32))
+    if sides:
+        earlier = len(past_blocks) * rows
+        scratch += [
+            pltpu.VMEM((len(sides), 2, earlier, size), BF16),
+            pltpu.VMEM((earlier, stacked), BF16),
+            pltpu.VMEM((size, stacked), BF16),
+            pltpu.VMEM((len(sides), size, stacked), BF16),
+        ]
+    halves = (len(past_blocks), len(past_kept), sides, more is not None)
     return pl.pallas_call(
-        functools.partial(rows_kernel, experts, count, sizes, which),
+        functools.partial(rows_kernel, experts, count, sizes, which, halves),
         out_shape=out,
         in_specs=[smem()] + [hbm()] * len(operands),
         out_specs=[hbm()] * len(out),
@@ -221,101 +251,70 @@
     )(scal, *operands)
 
 
-def half_kernel(count, groups, joined, adds, at, sides, *refs):
+def half_kernel(count, groups, sides, *refs):
     refs = list(refs)
     blocks = [refs.pop(0) for _ in range(count)]
     scaled = [refs.pop(0) for _ in range(groups)]
     grads = [refs.pop(0) for _ in range(groups)]
-    last = refs.pop(0) if joined else None
-    more = refs.pop(0) if adds else None
-    out, lefts, made, extra, done, sems, out_sems = refs
-    size, stacked = done.shape[1:]
+    more, out, lefts, made, extra, done, sems, out_sems = refs
+    size, stacked = done.shape
     both = stacked // 3 * 2
     rows = blocks[0].shape[0]
-    steps = done.shape[0]
+    at = pl.multiple_of(sides[0] * size, size)
     started = []
 
     def start(source, target):
         copy = pltpu.make_async_copy(source, target, sems.at[len(started)])
         copy.start()
         started.append(copy)
-        return copy
-
-    loads = [[[], []] for _ in range(steps)]
-    offsets = [pl.multiple_of(sides[i] * size, size) for i in range(steps)]
-    row = 0
+
     for i, b in enumerate(blocks):
-        loads[0][0].append(start(b.at[:, pl.ds(offsets[0], size)], lefts.at[0, 0, pl.ds(row, rows), :]))
-        row += rows
-    if joined:
-        first = pl.multiple_of(stacked + 2 * size + offsets[0], LANES)
-        loads[0][0].append(start(last.at[:, pl.ds(first, size)], lefts.at[0, 0, pl.ds(row, rows), :]))
+        start(b.at[:, pl.ds(at, size)], lefts.at[0, pl.ds(i * rows, rows), :])
     row = 0
     for g in grads:
-        loads[0][0].append(start(g, made.at[pl.ds(row, g.shape[0]), :]))
+        start(g, made.at[pl.ds(row, g.shape[0]), :])
         row += g.shape[0]
-    if joined:
-        loads[0][0].append(start(last.at[:, pl.ds(0, stacked)], made.at[pl.ds(row, rows), :]))
-    if adds:
-        loads[0][0].append(start(more.at[pl.ds(at * size, size), :], extra))
-    for step in range(steps):
-        if step > 0:
-            for i, b in enumerate(blocks):
-                loads[step][0].append(
-                    start(b.at[:, pl.ds(offsets[step], size)], lefts.at[step, 0, pl.ds(i * rows, rows), :])
-                )
-        row = 0
-        for x in scaled:
-            n = x.shape[0]
-            loads[step][1].append(start(x.at[:, pl.ds(offsets[step], size)], lefts.at[step, 1, pl.ds(row, n), :]))
-            row += n
-        if joined:
-            first = pl.multiple_of(stacked + offsets[step], LANES)
-            loads[step][1].append(start(last.at[:, pl.ds(first, size)], lefts.at[step, 1, pl.ds(row, rows), :]))
+    start(more, extra)
+    early = len(started)
+    row = 0
+    for x in scaled:
+        start(x.at[:, pl.ds(at, size)], lefts.at[1, pl.ds(row, x.shape[0]), :])
+        row += x.shape[0]
     leaving = []
-    for step in range(steps):
-        for kind in range(2):
-            for c in loads[step][kind]:
-                c.wait()
-            first, wide = (0, both) if kind == 0 else (both, stacked - both)
-            new = dot(lefts[step, kind], made[:, first : first + wide], ((0,), (0,)))
-            if adds:
-                new = new + extra[:, first : first + wide].astype(F32)
-            done[step, :, first : first + wide] = new.astype(BF16)
-            copy = pltpu.make_async_copy(
-                done.at[step, :, pl.ds(first, wide)],
-                out.at[pl.ds(step * size, size), pl.ds(first, wide)],
-                out_sems.at[len(leaving)],
-            )
-            copy.start()
-            leaving.append(copy)
+    for kind, (first, wide) in enumerate(((0, both), (both, stacked - both))):
+        for c in started[:early] if kind == 0 else started[early:]:
+            c.wait()
+        new = dot(lefts[kind], made[:, first : first + wide], ((0,), (0,)))
+        done[:, first : first + wide] = (new + extra[:, first : first + wide].astype(F32)).astype(BF16)
+        copy = pltpu.make_async_copy(
+            done.at[:, pl.ds(first, wide)], out.at[:, pl.ds(first, wide)], out_sems.at[len(leaving)]
+        )
+        copy.start()
+        leaving.append(copy)
     for c in leaving:
         c.wait()
 
 
-def half_call(sides, blocks, kept, last=None, more=None, at=0, weight=0):
+def half_call(sides, blocks, kept, more):
     grads, scaled = [k[0] for k in kept], [k[1] for k in kept]
     size = scaled[0].shape[1] // 2
     stacked = grads[0].shape[1]
-    rows = blocks[0].shape[0]
-    extra = [a for a in (last, more) if a is not None]
-    operands = [*blocks, *scaled, *grads, *extra]
-    steps = sides.shape[0]
-    total = (len(blocks) + (last is not None)) * rows
+    total = len(blocks) * blocks[0].shape[0]
+    operands = [*blocks, *scaled, *grads, more]
     return pl.pallas_call(
-        functools.partial(half_kernel, len(blocks), len(kept), last is not None, more is not None, at),
-        out_shape=jax.ShapeDtypeStruct((steps * size, stacked), BF16),
+        functools.partial(half_kernel, len(blocks), len(kept)),
+        out_shape=jax.ShapeDtypeStruct((size, stacked), BF16),
         in_specs=[smem()] + [hbm()] * len(operands),
         out_specs=hbm(),
         scratch_shapes=[
-            pltpu.VMEM((steps, 2, total, size), BF16),
+            pltpu.VMEM((2, total, size), BF16),
             pltpu.VMEM((total, stacked), BF16),
             pltpu.VMEM((size, stacked), BF16),
-            pltpu.VMEM((steps, size, stacked), BF16),
-            pltpu.SemaphoreType.DMA((steps * (len(blocks) + len(kept) + 2) + len(kept) + 2,)),
-            pltpu.SemaphoreType.DMA((2 * steps,)),
+            pltpu.VMEM((size, stacked), BF16),
+            pltpu.SemaphoreType.DMA((len(operands),)),
+            pltpu.SemaphoreType.DMA((2,)),
         ],
-        cost_estimate=cost(8 * weight * size * stacked * 1024 + 1024, 1024),
+        cost_estimate=cost(1024, 1024),
         compiler_params=params(),
     )(sides, *operands)
 
@@ -381,38 +380,37 @@
     w_core = swap(after(w_own, y1, f2))
     w_both = swap(after(w_part, y1, f2))
     weights = [w_own, w_part, w_core, w_both]
-    p0, p1, p2, q01, *kept_a = rows_call(experts, scal, [[own], [b1], [b2], [y0, y1]], weights)
+    p0, p1, p2, q0, q1, *kept_a = rows_call(experts, scal, [[own], [b1], [b2], [y0], [y1]], weights)
     b3 = jnp.where(inner, f2, after(g2, p0))
     y3 = move(after(b3, y2), SWAP_Y)
-    p3, q2, *kept_b = rows_call(experts, scal, [[b3], [y2]], weights)
-
-    blocks = [own, b1, b2, y0, y1, b3, y2]
-    kept = [kept_a, kept_b]
-    to_core = half_call(jnp.concatenate([other, mine]), blocks, [k[2:] for k in kept])
-    y3 = after(y3, q2, to_core)
+    early = [own, b1, b2, y0, y1]
+
+    p3, q2, *kept_b, to_other, to_mine = rows_call(
+        experts, scal, [[b3], [y2]], weights, past=(early, [kept_a[2:]]), sides=(1, 0)
+    )
+    y3 = after(y3, q2)
+    cy3 = swap(y3)
+    got_other, got_mine = swap(after(to_other, y3)), swap(after(to_mine, y3, cy3))
     r2 = move(after(q2, y3), SWAP_Y)
-
-    partial, joined = rows_call(experts, scal, [[y3]], weights[2:], which=(1,))
-    q3, *kept_d = rows_call(experts, scal, [[y3]], weights[:2], which=(0,), partial=partial)
-    last = swap(joined)
-    all_blocks = blocks + [y3]
-    all_kept = [k[:2] for k in kept] + [kept_d]
-    got = swap(to_core)
-    send = half_call(other, all_blocks, all_kept, last, got, weight=1)
+    r1 = move(after(q1, y3), SWAP_Y)
+
+    blocks = early + [b3, y2]
+    kept = [kept_a[:2], kept_b[:2]]
+    last, pair, *kept_c, send = rows_call(
+        experts, scal, [[y3], [cy3]], weights[:2], which=(0,), past=(blocks, kept), sides=(1,), more=got_other
+    )
     from_part = across(send)
-    r3 = move(after(q3, send), SWAP_Y)
-    r01 = move(after(q01, r3), SWAP_Y)
-    rows = own.shape[0]
-    r0, r1 = r01[:rows], r01[rows:]
-    keep = half_call(after(mine, send), all_blocks, all_kept, last, got, at=1)
-
     add = lambda *terms: sum(t.astype(F32) for t in terms).astype(BF16)
+    r3 = move(add(last, swap(after(pair, r2, r1, got_mine))), SWAP_Y)
+    r0 = move(after(q0, r3), SWAP_Y)
+    keep = half_call(after(mine, send), blocks + [y3, cy3], kept + [kept_c], more=got_mine)
+
     s1 = add(p1, r1)
     s2 = add(p2, r2)
     s2 = add(s2, move(s2, INWARD))
     s3 = add(p3, r3)
     s3 = add(s3, move(s3, INWARD))
-    d_weights = keep.astype(F32) + after(from_part, s2).astype(F32)
+    d_weights = keep.astype(F32) + after(from_part, s3).astype(F32)
     hidden_units = gate_weight.shape[2]
     d_gate, d_up = d_weights[:, :hidden_units], d_weights[:, hidden_units : 2 * hidden_units]
     d_down = d_weights[:, 2 * hidden_units :].T

time: 125 us -> 119 us (0.952)
  Pallas kernels: 49.1 us -> 37.5 us
  starting transfers between devices: 28.9 us -> 32.3 us
  other arithmetic: 2.92 us -> 4.59 us
    pallas_call x3 -> x1, Pallas kernels: 19.5 us -> 5.81 us  [half_call(): pl.pallas_call(functools.partial(half_kernel, len(blocks), len(kept)), ou...]
    ppermute x21 -> x24, starting transfers between devices: 25.4 us -> 28.8 us  [dense_body(): move = lambda a, pairs: lax.ppermute(a, 'expert', pairs)]
    pallas_call x4 -> x3, Pallas kernels: 26.9 us -> 29 us  [rows_call(): pl.pallas_call(functools.partial(rows_kernel, experts, count, sizes, whic...]
    unnamed x35 -> x33, local copies, waits for them, and re-layouts: 3.66 us -> 2.52 us
    ppermute x21 -> x24, waiting for transfers between devices: 32.3 us -> 33.2 us  [dense_body(): move = lambda a, pairs: lax.ppermute(a, 'expert', pairs)]
  transfers between devices with their start and end apart: 23 -> 26, of which waited for: 9 -> 13; matrix products, arithmetic and copies ran while one was open for 4% -> 4% of each run, Pallas kernels for 37% -> 30%
where the time goes in v13:
time: 119 us; the launch traced here: 118 us
  waiting for transfers between devices  38.5 us (32%)
  Pallas kernels  37.5 us (32%)
  starting transfers between devices  32.3 us (27%)
  other arithmetic  4.59 us (4%)
  local copies, waits for them, and re-layouts  3.81 us (3%)
    ppermute x24, waiting for transfers between devices, dense_body(): move = lambda a, pairs: lax.ppermute(a, 'expert', pairs)  33.2 us
    pallas_call x3, Pallas kernels, rows_call(): pl.pallas_call(functools.partial(rows_kernel, experts, count, sizes, whic...  29 us
    ppermute x24, starting transfers between devices, dense_body(): move = lambda a, pairs: lax.ppermute(a, 'expert', pairs)  28.8 us
    pallas_call x1, Pallas kernels, half_call(): pl.pallas_call(functools.partial(half_kernel, len(blocks), len(kept)), ou...  5.81 us
    ppermute x2, waiting for transfers between devices, dense_body(): across = lambda a: lax.ppermute(a, 'dp', [(0, 1), (1, 0)])  5.26 us
    ppermute x2, starting transfers between devices, dense_body(): across = lambda a: lax.ppermute(a, 'dp', [(0, 1), (1, 0)])  3.52 us
    pallas_call x1, Pallas kernels, pack(): pl.pallas_call(functools.partial(pack_kernel, experts), out_shape=[jax.Sh...  2.73 us
    unnamed x33, local copies, waits for them, and re-layouts  2.52 us
  transfers between devices with their start and end apart: 26, of which 13 were waited for; matrix products, arithmetic and copies ran while one was open for 4% of the time, Pallas kernels for 30%

profile of v13, /device:TPU:0, one launch (start us, length us, event | category | flops | bytes accessed | tf_op | source)
XLA Modules:
  0.0 117.7 jit_solution(5180468758860400405)
XLA Ops:
  0.6 2.7 %shard_map.102 = (bf16[128,2176]{1,0:T(8,128)(2,1)}, bf16[512,1152]{1,0:T(8,128)(2,1)}) custom-call(bf16[128,1024]{1,0:T(8,128)(2,1)} %tokens.1, bf16[128,1024]{1,0:T(8,128)(2,1)} %d_output.1, f32[8,128]{1,0:T(8,128)} %bitcast.18, s32[8,128]{1,0:T(8,128)} %bitcast.19, bf16[512,384]{1,0:T(8,128)(2,1)} %bitcast.15, bf16[512,384]{1,0:T(8,128)(2,1)} %bitcast.16, ...), custom_call_target="tpu_custom_call" | custom-call | bytes 1048576 | tf_op jit(solution)/shard_map/pallas_call | solution.py:79
  3.4 3.0 %collective-permute-start.5 = (bf16[512,1152]{1,0:T(8,128)(2,1)}, bf16[512,1152]{1,0:T(8,128)(2,1)}, u32[]{:S(2)}, u32[]{:S(2)}) collective-permute-start(bf16[512,1152]{1,0:T(8,128)(2,1)} %get-tuple-element.45.refs_5_.refs_2_), channel_id=1, source_target_pairs={{0,16},{16,0},{1,17},{17,1},{2,18},{18,2},{3,19},{19,3},{4,20},{20... | collective-permute-start | bytes 3538952 | tf_op jit(solution)/shard_map/ppermute | solution.py:364
  6.4 1.5 %collective-permute-start.3 = (bf16[128,2176]{1,0:T(8,128)(2,1)}, bf16[128,2176]{1,0:T(8,128)(2,1)S(1)}, u32[]{:S(2)}, u32[]{:S(2)}) collective-permute-start(bf16[128,2176]{1,0:T(8,128)(2,1)} %get-tuple-element.42.refs_0_.refs_6_.refs_4_), channel_id=1, source_target_pairs={{0,2},{1,3},{2,0},{3,1},{4,6},{5,7},{6,4},{7,5},{8,10},{9,11},{10,... | collective-permute-start | bytes 1671176 | tf_op jit(solution)/shard_map/ppermute | solution.py:363
  7.9 1.6 %collective-permute-start = (bf16[128,2176]{1,0:T(8,128)(2,1)}, bf16[128,2176]{1,0:T(8,128)(2,1)S(1)}, u32[]{:S(2)}, u32[]{:S(2)}) collective-permute-start(bf16[128,2176]{1,0:T(8,128)(2,1)} %get-tuple-element.42.refs_0_.refs_6_.refs_4_), channel_id=1, source_target_pairs={{0,4},{1,5},{2,6},{3,7},{4,0},{5,1},{6,2},{7,3},{8,12},{9,13},{10,... | collective-permute-start | bytes 1671176 | tf_op jit(solution)/shard_map/ppermute | solution.py:363
  10.2 10.5 %collective-permute-done.3.refs_3_.refs_9_.refs_7_ = bf16[128,2176]{1,0:T(8,128)(2,1)S(1)} collective-permute-done((bf16[128,2176]{1,0:T(8,128)(2,1)}, bf16[128,2176]{1,0:T(8,128)(2,1)S(1)}, u32[]{:S(2)}, u32[]{:S(2)}) %collective-permute-start.3) | collective-permute-done | bytes 557088 | tf_op jit(solution)/shard_map/ppermute | solution.py:363
  20.7 1.2 %collective-permute-done.refs_1_.refs_7_.refs_5_ = bf16[128,2176]{1,0:T(8,128)(2,1)S(1)} collective-permute-done((bf16[128,2176]{1,0:T(8,128)(2,1)}, bf16[128,2176]{1,0:T(8,128)(2,1)S(1)}, u32[]{:S(2)}, u32[]{:S(2)}) %collective-permute-start) | collective-permute-done | bytes 557088 | tf_op jit(solution)/shard_map/ppermute | solution.py:363
  23.1 1.3 %collective-permute-start.2 = (bf16[128,2176]{1,0:T(8,128)(2,1)S(1)}, bf16[128,2176]{1,0:T(8,128)(2,1)S(1)}, u32[]{:S(2)}, u32[]{:S(2)}) collective-permute-start(bf16[128,2176]{1,0:T(8,128)(2,1)S(1)} %collective-permute-done.1), channel_id=1, source_target_pairs={{4,0},{5,1},{6,2},{7,3},{8,12},{9,13},{10,14},{11,15},{20,16},{21,... | collective-permute-start | bytes 1671176 | tf_op jit(solution)/shard_map/ppermute | solution.py:363
  24.4 10.5 %collective-permute-done.4.refs_4_.refs_10_.refs_8_ = bf16[128,2176]{1,0:T(8,128)(2,1)S(1)} collective-permute-done((bf16[128,2176]{1,0:T(8,128)(2,1)S(1)}, bf16[128,2176]{1,0:T(8,128)(2,1)S(1)}, u32[]{:S(2)}, u32[]{:S(2)}) %collective-permute-start.4) | collective-permute-done | bytes 557088 | tf_op jit(solution)/shard_map/ppermute | solution.py:363
  36.1 3.5 %collective-permute-done.2 = bf16[128,2176]{1,0:T(8,128)(2,1)S(1)} collective-permute-done((bf16[128,2176]{1,0:T(8,128)(2,1)S(1)}, bf16[128,2176]{1,0:T(8,128)(2,1)S(1)}, u32[]{:S(2)}, u32[]{:S(2)}) %collective-permute-start.2) | collective-permute-done | bytes 557088 | tf_op jit(solution)/shard_map/ppermute | solution.py:363
  39.7 1.4 %collective-permute-start.10 = (bf16[128,2176]{1,0:T(8,128)(2,1)S(1)}, bf16[128,2176]{1,0:T(8,128)(2,1)S(1)}, u32[]{:S(2)}, u32[]{:S(2)}) collective-permute-start(bf16[128,2176]{1,0:T(8,128)(2,1)S(1)} %broadcast_select_fusion.1.refs_2_.refs_8_.refs_6_), channel_id=1, source_target_pairs={{0,2},{1,3},{2,0},{3,1},{4,6},{5,7},{6,4},{7,5},{8,10},{9,11},{10,... | collective-permute-start | bytes 1671176 | tf_op jit(solution)/shard_map/ppermute | solution.py:363
  41.1 1.3 %collective-permute-start.9 = (bf16[128,2176]{1,0:T(8,128)(2,1)S(1)}, bf16[128,2176]{1,0:T(8,128)(2,1)S(1)}, u32[]{:S(2)}, u32[]{:S(2)}) collective-permute-start(bf16[128,2176]{1,0:T(8,128)(2,1)S(1)} %collective-permute-done.6), channel_id=1, source_target_pairs={{4,0},{5,1},{6,2},{7,3},{8,12},{9,13},{10,14},{11,15},{20,16},{21,... | collective-permute-start | bytes 1671176 | tf_op jit(solution)/shard_map/ppermute | solution.py:363
  42.5 11.6 %shard_map.103 = (bf16[128,1024]{1,0:T(8,128)(2,1)}, bf16[128,1024]{1,0:T(8,128)(2,1)}, bf16[128,1024]{1,0:T(8,128)(2,1)}, bf16[128,1024]{1,0:T(8,128)(2,1)}, bf...) custom-call(s32[2]{0:T(128)} %pad_add_fusion.scal, ...), custom_call_target="tpu_custom_call" | custom-call | flops 18119393280 | bytes 1048576 | tf_op jit(solution)/shard_map/pallas_call | solution.py:243
  54.0 1.1 collective-permute-done.9
  56.3 9.8 %shard_map.104 = (bf16[128,1024]{1,0:T(8,128)(2,1)}, bf16[128,1024]{1,0:T(8,128)(2,1)}, bf16[256,1152]{1,0:T(8,128)(2,1)}, bf16[256,1024]{1,0:T(8,128)(2,1)}, bf...) custom-call(s32[2]{0:T(128)} %pad_add_fusion.scal, ...), custom_call_target="tpu_custom_call" | custom-call | flops 7247757312 | bytes 1048576 | tf_op jit(solution)/shard_map/pallas_call | solution.py:243
  67.8 1.4 %collective-permute-start.17 = (bf16[128,1024]{1,0:T(8,128)(2,1)S(1)}, bf16[128,1024]{1,0:T(8,128)(2,1)S(1)}, u32[]{:S(2)}, u32[]{:S(2)}) collective-permute-start(bf16[128,1024]{1,0:T(8,128)(2,1)S(1)} %copy-done.15), channel_id=1, source_target_pairs={{0,2},{1,3},{2,0},{3,1},{4,6},{5,7},{6,4},{7,5},{8,10},{9,11},{10,... | collective-permute-start | bytes 786440 | tf_op jit(solution)/shard_map/ppermute | solution.py:363
  70.7 0.8 copy-done.13
  71.5 7.6 %shard_map.105 = (bf16[128,1024]{1,0:T(8,128)(2,1)}, bf16[128,1024]{1,0:T(8,128)(2,1)}, bf16[256,1152]{1,0:T(8,128)(2,1)}, bf16[256,1024]{1,0:T(8,128)(2,1)}, bf16[512,1152]{1,0:T(8,128)(2,1)}) custom-call(s32[2]{0:T(128)} %pad_add_fusion.scal, bf16[128,2176]{1,0:T(8,128)(2,1)} %copy-done.7, bf16[128,2176]{1,0:T(8,128)(2,1)} %copy-done.8, ...), custom_call_target="tpu_custom_call" | custom-call | flops 36238786560 | bytes 1048576 | tf_op jit(solution)/shard_map/pallas_call | solution.py:243
  79.2 2.0 %collective-permute-done.17 = bf16[128,1024]{1,0:T(8,128)(2,1)S(1)} collective-permute-done((bf16[128,1024]{1,0:T(8,128)(2,1)S(1)}, bf16[128,1024]{1,0:T(8,128)(2,1)S(1)}, u32[]{:S(2)}, u32[]{:S(2)}) %collective-permute-start.17) | collective-permute-done | bytes 262176 | tf_op jit(solution)/shard_map/ppermute | solution.py:363
  81.2 1.7 %collective-permute-done.18 = bf16[128,1024]{1,0:T(8,128)(2,1)S(1)} collective-permute-done((bf16[128,1024]{1,0:T(8,128)(2,1)}, bf16[128,1024]{1,0:T(8,128)(2,1)S(1)}, u32[]{:S(2)}, u32[]{:S(2)}) %collective-permute-start.18) | collective-permute-done | bytes 262176 | tf_op jit(solution)/shard_map/ppermute | solution.py:363
  82.9 1.1 add_convert_fusion.6
  84.0 0.8 collective-permute-start.19
  85.4 6.1 %collective-permute-start.23 = (bf16[128,1024]{1,0:T(8,128)(2,1)S(1)}, bf16[128,1024]{1,0:T(8,128)(2,1)S(1)}, u32[]{:S(2)}, u32[]{:S(2)}) collective-permute-start(bf16[128,1024]{1,0:T(8,128)(2,1)S(1)} %add_convert_fusion.2), channel_id=1, source_target_pairs={{0,4},{1,5},{2,6},{3,7},{12,8},{13,9},{14,10},{15,11},{16,20},{17,... | collective-permute-start | bytes 786440 | tf_op jit(solution)/shard_map/ppermute | solution.py:363
  91.4 1.0 collective-permute-done.19
  92.5 5.3 %collective-permute-start.20 = (bf16[128,1024]{1,0:T(8,128)(2,1)S(1)}, bf16[128,1024]{1,0:T(8,128)(2,1)S(1)}, u32[]{:S(2)}, u32[]{:S(2)}) collective-permute-start(bf16[128,1024]{1,0:T(8,128)(2,1)S(1)} %add_convert_fusion.5), channel_id=1, source_target_pairs={{0,4},{1,5},{2,6},{3,7},{12,8},{13,9},{14,10},{15,11},{16,20},{17,... | collective-permute-start | bytes 786440 | tf_op jit(solution)/shard_map/ppermute | solution.py:363
  98.8 5.8 %shard_map.106 = bf16[512,1152]{1,0:T(8,128)(2,1)} custom-call(s32[1]{0:T(128)} %bitcast.sides, bf16[128,2176]{1,0:T(8,128)(2,1)} %get-tuple-element.42.refs_0_.refs_6_.refs_4_, bf16[128,2176]{1,0:T(8,128)(2,1)} %copy-done.4, bf16[128,2176]{1,0:T(8,128)(2,1)} %copy-done, bf16[128,2176]{1,0:T(8,128)(2,1)} %copy-done.3, bf16[128,2176]{1,0:T(8,128)(2,1)} %copy-done.5, ...), custom_call_target="tpu_custom_call" | custom-call | flops 1024 | bytes 1024 | tf_op jit(solution)/shard_map/pallas_call | solution.py:304
  104.6 1.4 %collective-permute-start.21 = (bf16[128,1024]{1,0:T(8,128)(2,1)S(1)}, bf16[128,1024]{1,0:T(8,128)(2,1)S(1)}, u32[]{:S(2)}, u32[]{:S(2)}) collective-permute-start(bf16[128,1024]{1,0:T(8,128)(2,1)S(1)} %copy-done.14), channel_id=1, source_target_pairs={{0,2},{1,3},{2,0},{3,1},{4,6},{5,7},{6,4},{7,5},{8,10},{9,11},{10,... | collective-permute-start | bytes 786440 | tf_op jit(solution)/shard_map/ppermute | solution.py:363
  106.1 1.3 %collective-permute-start.25 = (bf16[128,1024]{1,0:T(8,128)(2,1)S(1)}, bf16[128,1024]{1,0:T(8,128)(2,1)S(1)}, u32[]{:S(2)}, u32[]{:S(2)}) collective-permute-start(bf16[128,1024]{1,0:T(8,128)(2,1)S(1)} %add_convert_fusion.4), channel_id=1, source_target_pairs={{4,12},{5,13},{6,14},{7,15},{8,0},{9,1},{10,2},{11,3},{20,28},{21,... | collective-permute-start | bytes 786440 | tf_op jit(solution)/shard_map/ppermute | solution.py:363
  107.4 5.3 %collective-permute-done.15 = bf16[512,1152]{1,0:T(8,128)(2,1)S(1)} collective-permute-done((bf16[512,1152]{1,0:T(8,128)(2,1)}, bf16[512,1152]{1,0:T(8,128)(2,1)S(1)}, u32[]{:S(2)}, u32[]{:S(2)}) %collective-permute-start.15) | collective-permute-done | bytes 1179680 | tf_op jit(solution)/shard_map/ppermute | solution.py:364
  112.7 1.5 %convert_add_fusion = f32[512,1152]{1,0:T(8,128)S(1)} fusion(bf16[512,1152]{1,0:T(8,128)(2,1)S(1)} %collective-permute-done.15, bf16[512,1152]{1,0:T(8,128)(2,1)} %shard_map.106), kind=kLoop, calls=%fused_computation | loop fusion | flops 1769472 | bytes 4718592 | tf_op jit(solution)/shard_map/add | solution.py:413
  114.2 1.3 %slice_bitcast_fusion = (f32[1,384,512]{1,2,0:T(8,128)S(1)}, f32[1,512,384]{2,1,0:T(8,128)}, f32[1,512,384]{2,1,0:T(8,128)}) fusion(f32[512,1152]{1,0:T(8,128)S(1)} %convert_add_fusion), kind=kLoop, calls=%fused_computation.1 | loop fusion | bytes 4718592 | tf_op jit(solution)/shard_map/broadcast_in_dim | solution.py:418
  115.5 1.1 copy.11
  116.8 0.9 add_convert_fusion
  (70 shorter events, 9.2 us)
Async XLA Ops:
  3.4 31.5 %collective-permute-start.5 = (bf16[512,1152]{1,0:T(8,128)(2,1)}, bf16[512,1152]{1,0:T(8,128)(2,1)}, u32[]{:S(2)}, u32[]{:S(2)}) collective-permute-start(bf16[512,1152]{1,0:T(8,128)(2,1)} %get-tuple-element.45.refs_5_.refs_2_), channel_id=1, source_target_pairs={{0,16},{16,0},{1,17},{17,1},{2,18},{18,2},{3,19},{19,3},{4,20},{20... | collective-permute-start | bytes 3538952 | tf_op jit(solution)/shard_map/ppermute | solution.py:364
  6.4 14.3 %collective-permute-start.3 = (bf16[128,2176]{1,0:T(8,128)(2,1)}, bf16[128,2176]{1,0:T(8,128)(2,1)S(1)}, u32[]{:S(2)}, u32[]{:S(2)}) collective-permute-start(bf16[128,2176]{1,0:T(8,128)(2,1)} %get-tuple-element.42.refs_0_.refs_6_.refs_4_), channel_id=1, source_target_pairs={{0,2},{1,3},{2,0},{3,1},{4,6},{5,7},{6,4},{7,5},{8,10},{9,11},{10,... | collective-permute-start | bytes 1671176 | tf_op jit(solution)/shard_map/ppermute | solution.py:363
  7.9 14.0 %collective-permute-start = (bf16[128,2176]{1,0:T(8,128)(2,1)}, bf16[128,2176]{1,0:T(8,128)(2,1)S(1)}, u32[]{:S(2)}, u32[]{:S(2)}) collective-permute-start(bf16[128,2176]{1,0:T(8,128)(2,1)} %get-tuple-element.42.refs_0_.refs_6_.refs_4_), channel_id=1, source_target_pairs={{0,4},{1,5},{2,6},{3,7},{4,0},{5,1},{6,2},{7,3},{8,12},{9,13},{10,... | collective-permute-start | bytes 1671176 | tf_op jit(solution)/shard_map/ppermute | solution.py:363
  9.5 13.6 %collective-permute-start.1 = (bf16[128,2176]{1,0:T(8,128)(2,1)}, bf16[128,2176]{1,0:T(8,128)(2,1)S(1)}, u32[]{:S(2)}, u32[]{:S(2)}) collective-permute-start(bf16[128,2176]{1,0:T(8,128)(2,1)} %get-tuple-element.42.refs_0_.refs_6_.refs_4_), channel_id=1, source_target_pairs={{4,8},{5,9},{6,10},{7,11},{8,4},{9,5},{10,6},{11,7},{20,24},{21,25... | collective-permute-start | bytes 1671176 | tf_op jit(solution)/shard_map/ppermute | solution.py:363
  20.7 21.7 %copy-start.3 = (bf16[128,2176]{1,0:T(8,128)(2,1)}, bf16[128,2176]{1,0:T(8,128)(2,1)S(1)}, u32[]{:S(2)}) copy-start(bf16[128,2176]{1,0:T(8,128)(2,1)S(1)} %collective-permute-done.3.refs_3_.refs_9_.refs_7_) | copy-start | bytes 1671172
  21.9 20.5 %copy-start.4 = (bf16[128,2176]{1,0:T(8,128)(2,1)}, bf16[128,2176]{1,0:T(8,128)(2,1)S(1)}, u32[]{:S(2)}) copy-start(bf16[128,2176]{1,0:T(8,128)(2,1)S(1)} %collective-permute-done.refs_1_.refs_7_.refs_5_) | copy-start | bytes 1671172
  21.9 13.0 %collective-permute-start.4 = (bf16[128,2176]{1,0:T(8,128)(2,1)S(1)}, bf16[128,2176]{1,0:T(8,128)(2,1)S(1)}, u32[]{:S(2)}, u32[]{:S(2)}) collective-permute-start(bf16[128,2176]{1,0:T(8,128)(2,1)S(1)} %collective-permute-done.refs_1_.refs_7_.refs_5_), channel_id=1, source_target_pairs={{0,2},{1,3},{2,0},{3,1},{4,6},{5,7},{6,4},{7,5},{8,10},{9,11},{10,... | collective-permute-start | bytes 1671176 | tf_op jit(solution)/shard_map/ppermute | solution.py:363
  22.4 12.5 %collective-permute-start.6 = (bf16[128,2176]{1,0:T(8,128)(2,1)S(1)}, bf16[128,2176]{1,0:T(8,128)(2,1)S(1)}, u32[]{:S(2)}, u32[]{:S(2)}) collective-permute-start(bf16[128,2176]{1,0:T(8,128)(2,1)S(1)} %collective-permute-done.refs_1_.refs_7_.refs_5_), channel_id=1, source_target_pairs={{4,8},{5,9},{6,10},{7,11},{8,4},{9,5},{10,6},{11,7},{20,24},{21,25... | collective-permute-start | bytes 1671176 | tf_op jit(solution)/shard_map/ppermute | solution.py:363
  23.1 16.5 %collective-permute-start.2 = (bf16[128,2176]{1,0:T(8,128)(2,1)S(1)}, bf16[128,2176]{1,0:T(8,128)(2,1)S(1)}, u32[]{:S(2)}, u32[]{:S(2)}) collective-permute-start(bf16[128,2176]{1,0:T(8,128)(2,1)S(1)} %collective-permute-done.1), channel_id=1, source_target_pairs={{4,0},{5,1},{6,2},{7,3},{8,12},{9,13},{10,14},{11,15},{20,16},{21,... | collective-permute-start | bytes 1671176 | tf_op jit(solution)/shard_map/ppermute | solution.py:363
  34.9 7.5 %collective-permute-start.7 = (bf16[512,1152]{1,0:T(8,128)(2,1)}, bf16[512,1152]{1,0:T(8,128)(2,1)}, u32[]{:S(2)}, u32[]{:S(2)}) collective-permute-start(bf16[512,1152]{1,0:T(8,128)(2,1)} %get-tuple-element.45.refs_5_.refs_2_), channel_id=1, source_target_pairs={{0,1},{1,0},{2,3},{3,2},{4,5},{5,4},{6,7},{7,6},{8,9},{9,8},{10,11... | collective-permute-start | bytes 3538952 | tf_op jit(solution)/shard_map/ppermute | solution.py:363
  34.9 7.5 %collective-permute-start.8 = (bf16[512,1152]{1,0:T(8,128)(2,1)}, bf16[512,1152]{1,0:T(8,128)(2,1)}, u32[]{:S(2)}, u32[]{:S(2)}) collective-permute-start(bf16[512,1152]{1,0:T(8,128)(2,1)} %collective-permute-done.5.refs_6_.refs_3_), channel_id=1, source_target_pairs={{0,1},{1,0},{2,3},{3,2},{4,5},{5,4},{6,7},{7,6},{8,9},{9,8},{10,11... | collective-permute-start | bytes 3538952 | tf_op jit(solution)/shard_map/ppermute | solution.py:363
  39.7 15.6 %collective-permute-start.10 = (bf16[128,2176]{1,0:T(8,128)(2,1)S(1)}, bf16[128,2176]{1,0:T(8,128)(2,1)S(1)}, u32[]{:S(2)}, u32[]{:S(2)}) collective-permute-start(bf16[128,2176]{1,0:T(8,128)(2,1)S(1)} %broadcast_select_fusion.1.refs_2_.refs_8_.refs_6_), channel_id=1, source_target_pairs={{0,2},{1,3},{2,0},{3,1},{4,6},{5,7},{6,4},{7,5},{8,10},{9,11},{10,... | collective-permute-start | bytes 1671176 | tf_op jit(solution)/shard_map/ppermute | solution.py:363
  41.1 14.1 %collective-permute-start.9 = (bf16[128,2176]{1,0:T(8,128)(2,1)S(1)}, bf16[128,2176]{1,0:T(8,128)(2,1)S(1)}, u32[]{:S(2)}, u32[]{:S(2)}) collective-permute-start(bf16[128,2176]{1,0:T(8,128)(2,1)S(1)} %collective-permute-done.6), channel_id=1, source_target_pairs={{4,0},{5,1},{6,2},{7,3},{8,12},{9,13},{10,14},{11,15},{20,16},{21,... | collective-permute-start | bytes 1671176 | tf_op jit(solution)/shard_map/ppermute | solution.py:363
  55.3 11.3 %collective-permute-start.11 = (bf16[128,2176]{1,0:T(8,128)(2,1)S(1)}, bf16[128,2176]{1,0:T(8,128)(2,1)S(1)}, u32[]{:S(2)}, u32[]{:S(2)}) collective-permute-start(bf16[128,2176]{1,0:T(8,128)(2,1)S(1)} %broadcast_select_fusion.refs_0_.refs_9_.refs_5_), channel_id=1, source_target_pairs={{0,2},{1,3},{2,0},{3,1},{4,6},{5,7},{6,4},{7,5},{8,10},{9,11},{10,... | collective-permute-start | bytes 1671176 | tf_op jit(solution)/shard_map/ppermute | solution.py:363
  56.3 11.5 %copy-start.15 = (bf16[128,1024]{1,0:T(8,128)(2,1)S(1)}, bf16[128,1024]{1,0:T(8,128)(2,1)}, u32[]{:S(2)}) copy-start(bf16[128,1024]{1,0:T(8,128)(2,1)} %get-tuple-element.72) | copy-start | bytes 786436
  66.6 3.9 %collective-permute-start.13 = (bf16[512,1152]{1,0:T(8,128)(2,1)}, bf16[512,1152]{1,0:T(8,128)(2,1)S(1)}, u32[]{:S(2)}, u32[]{:S(2)}) collective-permute-start(bf16[512,1152]{1,0:T(8,128)(2,1)} %get-tuple-element.60), channel_id=1, source_target_pairs={{0,1},{1,0},{2,3},{3,2},{4,5},{5,4},{6,7},{7,6},{8,9},{9,8},{10,11... | collective-permute-start | bytes 3538952 | tf_op jit(solution)/shard_map/ppermute | solution.py:363
  66.6 3.3 %collective-permute-start.12 = (bf16[128,2176]{1,0:T(8,128)(2,1)S(1)}, bf16[128,2176]{1,0:T(8,128)(2,1)S(1)}, u32[]{:S(2)}, u32[]{:S(2)}) collective-permute-start(bf16[128,2176]{1,0:T(8,128)(2,1)S(1)} %collective-permute-done.11.refs_0_.refs_7_), channel_id=1, source_target_pairs={{0,1},{1,0},{2,3},{3,2},{4,5},{5,4},{6,7},{7,6},{8,9},{9,8},{10,11... | collective-permute-start | bytes 1671176 | tf_op jit(solution)/shard_map/ppermute | solution.py:363
  67.1 12.0 %collective-permute-start.16 = (bf16[128,1024]{1,0:T(8,128)(2,1)}, bf16[128,1024]{1,0:T(8,128)(2,1)S(1)}, u32[]{:S(2)}, u32[]{:S(2)}) collective-permute-start(bf16[128,1024]{1,0:T(8,128)(2,1)} %get-tuple-element.70), channel_id=1, source_target_pairs={{0,2},{1,3},{2,0},{3,1},{4,6},{5,7},{6,4},{7,5},{8,10},{9,11},{10,... | collective-permute-start | bytes 786440 | tf_op jit(solution)/shard_map/ppermute | solution.py:363
  67.8 13.4 %collective-permute-start.17 = (bf16[128,1024]{1,0:T(8,128)(2,1)S(1)}, bf16[128,1024]{1,0:T(8,128)(2,1)S(1)}, u32[]{:S(2)}, u32[]{:S(2)}) collective-permute-start(bf16[128,1024]{1,0:T(8,128)(2,1)S(1)} %copy-done.15), channel_id=1, source_target_pairs={{0,2},{1,3},{2,0},{3,1},{4,6},{5,7},{6,4},{7,5},{8,10},{9,11},{10,... | collective-permute-start | bytes 786440 | tf_op jit(solution)/shard_map/ppermute | solution.py:363
  69.9 11.3 %collective-permute-start.14 = (bf16[512,1152]{1,0:T(8,128)(2,1)}, bf16[512,1152]{1,0:T(8,128)(2,1)S(1)}, u32[]{:S(2)}, u32[]{:S(2)}) collective-permute-start(bf16[512,1152]{1,0:T(8,128)(2,1)} %get-tuple-element.66), channel_id=1, source_target_pairs={{0,1},{1,0},{2,3},{3,2},{4,5},{5,4},{6,7},{7,6},{8,9},{9,8},{10,11... | collective-permute-start | bytes 3538952 | tf_op jit(solution)/shard_map/ppermute | solution.py:363
  71.5 13.8 %copy-start.10 = (bf16[128,1024]{1,0:T(8,128)(2,1)S(1)}, bf16[128,1024]{1,0:T(8,128)(2,1)}, u32[]{:S(2)}) copy-start(bf16[128,1024]{1,0:T(8,128)(2,1)} %get-tuple-element.79) | copy-start | bytes 786436
  79.2 13.3 %copy-start.11 = (bf16[128,1024]{1,0:T(8,128)(2,1)S(1)}, bf16[128,1024]{1,0:T(8,128)(2,1)}, u32[]{:S(2)}) copy-start(bf16[128,1024]{1,0:T(8,128)(2,1)} %get-tuple-element.67) | copy-start | bytes 786436
  81.2 1.7 %collective-permute-start.18 = (bf16[128,1024]{1,0:T(8,128)(2,1)}, bf16[128,1024]{1,0:T(8,128)(2,1)S(1)}, u32[]{:S(2)}, u32[]{:S(2)}) collective-permute-start(bf16[128,1024]{1,0:T(8,128)(2,1)} %get-tuple-element.73), channel_id=1, source_target_pairs={{0,1},{1,0},{2,3},{3,2},{4,5},{5,4},{6,7},{7,6},{8,9},{9,8},{10,11... | collective-permute-start | bytes 786440 | tf_op jit(solution)/shard_map/ppermute | solution.py:363
  82.9 14.9 %copy-start.9 = (bf16[128,1024]{1,0:T(8,128)(2,1)S(1)}, bf16[128,1024]{1,0:T(8,128)(2,1)}, u32[]{:S(2)}) copy-start(bf16[128,1024]{1,0:T(8,128)(2,1)} %get-tuple-element.78) | copy-start | bytes 786436
  84.0 8.4 %collective-permute-start.19 = (bf16[128,1024]{1,0:T(8,128)(2,1)S(1)}, bf16[128,1024]{1,0:T(8,128)(2,1)S(1)}, u32[]{:S(2)}, u32[]{:S(2)}) collective-permute-start(bf16[128,1024]{1,0:T(8,128)(2,1)S(1)} %add_convert_fusion.6), channel_id=1, source_target_pairs={{0,2},{1,3},{2,0},{3,1},{4,6},{5,7},{6,4},{7,5},{8,10},{9,11},{10,... | collective-permute-start | bytes 786440 | tf_op jit(solution)/shard_map/ppermute | solution.py:363
  84.8 27.9 %collective-permute-start.15 = (bf16[512,1152]{1,0:T(8,128)(2,1)}, bf16[512,1152]{1,0:T(8,128)(2,1)S(1)}, u32[]{:S(2)}, u32[]{:S(2)}) collective-permute-start(bf16[512,1152]{1,0:T(8,128)(2,1)} %get-tuple-element.61), channel_id=1, source_target_pairs={{0,16},{16,0},{1,17},{17,1},{2,18},{18,2},{3,19},{19,3},{4,20},{20... | collective-permute-start | bytes 3538952 | tf_op jit(solution)/shard_map/ppermute | solution.py:364
  85.4 12.7 %collective-permute-start.23 = (bf16[128,1024]{1,0:T(8,128)(2,1)S(1)}, bf16[128,1024]{1,0:T(8,128)(2,1)S(1)}, u32[]{:S(2)}, u32[]{:S(2)}) collective-permute-start(bf16[128,1024]{1,0:T(8,128)(2,1)S(1)} %add_convert_fusion.2), channel_id=1, source_target_pairs={{0,4},{1,5},{2,6},{3,7},{12,8},{13,9},{14,10},{15,11},{16,20},{17,... | collective-permute-start | bytes 786440 | tf_op jit(solution)/shard_map/ppermute | solution.py:363
  92.5 13.6 %collective-permute-start.20 = (bf16[128,1024]{1,0:T(8,128)(2,1)S(1)}, bf16[128,1024]{1,0:T(8,128)(2,1)S(1)}, u32[]{:S(2)}, u32[]{:S(2)}) collective-permute-start(bf16[128,1024]{1,0:T(8,128)(2,1)S(1)} %add_convert_fusion.5), channel_id=1, source_target_pairs={{0,4},{1,5},{2,6},{3,7},{12,8},{13,9},{14,10},{15,11},{16,20},{17,... | collective-permute-start | bytes 786440 | tf_op jit(solution)/shard_map/ppermute | solution.py:363
  97.9 18.7 %collective-permute-start.22 = (bf16[128,1024]{1,0:T(8,128)(2,1)S(1)}, bf16[128,1024]{1,0:T(8,128)(2,1)S(1)}, u32[]{:S(2)}, u32[]{:S(2)}) collective-permute-start(bf16[128,1024]{1,0:T(8,128)(2,1)S(1)} %add_convert_fusion.3), channel_id=1, source_target_pairs={{0,4},{1,5},{2,6},{3,7},{4,0},{5,1},{6,2},{7,3},{8,12},{9,13},{10,... | collective-permute-start | bytes 786440 | tf_op jit(solution)/shard_map/ppermute | solution.py:363
  98.1 18.6 %collective-permute-start.24 = (bf16[128,1024]{1,0:T(8,128)(2,1)S(1)}, bf16[128,1024]{1,0:T(8,128)(2,1)S(1)}, u32[]{:S(2)}, u32[]{:S(2)}) collective-permute-start(bf16[128,1024]{1,0:T(8,128)(2,1)S(1)} %add_convert_fusion.1), channel_id=1, source_target_pairs={{4,8},{5,9},{6,10},{7,11},{8,4},{9,5},{10,6},{11,7},{20,24},{21,25... | collective-permute-start | bytes 786440 | tf_op jit(solution)/shard_map/ppermute | solution.py:363
  104.6 12.0 %collective-permute-start.21 = (bf16[128,1024]{1,0:T(8,128)(2,1)S(1)}, bf16[128,1024]{1,0:T(8,128)(2,1)S(1)}, u32[]{:S(2)}, u32[]{:S(2)}) collective-permute-start(bf16[128,1024]{1,0:T(8,128)(2,1)S(1)} %copy-done.14), channel_id=1, source_target_pairs={{0,2},{1,3},{2,0},{3,1},{4,6},{5,7},{6,4},{7,5},{8,10},{9,11},{10,... | collective-permute-start | bytes 786440 | tf_op jit(solution)/shard_map/ppermute | solution.py:363
  106.1 10.6 %collective-permute-start.25 = (bf16[128,1024]{1,0:T(8,128)(2,1)S(1)}, bf16[128,1024]{1,0:T(8,128)(2,1)S(1)}, u32[]{:S(2)}, u32[]{:S(2)}) collective-permute-start(bf16[128,1024]{1,0:T(8,128)(2,1)S(1)} %add_convert_fusion.4), channel_id=1, source_target_pairs={{4,12},{5,13},{6,14},{7,15},{8,0},{9,1},{10,2},{11,3},{20,28},{21,... | collective-permute-start | bytes 786440 | tf_op jit(solution)/shard_map/ppermute | solution.py:363
  (10 other events, 36.3 us)

commit v14 on v13

--- a/solution.py
+++ b/solution.py
@@ -402,19 +402,19 @@
     from_part = across(send)
     add = lambda *terms: sum(t.astype(F32) for t in terms).astype(BF16)
     r3 = move(add(last, swap(after(pair, r2, r1, got_mine))), SWAP_Y)
-    r0 = move(after(q0, r3), SWAP_Y)
-    keep = half_call(after(mine, send), blocks + [y3, cy3], kept + [kept_c], more=got_mine)
-
     s1 = add(p1, r1)
     s2 = add(p2, r2)
     s2 = add(s2, move(s2, INWARD))
     s3 = add(p3, r3)
     s3 = add(s3, move(s3, INWARD))
-    d_weights = keep.astype(F32) + after(from_part, s3).astype(F32)
+    keep = half_call(after(mine, send, s3), blocks + [y3, cy3], kept + [kept_c], more=got_mine)
+
+    r0 = move(after(q0, r3, keep), SWAP_Y)
+    from_part = after(from_part, s3)
     hidden_units = gate_weight.shape[2]
-    d_gate, d_up = d_weights[:, :hidden_units], d_weights[:, hidden_units : 2 * hidden_units]
-    d_down = d_weights[:, 2 * hidden_units :].T
-    d_tokens = add(after(p0, d_weights), r0, move(s1, OUTER), move(s2, INNER), move(s3, SKIP_TO_OUTER))
+    whole = lambda a: keep[:, a : a + hidden_units].astype(F32) + from_part[:, a : a + hidden_units].astype(F32)
+    d_gate, d_up, d_down = whole(0), whole(hidden_units), whole(2 * hidden_units).T
+    d_tokens = add(after(p0, from_part), r0, move(s1, OUTER), move(s2, INNER), move(s3, SKIP_TO_OUTER))
     return (d_tokens, d_gate[None], d_up[None], d_down[None])
 
 

time: 119 us -> 120 us (level)
  waiting for transfers between devices: 38.5 us -> 40.1 us
  local copies, waits for them, and re-layouts: 3.81 us -> 2.52 us
    ppermute x24, waiting for transfers between devices: 33.2 us -> 40.1 us  [dense_body(): move = lambda a, pairs: lax.ppermute(a, 'expert', pairs)]
    ppermute x2, waiting for transfers between devices: 5.26 us -> 0.01 us  [dense_body(): across = lambda a: lax.ppermute(a, 'dp', [(0, 1), (1, 0)])]
    broadcast_in_dim x0 -> x1, other arithmetic: none -> 2.61 us  [dense_body(): return (d_tokens, d_gate[None], d_up[None], d_down[None])]
    add x1 -> x0, other arithmetic: 1.5 us -> none  [dense_body(): d_weights = keep.astype(F32) + after(from_part, s3).astype(F32)]
    broadcast_in_dim x1 -> x0, local copies, waits for them, and re-layouts: 1.29 us -> none  [dense_body(): return (d_tokens, d_gate[None], d_up[None], d_down[None])]
  transfers between devices with their start and end apart: 26 -> 26, of which waited for: 13 -> 13; matrix products, arithmetic and copies ran while one was open for 4% -> 4% of each run, Pallas kernels for 30% -> 29%
where the time goes in v14:
time: 120 us; the launch traced here: 119 us
  waiting for transfers between devices  40.1 us (33%)
  Pallas kernels  37.5 us (31%)
  starting transfers between devices  32.3 us (27%)
  other arithmetic  5.7 us (5%)
  local copies, waits for them, and re-layouts  2.52 us (2%)
    ppermute x24, waiting for transfers between devices, dense_body(): move = lambda a, pairs: lax.ppermute(a, 'expert', pairs)  40.1 us
    pallas_call x3, Pallas kernels, rows_call(): pl.pallas_call(functools.partial(rows_kernel, experts, count, sizes, whic...  29 us
    ppermute x24, starting transfers between devices, dense_body(): move = lambda a, pairs: lax.ppermute(a, 'expert', pairs)  28.8 us
    pallas_call x1, Pallas kernels, half_call(): pl.pallas_call(functools.partial(half_kernel, len(blocks), len(kept)), ou...  5.81 us
    ppermute x2, starting transfers between devices, dense_body(): across = lambda a: lax.ppermute(a, 'dp', [(0, 1), (1, 0)])  3.52 us
    pallas_call x1, Pallas kernels, pack(): pl.pallas_call(functools.partial(pack_kernel, experts), out_shape=[jax.Sh...  2.73 us
    broadcast_in_dim x1, other arithmetic, dense_body(): return (d_tokens, d_gate[None], d_up[None], d_down[None])  2.61 us
    unnamed x33, local copies, waits for them, and re-layouts  2.52 us
  transfers between devices with their start and end apart: 26, of which 13 were waited for; matrix products, arithmetic and copies ran while one was open for 4% of the time, Pallas kernels for 29%

profile of v14, /device:TPU:0, one launch (start us, length us, event | category | flops | bytes accessed | tf_op | source)
XLA Modules:
  0.0 119.2 jit_solution(11629361855341175523)
XLA Ops:
  0.6 2.7 %shard_map.102 = (bf16[128,2176]{1,0:T(8,128)(2,1)}, bf16[512,1152]{1,0:T(8,128)(2,1)}) custom-call(bf16[128,1024]{1,0:T(8,128)(2,1)} %tokens.1, bf16[128,1024]{1,0:T(8,128)(2,1)} %d_output.1, f32[8,128]{1,0:T(8,128)} %bitcast.18, s32[8,128]{1,0:T(8,128)} %bitcast.19, bf16[512,384]{1,0:T(8,128)(2,1)} %bitcast.15, bf16[512,384]{1,0:T(8,128)(2,1)} %bitcast.16, ...), custom_call_target="tpu_custom_call" | custom-call | bytes 1048576 | tf_op jit(solution)/shard_map/pallas_call | solution.py:79
  3.4 3.0 %collective-permute-start.5 = (bf16[512,1152]{1,0:T(8,128)(2,1)}, bf16[512,1152]{1,0:T(8,128)(2,1)}, u32[]{:S(2)}, u32[]{:S(2)}) collective-permute-start(bf16[512,1152]{1,0:T(8,128)(2,1)} %get-tuple-element.45.refs_5_.refs_2_), channel_id=1, source_target_pairs={{0,16},{16,0},{1,17},{17,1},{2,18},{18,2},{3,19},{19,3},{4,20},{20... | collective-permute-start | bytes 3538952 | tf_op jit(solution)/shard_map/ppermute | solution.py:364
  6.4 1.5 %collective-permute-start.3 = (bf16[128,2176]{1,0:T(8,128)(2,1)}, bf16[128,2176]{1,0:T(8,128)(2,1)S(1)}, u32[]{:S(2)}, u32[]{:S(2)}) collective-permute-start(bf16[128,2176]{1,0:T(8,128)(2,1)} %get-tuple-element.42.refs_0_.refs_6_.refs_4_), channel_id=1, source_target_pairs={{0,2},{1,3},{2,0},{3,1},{4,6},{5,7},{6,4},{7,5},{8,10},{9,11},{10,... | collective-permute-start | bytes 1671176 | tf_op jit(solution)/shard_map/ppermute | solution.py:363
  7.9 1.6 %collective-permute-start = (bf16[128,2176]{1,0:T(8,128)(2,1)}, bf16[128,2176]{1,0:T(8,128)(2,1)S(1)}, u32[]{:S(2)}, u32[]{:S(2)}) collective-permute-start(bf16[128,2176]{1,0:T(8,128)(2,1)} %get-tuple-element.42.refs_0_.refs_6_.refs_4_), channel_id=1, source_target_pairs={{0,4},{1,5},{2,6},{3,7},{4,0},{5,1},{6,2},{7,3},{8,12},{9,13},{10,... | collective-permute-start | bytes 1671176 | tf_op jit(solution)/shard_map/ppermute | solution.py:363
  10.2 10.5 %collective-permute-done.3.refs_3_.refs_9_.refs_7_ = bf16[128,2176]{1,0:T(8,128)(2,1)S(1)} collective-permute-done((bf16[128,2176]{1,0:T(8,128)(2,1)}, bf16[128,2176]{1,0:T(8,128)(2,1)S(1)}, u32[]{:S(2)}, u32[]{:S(2)}) %collective-permute-start.3) | collective-permute-done | bytes 557088 | tf_op jit(solution)/shard_map/ppermute | solution.py:363
  20.7 1.2 %collective-permute-done.refs_1_.refs_7_.refs_5_ = bf16[128,2176]{1,0:T(8,128)(2,1)S(1)} collective-permute-done((bf16[128,2176]{1,0:T(8,128)(2,1)}, bf16[128,2176]{1,0:T(8,128)(2,1)S(1)}, u32[]{:S(2)}, u32[]{:S(2)}) %collective-permute-start) | collective-permute-done | bytes 557088 | tf_op jit(solution)/shard_map/ppermute | solution.py:363
  23.1 1.3 %collective-permute-start.2 = (bf16[128,2176]{1,0:T(8,128)(2,1)S(1)}, bf16[128,2176]{1,0:T(8,128)(2,1)S(1)}, u32[]{:S(2)}, u32[]{:S(2)}) collective-permute-start(bf16[128,2176]{1,0:T(8,128)(2,1)S(1)} %collective-permute-done.1), channel_id=1, source_target_pairs={{4,0},{5,1},{6,2},{7,3},{8,12},{9,13},{10,14},{11,15},{20,16},{21,... | collective-permute-start | bytes 1671176 | tf_op jit(solution)/shard_map/ppermute | solution.py:363
  24.4 10.5 %collective-permute-done.4.refs_4_.refs_10_.refs_8_ = bf16[128,2176]{1,0:T(8,128)(2,1)S(1)} collective-permute-done((bf16[128,2176]{1,0:T(8,128)(2,1)S(1)}, bf16[128,2176]{1,0:T(8,128)(2,1)S(1)}, u32[]{:S(2)}, u32[]{:S(2)}) %collective-permute-start.4) | collective-permute-done | bytes 557088 | tf_op jit(solution)/shard_map/ppermute | solution.py:363
  36.1 3.5 %collective-permute-done.2 = bf16[128,2176]{1,0:T(8,128)(2,1)S(1)} collective-permute-done((bf16[128,2176]{1,0:T(8,128)(2,1)S(1)}, bf16[128,2176]{1,0:T(8,128)(2,1)S(1)}, u32[]{:S(2)}, u32[]{:S(2)}) %collective-permute-start.2) | collective-permute-done | bytes 557088 | tf_op jit(solution)/shard_map/ppermute | solution.py:363
  39.7 1.4 %collective-permute-start.10 = (bf16[128,2176]{1,0:T(8,128)(2,1)S(1)}, bf16[128,2176]{1,0:T(8,128)(2,1)S(1)}, u32[]{:S(2)}, u32[]{:S(2)}) collective-permute-start(bf16[128,2176]{1,0:T(8,128)(2,1)S(1)} %broadcast_select_fusion.1.refs_2_.refs_8_.refs_6_), channel_id=1, source_target_pairs={{0,2},{1,3},{2,0},{3,1},{4,6},{5,7},{6,4},{7,5},{8,10},{9,11},{10,... | collective-permute-start | bytes 1671176 | tf_op jit(solution)/shard_map/ppermute | solution.py:363
  41.1 1.3 %collective-permute-start.9 = (bf16[128,2176]{1,0:T(8,128)(2,1)S(1)}, bf16[128,2176]{1,0:T(8,128)(2,1)S(1)}, u32[]{:S(2)}, u32[]{:S(2)}) collective-permute-start(bf16[128,2176]{1,0:T(8,128)(2,1)S(1)} %collective-permute-done.6), channel_id=1, source_target_pairs={{4,0},{5,1},{6,2},{7,3},{8,12},{9,13},{10,14},{11,15},{20,16},{21,... | collective-permute-start | bytes 1671176 | tf_op jit(solution)/shard_map/ppermute | solution.py:363
  42.5 11.6 %shard_map.103 = (bf16[128,1024]{1,0:T(8,128)(2,1)}, bf16[128,1024]{1,0:T(8,128)(2,1)}, bf16[128,1024]{1,0:T(8,128)(2,1)}, bf16[128,1024]{1,0:T(8,128)(2,1)}, bf...) custom-call(s32[2]{0:T(128)} %pad_add_fusion.scal, ...), custom_call_target="tpu_custom_call" | custom-call | flops 18119393280 | bytes 1048576 | tf_op jit(solution)/shard_map/pallas_call | solution.py:243
  54.0 1.1 collective-permute-done.9
  56.3 9.8 %shard_map.104 = (bf16[128,1024]{1,0:T(8,128)(2,1)}, bf16[128,1024]{1,0:T(8,128)(2,1)}, bf16[256,1152]{1,0:T(8,128)(2,1)}, bf16[256,1024]{1,0:T(8,128)(2,1)}, bf...) custom-call(s32[2]{0:T(128)} %pad_add_fusion.scal, ...), custom_call_target="tpu_custom_call" | custom-call | flops 7247757312 | bytes 1048576 | tf_op jit(solution)/shard_map/pallas_call | solution.py:243
  67.8 1.4 %collective-permute-start.16 = (bf16[128,1024]{1,0:T(8,128)(2,1)S(1)}, bf16[128,1024]{1,0:T(8,128)(2,1)S(1)}, u32[]{:S(2)}, u32[]{:S(2)}) collective-permute-start(bf16[128,1024]{1,0:T(8,128)(2,1)S(1)} %copy-done.15), channel_id=1, source_target_pairs={{0,2},{1,3},{2,0},{3,1},{4,6},{5,7},{6,4},{7,5},{8,10},{9,11},{10,... | collective-permute-start | bytes 786440 | tf_op jit(solution)/shard_map/ppermute | solution.py:363
  70.7 0.8 copy-done.13
  71.5 7.6 %shard_map.105 = (bf16[128,1024]{1,0:T(8,128)(2,1)}, bf16[128,1024]{1,0:T(8,128)(2,1)}, bf16[256,1152]{1,0:T(8,128)(2,1)}, bf16[256,1024]{1,0:T(8,128)(2,1)}, bf16[512,1152]{1,0:T(8,128)(2,1)}) custom-call(s32[2]{0:T(128)} %pad_add_fusion.scal, bf16[128,2176]{1,0:T(8,128)(2,1)} %copy-done.7, bf16[128,2176]{1,0:T(8,128)(2,1)} %copy-done.8, ...), custom_call_target="tpu_custom_call" | custom-call | flops 36238786560 | bytes 1048576 | tf_op jit(solution)/shard_map/pallas_call | solution.py:243
  79.2 2.0 %collective-permute-done.16 = bf16[128,1024]{1,0:T(8,128)(2,1)S(1)} collective-permute-done((bf16[128,1024]{1,0:T(8,128)(2,1)S(1)}, bf16[128,1024]{1,0:T(8,128)(2,1)S(1)}, u32[]{:S(2)}, u32[]{:S(2)}) %collective-permute-start.16) | collective-permute-done | bytes 262176 | tf_op jit(solution)/shard_map/ppermute | solution.py:363
  81.2 1.7 %collective-permute-done.18 = bf16[128,1024]{1,0:T(8,128)(2,1)S(1)} collective-permute-done((bf16[128,1024]{1,0:T(8,128)(2,1)}, bf16[128,1024]{1,0:T(8,128)(2,1)S(1)}, u32[]{:S(2)}, u32[]{:S(2)}) %collective-permute-start.18) | collective-permute-done | bytes 262176 | tf_op jit(solution)/shard_map/ppermute | solution.py:363
  82.9 1.1 add_convert_fusion.6
  84.0 0.8 collective-permute-start.19
  85.4 6.1 %collective-permute-start.23 = (bf16[128,1024]{1,0:T(8,128)(2,1)S(1)}, bf16[128,1024]{1,0:T(8,128)(2,1)S(1)}, u32[]{:S(2)}, u32[]{:S(2)}) collective-permute-start(bf16[128,1024]{1,0:T(8,128)(2,1)S(1)} %add_convert_fusion.2), channel_id=1, source_target_pairs={{0,4},{1,5},{2,6},{3,7},{12,8},{13,9},{14,10},{15,11},{16,20},{17,... | collective-permute-start | bytes 786440 | tf_op jit(solution)/shard_map/ppermute | solution.py:363
  91.4 1.0 collective-permute-done.19
  92.5 5.3 %collective-permute-start.20 = (bf16[128,1024]{1,0:T(8,128)(2,1)S(1)}, bf16[128,1024]{1,0:T(8,128)(2,1)S(1)}, u32[]{:S(2)}, u32[]{:S(2)}) collective-permute-start(bf16[128,1024]{1,0:T(8,128)(2,1)S(1)} %add_convert_fusion.5), channel_id=1, source_target_pairs={{0,4},{1,5},{2,6},{3,7},{12,8},{13,9},{14,10},{15,11},{16,20},{17,... | collective-permute-start | bytes 786440 | tf_op jit(solution)/shard_map/ppermute | solution.py:363
  98.8 5.8 %collective-permute-done.20 = bf16[128,1024]{1,0:T(8,128)(2,1)S(1)} collective-permute-done((bf16[128,1024]{1,0:T(8,128)(2,1)S(1)}, bf16[128,1024]{1,0:T(8,128)(2,1)S(1)}, u32[]{:S(2)}, u32[]{:S(2)}) %collective-permute-start.20) | collective-permute-done | bytes 262176 | tf_op jit(solution)/shard_map/ppermute | solution.py:363
  104.7 1.3 %collective-permute-start.25 = (bf16[128,1024]{1,0:T(8,128)(2,1)S(1)}, bf16[128,1024]{1,0:T(8,128)(2,1)S(1)}, u32[]{:S(2)}, u32[]{:S(2)}) collective-permute-start(bf16[128,1024]{1,0:T(8,128)(2,1)S(1)} %add_convert_fusion.4), channel_id=1, source_target_pairs={{4,12},{5,13},{6,14},{7,15},{8,0},{9,1},{10,2},{11,3},{20,28},{21,... | collective-permute-start | bytes 786440 | tf_op jit(solution)/shard_map/ppermute | solution.py:363
  106.0 5.8 %shard_map.106 = bf16[512,1152]{1,0:T(8,128)(2,1)} custom-call(s32[1]{0:T(128)} %bitcast.sides, bf16[128,2176]{1,0:T(8,128)(2,1)} %get-tuple-element.42.refs_0_.refs_6_.refs_4_, bf16[128,2176]{1,0:T(8,128)(2,1)} %copy-done.4, bf16[128,2176]{1,0:T(8,128)(2,1)} %copy-done, bf16[128,2176]{1,0:T(8,128)(2,1)} %copy-done.3, bf16[128,2176]{1,0:T(8,128)(2,1)} %copy-done.5, ...), custom_call_target="tpu_custom_call" | custom-call | flops 1024 | bytes 1024 | tf_op jit(solution)/shard_map/pallas_call | solution.py:304
  111.8 1.4 %collective-permute-start.21 = (bf16[128,1024]{1,0:T(8,128)(2,1)S(1)}, bf16[128,1024]{1,0:T(8,128)(2,1)S(1)}, u32[]{:S(2)}, u32[]{:S(2)}) collective-permute-start(bf16[128,1024]{1,0:T(8,128)(2,1)S(1)} %copy-done.14), channel_id=1, source_target_pairs={{0,2},{1,3},{2,0},{3,1},{4,6},{5,7},{6,4},{7,5},{8,10},{9,11},{10,... | collective-permute-start | bytes 786440 | tf_op jit(solution)/shard_map/ppermute | solution.py:363
  113.2 2.6 %add_bitcast_fusion = (f32[1,384,512]{1,2,0:T(8,128)S(1)}, f32[1,512,384]{2,1,0:T(8,128)}, f32[1,512,384]{2,1,0:T(8,128)}) fusion(bf16[512,1152]{1,0:T(8,128)(2,1)} %shard_map.106, bf16[512,1152]{1,0:T(8,128)(2,1)S(1)} %collective-permute-done.14), kind=kLoop, calls=%fused_computation | loop fusion | flops 1769472 | bytes 4718592 | tf_op jit(solution)/shard_map/broadcast_in_dim | solution.py:418
  115.9 1.1 copy.11
  117.0 1.2 %collective-permute-done.21 = bf16[128,1024]{1,0:T(8,128)(2,1)S(1)} collective-permute-done((bf16[128,1024]{1,0:T(8,128)(2,1)S(1)}, bf16[128,1024]{1,0:T(8,128)(2,1)S(1)}, u32[]{:S(2)}, u32[]{:S(2)}) %collective-permute-start.21) | collective-permute-done | bytes 262176 | tf_op jit(solution)/shard_map/ppermute | solution.py:363
  118.2 0.9 add_convert_fusion
  (69 shorter events, 9.1 us)
Async XLA Ops:
  3.4 31.5 %collective-permute-start.5 = (bf16[512,1152]{1,0:T(8,128)(2,1)}, bf16[512,1152]{1,0:T(8,128)(2,1)}, u32[]{:S(2)}, u32[]{:S(2)}) collective-permute-start(bf16[512,1152]{1,0:T(8,128)(2,1)} %get-tuple-element.45.refs_5_.refs_2_), channel_id=1, source_target_pairs={{0,16},{16,0},{1,17},{17,1},{2,18},{18,2},{3,19},{19,3},{4,20},{20... | collective-permute-start | bytes 3538952 | tf_op jit(solution)/shard_map/ppermute | solution.py:364
  6.4 14.3 %collective-permute-start.3 = (bf16[128,2176]{1,0:T(8,128)(2,1)}, bf16[128,2176]{1,0:T(8,128)(2,1)S(1)}, u32[]{:S(2)}, u32[]{:S(2)}) collective-permute-start(bf16[128,2176]{1,0:T(8,128)(2,1)} %get-tuple-element.42.refs_0_.refs_6_.refs_4_), channel_id=1, source_target_pairs={{0,2},{1,3},{2,0},{3,1},{4,6},{5,7},{6,4},{7,5},{8,10},{9,11},{10,... | collective-permute-start | bytes 1671176 | tf_op jit(solution)/shard_map/ppermute | solution.py:363
  7.9 14.0 %collective-permute-start = (bf16[128,2176]{1,0:T(8,128)(2,1)}, bf16[128,2176]{1,0:T(8,128)(2,1)S(1)}, u32[]{:S(2)}, u32[]{:S(2)}) collective-permute-start(bf16[128,2176]{1,0:T(8,128)(2,1)} %get-tuple-element.42.refs_0_.refs_6_.refs_4_), channel_id=1, source_target_pairs={{0,4},{1,5},{2,6},{3,7},{4,0},{5,1},{6,2},{7,3},{8,12},{9,13},{10,... | collective-permute-start | bytes 1671176 | tf_op jit(solution)/shard_map/ppermute | solution.py:363
  9.5 13.6 %collective-permute-start.1 = (bf16[128,2176]{1,0:T(8,128)(2,1)}, bf16[128,2176]{1,0:T(8,128)(2,1)S(1)}, u32[]{:S(2)}, u32[]{:S(2)}) collective-permute-start(bf16[128,2176]{1,0:T(8,128)(2,1)} %get-tuple-element.42.refs_0_.refs_6_.refs_4_), channel_id=1, source_target_pairs={{4,8},{5,9},{6,10},{7,11},{8,4},{9,5},{10,6},{11,7},{20,24},{21,25... | collective-permute-start | bytes 1671176 | tf_op jit(solution)/shard_map/ppermute | solution.py:363
  20.7 21.7 %copy-start.3 = (bf16[128,2176]{1,0:T(8,128)(2,1)}, bf16[128,2176]{1,0:T(8,128)(2,1)S(1)}, u32[]{:S(2)}) copy-start(bf16[128,2176]{1,0:T(8,128)(2,1)S(1)} %collective-permute-done.3.refs_3_.refs_9_.refs_7_) | copy-start | bytes 1671172
  21.9 20.5 %copy-start.4 = (bf16[128,2176]{1,0:T(8,128)(2,1)}, bf16[128,2176]{1,0:T(8,128)(2,1)S(1)}, u32[]{:S(2)}) copy-start(bf16[128,2176]{1,0:T(8,128)(2,1)S(1)} %collective-permute-done.refs_1_.refs_7_.refs_5_) | copy-start | bytes 1671172
  21.9 13.0 %collective-permute-start.4 = (bf16[128,2176]{1,0:T(8,128)(2,1)S(1)}, bf16[128,2176]{1,0:T(8,128)(2,1)S(1)}, u32[]{:S(2)}, u32[]{:S(2)}) collective-permute-start(bf16[128,2176]{1,0:T(8,128)(2,1)S(1)} %collective-permute-done.refs_1_.refs_7_.refs_5_), channel_id=1, source_target_pairs={{0,2},{1,3},{2,0},{3,1},{4,6},{5,7},{6,4},{7,5},{8,10},{9,11},{10,... | collective-permute-start | bytes 1671176 | tf_op jit(solution)/shard_map/ppermute | solution.py:363
  22.4 12.5 %collective-permute-start.6 = (bf16[128,2176]{1,0:T(8,128)(2,1)S(1)}, bf16[128,2176]{1,0:T(8,128)(2,1)S(1)}, u32[]{:S(2)}, u32[]{:S(2)}) collective-permute-start(bf16[128,2176]{1,0:T(8,128)(2,1)S(1)} %collective-permute-done.refs_1_.refs_7_.refs_5_), channel_id=1, source_target_pairs={{4,8},{5,9},{6,10},{7,11},{8,4},{9,5},{10,6},{11,7},{20,24},{21,25... | collective-permute-start | bytes 1671176 | tf_op jit(solution)/shard_map/ppermute | solution.py:363
  23.1 16.5 %collective-permute-start.2 = (bf16[128,2176]{1,0:T(8,128)(2,1)S(1)}, bf16[128,2176]{1,0:T(8,128)(2,1)S(1)}, u32[]{:S(2)}, u32[]{:S(2)}) collective-permute-start(bf16[128,2176]{1,0:T(8,128)(2,1)S(1)} %collective-permute-done.1), channel_id=1, source_target_pairs={{4,0},{5,1},{6,2},{7,3},{8,12},{9,13},{10,14},{11,15},{20,16},{21,... | collective-permute-start | bytes 1671176 | tf_op jit(solution)/shard_map/ppermute | solution.py:363
  34.9 7.5 %collective-permute-start.7 = (bf16[512,1152]{1,0:T(8,128)(2,1)}, bf16[512,1152]{1,0:T(8,128)(2,1)}, u32[]{:S(2)}, u32[]{:S(2)}) collective-permute-start(bf16[512,1152]{1,0:T(8,128)(2,1)} %get-tuple-element.45.refs_5_.refs_2_), channel_id=1, source_target_pairs={{0,1},{1,0},{2,3},{3,2},{4,5},{5,4},{6,7},{7,6},{8,9},{9,8},{10,11... | collective-permute-start | bytes 3538952 | tf_op jit(solution)/shard_map/ppermute | solution.py:363
  34.9 7.5 %collective-permute-start.8 = (bf16[512,1152]{1,0:T(8,128)(2,1)}, bf16[512,1152]{1,0:T(8,128)(2,1)}, u32[]{:S(2)}, u32[]{:S(2)}) collective-permute-start(bf16[512,1152]{1,0:T(8,128)(2,1)} %collective-permute-done.5.refs_6_.refs_3_), channel_id=1, source_target_pairs={{0,1},{1,0},{2,3},{3,2},{4,5},{5,4},{6,7},{7,6},{8,9},{9,8},{10,11... | collective-permute-start | bytes 3538952 | tf_op jit(solution)/shard_map/ppermute | solution.py:363
  39.7 15.6 %collective-permute-start.10 = (bf16[128,2176]{1,0:T(8,128)(2,1)S(1)}, bf16[128,2176]{1,0:T(8,128)(2,1)S(1)}, u32[]{:S(2)}, u32[]{:S(2)}) collective-permute-start(bf16[128,2176]{1,0:T(8,128)(2,1)S(1)} %broadcast_select_fusion.1.refs_2_.refs_8_.refs_6_), channel_id=1, source_target_pairs={{0,2},{1,3},{2,0},{3,1},{4,6},{5,7},{6,4},{7,5},{8,10},{9,11},{10,... | collective-permute-start | bytes 1671176 | tf_op jit(solution)/shard_map/ppermute | solution.py:363
  41.1 14.1 %collective-permute-start.9 = (bf16[128,2176]{1,0:T(8,128)(2,1)S(1)}, bf16[128,2176]{1,0:T(8,128)(2,1)S(1)}, u32[]{:S(2)}, u32[]{:S(2)}) collective-permute-start(bf16[128,2176]{1,0:T(8,128)(2,1)S(1)} %collective-permute-done.6), channel_id=1, source_target_pairs={{4,0},{5,1},{6,2},{7,3},{8,12},{9,13},{10,14},{11,15},{20,16},{21,... | collective-permute-start | bytes 1671176 | tf_op jit(solution)/shard_map/ppermute | solution.py:363
  55.3 11.3 %collective-permute-start.11 = (bf16[128,2176]{1,0:T(8,128)(2,1)S(1)}, bf16[128,2176]{1,0:T(8,128)(2,1)S(1)}, u32[]{:S(2)}, u32[]{:S(2)}) collective-permute-start(bf16[128,2176]{1,0:T(8,128)(2,1)S(1)} %broadcast_select_fusion.refs_0_.refs_9_.refs_5_), channel_id=1, source_target_pairs={{0,2},{1,3},{2,0},{3,1},{4,6},{5,7},{6,4},{7,5},{8,10},{9,11},{10,... | collective-permute-start | bytes 1671176 | tf_op jit(solution)/shard_map/ppermute | solution.py:363
  56.3 11.5 %copy-start.15 = (bf16[128,1024]{1,0:T(8,128)(2,1)S(1)}, bf16[128,1024]{1,0:T(8,128)(2,1)}, u32[]{:S(2)}) copy-start(bf16[128,1024]{1,0:T(8,128)(2,1)} %get-tuple-element.67) | copy-start | bytes 786436
  66.6 3.9 %collective-permute-start.13 = (bf16[512,1152]{1,0:T(8,128)(2,1)}, bf16[512,1152]{1,0:T(8,128)(2,1)S(1)}, u32[]{:S(2)}, u32[]{:S(2)}) collective-permute-start(bf16[512,1152]{1,0:T(8,128)(2,1)} %get-tuple-element.60), channel_id=1, source_target_pairs={{0,1},{1,0},{2,3},{3,2},{4,5},{5,4},{6,7},{7,6},{8,9},{9,8},{10,11... | collective-permute-start | bytes 3538952 | tf_op jit(solution)/shard_map/ppermute | solution.py:363
  66.6 3.3 %collective-permute-start.12 = (bf16[128,2176]{1,0:T(8,128)(2,1)S(1)}, bf16[128,2176]{1,0:T(8,128)(2,1)S(1)}, u32[]{:S(2)}, u32[]{:S(2)}) collective-permute-start(bf16[128,2176]{1,0:T(8,128)(2,1)S(1)} %collective-permute-done.11.refs_0_.refs_7_), channel_id=1, source_target_pairs={{0,1},{1,0},{2,3},{3,2},{4,5},{5,4},{6,7},{7,6},{8,9},{9,8},{10,11... | collective-permute-start | bytes 1671176 | tf_op jit(solution)/shard_map/ppermute | solution.py:363
  67.1 12.0 %collective-permute-start.15 = (bf16[128,1024]{1,0:T(8,128)(2,1)}, bf16[128,1024]{1,0:T(8,128)(2,1)S(1)}, u32[]{:S(2)}, u32[]{:S(2)}) collective-permute-start(bf16[128,1024]{1,0:T(8,128)(2,1)} %get-tuple-element.65), channel_id=1, source_target_pairs={{0,2},{1,3},{2,0},{3,1},{4,6},{5,7},{6,4},{7,5},{8,10},{9,11},{10,... | collective-permute-start | bytes 786440 | tf_op jit(solution)/shard_map/ppermute | solution.py:363
  67.8 13.4 %collective-permute-start.16 = (bf16[128,1024]{1,0:T(8,128)(2,1)S(1)}, bf16[128,1024]{1,0:T(8,128)(2,1)S(1)}, u32[]{:S(2)}, u32[]{:S(2)}) collective-permute-start(bf16[128,1024]{1,0:T(8,128)(2,1)S(1)} %copy-done.15), channel_id=1, source_target_pairs={{0,2},{1,3},{2,0},{3,1},{4,6},{5,7},{6,4},{7,5},{8,10},{9,11},{10,... | collective-permute-start | bytes 786440 | tf_op jit(solution)/shard_map/ppermute | solution.py:363
  69.9 11.3 %collective-permute-start.17 = (bf16[512,1152]{1,0:T(8,128)(2,1)}, bf16[512,1152]{1,0:T(8,128)(2,1)S(1)}, u32[]{:S(2)}, u32[]{:S(2)}) collective-permute-start(bf16[512,1152]{1,0:T(8,128)(2,1)} %get-tuple-element.69), channel_id=1, source_target_pairs={{0,1},{1,0},{2,3},{3,2},{4,5},{5,4},{6,7},{7,6},{8,9},{9,8},{10,11... | collective-permute-start | bytes 3538952 | tf_op jit(solution)/shard_map/ppermute | solution.py:363
  71.5 13.8 %copy-start.10 = (bf16[128,1024]{1,0:T(8,128)(2,1)S(1)}, bf16[128,1024]{1,0:T(8,128)(2,1)}, u32[]{:S(2)}) copy-start(bf16[128,1024]{1,0:T(8,128)(2,1)} %get-tuple-element.79) | copy-start | bytes 786436
  79.2 13.3 %copy-start.11 = (bf16[128,1024]{1,0:T(8,128)(2,1)S(1)}, bf16[128,1024]{1,0:T(8,128)(2,1)}, u32[]{:S(2)}) copy-start(bf16[128,1024]{1,0:T(8,128)(2,1)} %get-tuple-element.62) | copy-start | bytes 786436
  81.2 1.7 %collective-permute-start.18 = (bf16[128,1024]{1,0:T(8,128)(2,1)}, bf16[128,1024]{1,0:T(8,128)(2,1)S(1)}, u32[]{:S(2)}, u32[]{:S(2)}) collective-permute-start(bf16[128,1024]{1,0:T(8,128)(2,1)} %get-tuple-element.70), channel_id=1, source_target_pairs={{0,1},{1,0},{2,3},{3,2},{4,5},{5,4},{6,7},{7,6},{8,9},{9,8},{10,11... | collective-permute-start | bytes 786440 | tf_op jit(solution)/shard_map/ppermute | solution.py:363
  82.9 14.9 %copy-start.9 = (bf16[128,1024]{1,0:T(8,128)(2,1)S(1)}, bf16[128,1024]{1,0:T(8,128)(2,1)}, u32[]{:S(2)}) copy-start(bf16[128,1024]{1,0:T(8,128)(2,1)} %get-tuple-element.78) | copy-start | bytes 786436
  84.0 8.4 %collective-permute-start.19 = (bf16[128,1024]{1,0:T(8,128)(2,1)S(1)}, bf16[128,1024]{1,0:T(8,128)(2,1)S(1)}, u32[]{:S(2)}, u32[]{:S(2)}) collective-permute-start(bf16[128,1024]{1,0:T(8,128)(2,1)S(1)} %add_convert_fusion.6), channel_id=1, source_target_pairs={{0,2},{1,3},{2,0},{3,1},{4,6},{5,7},{6,4},{7,5},{8,10},{9,11},{10,... | collective-permute-start | bytes 786440 | tf_op jit(solution)/shard_map/ppermute | solution.py:363
  84.8 28.5 %collective-permute-start.14 = (bf16[512,1152]{1,0:T(8,128)(2,1)}, bf16[512,1152]{1,0:T(8,128)(2,1)S(1)}, u32[]{:S(2)}, u32[]{:S(2)}) collective-permute-start(bf16[512,1152]{1,0:T(8,128)(2,1)} %get-tuple-element.61), channel_id=1, source_target_pairs={{0,16},{16,0},{1,17},{17,1},{2,18},{18,2},{3,19},{19,3},{4,20},{20... | collective-permute-start | bytes 3538952 | tf_op jit(solution)/shard_map/ppermute | solution.py:364
  85.4 12.7 %collective-permute-start.23 = (bf16[128,1024]{1,0:T(8,128)(2,1)S(1)}, bf16[128,1024]{1,0:T(8,128)(2,1)S(1)}, u32[]{:S(2)}, u32[]{:S(2)}) collective-permute-start(bf16[128,1024]{1,0:T(8,128)(2,1)S(1)} %add_convert_fusion.2), channel_id=1, source_target_pairs={{0,4},{1,5},{2,6},{3,7},{12,8},{13,9},{14,10},{15,11},{16,20},{17,... | collective-permute-start | bytes 786440 | tf_op jit(solution)/shard_map/ppermute | solution.py:363
  92.5 12.1 %collective-permute-start.20 = (bf16[128,1024]{1,0:T(8,128)(2,1)S(1)}, bf16[128,1024]{1,0:T(8,128)(2,1)S(1)}, u32[]{:S(2)}, u32[]{:S(2)}) collective-permute-start(bf16[128,1024]{1,0:T(8,128)(2,1)S(1)} %add_convert_fusion.5), channel_id=1, source_target_pairs={{0,4},{1,5},{2,6},{3,7},{12,8},{13,9},{14,10},{15,11},{16,20},{17,... | collective-permute-start | bytes 786440 | tf_op jit(solution)/shard_map/ppermute | solution.py:363
  97.9 19.1 %collective-permute-start.22 = (bf16[128,1024]{1,0:T(8,128)(2,1)S(1)}, bf16[128,1024]{1,0:T(8,128)(2,1)S(1)}, u32[]{:S(2)}, u32[]{:S(2)}) collective-permute-start(bf16[128,1024]{1,0:T(8,128)(2,1)S(1)} %add_convert_fusion.3), channel_id=1, source_target_pairs={{0,4},{1,5},{2,6},{3,7},{4,0},{5,1},{6,2},{7,3},{8,12},{9,13},{10,... | collective-permute-start | bytes 786440 | tf_op jit(solution)/shard_map/ppermute | solution.py:363
  98.1 18.9 %collective-permute-start.24 = (bf16[128,1024]{1,0:T(8,128)(2,1)S(1)}, bf16[128,1024]{1,0:T(8,128)(2,1)S(1)}, u32[]{:S(2)}, u32[]{:S(2)}) collective-permute-start(bf16[128,1024]{1,0:T(8,128)(2,1)S(1)} %add_convert_fusion.1), channel_id=1, source_target_pairs={{4,8},{5,9},{6,10},{7,11},{8,4},{9,5},{10,6},{11,7},{20,24},{21,25... | collective-permute-start | bytes 786440 | tf_op jit(solution)/shard_map/ppermute | solution.py:363
  104.7 13.6 %collective-permute-start.25 = (bf16[128,1024]{1,0:T(8,128)(2,1)S(1)}, bf16[128,1024]{1,0:T(8,128)(2,1)S(1)}, u32[]{:S(2)}, u32[]{:S(2)}) collective-permute-start(bf16[128,1024]{1,0:T(8,128)(2,1)S(1)} %add_convert_fusion.4), channel_id=1, source_target_pairs={{4,12},{5,13},{6,14},{7,15},{8,0},{9,1},{10,2},{11,3},{20,28},{21,... | collective-permute-start | bytes 786440 | tf_op jit(solution)/shard_map/ppermute | solution.py:363
  111.8 6.4 %collective-permute-start.21 = (bf16[128,1024]{1,0:T(8,128)(2,1)S(1)}, bf16[128,1024]{1,0:T(8,128)(2,1)S(1)}, u32[]{:S(2)}, u32[]{:S(2)}) collective-permute-start(bf16[128,1024]{1,0:T(8,128)(2,1)S(1)} %copy-done.14), channel_id=1, source_target_pairs={{0,2},{1,3},{2,0},{3,1},{4,6},{5,7},{6,4},{7,5},{8,10},{9,11},{10,... | collective-permute-start | bytes 786440 | tf_op jit(solution)/shard_map/ppermute | solution.py:363
  (10 other events, 37.4 us)

commit v15 on v14

--- a/solution.py
+++ b/solution.py
@@ -402,14 +402,14 @@
     from_part = across(send)
     add = lambda *terms: sum(t.astype(F32) for t in terms).astype(BF16)
     r3 = move(add(last, swap(after(pair, r2, r1, got_mine))), SWAP_Y)
-    s1 = add(p1, r1)
+    r0 = move(after(q0, r3), SWAP_Y)
     s2 = add(p2, r2)
     s2 = add(s2, move(s2, INWARD))
     s3 = add(p3, r3)
     s3 = add(s3, move(s3, INWARD))
     keep = half_call(after(mine, send, s3), blocks + [y3, cy3], kept + [kept_c], more=got_mine)
 
-    r0 = move(after(q0, r3, keep), SWAP_Y)
+    s1 = after(add(p1, r1), keep)
     from_part = after(from_part, s3)
     hidden_units = gate_weight.shape[2]
     whole = lambda a: keep[:, a : a + hidden_units].astype(F32) + from_part[:, a : a + hidden_units].astype(F32)

time: 120 us -> 120 us (level)
  starting transfers between devices: 32.3 us -> 35.9 us
  waiting for transfers between devices: 40.1 us -> 37 us
    ppermute x24, starting transfers between devices: 28.8 us -> 32.4 us  [dense_body(): move = lambda a, pairs: lax.ppermute(a, 'expert', pairs)]
    ppermute x24, waiting for transfers between devices: 40.1 us -> 37 us  [dense_body(): move = lambda a, pairs: lax.ppermute(a, 'expert', pairs)]
where the time goes in v15:
time: 120 us
  Pallas kernels  37.5 us (31%)
  waiting for transfers between devices  37 us (31%)
  starting transfers between devices  35.9 us (30%)
  other arithmetic  5.7 us (5%)
  local copies, waits for them, and re-layouts  2.52 us (2%)
    ppermute x24, waiting for transfers between devices, dense_body(): move = lambda a, pairs: lax.ppermute(a, 'expert', pairs)  37 us
    ppermute x24, starting transfers between devices, dense_body(): move = lambda a, pairs: lax.ppermute(a, 'expert', pairs)  32.4 us
    pallas_call x3, Pallas kernels, rows_call(): pl.pallas_call(functools.partial(rows_kernel, experts, count, sizes, whic...  29 us
    pallas_call x1, Pallas kernels, half_call(): pl.pallas_call(functools.partial(half_kernel, len(blocks), len(kept)), ou...  5.78 us
    ppermute x2, starting transfers between devices, dense_body(): across = lambda a: lax.ppermute(a, 'dp', [(0, 1), (1, 0)])  3.52 us
    pallas_call x1, Pallas kernels, pack(): pl.pallas_call(functools.partial(pack_kernel, experts), out_shape=[jax.Sh...  2.73 us
    broadcast_in_dim x1, other arithmetic, dense_body(): return (d_tokens, d_gate[None], d_up[None], d_down[None])  2.61 us
    unnamed x33, local copies, waits for them, and re-layouts  2.52 us
  transfers between devices with their start and end apart: 26, of which 13 were waited for; matrix products, arithmetic and copies ran while one was open for 4% of the time, Pallas kernels for 29%

profile of v15, /device:TPU:0, one launch (start us, length us, event | category | flops | bytes accessed | tf_op | source)
XLA Modules:
  0.0 119.6 jit_solution(2296250630818486288)
XLA Ops:
  0.6 2.7 %shard_map.102 = (bf16[128,2176]{1,0:T(8,128)(2,1)}, bf16[512,1152]{1,0:T(8,128)(2,1)}) custom-call(bf16[128,1024]{1,0:T(8,128)(2,1)} %tokens.1, bf16[128,1024]{1,0:T(8,128)(2,1)} %d_output.1, f32[8,128]{1,0:T(8,128)} %bitcast.18, s32[8,128]{1,0:T(8,128)} %bitcast.19, bf16[512,384]{1,0:T(8,128)(2,1)} %bitcast.15, bf16[512,384]{1,0:T(8,128)(2,1)} %bitcast.16, ...), custom_call_target="tpu_custom_call" | custom-call | bytes 1048576 | tf_op jit(solution)/shard_map/pallas_call | solution.py:79
  3.4 3.0 %collective-permute-start.5 = (bf16[512,1152]{1,0:T(8,128)(2,1)}, bf16[512,1152]{1,0:T(8,128)(2,1)}, u32[]{:S(2)}, u32[]{:S(2)}) collective-permute-start(bf16[512,1152]{1,0:T(8,128)(2,1)} %get-tuple-element.46.refs_5_.refs_2_), channel_id=1, source_target_pairs={{0,16},{16,0},{1,17},{17,1},{2,18},{18,2},{3,19},{19,3},{4,20},{20... | collective-permute-start | bytes 3538952 | tf_op jit(solution)/shard_map/ppermute | solution.py:364
  6.4 1.5 %collective-permute-start.3 = (bf16[128,2176]{1,0:T(8,128)(2,1)}, bf16[128,2176]{1,0:T(8,128)(2,1)S(1)}, u32[]{:S(2)}, u32[]{:S(2)}) collective-permute-start(bf16[128,2176]{1,0:T(8,128)(2,1)} %get-tuple-element.43.refs_0_.refs_6_.refs_4_), channel_id=1, source_target_pairs={{0,2},{1,3},{2,0},{3,1},{4,6},{5,7},{6,4},{7,5},{8,10},{9,11},{10,... | collective-permute-start | bytes 1671176 | tf_op jit(solution)/shard_map/ppermute | solution.py:363
  7.9 1.6 %collective-permute-start = (bf16[128,2176]{1,0:T(8,128)(2,1)}, bf16[128,2176]{1,0:T(8,128)(2,1)S(1)}, u32[]{:S(2)}, u32[]{:S(2)}) collective-permute-start(bf16[128,2176]{1,0:T(8,128)(2,1)} %get-tuple-element.43.refs_0_.refs_6_.refs_4_), channel_id=1, source_target_pairs={{0,4},{1,5},{2,6},{3,7},{4,0},{5,1},{6,2},{7,3},{8,12},{9,13},{10,... | collective-permute-start | bytes 1671176 | tf_op jit(solution)/shard_map/ppermute | solution.py:363
  10.2 10.5 %collective-permute-done.3.refs_3_.refs_9_.refs_7_ = bf16[128,2176]{1,0:T(8,128)(2,1)S(1)} collective-permute-done((bf16[128,2176]{1,0:T(8,128)(2,1)}, bf16[128,2176]{1,0:T(8,128)(2,1)S(1)}, u32[]{:S(2)}, u32[]{:S(2)}) %collective-permute-start.3) | collective-permute-done | bytes 557088 | tf_op jit(solution)/shard_map/ppermute | solution.py:363
  20.7 1.2 %collective-permute-done.refs_1_.refs_7_.refs_5_ = bf16[128,2176]{1,0:T(8,128)(2,1)S(1)} collective-permute-done((bf16[128,2176]{1,0:T(8,128)(2,1)}, bf16[128,2176]{1,0:T(8,128)(2,1)S(1)}, u32[]{:S(2)}, u32[]{:S(2)}) %collective-permute-start) | collective-permute-done | bytes 557088 | tf_op jit(solution)/shard_map/ppermute | solution.py:363
  23.1 1.3 %collective-permute-start.2 = (bf16[128,2176]{1,0:T(8,128)(2,1)S(1)}, bf16[128,2176]{1,0:T(8,128)(2,1)S(1)}, u32[]{:S(2)}, u32[]{:S(2)}) collective-permute-start(bf16[128,2176]{1,0:T(8,128)(2,1)S(1)} %collective-permute-done.1), channel_id=1, source_target_pairs={{4,0},{5,1},{6,2},{7,3},{8,12},{9,13},{10,14},{11,15},{20,16},{21,... | collective-permute-start | bytes 1671176 | tf_op jit(solution)/shard_map/ppermute | solution.py:363
  24.4 10.5 %collective-permute-done.4.refs_4_.refs_10_.refs_8_ = bf16[128,2176]{1,0:T(8,128)(2,1)S(1)} collective-permute-done((bf16[128,2176]{1,0:T(8,128)(2,1)S(1)}, bf16[128,2176]{1,0:T(8,128)(2,1)S(1)}, u32[]{:S(2)}, u32[]{:S(2)}) %collective-permute-start.4) | collective-permute-done | bytes 557088 | tf_op jit(solution)/shard_map/ppermute | solution.py:363
  36.1 3.5 %collective-permute-done.2 = bf16[128,2176]{1,0:T(8,128)(2,1)S(1)} collective-permute-done((bf16[128,2176]{1,0:T(8,128)(2,1)S(1)}, bf16[128,2176]{1,0:T(8,128)(2,1)S(1)}, u32[]{:S(2)}, u32[]{:S(2)}) %collective-permute-start.2) | collective-permute-done | bytes 557088 | tf_op jit(solution)/shard_map/ppermute | solution.py:363
  39.7 1.4 %collective-permute-start.10 = (bf16[128,2176]{1,0:T(8,128)(2,1)S(1)}, bf16[128,2176]{1,0:T(8,128)(2,1)S(1)}, u32[]{:S(2)}, u32[]{:S(2)}) collective-permute-start(bf16[128,2176]{1,0:T(8,128)(2,1)S(1)} %broadcast_select_fusion.1.refs_2_.refs_8_.refs_6_), channel_id=1, source_target_pairs={{0,2},{1,3},{2,0},{3,1},{4,6},{5,7},{6,4},{7,5},{8,10},{9,11},{10,... | collective-permute-start | bytes 1671176 | tf_op jit(solution)/shard_map/ppermute | solution.py:363
  41.1 1.3 %collective-permute-start.9 = (bf16[128,2176]{1,0:T(8,128)(2,1)S(1)}, bf16[128,2176]{1,0:T(8,128)(2,1)S(1)}, u32[]{:S(2)}, u32[]{:S(2)}) collective-permute-start(bf16[128,2176]{1,0:T(8,128)(2,1)S(1)} %collective-permute-done.6), channel_id=1, source_target_pairs={{4,0},{5,1},{6,2},{7,3},{8,12},{9,13},{10,14},{11,15},{20,16},{21,... | collective-permute-start | bytes 1671176 | tf_op jit(solution)/shard_map/ppermute | solution.py:363
  42.5 11.6 %shard_map.103 = (bf16[128,1024]{1,0:T(8,128)(2,1)}, bf16[128,1024]{1,0:T(8,128)(2,1)}, bf16[128,1024]{1,0:T(8,128)(2,1)}, bf16[128,1024]{1,0:T(8,128)(2,1)}, bf...) custom-call(s32[2]{0:T(128)} %pad_add_fusion.scal, ...), custom_call_target="tpu_custom_call" | custom-call | flops 18119393280 | bytes 1048576 | tf_op jit(solution)/shard_map/pallas_call | solution.py:243
  54.0 1.1 collective-permute-done.9
  56.3 9.8 %shard_map.104 = (bf16[128,1024]{1,0:T(8,128)(2,1)}, bf16[128,1024]{1,0:T(8,128)(2,1)}, bf16[256,1152]{1,0:T(8,128)(2,1)}, bf16[256,1024]{1,0:T(8,128)(2,1)}, bf...) custom-call(s32[2]{0:T(128)} %pad_add_fusion.scal, ...), custom_call_target="tpu_custom_call" | custom-call | flops 7247757312 | bytes 1048576 | tf_op jit(solution)/shard_map/pallas_call | solution.py:243
  67.8 1.4 %collective-permute-start.16 = (bf16[128,1024]{1,0:T(8,128)(2,1)S(1)}, bf16[128,1024]{1,0:T(8,128)(2,1)S(1)}, u32[]{:S(2)}, u32[]{:S(2)}) collective-permute-start(bf16[128,1024]{1,0:T(8,128)(2,1)S(1)} %copy-done.15), channel_id=1, source_target_pairs={{0,2},{1,3},{2,0},{3,1},{4,6},{5,7},{6,4},{7,5},{8,10},{9,11},{10,... | collective-permute-start | bytes 786440 | tf_op jit(solution)/shard_map/ppermute | solution.py:363
  70.7 0.8 copy-done.13
  71.5 7.6 %shard_map.105 = (bf16[128,1024]{1,0:T(8,128)(2,1)}, bf16[128,1024]{1,0:T(8,128)(2,1)}, bf16[256,1152]{1,0:T(8,128)(2,1)}, bf16[256,1024]{1,0:T(8,128)(2,1)}, bf16[512,1152]{1,0:T(8,128)(2,1)}) custom-call(s32[2]{0:T(128)} %pad_add_fusion.scal, bf16[128,2176]{1,0:T(8,128)(2,1)} %copy-done.7, bf16[128,2176]{1,0:T(8,128)(2,1)} %copy-done.8, ...), custom_call_target="tpu_custom_call" | custom-call | flops 36238786560 | bytes 1048576 | tf_op jit(solution)/shard_map/pallas_call | solution.py:243
  79.2 2.0 %collective-permute-done.16 = bf16[128,1024]{1,0:T(8,128)(2,1)S(1)} collective-permute-done((bf16[128,1024]{1,0:T(8,128)(2,1)S(1)}, bf16[128,1024]{1,0:T(8,128)(2,1)S(1)}, u32[]{:S(2)}, u32[]{:S(2)}) %collective-permute-start.16) | collective-permute-done | bytes 262176 | tf_op jit(solution)/shard_map/ppermute | solution.py:363
  81.2 1.7 %collective-permute-done.18 = bf16[128,1024]{1,0:T(8,128)(2,1)S(1)} collective-permute-done((bf16[128,1024]{1,0:T(8,128)(2,1)}, bf16[128,1024]{1,0:T(8,128)(2,1)S(1)}, u32[]{:S(2)}, u32[]{:S(2)}) %collective-permute-start.18) | collective-permute-done | bytes 262176 | tf_op jit(solution)/shard_map/ppermute | solution.py:363
  82.9 1.1 add_convert_fusion.6
  85.4 6.1 %collective-permute-start.23 = (bf16[128,1024]{1,0:T(8,128)(2,1)S(1)}, bf16[128,1024]{1,0:T(8,128)(2,1)S(1)}, u32[]{:S(2)}, u32[]{:S(2)}) collective-permute-start(bf16[128,1024]{1,0:T(8,128)(2,1)S(1)} %add_convert_fusion.2), channel_id=1, source_target_pairs={{0,4},{1,5},{2,6},{3,7},{12,8},{13,9},{14,10},{15,11},{16,20},{17,... | collective-permute-start | bytes 786440 | tf_op jit(solution)/shard_map/ppermute | solution.py:363
  91.4 1.0 collective-permute-done.19
  92.5 5.3 %collective-permute-start.20 = (bf16[128,1024]{1,0:T(8,128)(2,1)S(1)}, bf16[128,1024]{1,0:T(8,128)(2,1)S(1)}, u32[]{:S(2)}, u32[]{:S(2)}) collective-permute-start(bf16[128,1024]{1,0:T(8,128)(2,1)S(1)} %add_convert_fusion.5), channel_id=1, source_target_pairs={{0,4},{1,5},{2,6},{3,7},{12,8},{13,9},{14,10},{15,11},{16,20},{17,... | collective-permute-start | bytes 786440 | tf_op jit(solution)/shard_map/ppermute | solution.py:363
  98.7 1.4 %collective-permute-start.21 = (bf16[128,1024]{1,0:T(8,128)(2,1)S(1)}, bf16[128,1024]{1,0:T(8,128)(2,1)S(1)}, u32[]{:S(2)}, u32[]{:S(2)}) collective-permute-start(bf16[128,1024]{1,0:T(8,128)(2,1)S(1)} %copy-done.14), channel_id=1, source_target_pairs={{0,2},{1,3},{2,0},{3,1},{4,6},{5,7},{6,4},{7,5},{8,10},{9,11},{10,... | collective-permute-start | bytes 786440 | tf_op jit(solution)/shard_map/ppermute | solution.py:363
  100.2 2.7 %collective-permute-done.20 = bf16[128,1024]{1,0:T(8,128)(2,1)S(1)} collective-permute-done((bf16[128,1024]{1,0:T(8,128)(2,1)S(1)}, bf16[128,1024]{1,0:T(8,128)(2,1)S(1)}, u32[]{:S(2)}, u32[]{:S(2)}) %collective-permute-start.20) | collective-permute-done | bytes 262176 | tf_op jit(solution)/shard_map/ppermute | solution.py:363
  102.9 1.3 %collective-permute-start.25 = (bf16[128,1024]{1,0:T(8,128)(2,1)S(1)}, bf16[128,1024]{1,0:T(8,128)(2,1)S(1)}, u32[]{:S(2)}, u32[]{:S(2)}) collective-permute-start(bf16[128,1024]{1,0:T(8,128)(2,1)S(1)} %add_convert_fusion.4), channel_id=1, source_target_pairs={{4,12},{5,13},{6,14},{7,15},{8,0},{9,1},{10,2},{11,3},{20,28},{21,... | collective-permute-start | bytes 786440 | tf_op jit(solution)/shard_map/ppermute | solution.py:363
  104.2 5.8 %shard_map.106 = bf16[512,1152]{1,0:T(8,128)(2,1)} custom-call(s32[1]{0:T(128)} %bitcast.sides, bf16[128,2176]{1,0:T(8,128)(2,1)} %get-tuple-element.43.refs_0_.refs_6_.refs_4_, bf16[128,2176]{1,0:T(8,128)(2,1)} %copy-done.4, bf16[128,2176]{1,0:T(8,128)(2,1)} %copy-done, bf16[128,2176]{1,0:T(8,128)(2,1)} %copy-done.3, bf16[128,2176]{1,0:T(8,128)(2,1)} %copy-done.5, ...), custom_call_target="tpu_custom_call" | custom-call | flops 1024 | bytes 1024 | tf_op jit(solution)/shard_map/pallas_call | solution.py:304
  110.0 3.7 %collective-permute-start.22 = (bf16[128,1024]{1,0:T(8,128)(2,1)S(1)}, bf16[128,1024]{1,0:T(8,128)(2,1)S(1)}, u32[]{:S(2)}, u32[]{:S(2)}) collective-permute-start(bf16[128,1024]{1,0:T(8,128)(2,1)S(1)} %add_convert_fusion.3), channel_id=1, source_target_pairs={{0,4},{1,5},{2,6},{3,7},{4,0},{5,1},{6,2},{7,3},{8,12},{9,13},{10,... | collective-permute-start | bytes 786440 | tf_op jit(solution)/shard_map/ppermute | solution.py:363
  113.8 2.6 %add_bitcast_fusion = (f32[1,384,512]{1,2,0:T(8,128)S(1)}, f32[1,512,384]{2,1,0:T(8,128)}, f32[1,512,384]{2,1,0:T(8,128)}) fusion(bf16[512,1152]{1,0:T(8,128)(2,1)} %shard_map.106, bf16[512,1152]{1,0:T(8,128)(2,1)S(1)} %collective-permute-done.14), kind=kLoop, calls=%fused_computation | loop fusion | flops 1769472 | bytes 4718592 | tf_op jit(solution)/shard_map/broadcast_in_dim | solution.py:418
  116.4 1.1 copy.11
  117.5 1.2 collective-permute-done.22
  118.7 0.9 add_convert_fusion
  (69 shorter events, 9.8 us)
Async XLA Ops:
  3.4 31.5 %collective-permute-start.5 = (bf16[512,1152]{1,0:T(8,128)(2,1)}, bf16[512,1152]{1,0:T(8,128)(2,1)}, u32[]{:S(2)}, u32[]{:S(2)}) collective-permute-start(bf16[512,1152]{1,0:T(8,128)(2,1)} %get-tuple-element.46.refs_5_.refs_2_), channel_id=1, source_target_pairs={{0,16},{16,0},{1,17},{17,1},{2,18},{18,2},{3,19},{19,3},{4,20},{20... | collective-permute-start | bytes 3538952 | tf_op jit(solution)/shard_map/ppermute | solution.py:364
  6.4 14.3 %collective-permute-start.3 = (bf16[128,2176]{1,0:T(8,128)(2,1)}, bf16[128,2176]{1,0:T(8,128)(2,1)S(1)}, u32[]{:S(2)}, u32[]{:S(2)}) collective-permute-start(bf16[128,2176]{1,0:T(8,128)(2,1)} %get-tuple-element.43.refs_0_.refs_6_.refs_4_), channel_id=1, source_target_pairs={{0,2},{1,3},{2,0},{3,1},{4,6},{5,7},{6,4},{7,5},{8,10},{9,11},{10,... | collective-permute-start | bytes 1671176 | tf_op jit(solution)/shard_map/ppermute | solution.py:363
  7.9 14.0 %collective-permute-start = (bf16[128,2176]{1,0:T(8,128)(2,1)}, bf16[128,2176]{1,0:T(8,128)(2,1)S(1)}, u32[]{:S(2)}, u32[]{:S(2)}) collective-permute-start(bf16[128,2176]{1,0:T(8,128)(2,1)} %get-tuple-element.43.refs_0_.refs_6_.refs_4_), channel_id=1, source_target_pairs={{0,4},{1,5},{2,6},{3,7},{4,0},{5,1},{6,2},{7,3},{8,12},{9,13},{10,... | collective-permute-start | bytes 1671176 | tf_op jit(solution)/shard_map/ppermute | solution.py:363
  9.5 13.6 %collective-permute-start.1 = (bf16[128,2176]{1,0:T(8,128)(2,1)}, bf16[128,2176]{1,0:T(8,128)(2,1)S(1)}, u32[]{:S(2)}, u32[]{:S(2)}) collective-permute-start(bf16[128,2176]{1,0:T(8,128)(2,1)} %get-tuple-element.43.refs_0_.refs_6_.refs_4_), channel_id=1, source_target_pairs={{4,8},{5,9},{6,10},{7,11},{8,4},{9,5},{10,6},{11,7},{20,24},{21,25... | collective-permute-start | bytes 1671176 | tf_op jit(solution)/shard_map/ppermute | solution.py:363
  20.7 21.7 %copy-start.3 = (bf16[128,2176]{1,0:T(8,128)(2,1)}, bf16[128,2176]{1,0:T(8,128)(2,1)S(1)}, u32[]{:S(2)}) copy-start(bf16[128,2176]{1,0:T(8,128)(2,1)S(1)} %collective-permute-done.3.refs_3_.refs_9_.refs_7_) | copy-start | bytes 1671172
  21.9 20.5 %copy-start.4 = (bf16[128,2176]{1,0:T(8,128)(2,1)}, bf16[128,2176]{1,0:T(8,128)(2,1)S(1)}, u32[]{:S(2)}) copy-start(bf16[128,2176]{1,0:T(8,128)(2,1)S(1)} %collective-permute-done.refs_1_.refs_7_.refs_5_) | copy-start | bytes 1671172
  21.9 13.0 %collective-permute-start.4 = (bf16[128,2176]{1,0:T(8,128)(2,1)S(1)}, bf16[128,2176]{1,0:T(8,128)(2,1)S(1)}, u32[]{:S(2)}, u32[]{:S(2)}) collective-permute-start(bf16[128,2176]{1,0:T(8,128)(2,1)S(1)} %collective-permute-done.refs_1_.refs_7_.refs_5_), channel_id=1, source_target_pairs={{0,2},{1,3},{2,0},{3,1},{4,6},{5,7},{6,4},{7,5},{8,10},{9,11},{10,... | collective-permute-start | bytes 1671176 | tf_op jit(solution)/shard_map/ppermute | solution.py:363
  22.4 12.5 %collective-permute-start.6 = (bf16[128,2176]{1,0:T(8,128)(2,1)S(1)}, bf16[128,2176]{1,0:T(8,128)(2,1)S(1)}, u32[]{:S(2)}, u32[]{:S(2)}) collective-permute-start(bf16[128,2176]{1,0:T(8,128)(2,1)S(1)} %collective-permute-done.refs_1_.refs_7_.refs_5_), channel_id=1, source_target_pairs={{4,8},{5,9},{6,10},{7,11},{8,4},{9,5},{10,6},{11,7},{20,24},{21,25... | collective-permute-start | bytes 1671176 | tf_op jit(solution)/shard_map/ppermute | solution.py:363
  23.1 16.5 %collective-permute-start.2 = (bf16[128,2176]{1,0:T(8,128)(2,1)S(1)}, bf16[128,2176]{1,0:T(8,128)(2,1)S(1)}, u32[]{:S(2)}, u32[]{:S(2)}) collective-permute-start(bf16[128,2176]{1,0:T(8,128)(2,1)S(1)} %collective-permute-done.1), channel_id=1, source_target_pairs={{4,0},{5,1},{6,2},{7,3},{8,12},{9,13},{10,14},{11,15},{20,16},{21,... | collective-permute-start | bytes 1671176 | tf_op jit(solution)/shard_map/ppermute | solution.py:363
  34.9 7.5 %collective-permute-start.7 = (bf16[512,1152]{1,0:T(8,128)(2,1)}, bf16[512,1152]{1,0:T(8,128)(2,1)}, u32[]{:S(2)}, u32[]{:S(2)}) collective-permute-start(bf16[512,1152]{1,0:T(8,128)(2,1)} %get-tuple-element.46.refs_5_.refs_2_), channel_id=1, source_target_pairs={{0,1},{1,0},{2,3},{3,2},{4,5},{5,4},{6,7},{7,6},{8,9},{9,8},{10,11... | collective-permute-start | bytes 3538952 | tf_op jit(solution)/shard_map/ppermute | solution.py:363
  34.9 7.5 %collective-permute-start.8 = (bf16[512,1152]{1,0:T(8,128)(2,1)}, bf16[512,1152]{1,0:T(8,128)(2,1)}, u32[]{:S(2)}, u32[]{:S(2)}) collective-permute-start(bf16[512,1152]{1,0:T(8,128)(2,1)} %collective-permute-done.5.refs_6_.refs_3_), channel_id=1, source_target_pairs={{0,1},{1,0},{2,3},{3,2},{4,5},{5,4},{6,7},{7,6},{8,9},{9,8},{10,11... | collective-permute-start | bytes 3538952 | tf_op jit(solution)/shard_map/ppermute | solution.py:363
  39.7 15.6 %collective-permute-start.10 = (bf16[128,2176]{1,0:T(8,128)(2,1)S(1)}, bf16[128,2176]{1,0:T(8,128)(2,1)S(1)}, u32[]{:S(2)}, u32[]{:S(2)}) collective-permute-start(bf16[128,2176]{1,0:T(8,128)(2,1)S(1)} %broadcast_select_fusion.1.refs_2_.refs_8_.refs_6_), channel_id=1, source_target_pairs={{0,2},{1,3},{2,0},{3,1},{4,6},{5,7},{6,4},{7,5},{8,10},{9,11},{10,... | collective-permute-start | bytes 1671176 | tf_op jit(solution)/shard_map/ppermute | solution.py:363
  41.1 14.1 %collective-permute-start.9 = (bf16[128,2176]{1,0:T(8,128)(2,1)S(1)}, bf16[128,2176]{1,0:T(8,128)(2,1)S(1)}, u32[]{:S(2)}, u32[]{:S(2)}) collective-permute-start(bf16[128,2176]{1,0:T(8,128)(2,1)S(1)} %collective-permute-done.6), channel_id=1, source_target_pairs={{4,0},{5,1},{6,2},{7,3},{8,12},{9,13},{10,14},{11,15},{20,16},{21,... | collective-permute-start | bytes 1671176 | tf_op jit(solution)/shard_map/ppermute | solution.py:363
  55.3 11.3 %collective-permute-start.11 = (bf16[128,2176]{1,0:T(8,128)(2,1)S(1)}, bf16[128,2176]{1,0:T(8,128)(2,1)S(1)}, u32[]{:S(2)}, u32[]{:S(2)}) collective-permute-start(bf16[128,2176]{1,0:T(8,128)(2,1)S(1)} %broadcast_select_fusion.refs_0_.refs_9_.refs_5_), channel_id=1, source_target_pairs={{0,2},{1,3},{2,0},{3,1},{4,6},{5,7},{6,4},{7,5},{8,10},{9,11},{10,... | collective-permute-start | bytes 1671176 | tf_op jit(solution)/shard_map/ppermute | solution.py:363
  56.3 11.5 %copy-start.15 = (bf16[128,1024]{1,0:T(8,128)(2,1)S(1)}, bf16[128,1024]{1,0:T(8,128)(2,1)}, u32[]{:S(2)}) copy-start(bf16[128,1024]{1,0:T(8,128)(2,1)} %get-tuple-element.68) | copy-start | bytes 786436
  66.6 3.9 %collective-permute-start.13 = (bf16[512,1152]{1,0:T(8,128)(2,1)}, bf16[512,1152]{1,0:T(8,128)(2,1)S(1)}, u32[]{:S(2)}, u32[]{:S(2)}) collective-permute-start(bf16[512,1152]{1,0:T(8,128)(2,1)} %get-tuple-element.61), channel_id=1, source_target_pairs={{0,1},{1,0},{2,3},{3,2},{4,5},{5,4},{6,7},{7,6},{8,9},{9,8},{10,11... | collective-permute-start | bytes 3538952 | tf_op jit(solution)/shard_map/ppermute | solution.py:363
  66.6 3.3 %collective-permute-start.12 = (bf16[128,2176]{1,0:T(8,128)(2,1)S(1)}, bf16[128,2176]{1,0:T(8,128)(2,1)S(1)}, u32[]{:S(2)}, u32[]{:S(2)}) collective-permute-start(bf16[128,2176]{1,0:T(8,128)(2,1)S(1)} %collective-permute-done.11.refs_0_.refs_7_), channel_id=1, source_target_pairs={{0,1},{1,0},{2,3},{3,2},{4,5},{5,4},{6,7},{7,6},{8,9},{9,8},{10,11... | collective-permute-start | bytes 1671176 | tf_op jit(solution)/shard_map/ppermute | solution.py:363
  67.1 12.0 %collective-permute-start.15 = (bf16[128,1024]{1,0:T(8,128)(2,1)}, bf16[128,1024]{1,0:T(8,128)(2,1)S(1)}, u32[]{:S(2)}, u32[]{:S(2)}) collective-permute-start(bf16[128,1024]{1,0:T(8,128)(2,1)} %get-tuple-element.66), channel_id=1, source_target_pairs={{0,2},{1,3},{2,0},{3,1},{4,6},{5,7},{6,4},{7,5},{8,10},{9,11},{10,... | collective-permute-start | bytes 786440 | tf_op jit(solution)/shard_map/ppermute | solution.py:363
  67.8 13.4 %collective-permute-start.16 = (bf16[128,1024]{1,0:T(8,128)(2,1)S(1)}, bf16[128,1024]{1,0:T(8,128)(2,1)S(1)}, u32[]{:S(2)}, u32[]{:S(2)}) collective-permute-start(bf16[128,1024]{1,0:T(8,128)(2,1)S(1)} %copy-done.15), channel_id=1, source_target_pairs={{0,2},{1,3},{2,0},{3,1},{4,6},{5,7},{6,4},{7,5},{8,10},{9,11},{10,... | collective-permute-start | bytes 786440 | tf_op jit(solution)/shard_map/ppermute | solution.py:363
  69.9 11.3 %collective-permute-start.17 = (bf16[512,1152]{1,0:T(8,128)(2,1)}, bf16[512,1152]{1,0:T(8,128)(2,1)S(1)}, u32[]{:S(2)}, u32[]{:S(2)}) collective-permute-start(bf16[512,1152]{1,0:T(8,128)(2,1)} %get-tuple-element.70), channel_id=1, source_target_pairs={{0,1},{1,0},{2,3},{3,2},{4,5},{5,4},{6,7},{7,6},{8,9},{9,8},{10,11... | collective-permute-start | bytes 3538952 | tf_op jit(solution)/shard_map/ppermute | solution.py:363
  71.5 13.8 %copy-start.10 = (bf16[128,1024]{1,0:T(8,128)(2,1)S(1)}, bf16[128,1024]{1,0:T(8,128)(2,1)}, u32[]{:S(2)}) copy-start(bf16[128,1024]{1,0:T(8,128)(2,1)} %get-tuple-element.81) | copy-start | bytes 786436
  79.2 13.3 %copy-start.11 = (bf16[128,1024]{1,0:T(8,128)(2,1)S(1)}, bf16[128,1024]{1,0:T(8,128)(2,1)}, u32[]{:S(2)}) copy-start(bf16[128,1024]{1,0:T(8,128)(2,1)} %get-tuple-element.63) | copy-start | bytes 786436
  81.2 1.7 %collective-permute-start.18 = (bf16[128,1024]{1,0:T(8,128)(2,1)}, bf16[128,1024]{1,0:T(8,128)(2,1)S(1)}, u32[]{:S(2)}, u32[]{:S(2)}) collective-permute-start(bf16[128,1024]{1,0:T(8,128)(2,1)} %get-tuple-element.71), channel_id=1, source_target_pairs={{0,1},{1,0},{2,3},{3,2},{4,5},{5,4},{6,7},{7,6},{8,9},{9,8},{10,11... | collective-permute-start | bytes 786440 | tf_op jit(solution)/shard_map/ppermute | solution.py:363
  82.9 14.9 %copy-start.9 = (bf16[128,1024]{1,0:T(8,128)(2,1)S(1)}, bf16[128,1024]{1,0:T(8,128)(2,1)}, u32[]{:S(2)}) copy-start(bf16[128,1024]{1,0:T(8,128)(2,1)} %get-tuple-element.76) | copy-start | bytes 786436
  84.0 8.4 %collective-permute-start.19 = (bf16[128,1024]{1,0:T(8,128)(2,1)S(1)}, bf16[128,1024]{1,0:T(8,128)(2,1)S(1)}, u32[]{:S(2)}, u32[]{:S(2)}) collective-permute-start(bf16[128,1024]{1,0:T(8,128)(2,1)S(1)} %add_convert_fusion.6), channel_id=1, source_target_pairs={{0,2},{1,3},{2,0},{3,1},{4,6},{5,7},{6,4},{7,5},{8,10},{9,11},{10,... | collective-permute-start | bytes 786440 | tf_op jit(solution)/shard_map/ppermute | solution.py:363
  84.8 29.0 %collective-permute-start.14 = (bf16[512,1152]{1,0:T(8,128)(2,1)}, bf16[512,1152]{1,0:T(8,128)(2,1)S(1)}, u32[]{:S(2)}, u32[]{:S(2)}) collective-permute-start(bf16[512,1152]{1,0:T(8,128)(2,1)} %get-tuple-element.62), channel_id=1, source_target_pairs={{0,16},{16,0},{1,17},{17,1},{2,18},{18,2},{3,19},{19,3},{4,20},{20... | collective-permute-start | bytes 3538952 | tf_op jit(solution)/shard_map/ppermute | solution.py:364
  85.4 12.6 %collective-permute-start.23 = (bf16[128,1024]{1,0:T(8,128)(2,1)S(1)}, bf16[128,1024]{1,0:T(8,128)(2,1)S(1)}, u32[]{:S(2)}, u32[]{:S(2)}) collective-permute-start(bf16[128,1024]{1,0:T(8,128)(2,1)S(1)} %add_convert_fusion.2), channel_id=1, source_target_pairs={{0,4},{1,5},{2,6},{3,7},{12,8},{13,9},{14,10},{15,11},{16,20},{17,... | collective-permute-start | bytes 786440 | tf_op jit(solution)/shard_map/ppermute | solution.py:363
  92.5 10.3 %collective-permute-start.20 = (bf16[128,1024]{1,0:T(8,128)(2,1)S(1)}, bf16[128,1024]{1,0:T(8,128)(2,1)S(1)}, u32[]{:S(2)}, u32[]{:S(2)}) collective-permute-start(bf16[128,1024]{1,0:T(8,128)(2,1)S(1)} %add_convert_fusion.5), channel_id=1, source_target_pairs={{0,4},{1,5},{2,6},{3,7},{12,8},{13,9},{14,10},{15,11},{16,20},{17,... | collective-permute-start | bytes 786440 | tf_op jit(solution)/shard_map/ppermute | solution.py:363
  98.0 19.5 %collective-permute-start.24 = (bf16[128,1024]{1,0:T(8,128)(2,1)S(1)}, bf16[128,1024]{1,0:T(8,128)(2,1)S(1)}, u32[]{:S(2)}, u32[]{:S(2)}) collective-permute-start(bf16[128,1024]{1,0:T(8,128)(2,1)S(1)} %add_convert_fusion.1), channel_id=1, source_target_pairs={{4,8},{5,9},{6,10},{7,11},{8,4},{9,5},{10,6},{11,7},{20,24},{21,25... | collective-permute-start | bytes 786440 | tf_op jit(solution)/shard_map/ppermute | solution.py:363
  98.7 18.8 %collective-permute-start.21 = (bf16[128,1024]{1,0:T(8,128)(2,1)S(1)}, bf16[128,1024]{1,0:T(8,128)(2,1)S(1)}, u32[]{:S(2)}, u32[]{:S(2)}) collective-permute-start(bf16[128,1024]{1,0:T(8,128)(2,1)S(1)} %copy-done.14), channel_id=1, source_target_pairs={{0,2},{1,3},{2,0},{3,1},{4,6},{5,7},{6,4},{7,5},{8,10},{9,11},{10,... | collective-permute-start | bytes 786440 | tf_op jit(solution)/shard_map/ppermute | solution.py:363
  102.9 15.8 %collective-permute-start.25 = (bf16[128,1024]{1,0:T(8,128)(2,1)S(1)}, bf16[128,1024]{1,0:T(8,128)(2,1)S(1)}, u32[]{:S(2)}, u32[]{:S(2)}) collective-permute-start(bf16[128,1024]{1,0:T(8,128)(2,1)S(1)} %add_convert_fusion.4), channel_id=1, source_target_pairs={{4,12},{5,13},{6,14},{7,15},{8,0},{9,1},{10,2},{11,3},{20,28},{21,... | collective-permute-start | bytes 786440 | tf_op jit(solution)/shard_map/ppermute | solution.py:363
  110.0 8.7 %collective-permute-start.22 = (bf16[128,1024]{1,0:T(8,128)(2,1)S(1)}, bf16[128,1024]{1,0:T(8,128)(2,1)S(1)}, u32[]{:S(2)}, u32[]{:S(2)}) collective-permute-start(bf16[128,1024]{1,0:T(8,128)(2,1)S(1)} %add_convert_fusion.3), channel_id=1, source_target_pairs={{0,4},{1,5},{2,6},{3,7},{4,0},{5,1},{6,2},{7,3},{8,12},{9,13},{10,... | collective-permute-start | bytes 786440 | tf_op jit(solution)/shard_map/ppermute | solution.py:363
  (10 other events, 37.8 us)

commit v16 on v15

--- a/solution.py
+++ b/solution.py
@@ -392,7 +392,6 @@
     cy3 = swap(y3)
     got_other, got_mine = swap(after(to_other, y3)), swap(after(to_mine, y3, cy3))
     r2 = move(after(q2, y3), SWAP_Y)
-    r1 = move(after(q1, y3), SWAP_Y)
 
     blocks = early + [b3, y2]
     kept = [kept_a[:2], kept_b[:2]]
@@ -401,8 +400,8 @@
     )
     from_part = across(send)
     add = lambda *terms: sum(t.astype(F32) for t in terms).astype(BF16)
-    r3 = move(add(last, swap(after(pair, r2, r1, got_mine))), SWAP_Y)
-    r0 = move(after(q0, r3), SWAP_Y)
+    r3 = move(add(last, swap(after(pair, r2, got_mine))), SWAP_Y)
+    r1, r0 = (move(after(q, r3), SWAP_Y) for q in (q1, q0))
     s2 = add(p2, r2)
     s2 = add(s2, move(s2, INWARD))
     s3 = add(p3, r3)

time: 120 us -> 118 us (0.983)
  waiting for transfers between devices: 37 us -> 35.7 us
    ppermute x24, waiting for transfers between devices: 37 us -> 35.7 us  [dense_body(): move = lambda a, pairs: lax.ppermute(a, 'expert', pairs)]
  transfers between devices with their start and end apart: 26 -> 26, of which waited for: 13 -> 12; matrix products, arithmetic and copies ran while one was open for 4% -> 4% of each run, Pallas kernels for 29% -> 29%
where the time goes in v16:
time: 118 us
  Pallas kernels  37.3 us (32%)
  waiting for transfers between devices  35.7 us (30%)
  starting transfers between devices  35.5 us (30%)
  other arithmetic  5.7 us (5%)
  local copies, waits for them, and re-layouts  2.52 us (2%)
    ppermute x24, waiting for transfers between devices, dense_body(): move = lambda a, pairs: lax.ppermute(a, 'expert', pairs)  35.7 us
    ppermute x24, starting transfers between devices, dense_body(): move = lambda a, pairs: lax.ppermute(a, 'expert', pairs)  31.9 us
    pallas_call x3, Pallas kernels, rows_call(): pl.pallas_call(functools.partial(rows_kernel, experts, count, sizes, whic...  28.8 us
    pallas_call x1, Pallas kernels, half_call(): pl.pallas_call(functools.partial(half_kernel, len(blocks), len(kept)), ou...  5.81 us
    ppermute x2, starting transfers between devices, dense_body(): across = lambda a: lax.ppermute(a, 'dp', [(0, 1), (1, 0)])  3.53 us
    pallas_call x1, Pallas kernels, pack(): pl.pallas_call(functools.partial(pack_kernel, experts), out_shape=[jax.Sh...  2.73 us
    broadcast_in_dim x1, other arithmetic, dense_body(): return (d_tokens, d_gate[None], d_up[None], d_down[None])  2.61 us
    unnamed x33, local copies, waits for them, and re-layouts  2.52 us
  transfers between devices with their start and end apart: 26, of which 12 were waited for; matrix products, arithmetic and copies ran while one was open for 4% of the time, Pallas kernels for 29%

profile of v16, /device:TPU:0, one launch (start us, length us, event | category | flops | bytes accessed | tf_op | source)
XLA Modules:
  0.0 117.7 jit_solution(2334241278395177132)
XLA Ops:
  0.6 2.7 %shard_map.102 = (bf16[128,2176]{1,0:T(8,128)(2,1)}, bf16[512,1152]{1,0:T(8,128)(2,1)}) custom-call(bf16[128,1024]{1,0:T(8,128)(2,1)} %tokens.1, bf16[128,1024]{1,0:T(8,128)(2,1)} %d_output.1, f32[8,128]{1,0:T(8,128)} %bitcast.18, s32[8,128]{1,0:T(8,128)} %bitcast.19, bf16[512,384]{1,0:T(8,128)(2,1)} %bitcast.15, bf16[512,384]{1,0:T(8,128)(2,1)} %bitcast.16, ...), custom_call_target="tpu_custom_call" | custom-call | bytes 1048576 | tf_op jit(solution)/shard_map/pallas_call | solution.py:79
  3.4 3.0 %collective-permute-start.5 = (bf16[512,1152]{1,0:T(8,128)(2,1)}, bf16[512,1152]{1,0:T(8,128)(2,1)}, u32[]{:S(2)}, u32[]{:S(2)}) collective-permute-start(bf16[512,1152]{1,0:T(8,128)(2,1)} %get-tuple-element.46.refs_5_.refs_2_), channel_id=1, source_target_pairs={{0,16},{16,0},{1,17},{17,1},{2,18},{18,2},{3,19},{19,3},{4,20},{20... | collective-permute-start | bytes 3538952 | tf_op jit(solution)/shard_map/ppermute | solution.py:364
  6.4 1.5 %collective-permute-start.3 = (bf16[128,2176]{1,0:T(8,128)(2,1)}, bf16[128,2176]{1,0:T(8,128)(2,1)S(1)}, u32[]{:S(2)}, u32[]{:S(2)}) collective-permute-start(bf16[128,2176]{1,0:T(8,128)(2,1)} %get-tuple-element.43.refs_0_.refs_6_.refs_4_), channel_id=1, source_target_pairs={{0,2},{1,3},{2,0},{3,1},{4,6},{5,7},{6,4},{7,5},{8,10},{9,11},{10,... | collective-permute-start | bytes 1671176 | tf_op jit(solution)/shard_map/ppermute | solution.py:363
  7.9 1.6 %collective-permute-start = (bf16[128,2176]{1,0:T(8,128)(2,1)}, bf16[128,2176]{1,0:T(8,128)(2,1)S(1)}, u32[]{:S(2)}, u32[]{:S(2)}) collective-permute-start(bf16[128,2176]{1,0:T(8,128)(2,1)} %get-tuple-element.43.refs_0_.refs_6_.refs_4_), channel_id=1, source_target_pairs={{0,4},{1,5},{2,6},{3,7},{4,0},{5,1},{6,2},{7,3},{8,12},{9,13},{10,... | collective-permute-start | bytes 1671176 | tf_op jit(solution)/shard_map/ppermute | solution.py:363
  10.2 10.5 %collective-permute-done.3.refs_3_.refs_9_.refs_7_ = bf16[128,2176]{1,0:T(8,128)(2,1)S(1)} collective-permute-done((bf16[128,2176]{1,0:T(8,128)(2,1)}, bf16[128,2176]{1,0:T(8,128)(2,1)S(1)}, u32[]{:S(2)}, u32[]{:S(2)}) %collective-permute-start.3) | collective-permute-done | bytes 557088 | tf_op jit(solution)/shard_map/ppermute | solution.py:363
  20.7 1.2 %collective-permute-done.refs_1_.refs_7_.refs_5_ = bf16[128,2176]{1,0:T(8,128)(2,1)S(1)} collective-permute-done((bf16[128,2176]{1,0:T(8,128)(2,1)}, bf16[128,2176]{1,0:T(8,128)(2,1)S(1)}, u32[]{:S(2)}, u32[]{:S(2)}) %collective-permute-start) | collective-permute-done | bytes 557088 | tf_op jit(solution)/shard_map/ppermute | solution.py:363
  23.1 1.3 %collective-permute-start.2 = (bf16[128,2176]{1,0:T(8,128)(2,1)S(1)}, bf16[128,2176]{1,0:T(8,128)(2,1)S(1)}, u32[]{:S(2)}, u32[]{:S(2)}) collective-permute-start(bf16[128,2176]{1,0:T(8,128)(2,1)S(1)} %collective-permute-done.1), channel_id=1, source_target_pairs={{4,0},{5,1},{6,2},{7,3},{8,12},{9,13},{10,14},{11,15},{20,16},{21,... | collective-permute-start | bytes 1671176 | tf_op jit(solution)/shard_map/ppermute | solution.py:363
  24.4 10.5 %collective-permute-done.4.refs_4_.refs_10_.refs_8_ = bf16[128,2176]{1,0:T(8,128)(2,1)S(1)} collective-permute-done((bf16[128,2176]{1,0:T(8,128)(2,1)S(1)}, bf16[128,2176]{1,0:T(8,128)(2,1)S(1)}, u32[]{:S(2)}, u32[]{:S(2)}) %collective-permute-start.4) | collective-permute-done | bytes 557088 | tf_op jit(solution)/shard_map/ppermute | solution.py:363
  36.1 3.5 %collective-permute-done.2 = bf16[128,2176]{1,0:T(8,128)(2,1)S(1)} collective-permute-done((bf16[128,2176]{1,0:T(8,128)(2,1)S(1)}, bf16[128,2176]{1,0:T(8,128)(2,1)S(1)}, u32[]{:S(2)}, u32[]{:S(2)}) %collective-permute-start.2) | collective-permute-done | bytes 557088 | tf_op jit(solution)/shard_map/ppermute | solution.py:363
  39.7 1.4 %collective-permute-start.10 = (bf16[128,2176]{1,0:T(8,128)(2,1)S(1)}, bf16[128,2176]{1,0:T(8,128)(2,1)S(1)}, u32[]{:S(2)}, u32[]{:S(2)}) collective-permute-start(bf16[128,2176]{1,0:T(8,128)(2,1)S(1)} %broadcast_select_fusion.1.refs_2_.refs_8_.refs_6_), channel_id=1, source_target_pairs={{0,2},{1,3},{2,0},{3,1},{4,6},{5,7},{6,4},{7,5},{8,10},{9,11},{10,... | collective-permute-start | bytes 1671176 | tf_op jit(solution)/shard_map/ppermute | solution.py:363
  41.1 1.3 %collective-permute-start.9 = (bf16[128,2176]{1,0:T(8,128)(2,1)S(1)}, bf16[128,2176]{1,0:T(8,128)(2,1)S(1)}, u32[]{:S(2)}, u32[]{:S(2)}) collective-permute-start(bf16[128,2176]{1,0:T(8,128)(2,1)S(1)} %collective-permute-done.6), channel_id=1, source_target_pairs={{4,0},{5,1},{6,2},{7,3},{8,12},{9,13},{10,14},{11,15},{20,16},{21,... | collective-permute-start | bytes 1671176 | tf_op jit(solution)/shard_map/ppermute | solution.py:363
  42.5 11.6 %shard_map.103 = (bf16[128,1024]{1,0:T(8,128)(2,1)}, bf16[128,1024]{1,0:T(8,128)(2,1)}, bf16[128,1024]{1,0:T(8,128)(2,1)}, bf16[128,1024]{1,0:T(8,128)(2,1)}, bf...) custom-call(s32[2]{0:T(128)} %pad_add_fusion.scal, ...), custom_call_target="tpu_custom_call" | custom-call | flops 18119393280 | bytes 1048576 | tf_op jit(solution)/shard_map/pallas_call | solution.py:243
  54.1 1.1 collective-permute-done.9
  56.3 9.5 %shard_map.104 = (bf16[128,1024]{1,0:T(8,128)(2,1)}, bf16[128,1024]{1,0:T(8,128)(2,1)}, bf16[256,1152]{1,0:T(8,128)(2,1)}, bf16[256,1024]{1,0:T(8,128)(2,1)}, bf...) custom-call(s32[2]{0:T(128)} %pad_add_fusion.scal, ...), custom_call_target="tpu_custom_call" | custom-call | flops 7247757312 | bytes 1048576 | tf_op jit(solution)/shard_map/pallas_call | solution.py:243
  65.9 0.8 collective-permute-done.11.refs_0_.refs_7_
  67.8 2.1 %collective-permute-done.12.refs_1_.refs_8_ = bf16[128,2176]{1,0:T(8,128)(2,1)S(1)} collective-permute-done((bf16[128,2176]{1,0:T(8,128)(2,1)S(1)}, bf16[128,2176]{1,0:T(8,128)(2,1)S(1)}, u32[]{:S(2)}, u32[]{:S(2)}) %collective-permute-start.12) | collective-permute-done | bytes 557088 | tf_op jit(solution)/shard_map/ppermute | solution.py:363
  70.7 0.8 copy-done.13
  71.5 7.6 %shard_map.105 = (bf16[128,1024]{1,0:T(8,128)(2,1)}, bf16[128,1024]{1,0:T(8,128)(2,1)}, bf16[256,1152]{1,0:T(8,128)(2,1)}, bf16[256,1024]{1,0:T(8,128)(2,1)}, bf16[512,1152]{1,0:T(8,128)(2,1)}) custom-call(s32[2]{0:T(128)} %pad_add_fusion.scal, bf16[128,2176]{1,0:T(8,128)(2,1)} %copy-done.7, bf16[128,2176]{1,0:T(8,128)(2,1)} %copy-done.8, ...), custom_call_target="tpu_custom_call" | custom-call | flops 36238786560 | bytes 1048576 | tf_op jit(solution)/shard_map/pallas_call | solution.py:243
  79.4 1.6 %collective-permute-done.17 = bf16[128,1024]{1,0:T(8,128)(2,1)S(1)} collective-permute-done((bf16[128,1024]{1,0:T(8,128)(2,1)}, bf16[128,1024]{1,0:T(8,128)(2,1)S(1)}, u32[]{:S(2)}, u32[]{:S(2)}) %collective-permute-start.17) | collective-permute-done | bytes 262176 | tf_op jit(solution)/shard_map/ppermute | solution.py:363
  81.0 1.1 add_convert_fusion.6
  83.4 6.1 %collective-permute-start.23 = (bf16[128,1024]{1,0:T(8,128)(2,1)S(1)}, bf16[128,1024]{1,0:T(8,128)(2,1)S(1)}, u32[]{:S(2)}, u32[]{:S(2)}) collective-permute-start(bf16[128,1024]{1,0:T(8,128)(2,1)S(1)} %add_convert_fusion.2), channel_id=1, source_target_pairs={{0,4},{1,5},{2,6},{3,7},{12,8},{13,9},{14,10},{15,11},{16,20},{17,... | collective-permute-start | bytes 786440 | tf_op jit(solution)/shard_map/ppermute | solution.py:363
  89.5 1.0 collective-permute-done.18
  90.6 5.3 %collective-permute-start.19 = (bf16[128,1024]{1,0:T(8,128)(2,1)S(1)}, bf16[128,1024]{1,0:T(8,128)(2,1)S(1)}, u32[]{:S(2)}, u32[]{:S(2)}) collective-permute-start(bf16[128,1024]{1,0:T(8,128)(2,1)S(1)} %add_convert_fusion.5), channel_id=1, source_target_pairs={{0,4},{1,5},{2,6},{3,7},{12,8},{13,9},{14,10},{15,11},{16,20},{17,... | collective-permute-start | bytes 786440 | tf_op jit(solution)/shard_map/ppermute | solution.py:363
  96.0 1.4 %collective-permute-start.21 = (bf16[128,1024]{1,0:T(8,128)(2,1)S(1)}, bf16[128,1024]{1,0:T(8,128)(2,1)S(1)}, u32[]{:S(2)}, u32[]{:S(2)}) collective-permute-start(bf16[128,1024]{1,0:T(8,128)(2,1)S(1)} %copy-done.15), channel_id=1, source_target_pairs={{0,2},{1,3},{2,0},{3,1},{4,6},{5,7},{6,4},{7,5},{8,10},{9,11},{10,... | collective-permute-start | bytes 786440 | tf_op jit(solution)/shard_map/ppermute | solution.py:363
  98.9 2.1 %collective-permute-done.19 = bf16[128,1024]{1,0:T(8,128)(2,1)S(1)} collective-permute-done((bf16[128,1024]{1,0:T(8,128)(2,1)S(1)}, bf16[128,1024]{1,0:T(8,128)(2,1)S(1)}, u32[]{:S(2)}, u32[]{:S(2)}) %collective-permute-start.19) | collective-permute-done | bytes 262176 | tf_op jit(solution)/shard_map/ppermute | solution.py:363
  101.0 1.3 %collective-permute-start.25 = (bf16[128,1024]{1,0:T(8,128)(2,1)S(1)}, bf16[128,1024]{1,0:T(8,128)(2,1)S(1)}, u32[]{:S(2)}, u32[]{:S(2)}) collective-permute-start(bf16[128,1024]{1,0:T(8,128)(2,1)S(1)} %add_convert_fusion.4), channel_id=1, source_target_pairs={{4,12},{5,13},{6,14},{7,15},{8,0},{9,1},{10,2},{11,3},{20,28},{21,... | collective-permute-start | bytes 786440 | tf_op jit(solution)/shard_map/ppermute | solution.py:363
  102.3 5.8 %shard_map.106 = bf16[512,1152]{1,0:T(8,128)(2,1)} custom-call(s32[1]{0:T(128)} %bitcast.sides, bf16[128,2176]{1,0:T(8,128)(2,1)} %get-tuple-element.43.refs_0_.refs_6_.refs_4_, bf16[128,2176]{1,0:T(8,128)(2,1)} %copy-done.4, bf16[128,2176]{1,0:T(8,128)(2,1)} %copy-done, bf16[128,2176]{1,0:T(8,128)(2,1)} %copy-done.3, bf16[128,2176]{1,0:T(8,128)(2,1)} %copy-done.5, ...), custom_call_target="tpu_custom_call" | custom-call | flops 1024 | bytes 1024 | tf_op jit(solution)/shard_map/pallas_call | solution.py:304
  108.2 3.7 %collective-permute-start.22 = (bf16[128,1024]{1,0:T(8,128)(2,1)S(1)}, bf16[128,1024]{1,0:T(8,128)(2,1)S(1)}, u32[]{:S(2)}, u32[]{:S(2)}) collective-permute-start(bf16[128,1024]{1,0:T(8,128)(2,1)S(1)} %add_convert_fusion.3), channel_id=1, source_target_pairs={{0,4},{1,5},{2,6},{3,7},{4,0},{5,1},{6,2},{7,3},{8,12},{9,13},{10,... | collective-permute-start | bytes 786440 | tf_op jit(solution)/shard_map/ppermute | solution.py:363
  112.0 2.6 %add_bitcast_fusion = (f32[1,384,512]{1,2,0:T(8,128)S(1)}, f32[1,512,384]{2,1,0:T(8,128)}, f32[1,512,384]{2,1,0:T(8,128)}) fusion(bf16[512,1152]{1,0:T(8,128)(2,1)} %shard_map.106, bf16[512,1152]{1,0:T(8,128)(2,1)S(1)} %collective-permute-done.14), kind=kLoop, calls=%fused_computation | loop fusion | flops 1769472 | bytes 4718592 | tf_op jit(solution)/shard_map/broadcast_in_dim | solution.py:417
  114.6 1.1 copy.11
  115.7 1.0 collective-permute-done.22
  116.8 0.9 add_convert_fusion
  (69 shorter events, 9.4 us)
Async XLA Ops:
  3.4 31.5 %collective-permute-start.5 = (bf16[512,1152]{1,0:T(8,128)(2,1)}, bf16[512,1152]{1,0:T(8,128)(2,1)}, u32[]{:S(2)}, u32[]{:S(2)}) collective-permute-start(bf16[512,1152]{1,0:T(8,128)(2,1)} %get-tuple-element.46.refs_5_.refs_2_), channel_id=1, source_target_pairs={{0,16},{16,0},{1,17},{17,1},{2,18},{18,2},{3,19},{19,3},{4,20},{20... | collective-permute-start | bytes 3538952 | tf_op jit(solution)/shard_map/ppermute | solution.py:364
  6.4 14.3 %collective-permute-start.3 = (bf16[128,2176]{1,0:T(8,128)(2,1)}, bf16[128,2176]{1,0:T(8,128)(2,1)S(1)}, u32[]{:S(2)}, u32[]{:S(2)}) collective-permute-start(bf16[128,2176]{1,0:T(8,128)(2,1)} %get-tuple-element.43.refs_0_.refs_6_.refs_4_), channel_id=1, source_target_pairs={{0,2},{1,3},{2,0},{3,1},{4,6},{5,7},{6,4},{7,5},{8,10},{9,11},{10,... | collective-permute-start | bytes 1671176 | tf_op jit(solution)/shard_map/ppermute | solution.py:363
  7.9 14.0 %collective-permute-start = (bf16[128,2176]{1,0:T(8,128)(2,1)}, bf16[128,2176]{1,0:T(8,128)(2,1)S(1)}, u32[]{:S(2)}, u32[]{:S(2)}) collective-permute-start(bf16[128,2176]{1,0:T(8,128)(2,1)} %get-tuple-element.43.refs_0_.refs_6_.refs_4_), channel_id=1, source_target_pairs={{0,4},{1,5},{2,6},{3,7},{4,0},{5,1},{6,2},{7,3},{8,12},{9,13},{10,... | collective-permute-start | bytes 1671176 | tf_op jit(solution)/shard_map/ppermute | solution.py:363
  9.5 13.6 %collective-permute-start.1 = (bf16[128,2176]{1,0:T(8,128)(2,1)}, bf16[128,2176]{1,0:T(8,128)(2,1)S(1)}, u32[]{:S(2)}, u32[]{:S(2)}) collective-permute-start(bf16[128,2176]{1,0:T(8,128)(2,1)} %get-tuple-element.43.refs_0_.refs_6_.refs_4_), channel_id=1, source_target_pairs={{4,8},{5,9},{6,10},{7,11},{8,4},{9,5},{10,6},{11,7},{20,24},{21,25... | collective-permute-start | bytes 1671176 | tf_op jit(solution)/shard_map/ppermute | solution.py:363
  20.7 21.7 %copy-start.3 = (bf16[128,2176]{1,0:T(8,128)(2,1)}, bf16[128,2176]{1,0:T(8,128)(2,1)S(1)}, u32[]{:S(2)}) copy-start(bf16[128,2176]{1,0:T(8,128)(2,1)S(1)} %collective-permute-done.3.refs_3_.refs_9_.refs_7_) | copy-start | bytes 1671172
  21.9 20.5 %copy-start.4 = (bf16[128,2176]{1,0:T(8,128)(2,1)}, bf16[128,2176]{1,0:T(8,128)(2,1)S(1)}, u32[]{:S(2)}) copy-start(bf16[128,2176]{1,0:T(8,128)(2,1)S(1)} %collective-permute-done.refs_1_.refs_7_.refs_5_) | copy-start | bytes 1671172
  21.9 13.0 %collective-permute-start.4 = (bf16[128,2176]{1,0:T(8,128)(2,1)S(1)}, bf16[128,2176]{1,0:T(8,128)(2,1)S(1)}, u32[]{:S(2)}, u32[]{:S(2)}) collective-permute-start(bf16[128,2176]{1,0:T(8,128)(2,1)S(1)} %collective-permute-done.refs_1_.refs_7_.refs_5_), channel_id=1, source_target_pairs={{0,2},{1,3},{2,0},{3,1},{4,6},{5,7},{6,4},{7,5},{8,10},{9,11},{10,... | collective-permute-start | bytes 1671176 | tf_op jit(solution)/shard_map/ppermute | solution.py:363
  22.4 12.5 %collective-permute-start.6 = (bf16[128,2176]{1,0:T(8,128)(2,1)S(1)}, bf16[128,2176]{1,0:T(8,128)(2,1)S(1)}, u32[]{:S(2)}, u32[]{:S(2)}) collective-permute-start(bf16[128,2176]{1,0:T(8,128)(2,1)S(1)} %collective-permute-done.refs_1_.refs_7_.refs_5_), channel_id=1, source_target_pairs={{4,8},{5,9},{6,10},{7,11},{8,4},{9,5},{10,6},{11,7},{20,24},{21,25... | collective-permute-start | bytes 1671176 | tf_op jit(solution)/shard_map/ppermute | solution.py:363
  23.1 16.5 %collective-permute-start.2 = (bf16[128,2176]{1,0:T(8,128)(2,1)S(1)}, bf16[128,2176]{1,0:T(8,128)(2,1)S(1)}, u32[]{:S(2)}, u32[]{:S(2)}) collective-permute-start(bf16[128,2176]{1,0:T(8,128)(2,1)S(1)} %collective-permute-done.1), channel_id=1, source_target_pairs={{4,0},{5,1},{6,2},{7,3},{8,12},{9,13},{10,14},{11,15},{20,16},{21,... | collective-permute-start | bytes 1671176 | tf_op jit(solution)/shard_map/ppermute | solution.py:363
  34.9 7.5 %collective-permute-start.7 = (bf16[512,1152]{1,0:T(8,128)(2,1)}, bf16[512,1152]{1,0:T(8,128)(2,1)}, u32[]{:S(2)}, u32[]{:S(2)}) collective-permute-start(bf16[512,1152]{1,0:T(8,128)(2,1)} %get-tuple-element.46.refs_5_.refs_2_), channel_id=1, source_target_pairs={{0,1},{1,0},{2,3},{3,2},{4,5},{5,4},{6,7},{7,6},{8,9},{9,8},{10,11... | collective-permute-start | bytes 3538952 | tf_op jit(solution)/shard_map/ppermute | solution.py:363
  34.9 7.5 %collective-permute-start.8 = (bf16[512,1152]{1,0:T(8,128)(2,1)}, bf16[512,1152]{1,0:T(8,128)(2,1)}, u32[]{:S(2)}, u32[]{:S(2)}) collective-permute-start(bf16[512,1152]{1,0:T(8,128)(2,1)} %collective-permute-done.5.refs_6_.refs_3_), channel_id=1, source_target_pairs={{0,1},{1,0},{2,3},{3,2},{4,5},{5,4},{6,7},{7,6},{8,9},{9,8},{10,11... | collective-permute-start | bytes 3538952 | tf_op jit(solution)/shard_map/ppermute | solution.py:363
  39.7 15.6 %collective-permute-start.10 = (bf16[128,2176]{1,0:T(8,128)(2,1)S(1)}, bf16[128,2176]{1,0:T(8,128)(2,1)S(1)}, u32[]{:S(2)}, u32[]{:S(2)}) collective-permute-start(bf16[128,2176]{1,0:T(8,128)(2,1)S(1)} %broadcast_select_fusion.1.refs_2_.refs_8_.refs_6_), channel_id=1, source_target_pairs={{0,2},{1,3},{2,0},{3,1},{4,6},{5,7},{6,4},{7,5},{8,10},{9,11},{10,... | collective-permute-start | bytes 1671176 | tf_op jit(solution)/shard_map/ppermute | solution.py:363
  41.1 14.1 %collective-permute-start.9 = (bf16[128,2176]{1,0:T(8,128)(2,1)S(1)}, bf16[128,2176]{1,0:T(8,128)(2,1)S(1)}, u32[]{:S(2)}, u32[]{:S(2)}) collective-permute-start(bf16[128,2176]{1,0:T(8,128)(2,1)S(1)} %collective-permute-done.6), channel_id=1, source_target_pairs={{4,0},{5,1},{6,2},{7,3},{8,12},{9,13},{10,14},{11,15},{20,16},{21,... | collective-permute-start | bytes 1671176 | tf_op jit(solution)/shard_map/ppermute | solution.py:363
  55.3 11.3 %collective-permute-start.11 = (bf16[128,2176]{1,0:T(8,128)(2,1)S(1)}, bf16[128,2176]{1,0:T(8,128)(2,1)S(1)}, u32[]{:S(2)}, u32[]{:S(2)}) collective-permute-start(bf16[128,2176]{1,0:T(8,128)(2,1)S(1)} %broadcast_select_fusion.refs_0_.refs_9_.refs_5_), channel_id=1, source_target_pairs={{0,2},{1,3},{2,0},{3,1},{4,6},{5,7},{6,4},{7,5},{8,10},{9,11},{10,... | collective-permute-start | bytes 1671176 | tf_op jit(solution)/shard_map/ppermute | solution.py:363
  66.6 3.9 %collective-permute-start.13 = (bf16[512,1152]{1,0:T(8,128)(2,1)}, bf16[512,1152]{1,0:T(8,128)(2,1)S(1)}, u32[]{:S(2)}, u32[]{:S(2)}) collective-permute-start(bf16[512,1152]{1,0:T(8,128)(2,1)} %get-tuple-element.61), channel_id=1, source_target_pairs={{0,1},{1,0},{2,3},{3,2},{4,5},{5,4},{6,7},{7,6},{8,9},{9,8},{10,11... | collective-permute-start | bytes 3538952 | tf_op jit(solution)/shard_map/ppermute | solution.py:363
  66.6 3.3 %collective-permute-start.12 = (bf16[128,2176]{1,0:T(8,128)(2,1)S(1)}, bf16[128,2176]{1,0:T(8,128)(2,1)S(1)}, u32[]{:S(2)}, u32[]{:S(2)}) collective-permute-start(bf16[128,2176]{1,0:T(8,128)(2,1)S(1)} %collective-permute-done.11.refs_0_.refs_7_), channel_id=1, source_target_pairs={{0,1},{1,0},{2,3},{3,2},{4,5},{5,4},{6,7},{7,6},{8,9},{9,8},{10,11... | collective-permute-start | bytes 1671176 | tf_op jit(solution)/shard_map/ppermute | solution.py:363
  67.1 12.0 %collective-permute-start.15 = (bf16[128,1024]{1,0:T(8,128)(2,1)}, bf16[128,1024]{1,0:T(8,128)(2,1)S(1)}, u32[]{:S(2)}, u32[]{:S(2)}) collective-permute-start(bf16[128,1024]{1,0:T(8,128)(2,1)} %get-tuple-element.66), channel_id=1, source_target_pairs={{0,2},{1,3},{2,0},{3,1},{4,6},{5,7},{6,4},{7,5},{8,10},{9,11},{10,... | collective-permute-start | bytes 786440 | tf_op jit(solution)/shard_map/ppermute | solution.py:363
  69.9 9.3 %collective-permute-start.16 = (bf16[512,1152]{1,0:T(8,128)(2,1)}, bf16[512,1152]{1,0:T(8,128)(2,1)S(1)}, u32[]{:S(2)}, u32[]{:S(2)}) collective-permute-start(bf16[512,1152]{1,0:T(8,128)(2,1)} %get-tuple-element.68), channel_id=1, source_target_pairs={{0,1},{1,0},{2,3},{3,2},{4,5},{5,4},{6,7},{7,6},{8,9},{9,8},{10,11... | collective-permute-start | bytes 3538952 | tf_op jit(solution)/shard_map/ppermute | solution.py:363
  71.5 11.8 %copy-start.10 = (bf16[128,1024]{1,0:T(8,128)(2,1)S(1)}, bf16[128,1024]{1,0:T(8,128)(2,1)}, u32[]{:S(2)}) copy-start(bf16[128,1024]{1,0:T(8,128)(2,1)} %get-tuple-element.81) | copy-start | bytes 786436
  79.2 11.4 %copy-start.2 = (bf16[512,1152]{1,0:T(8,128)(2,1)}, bf16[512,1152]{1,0:T(8,128)(2,1)S(1)}, u32[]{:S(2)}) copy-start(bf16[512,1152]{1,0:T(8,128)(2,1)S(1)} %collective-permute-done.16.refs_15_) | copy-start | bytes 3538948
  79.2 1.8 %collective-permute-start.17 = (bf16[128,1024]{1,0:T(8,128)(2,1)}, bf16[128,1024]{1,0:T(8,128)(2,1)S(1)}, u32[]{:S(2)}, u32[]{:S(2)}) collective-permute-start(bf16[128,1024]{1,0:T(8,128)(2,1)} %get-tuple-element.69), channel_id=1, source_target_pairs={{0,1},{1,0},{2,3},{3,2},{4,5},{5,4},{6,7},{7,6},{8,9},{9,8},{10,11... | collective-permute-start | bytes 786440 | tf_op jit(solution)/shard_map/ppermute | solution.py:363
  81.0 14.9 %copy-start.15 = (bf16[128,1024]{1,0:T(8,128)(2,1)S(1)}, bf16[128,1024]{1,0:T(8,128)(2,1)}, u32[]{:S(2)}) copy-start(bf16[128,1024]{1,0:T(8,128)(2,1)} %get-tuple-element.76) | copy-start | bytes 786436
  82.1 8.4 %collective-permute-start.18 = (bf16[128,1024]{1,0:T(8,128)(2,1)S(1)}, bf16[128,1024]{1,0:T(8,128)(2,1)S(1)}, u32[]{:S(2)}, u32[]{:S(2)}) collective-permute-start(bf16[128,1024]{1,0:T(8,128)(2,1)S(1)} %add_convert_fusion.6), channel_id=1, source_target_pairs={{0,2},{1,3},{2,0},{3,1},{4,6},{5,7},{6,4},{7,5},{8,10},{9,11},{10,... | collective-permute-start | bytes 786440 | tf_op jit(solution)/shard_map/ppermute | solution.py:363
  82.8 29.2 %collective-permute-start.14 = (bf16[512,1152]{1,0:T(8,128)(2,1)}, bf16[512,1152]{1,0:T(8,128)(2,1)S(1)}, u32[]{:S(2)}, u32[]{:S(2)}) collective-permute-start(bf16[512,1152]{1,0:T(8,128)(2,1)} %get-tuple-element.62), channel_id=1, source_target_pairs={{0,16},{16,0},{1,17},{17,1},{2,18},{18,2},{3,19},{19,3},{4,20},{20... | collective-permute-start | bytes 3538952 | tf_op jit(solution)/shard_map/ppermute | solution.py:364
  83.3 14.8 %copy-start.14 = (bf16[128,1024]{1,0:T(8,128)(2,1)S(1)}, bf16[128,1024]{1,0:T(8,128)(2,1)}, u32[]{:S(2)}) copy-start(bf16[128,1024]{1,0:T(8,128)(2,1)} %get-tuple-element.73) | copy-start | bytes 786436
  83.4 14.0 %collective-permute-start.23 = (bf16[128,1024]{1,0:T(8,128)(2,1)S(1)}, bf16[128,1024]{1,0:T(8,128)(2,1)S(1)}, u32[]{:S(2)}, u32[]{:S(2)}) collective-permute-start(bf16[128,1024]{1,0:T(8,128)(2,1)S(1)} %add_convert_fusion.2), channel_id=1, source_target_pairs={{0,4},{1,5},{2,6},{3,7},{12,8},{13,9},{14,10},{15,11},{16,20},{17,... | collective-permute-start | bytes 786440 | tf_op jit(solution)/shard_map/ppermute | solution.py:363
  90.6 10.4 %collective-permute-start.19 = (bf16[128,1024]{1,0:T(8,128)(2,1)S(1)}, bf16[128,1024]{1,0:T(8,128)(2,1)S(1)}, u32[]{:S(2)}, u32[]{:S(2)}) collective-permute-start(bf16[128,1024]{1,0:T(8,128)(2,1)S(1)} %add_convert_fusion.5), channel_id=1, source_target_pairs={{0,4},{1,5},{2,6},{3,7},{12,8},{13,9},{14,10},{15,11},{16,20},{17,... | collective-permute-start | bytes 786440 | tf_op jit(solution)/shard_map/ppermute | solution.py:363
  96.0 12.2 %collective-permute-start.21 = (bf16[128,1024]{1,0:T(8,128)(2,1)S(1)}, bf16[128,1024]{1,0:T(8,128)(2,1)S(1)}, u32[]{:S(2)}, u32[]{:S(2)}) collective-permute-start(bf16[128,1024]{1,0:T(8,128)(2,1)S(1)} %copy-done.15), channel_id=1, source_target_pairs={{0,2},{1,3},{2,0},{3,1},{4,6},{5,7},{6,4},{7,5},{8,10},{9,11},{10,... | collective-permute-start | bytes 786440 | tf_op jit(solution)/shard_map/ppermute | solution.py:363
  97.5 18.3 %collective-permute-start.24 = (bf16[128,1024]{1,0:T(8,128)(2,1)S(1)}, bf16[128,1024]{1,0:T(8,128)(2,1)S(1)}, u32[]{:S(2)}, u32[]{:S(2)}) collective-permute-start(bf16[128,1024]{1,0:T(8,128)(2,1)S(1)} %add_convert_fusion.1), channel_id=1, source_target_pairs={{4,8},{5,9},{6,10},{7,11},{8,4},{9,5},{10,6},{11,7},{20,24},{21,25... | collective-permute-start | bytes 786440 | tf_op jit(solution)/shard_map/ppermute | solution.py:363
  98.2 17.6 %collective-permute-start.20 = (bf16[128,1024]{1,0:T(8,128)(2,1)S(1)}, bf16[128,1024]{1,0:T(8,128)(2,1)S(1)}, u32[]{:S(2)}, u32[]{:S(2)}) collective-permute-start(bf16[128,1024]{1,0:T(8,128)(2,1)S(1)} %copy-done.14), channel_id=1, source_target_pairs={{0,2},{1,3},{2,0},{3,1},{4,6},{5,7},{6,4},{7,5},{8,10},{9,11},{10,... | collective-permute-start | bytes 786440 | tf_op jit(solution)/shard_map/ppermute | solution.py:363
  101.0 15.8 %collective-permute-start.25 = (bf16[128,1024]{1,0:T(8,128)(2,1)S(1)}, bf16[128,1024]{1,0:T(8,128)(2,1)S(1)}, u32[]{:S(2)}, u32[]{:S(2)}) collective-permute-start(bf16[128,1024]{1,0:T(8,128)(2,1)S(1)} %add_convert_fusion.4), channel_id=1, source_target_pairs={{4,12},{5,13},{6,14},{7,15},{8,0},{9,1},{10,2},{11,3},{20,28},{21,... | collective-permute-start | bytes 786440 | tf_op jit(solution)/shard_map/ppermute | solution.py:363
  108.2 8.5 %collective-permute-start.22 = (bf16[128,1024]{1,0:T(8,128)(2,1)S(1)}, bf16[128,1024]{1,0:T(8,128)(2,1)S(1)}, u32[]{:S(2)}, u32[]{:S(2)}) collective-permute-start(bf16[128,1024]{1,0:T(8,128)(2,1)S(1)} %add_convert_fusion.3), channel_id=1, source_target_pairs={{0,4},{1,5},{2,6},{3,7},{4,0},{5,1},{6,2},{7,3},{8,12},{9,13},{10,... | collective-permute-start | bytes 786440 | tf_op jit(solution)/shard_map/ppermute | solution.py:363
  (10 other events, 37.2 us)

commit v17 on v16

--- a/solution.py
+++ b/solution.py
@@ -401,14 +401,15 @@
     from_part = across(send)
     add = lambda *terms: sum(t.astype(F32) for t in terms).astype(BF16)
     r3 = move(add(last, swap(after(pair, r2, got_mine))), SWAP_Y)
-    r1, r0 = (move(after(q, r3), SWAP_Y) for q in (q1, q0))
+    r1 = move(after(q1, r3), SWAP_Y)
     s2 = add(p2, r2)
     s2 = add(s2, move(s2, INWARD))
     s3 = add(p3, r3)
     s3 = add(s3, move(s3, INWARD))
     keep = half_call(after(mine, send, s3), blocks + [y3, cy3], kept + [kept_c], more=got_mine)
 
-    s1 = after(add(p1, r1), keep)
+    s1 = add(p1, r1)
+    r0 = move(after(q0, keep), SWAP_Y)
     from_part = after(from_part, s3)
     hidden_units = gate_weight.shape[2]
     whole = lambda a: keep[:, a : a + hidden_units].astype(F32) + from_part[:, a : a + hidden_units].astype(F32)

time: 118 us -> 120 us (1.017)
  waiting for transfers between devices: 35.7 us -> 37.5 us
    ppermute x24, waiting for transfers between devices: 35.7 us -> 37.5 us  [dense_body(): move = lambda a, pairs: lax.ppermute(a, 'expert', pairs)]
  transfers between devices with their start and end apart: 26 -> 26, of which waited for: 12 -> 13; matrix products, arithmetic and copies ran while one was open for 4% -> 4% of each run, Pallas kernels for 29% -> 29%
where the time goes in v17:
time: 120 us; the launch traced here: 119 us
  waiting for transfers between devices  37.5 us (31%)
  Pallas kernels  37.3 us (31%)
  starting transfers between devices  35.3 us (29%)
  other arithmetic  5.7 us (5%)
  local copies, waits for them, and re-layouts  2.52 us (2%)
    ppermute x24, waiting for transfers between devices, dense_body(): move = lambda a, pairs: lax.ppermute(a, 'expert', pairs)  37.5 us
    ppermute x24, starting transfers between devices, dense_body(): move = lambda a, pairs: lax.ppermute(a, 'expert', pairs)  31.8 us
    pallas_call x3, Pallas kernels, rows_call(): pl.pallas_call(functools.partial(rows_kernel, experts, count, sizes, whic...  28.8 us
    pallas_call x1, Pallas kernels, half_call(): pl.pallas_call(functools.partial(half_kernel, len(blocks), len(kept)), ou...  5.8 us
    ppermute x2, starting transfers between devices, dense_body(): across = lambda a: lax.ppermute(a, 'dp', [(0, 1), (1, 0)])  3.53 us
    pallas_call x1, Pallas kernels, pack(): pl.pallas_call(functools.partial(pack_kernel, experts), out_shape=[jax.Sh...  2.73 us
    broadcast_in_dim x1, other arithmetic, dense_body(): return (d_tokens, d_gate[None], d_up[None], d_down[None])  2.61 us
    unnamed x33, local copies, waits for them, and re-layouts  2.52 us
  transfers between devices with their start and end apart: 26, of which 13 were waited for; matrix products, arithmetic and copies ran while one was open for 4% of the time, Pallas kernels for 29%

profile of v17, /device:TPU:0, one launch (start us, length us, event | category | flops | bytes accessed | tf_op | source)
XLA Modules:
  0.0 119.3 jit_solution(13566307708394314365)
XLA Ops:
  0.6 2.7 %shard_map.102 = (bf16[128,2176]{1,0:T(8,128)(2,1)}, bf16[512,1152]{1,0:T(8,128)(2,1)}) custom-call(bf16[128,1024]{1,0:T(8,128)(2,1)} %tokens.1, bf16[128,1024]{1,0:T(8,128)(2,1)} %d_output.1, f32[8,128]{1,0:T(8,128)} %bitcast.18, s32[8,128]{1,0:T(8,128)} %bitcast.19, bf16[512,384]{1,0:T(8,128)(2,1)} %bitcast.15, bf16[512,384]{1,0:T(8,128)(2,1)} %bitcast.16, ...), custom_call_target="tpu_custom_call" | custom-call | bytes 1048576 | tf_op jit(solution)/shard_map/pallas_call | solution.py:79
  3.4 3.0 %collective-permute-start.5 = (bf16[512,1152]{1,0:T(8,128)(2,1)}, bf16[512,1152]{1,0:T(8,128)(2,1)}, u32[]{:S(2)}, u32[]{:S(2)}) collective-permute-start(bf16[512,1152]{1,0:T(8,128)(2,1)} %get-tuple-element.45.refs_5_.refs_2_), channel_id=1, source_target_pairs={{0,16},{16,0},{1,17},{17,1},{2,18},{18,2},{3,19},{19,3},{4,20},{20... | collective-permute-start | bytes 3538952 | tf_op jit(solution)/shard_map/ppermute | solution.py:364
  6.4 1.5 %collective-permute-start.3 = (bf16[128,2176]{1,0:T(8,128)(2,1)}, bf16[128,2176]{1,0:T(8,128)(2,1)S(1)}, u32[]{:S(2)}, u32[]{:S(2)}) collective-permute-start(bf16[128,2176]{1,0:T(8,128)(2,1)} %get-tuple-element.42.refs_0_.refs_6_.refs_4_), channel_id=1, source_target_pairs={{0,2},{1,3},{2,0},{3,1},{4,6},{5,7},{6,4},{7,5},{8,10},{9,11},{10,... | collective-permute-start | bytes 1671176 | tf_op jit(solution)/shard_map/ppermute | solution.py:363
  7.9 1.6 %collective-permute-start = (bf16[128,2176]{1,0:T(8,128)(2,1)}, bf16[128,2176]{1,0:T(8,128)(2,1)S(1)}, u32[]{:S(2)}, u32[]{:S(2)}) collective-permute-start(bf16[128,2176]{1,0:T(8,128)(2,1)} %get-tuple-element.42.refs_0_.refs_6_.refs_4_), channel_id=1, source_target_pairs={{0,4},{1,5},{2,6},{3,7},{4,0},{5,1},{6,2},{7,3},{8,12},{9,13},{10,... | collective-permute-start | bytes 1671176 | tf_op jit(solution)/shard_map/ppermute | solution.py:363
  10.2 10.5 %collective-permute-done.3.refs_3_.refs_9_.refs_7_ = bf16[128,2176]{1,0:T(8,128)(2,1)S(1)} collective-permute-done((bf16[128,2176]{1,0:T(8,128)(2,1)}, bf16[128,2176]{1,0:T(8,128)(2,1)S(1)}, u32[]{:S(2)}, u32[]{:S(2)}) %collective-permute-start.3) | collective-permute-done | bytes 557088 | tf_op jit(solution)/shard_map/ppermute | solution.py:363
  20.7 1.2 %collective-permute-done.refs_1_.refs_7_.refs_5_ = bf16[128,2176]{1,0:T(8,128)(2,1)S(1)} collective-permute-done((bf16[128,2176]{1,0:T(8,128)(2,1)}, bf16[128,2176]{1,0:T(8,128)(2,1)S(1)}, u32[]{:S(2)}, u32[]{:S(2)}) %collective-permute-start) | collective-permute-done | bytes 557088 | tf_op jit(solution)/shard_map/ppermute | solution.py:363
  23.1 1.3 %collective-permute-start.2 = (bf16[128,2176]{1,0:T(8,128)(2,1)S(1)}, bf16[128,2176]{1,0:T(8,128)(2,1)S(1)}, u32[]{:S(2)}, u32[]{:S(2)}) collective-permute-start(bf16[128,2176]{1,0:T(8,128)(2,1)S(1)} %collective-permute-done.1), channel_id=1, source_target_pairs={{4,0},{5,1},{6,2},{7,3},{8,12},{9,13},{10,14},{11,15},{20,16},{21,... | collective-permute-start | bytes 1671176 | tf_op jit(solution)/shard_map/ppermute | solution.py:363
  24.4 10.5 %collective-permute-done.4.refs_4_.refs_10_.refs_8_ = bf16[128,2176]{1,0:T(8,128)(2,1)S(1)} collective-permute-done((bf16[128,2176]{1,0:T(8,128)(2,1)S(1)}, bf16[128,2176]{1,0:T(8,128)(2,1)S(1)}, u32[]{:S(2)}, u32[]{:S(2)}) %collective-permute-start.4) | collective-permute-done | bytes 557088 | tf_op jit(solution)/shard_map/ppermute | solution.py:363
  36.1 3.5 %collective-permute-done.2 = bf16[128,2176]{1,0:T(8,128)(2,1)S(1)} collective-permute-done((bf16[128,2176]{1,0:T(8,128)(2,1)S(1)}, bf16[128,2176]{1,0:T(8,128)(2,1)S(1)}, u32[]{:S(2)}, u32[]{:S(2)}) %collective-permute-start.2) | collective-permute-done | bytes 557088 | tf_op jit(solution)/shard_map/ppermute | solution.py:363
  39.7 1.4 %collective-permute-start.10 = (bf16[128,2176]{1,0:T(8,128)(2,1)S(1)}, bf16[128,2176]{1,0:T(8,128)(2,1)S(1)}, u32[]{:S(2)}, u32[]{:S(2)}) collective-permute-start(bf16[128,2176]{1,0:T(8,128)(2,1)S(1)} %broadcast_select_fusion.1.refs_2_.refs_8_.refs_6_), channel_id=1, source_target_pairs={{0,2},{1,3},{2,0},{3,1},{4,6},{5,7},{6,4},{7,5},{8,10},{9,11},{10,... | collective-permute-start | bytes 1671176 | tf_op jit(solution)/shard_map/ppermute | solution.py:363
  41.1 1.3 %collective-permute-start.9 = (bf16[128,2176]{1,0:T(8,128)(2,1)S(1)}, bf16[128,2176]{1,0:T(8,128)(2,1)S(1)}, u32[]{:S(2)}, u32[]{:S(2)}) collective-permute-start(bf16[128,2176]{1,0:T(8,128)(2,1)S(1)} %collective-permute-done.6), channel_id=1, source_target_pairs={{4,0},{5,1},{6,2},{7,3},{8,12},{9,13},{10,14},{11,15},{20,16},{21,... | collective-permute-start | bytes 1671176 | tf_op jit(solution)/shard_map/ppermute | solution.py:363
  42.5 11.6 %shard_map.103 = (bf16[128,1024]{1,0:T(8,128)(2,1)}, bf16[128,1024]{1,0:T(8,128)(2,1)}, bf16[128,1024]{1,0:T(8,128)(2,1)}, bf16[128,1024]{1,0:T(8,128)(2,1)}, bf...) custom-call(s32[2]{0:T(128)} %pad_add_fusion.scal, ...), custom_call_target="tpu_custom_call" | custom-call | flops 18119393280 | bytes 1048576 | tf_op jit(solution)/shard_map/pallas_call | solution.py:243
  54.1 1.1 collective-permute-done.9
  56.3 9.5 %shard_map.104 = (bf16[128,1024]{1,0:T(8,128)(2,1)}, bf16[128,1024]{1,0:T(8,128)(2,1)}, bf16[256,1152]{1,0:T(8,128)(2,1)}, bf16[256,1024]{1,0:T(8,128)(2,1)}, bf...) custom-call(s32[2]{0:T(128)} %pad_add_fusion.scal, ...), custom_call_target="tpu_custom_call" | custom-call | flops 7247757312 | bytes 1048576 | tf_op jit(solution)/shard_map/pallas_call | solution.py:243
  67.8 2.1 %collective-permute-done.12.refs_1_.refs_8_ = bf16[128,2176]{1,0:T(8,128)(2,1)S(1)} collective-permute-done((bf16[128,2176]{1,0:T(8,128)(2,1)S(1)}, bf16[128,2176]{1,0:T(8,128)(2,1)S(1)}, u32[]{:S(2)}, u32[]{:S(2)}) %collective-permute-start.12) | collective-permute-done | bytes 557088 | tf_op jit(solution)/shard_map/ppermute | solution.py:363
  71.5 7.6 %shard_map.105 = (bf16[128,1024]{1,0:T(8,128)(2,1)}, bf16[128,1024]{1,0:T(8,128)(2,1)}, bf16[256,1152]{1,0:T(8,128)(2,1)}, bf16[256,1024]{1,0:T(8,128)(2,1)}, bf16[512,1152]{1,0:T(8,128)(2,1)}) custom-call(s32[2]{0:T(128)} %pad_add_fusion.scal, bf16[128,2176]{1,0:T(8,128)(2,1)} %copy-done.7, bf16[128,2176]{1,0:T(8,128)(2,1)} %copy-done.8, ...), custom_call_target="tpu_custom_call" | custom-call | flops 36238786560 | bytes 1048576 | tf_op jit(solution)/shard_map/pallas_call | solution.py:243
  79.4 1.6 %collective-permute-done.17 = bf16[128,1024]{1,0:T(8,128)(2,1)S(1)} collective-permute-done((bf16[128,1024]{1,0:T(8,128)(2,1)}, bf16[128,1024]{1,0:T(8,128)(2,1)S(1)}, u32[]{:S(2)}, u32[]{:S(2)}) %collective-permute-start.17) | collective-permute-done | bytes 262176 | tf_op jit(solution)/shard_map/ppermute | solution.py:363
  81.0 1.1 add_convert_fusion.6
  83.4 6.1 %collective-permute-start.23 = (bf16[128,1024]{1,0:T(8,128)(2,1)S(1)}, bf16[128,1024]{1,0:T(8,128)(2,1)S(1)}, u32[]{:S(2)}, u32[]{:S(2)}) collective-permute-start(bf16[128,1024]{1,0:T(8,128)(2,1)S(1)} %add_convert_fusion.2), channel_id=1, source_target_pairs={{0,4},{1,5},{2,6},{3,7},{12,8},{13,9},{14,10},{15,11},{16,20},{17,... | collective-permute-start | bytes 786440 | tf_op jit(solution)/shard_map/ppermute | solution.py:363
  89.5 1.0 collective-permute-done.18
  90.6 5.3 %collective-permute-start.19 = (bf16[128,1024]{1,0:T(8,128)(2,1)S(1)}, bf16[128,1024]{1,0:T(8,128)(2,1)S(1)}, u32[]{:S(2)}, u32[]{:S(2)}) collective-permute-start(bf16[128,1024]{1,0:T(8,128)(2,1)S(1)} %add_convert_fusion.5), channel_id=1, source_target_pairs={{0,4},{1,5},{2,6},{3,7},{12,8},{13,9},{14,10},{15,11},{16,20},{17,... | collective-permute-start | bytes 786440 | tf_op jit(solution)/shard_map/ppermute | solution.py:363
  96.0 1.4 %collective-permute-start.21 = (bf16[128,1024]{1,0:T(8,128)(2,1)S(1)}, bf16[128,1024]{1,0:T(8,128)(2,1)S(1)}, u32[]{:S(2)}, u32[]{:S(2)}) collective-permute-start(bf16[128,1024]{1,0:T(8,128)(2,1)S(1)} %copy-done.15), channel_id=1, source_target_pairs={{0,2},{1,3},{2,0},{3,1},{4,6},{5,7},{6,4},{7,5},{8,10},{9,11},{10,... | collective-permute-start | bytes 786440 | tf_op jit(solution)/shard_map/ppermute | solution.py:363
  98.2 2.8 %collective-permute-done.19 = bf16[128,1024]{1,0:T(8,128)(2,1)S(1)} collective-permute-done((bf16[128,1024]{1,0:T(8,128)(2,1)S(1)}, bf16[128,1024]{1,0:T(8,128)(2,1)S(1)}, u32[]{:S(2)}, u32[]{:S(2)}) %collective-permute-start.19) | collective-permute-done | bytes 262176 | tf_op jit(solution)/shard_map/ppermute | solution.py:363
  101.0 1.3 %collective-permute-start.25 = (bf16[128,1024]{1,0:T(8,128)(2,1)S(1)}, bf16[128,1024]{1,0:T(8,128)(2,1)S(1)}, u32[]{:S(2)}, u32[]{:S(2)}) collective-permute-start(bf16[128,1024]{1,0:T(8,128)(2,1)S(1)} %add_convert_fusion.4), channel_id=1, source_target_pairs={{4,12},{5,13},{6,14},{7,15},{8,0},{9,1},{10,2},{11,3},{20,28},{21,... | collective-permute-start | bytes 786440 | tf_op jit(solution)/shard_map/ppermute | solution.py:363
  102.3 0.9 collective-permute-done.21
  103.3 2.8 %collective-permute-start.22 = (bf16[128,1024]{1,0:T(8,128)(2,1)S(1)}, bf16[128,1024]{1,0:T(8,128)(2,1)S(1)}, u32[]{:S(2)}, u32[]{:S(2)}) collective-permute-start(bf16[128,1024]{1,0:T(8,128)(2,1)S(1)} %add_convert_fusion.3), channel_id=1, source_target_pairs={{0,4},{1,5},{2,6},{3,7},{4,0},{5,1},{6,2},{7,3},{8,12},{9,13},{10,... | collective-permute-start | bytes 786440 | tf_op jit(solution)/shard_map/ppermute | solution.py:363
  106.2 5.8 %shard_map.106 = bf16[512,1152]{1,0:T(8,128)(2,1)} custom-call(s32[1]{0:T(128)} %bitcast.sides, bf16[128,2176]{1,0:T(8,128)(2,1)} %get-tuple-element.42.refs_0_.refs_6_.refs_4_, bf16[128,2176]{1,0:T(8,128)(2,1)} %copy-done.4, bf16[128,2176]{1,0:T(8,128)(2,1)} %copy-done, bf16[128,2176]{1,0:T(8,128)(2,1)} %copy-done.3, bf16[128,2176]{1,0:T(8,128)(2,1)} %copy-done.5, ...), custom_call_target="tpu_custom_call" | custom-call | flops 1024 | bytes 1024 | tf_op jit(solution)/shard_map/pallas_call | solution.py:304
  112.0 1.4 %collective-permute-start.20 = (bf16[128,1024]{1,0:T(8,128)(2,1)S(1)}, bf16[128,1024]{1,0:T(8,128)(2,1)S(1)}, u32[]{:S(2)}, u32[]{:S(2)}) collective-permute-start(bf16[128,1024]{1,0:T(8,128)(2,1)S(1)} %copy-done.14), channel_id=1, source_target_pairs={{0,2},{1,3},{2,0},{3,1},{4,6},{5,7},{6,4},{7,5},{8,10},{9,11},{10,... | collective-permute-start | bytes 786440 | tf_op jit(solution)/shard_map/ppermute | solution.py:363
  113.4 2.6 %add_bitcast_fusion = (f32[1,384,512]{1,2,0:T(8,128)S(1)}, f32[1,512,384]{2,1,0:T(8,128)}, f32[1,512,384]{2,1,0:T(8,128)}) fusion(bf16[512,1152]{1,0:T(8,128)(2,1)} %shard_map.106, bf16[512,1152]{1,0:T(8,128)(2,1)S(1)} %collective-permute-done.14), kind=kLoop, calls=%fused_computation | loop fusion | flops 1769472 | bytes 4718592 | tf_op jit(solution)/shard_map/broadcast_in_dim | solution.py:418
  116.0 1.1 copy.11
  117.2 1.2 %collective-permute-done.20 = bf16[128,1024]{1,0:T(8,128)(2,1)S(1)} collective-permute-done((bf16[128,1024]{1,0:T(8,128)(2,1)S(1)}, bf16[128,1024]{1,0:T(8,128)(2,1)S(1)}, u32[]{:S(2)}, u32[]{:S(2)}) %collective-permute-start.20) | collective-permute-done | bytes 262176 | tf_op jit(solution)/shard_map/ppermute | solution.py:363
  118.4 0.9 add_convert_fusion
  (69 shorter events, 10.2 us)
Async XLA Ops:
  3.4 31.5 %collective-permute-start.5 = (bf16[512,1152]{1,0:T(8,128)(2,1)}, bf16[512,1152]{1,0:T(8,128)(2,1)}, u32[]{:S(2)}, u32[]{:S(2)}) collective-permute-start(bf16[512,1152]{1,0:T(8,128)(2,1)} %get-tuple-element.45.refs_5_.refs_2_), channel_id=1, source_target_pairs={{0,16},{16,0},{1,17},{17,1},{2,18},{18,2},{3,19},{19,3},{4,20},{20... | collective-permute-start | bytes 3538952 | tf_op jit(solution)/shard_map/ppermute | solution.py:364
  6.4 14.3 %collective-permute-start.3 = (bf16[128,2176]{1,0:T(8,128)(2,1)}, bf16[128,2176]{1,0:T(8,128)(2,1)S(1)}, u32[]{:S(2)}, u32[]{:S(2)}) collective-permute-start(bf16[128,2176]{1,0:T(8,128)(2,1)} %get-tuple-element.42.refs_0_.refs_6_.refs_4_), channel_id=1, source_target_pairs={{0,2},{1,3},{2,0},{3,1},{4,6},{5,7},{6,4},{7,5},{8,10},{9,11},{10,... | collective-permute-start | bytes 1671176 | tf_op jit(solution)/shard_map/ppermute | solution.py:363
  7.9 14.0 %collective-permute-start = (bf16[128,2176]{1,0:T(8,128)(2,1)}, bf16[128,2176]{1,0:T(8,128)(2,1)S(1)}, u32[]{:S(2)}, u32[]{:S(2)}) collective-permute-start(bf16[128,2176]{1,0:T(8,128)(2,1)} %get-tuple-element.42.refs_0_.refs_6_.refs_4_), channel_id=1, source_target_pairs={{0,4},{1,5},{2,6},{3,7},{4,0},{5,1},{6,2},{7,3},{8,12},{9,13},{10,... | collective-permute-start | bytes 1671176 | tf_op jit(solution)/shard_map/ppermute | solution.py:363
  9.5 13.6 %collective-permute-start.1 = (bf16[128,2176]{1,0:T(8,128)(2,1)}, bf16[128,2176]{1,0:T(8,128)(2,1)S(1)}, u32[]{:S(2)}, u32[]{:S(2)}) collective-permute-start(bf16[128,2176]{1,0:T(8,128)(2,1)} %get-tuple-element.42.refs_0_.refs_6_.refs_4_), channel_id=1, source_target_pairs={{4,8},{5,9},{6,10},{7,11},{8,4},{9,5},{10,6},{11,7},{20,24},{21,25... | collective-permute-start | bytes 1671176 | tf_op jit(solution)/shard_map/ppermute | solution.py:363
  20.7 21.7 %copy-start.3 = (bf16[128,2176]{1,0:T(8,128)(2,1)}, bf16[128,2176]{1,0:T(8,128)(2,1)S(1)}, u32[]{:S(2)}) copy-start(bf16[128,2176]{1,0:T(8,128)(2,1)S(1)} %collective-permute-done.3.refs_3_.refs_9_.refs_7_) | copy-start | bytes 1671172
  21.9 20.5 %copy-start.4 = (bf16[128,2176]{1,0:T(8,128)(2,1)}, bf16[128,2176]{1,0:T(8,128)(2,1)S(1)}, u32[]{:S(2)}) copy-start(bf16[128,2176]{1,0:T(8,128)(2,1)S(1)} %collective-permute-done.refs_1_.refs_7_.refs_5_) | copy-start | bytes 1671172
  21.9 13.0 %collective-permute-start.4 = (bf16[128,2176]{1,0:T(8,128)(2,1)S(1)}, bf16[128,2176]{1,0:T(8,128)(2,1)S(1)}, u32[]{:S(2)}, u32[]{:S(2)}) collective-permute-start(bf16[128,2176]{1,0:T(8,128)(2,1)S(1)} %collective-permute-done.refs_1_.refs_7_.refs_5_), channel_id=1, source_target_pairs={{0,2},{1,3},{2,0},{3,1},{4,6},{5,7},{6,4},{7,5},{8,10},{9,11},{10,... | collective-permute-start | bytes 1671176 | tf_op jit(solution)/shard_map/ppermute | solution.py:363
  22.4 12.5 %collective-permute-start.6 = (bf16[128,2176]{1,0:T(8,128)(2,1)S(1)}, bf16[128,2176]{1,0:T(8,128)(2,1)S(1)}, u32[]{:S(2)}, u32[]{:S(2)}) collective-permute-start(bf16[128,2176]{1,0:T(8,128)(2,1)S(1)} %collective-permute-done.refs_1_.refs_7_.refs_5_), channel_id=1, source_target_pairs={{4,8},{5,9},{6,10},{7,11},{8,4},{9,5},{10,6},{11,7},{20,24},{21,25... | collective-permute-start | bytes 1671176 | tf_op jit(solution)/shard_map/ppermute | solution.py:363
  23.1 16.5 %collective-permute-start.2 = (bf16[128,2176]{1,0:T(8,128)(2,1)S(1)}, bf16[128,2176]{1,0:T(8,128)(2,1)S(1)}, u32[]{:S(2)}, u32[]{:S(2)}) collective-permute-start(bf16[128,2176]{1,0:T(8,128)(2,1)S(1)} %collective-permute-done.1), channel_id=1, source_target_pairs={{4,0},{5,1},{6,2},{7,3},{8,12},{9,13},{10,14},{11,15},{20,16},{21,... | collective-permute-start | bytes 1671176 | tf_op jit(solution)/shard_map/ppermute | solution.py:363
  34.9 7.5 %collective-permute-start.7 = (bf16[512,1152]{1,0:T(8,128)(2,1)}, bf16[512,1152]{1,0:T(8,128)(2,1)}, u32[]{:S(2)}, u32[]{:S(2)}) collective-permute-start(bf16[512,1152]{1,0:T(8,128)(2,1)} %get-tuple-element.45.refs_5_.refs_2_), channel_id=1, source_target_pairs={{0,1},{1,0},{2,3},{3,2},{4,5},{5,4},{6,7},{7,6},{8,9},{9,8},{10,11... | collective-permute-start | bytes 3538952 | tf_op jit(solution)/shard_map/ppermute | solution.py:363
  34.9 7.5 %collective-permute-start.8 = (bf16[512,1152]{1,0:T(8,128)(2,1)}, bf16[512,1152]{1,0:T(8,128)(2,1)}, u32[]{:S(2)}, u32[]{:S(2)}) collective-permute-start(bf16[512,1152]{1,0:T(8,128)(2,1)} %collective-permute-done.5.refs_6_.refs_3_), channel_id=1, source_target_pairs={{0,1},{1,0},{2,3},{3,2},{4,5},{5,4},{6,7},{7,6},{8,9},{9,8},{10,11... | collective-permute-start | bytes 3538952 | tf_op jit(solution)/shard_map/ppermute | solution.py:363
  39.7 15.6 %collective-permute-start.10 = (bf16[128,2176]{1,0:T(8,128)(2,1)S(1)}, bf16[128,2176]{1,0:T(8,128)(2,1)S(1)}, u32[]{:S(2)}, u32[]{:S(2)}) collective-permute-start(bf16[128,2176]{1,0:T(8,128)(2,1)S(1)} %broadcast_select_fusion.1.refs_2_.refs_8_.refs_6_), channel_id=1, source_target_pairs={{0,2},{1,3},{2,0},{3,1},{4,6},{5,7},{6,4},{7,5},{8,10},{9,11},{10,... | collective-permute-start | bytes 1671176 | tf_op jit(solution)/shard_map/ppermute | solution.py:363
  41.1 14.1 %collective-permute-start.9 = (bf16[128,2176]{1,0:T(8,128)(2,1)S(1)}, bf16[128,2176]{1,0:T(8,128)(2,1)S(1)}, u32[]{:S(2)}, u32[]{:S(2)}) collective-permute-start(bf16[128,2176]{1,0:T(8,128)(2,1)S(1)} %collective-permute-done.6), channel_id=1, source_target_pairs={{4,0},{5,1},{6,2},{7,3},{8,12},{9,13},{10,14},{11,15},{20,16},{21,... | collective-permute-start | bytes 1671176 | tf_op jit(solution)/shard_map/ppermute | solution.py:363
  55.3 11.3 %collective-permute-start.11 = (bf16[128,2176]{1,0:T(8,128)(2,1)S(1)}, bf16[128,2176]{1,0:T(8,128)(2,1)S(1)}, u32[]{:S(2)}, u32[]{:S(2)}) collective-permute-start(bf16[128,2176]{1,0:T(8,128)(2,1)S(1)} %broadcast_select_fusion.refs_0_.refs_9_.refs_5_), channel_id=1, source_target_pairs={{0,2},{1,3},{2,0},{3,1},{4,6},{5,7},{6,4},{7,5},{8,10},{9,11},{10,... | collective-permute-start | bytes 1671176 | tf_op jit(solution)/shard_map/ppermute | solution.py:363
  66.6 3.9 %collective-permute-start.13 = (bf16[512,1152]{1,0:T(8,128)(2,1)}, bf16[512,1152]{1,0:T(8,128)(2,1)S(1)}, u32[]{:S(2)}, u32[]{:S(2)}) collective-permute-start(bf16[512,1152]{1,0:T(8,128)(2,1)} %get-tuple-element.60), channel_id=1, source_target_pairs={{0,1},{1,0},{2,3},{3,2},{4,5},{5,4},{6,7},{7,6},{8,9},{9,8},{10,11... | collective-permute-start | bytes 3538952 | tf_op jit(solution)/shard_map/ppermute | solution.py:363
  66.6 3.3 %collective-permute-start.12 = (bf16[128,2176]{1,0:T(8,128)(2,1)S(1)}, bf16[128,2176]{1,0:T(8,128)(2,1)S(1)}, u32[]{:S(2)}, u32[]{:S(2)}) collective-permute-start(bf16[128,2176]{1,0:T(8,128)(2,1)S(1)} %collective-permute-done.11.refs_0_.refs_7_), channel_id=1, source_target_pairs={{0,1},{1,0},{2,3},{3,2},{4,5},{5,4},{6,7},{7,6},{8,9},{9,8},{10,11... | collective-permute-start | bytes 1671176 | tf_op jit(solution)/shard_map/ppermute | solution.py:363
  67.1 12.0 %collective-permute-start.15 = (bf16[128,1024]{1,0:T(8,128)(2,1)}, bf16[128,1024]{1,0:T(8,128)(2,1)S(1)}, u32[]{:S(2)}, u32[]{:S(2)}) collective-permute-start(bf16[128,1024]{1,0:T(8,128)(2,1)} %get-tuple-element.65), channel_id=1, source_target_pairs={{0,2},{1,3},{2,0},{3,1},{4,6},{5,7},{6,4},{7,5},{8,10},{9,11},{10,... | collective-permute-start | bytes 786440 | tf_op jit(solution)/shard_map/ppermute | solution.py:363
  69.9 9.3 %collective-permute-start.16 = (bf16[512,1152]{1,0:T(8,128)(2,1)}, bf16[512,1152]{1,0:T(8,128)(2,1)S(1)}, u32[]{:S(2)}, u32[]{:S(2)}) collective-permute-start(bf16[512,1152]{1,0:T(8,128)(2,1)} %get-tuple-element.67), channel_id=1, source_target_pairs={{0,1},{1,0},{2,3},{3,2},{4,5},{5,4},{6,7},{7,6},{8,9},{9,8},{10,11... | collective-permute-start | bytes 3538952 | tf_op jit(solution)/shard_map/ppermute | solution.py:363
  71.5 11.8 %copy-start.10 = (bf16[128,1024]{1,0:T(8,128)(2,1)S(1)}, bf16[128,1024]{1,0:T(8,128)(2,1)}, u32[]{:S(2)}) copy-start(bf16[128,1024]{1,0:T(8,128)(2,1)} %get-tuple-element.79) | copy-start | bytes 786436
  79.2 11.4 %copy-start.2 = (bf16[512,1152]{1,0:T(8,128)(2,1)}, bf16[512,1152]{1,0:T(8,128)(2,1)S(1)}, u32[]{:S(2)}) copy-start(bf16[512,1152]{1,0:T(8,128)(2,1)S(1)} %collective-permute-done.16.refs_15_) | copy-start | bytes 3538948
  79.2 1.8 %collective-permute-start.17 = (bf16[128,1024]{1,0:T(8,128)(2,1)}, bf16[128,1024]{1,0:T(8,128)(2,1)S(1)}, u32[]{:S(2)}, u32[]{:S(2)}) collective-permute-start(bf16[128,1024]{1,0:T(8,128)(2,1)} %get-tuple-element.68), channel_id=1, source_target_pairs={{0,1},{1,0},{2,3},{3,2},{4,5},{5,4},{6,7},{7,6},{8,9},{9,8},{10,11... | collective-permute-start | bytes 786440 | tf_op jit(solution)/shard_map/ppermute | solution.py:363
  81.0 14.9 %copy-start.15 = (bf16[128,1024]{1,0:T(8,128)(2,1)S(1)}, bf16[128,1024]{1,0:T(8,128)(2,1)}, u32[]{:S(2)}) copy-start(bf16[128,1024]{1,0:T(8,128)(2,1)} %get-tuple-element.78) | copy-start | bytes 786436
  82.1 8.4 %collective-permute-start.18 = (bf16[128,1024]{1,0:T(8,128)(2,1)S(1)}, bf16[128,1024]{1,0:T(8,128)(2,1)S(1)}, u32[]{:S(2)}, u32[]{:S(2)}) collective-permute-start(bf16[128,1024]{1,0:T(8,128)(2,1)S(1)} %add_convert_fusion.6), channel_id=1, source_target_pairs={{0,2},{1,3},{2,0},{3,1},{4,6},{5,7},{6,4},{7,5},{8,10},{9,11},{10,... | collective-permute-start | bytes 786440 | tf_op jit(solution)/shard_map/ppermute | solution.py:363
  82.8 30.6 %collective-permute-start.14 = (bf16[512,1152]{1,0:T(8,128)(2,1)}, bf16[512,1152]{1,0:T(8,128)(2,1)S(1)}, u32[]{:S(2)}, u32[]{:S(2)}) collective-permute-start(bf16[512,1152]{1,0:T(8,128)(2,1)} %get-tuple-element.61), channel_id=1, source_target_pairs={{0,16},{16,0},{1,17},{17,1},{2,18},{18,2},{3,19},{19,3},{4,20},{20... | collective-permute-start | bytes 3538952 | tf_op jit(solution)/shard_map/ppermute | solution.py:364
  83.4 14.0 %collective-permute-start.23 = (bf16[128,1024]{1,0:T(8,128)(2,1)S(1)}, bf16[128,1024]{1,0:T(8,128)(2,1)S(1)}, u32[]{:S(2)}, u32[]{:S(2)}) collective-permute-start(bf16[128,1024]{1,0:T(8,128)(2,1)S(1)} %add_convert_fusion.2), channel_id=1, source_target_pairs={{0,4},{1,5},{2,6},{3,7},{12,8},{13,9},{14,10},{15,11},{16,20},{17,... | collective-permute-start | bytes 786440 | tf_op jit(solution)/shard_map/ppermute | solution.py:363
  90.5 12.8 %copy-start.9 = (bf16[128,1024]{1,0:T(8,128)(2,1)S(1)}, bf16[128,1024]{1,0:T(8,128)(2,1)}, u32[]{:S(2)}) copy-start(bf16[128,1024]{1,0:T(8,128)(2,1)} %get-tuple-element.76) | copy-start | bytes 786436
  90.6 10.4 %collective-permute-start.19 = (bf16[128,1024]{1,0:T(8,128)(2,1)S(1)}, bf16[128,1024]{1,0:T(8,128)(2,1)S(1)}, u32[]{:S(2)}, u32[]{:S(2)}) collective-permute-start(bf16[128,1024]{1,0:T(8,128)(2,1)S(1)} %add_convert_fusion.5), channel_id=1, source_target_pairs={{0,4},{1,5},{2,6},{3,7},{12,8},{13,9},{14,10},{15,11},{16,20},{17,... | collective-permute-start | bytes 786440 | tf_op jit(solution)/shard_map/ppermute | solution.py:363
  96.0 7.3 %collective-permute-start.21 = (bf16[128,1024]{1,0:T(8,128)(2,1)S(1)}, bf16[128,1024]{1,0:T(8,128)(2,1)S(1)}, u32[]{:S(2)}, u32[]{:S(2)}) collective-permute-start(bf16[128,1024]{1,0:T(8,128)(2,1)S(1)} %copy-done.15), channel_id=1, source_target_pairs={{0,2},{1,3},{2,0},{3,1},{4,6},{5,7},{6,4},{7,5},{8,10},{9,11},{10,... | collective-permute-start | bytes 786440 | tf_op jit(solution)/shard_map/ppermute | solution.py:363
  97.5 19.7 %collective-permute-start.24 = (bf16[128,1024]{1,0:T(8,128)(2,1)S(1)}, bf16[128,1024]{1,0:T(8,128)(2,1)S(1)}, u32[]{:S(2)}, u32[]{:S(2)}) collective-permute-start(bf16[128,1024]{1,0:T(8,128)(2,1)S(1)} %add_convert_fusion.1), channel_id=1, source_target_pairs={{4,8},{5,9},{6,10},{7,11},{8,4},{9,5},{10,6},{11,7},{20,24},{21,25... | collective-permute-start | bytes 786440 | tf_op jit(solution)/shard_map/ppermute | solution.py:363
  101.0 17.4 %collective-permute-start.25 = (bf16[128,1024]{1,0:T(8,128)(2,1)S(1)}, bf16[128,1024]{1,0:T(8,128)(2,1)S(1)}, u32[]{:S(2)}, u32[]{:S(2)}) collective-permute-start(bf16[128,1024]{1,0:T(8,128)(2,1)S(1)} %add_convert_fusion.4), channel_id=1, source_target_pairs={{4,12},{5,13},{6,14},{7,15},{8,0},{9,1},{10,2},{11,3},{20,28},{21,... | collective-permute-start | bytes 786440 | tf_op jit(solution)/shard_map/ppermute | solution.py:363
  103.3 13.8 %collective-permute-start.22 = (bf16[128,1024]{1,0:T(8,128)(2,1)S(1)}, bf16[128,1024]{1,0:T(8,128)(2,1)S(1)}, u32[]{:S(2)}, u32[]{:S(2)}) collective-permute-start(bf16[128,1024]{1,0:T(8,128)(2,1)S(1)} %add_convert_fusion.3), channel_id=1, source_target_pairs={{0,4},{1,5},{2,6},{3,7},{4,0},{5,1},{6,2},{7,3},{8,12},{9,13},{10,... | collective-permute-start | bytes 786440 | tf_op jit(solution)/shard_map/ppermute | solution.py:363
  112.0 6.4 %collective-permute-start.20 = (bf16[128,1024]{1,0:T(8,128)(2,1)S(1)}, bf16[128,1024]{1,0:T(8,128)(2,1)S(1)}, u32[]{:S(2)}, u32[]{:S(2)}) collective-permute-start(bf16[128,1024]{1,0:T(8,128)(2,1)S(1)} %copy-done.14), channel_id=1, source_target_pairs={{0,2},{1,3},{2,0},{3,1},{4,6},{5,7},{6,4},{7,5},{8,10},{9,11},{10,... | collective-permute-start | bytes 786440 | tf_op jit(solution)/shard_map/ppermute | solution.py:363
  (10 other events, 37.4 us)
